TPU v7x, 32 devices: a whole 2x2x4 slice. The times are simulated.
32 devices in a mesh: seq: 16 (over z, y, x), head: 2 (over core).
Axes of the slice: x: 2, y: 2, z: 4, core: 2. Of those that a mesh axis runs over, the one named last changes fastest.
Arguments:
- queries: bfloat16 [2048, 2048], P('seq', 'head'), may hold values from -8 to 8
- key_tokens: bfloat16 [2048, 2048], P('seq', 'head'), may hold values from -8 to 8
- value_tokens: bfloat16 [2048, 2048], P('seq', 'head'), may hold values from -6 to 6
- out_weight: bfloat16 [2048, 2048], P(None, 'head'), may hold values from -0.125 to 0.125
- output_grad: bfloat16 [2048, 2048], P('seq', 'head'), may hold values from -6 to 6
Outputs:
- output: bfloat16 [2048, 2048], P('seq', 'head')
- query_grad: bfloat16 [2048, 2048], P('seq', 'head')
- key_grad: bfloat16 [2048, 2048], P('seq', 'head')
- value_grad: bfloat16 [2048, 2048], P('seq', 'head')
All inputs are finite; a program needn't handle non-finite values.
Results may differ from a plain program's by a relative error of at most 0.024.
Values may be sent and summed in bfloat16 or wider, within the bound.
No kernel may reach another device: no remote copies, remote signals or barrier semaphores. Data moves between devices by JAX's collectives and lax.ppermute only.
A program may use at most 128 MiB of HBM per device.

v0:
```python
import math

import jax
import jax.numpy as jnp
from jax import lax
from jax.sharding import PartitionSpec as P

HDIM = 128
BLOCK = 128


def from_partner(array, axis, bit):
    return lax.ppermute(array, axis, [(i, i ^ 1 << bit) for i in range(lax.axis_size(axis))])


def coarsen(tokens, run_length, summed):
    grouped = tokens.astype(jnp.float32).reshape(-1, run_length, tokens.shape[1])
    if summed:
        reduced = jnp.sum(grouped, axis=1)
    else:
        reduced = jnp.mean(grouped, axis=1)
    return reduced.astype(jnp.bfloat16)


def split_rows(packed, counts):
    pieces = []
    first = 0
    for count in counts:
        pieces.append(packed[first : first + count])
        first = first + count
    return pieces


def join_pair(mine, other, upper):
    return jnp.where(
        upper, jnp.concatenate([other, mine], axis=0), jnp.concatenate([mine, other], axis=0)
    )


def contract_rows(left, right):
    return lax.dot_general(
        left, right, (((0,), (0,)), ((), ())), preferred_element_type=jnp.float32
    )


def contract_cols(left, right):
    return lax.dot_general(
        left, right, (((1,), (1,)), ((), ())), preferred_element_type=jnp.float32
    )


def on_device(queries, key_tokens, value_tokens, out_weight, output_grad):
    tok_rows, columns = queries.shape
    seq_count = lax.axis_size("seq")
    level_count = seq_count.bit_length() - 1
    my_index = lax.axis_index("seq")
    head_count = columns // HDIM
    inv_scale = 1.0 / math.sqrt(HDIM)
    row_counts = [BLOCK >> level for level in range(level_count)]
    run_lengths = [tok_rows // count for count in row_counts]
    piece_keys = [coarsen(key_tokens, run_lengths[level], False) for level in range(level_count)]
    piece_values = [coarsen(value_tokens, run_lengths[level], True) for level in range(level_count)]
    sibling_keys = [None] * level_count
    sibling_values = [None] * level_count
    held_keys = list(piece_keys[:level_count])
    held_values = list(piece_values[:level_count])
    for step in range(level_count):
        counts = [held_keys[level].shape[0] for level in range(step, level_count)]
        key_pack = jnp.concatenate(held_keys[step:level_count], axis=0)
        value_pack = jnp.concatenate(held_values[step:level_count], axis=0)
        got_keys, got_values = from_partner((key_pack, value_pack), "seq", step)
        upper = my_index >> step & 1 == 1
        key_parts = split_rows(got_keys, counts)
        value_parts = split_rows(got_values, counts)
        sibling_keys[step] = key_parts[0]
        sibling_values[step] = value_parts[0]
        for level in range(step + 1, level_count):
            held_keys[level] = join_pair(held_keys[level], key_parts[level - step], upper)
            held_values[level] = join_pair(held_values[level], value_parts[level - step], upper)
    key_list = jnp.concatenate([key_tokens] + sibling_keys, axis=0)
    value_list = jnp.concatenate([value_tokens] + sibling_values, axis=0)
    grad_total = jnp.dot(
        lax.all_gather(output_grad, "head", axis=1, tiled=True),
        out_weight,
        preferred_element_type=jnp.float32,
    )
    grad_attended = grad_total.astype(jnp.bfloat16)
    attended_cols = []
    query_cols = []
    key_local_cols = []
    value_local_cols = []
    key_coarse_cols = []
    value_coarse_cols = []
    for head in range(head_count):
        first_col = head * HDIM
        query_part = queries[:, first_col : first_col + HDIM]
        key_part = key_list[:, first_col : first_col + HDIM]
        value_part = value_list[:, first_col : first_col + HDIM]
        grad_part = grad_attended[:, first_col : first_col + HDIM]
        scores = contract_cols(query_part, key_part) * inv_scale
        shifted = jnp.exp(scores - jnp.max(scores, axis=1, keepdims=True))
        prob = shifted / jnp.sum(shifted, axis=1, keepdims=True)
        prob_low = prob.astype(jnp.bfloat16)
        attended_cols.append(
            jnp.dot(prob_low, value_part, preferred_element_type=jnp.float32).astype(jnp.bfloat16)
        )
        prob_grad = contract_cols(grad_part, value_part)
        centre = jnp.sum(prob * prob_grad, axis=1, keepdims=True)
        score_grad = (prob * (prob_grad - centre) * inv_scale).astype(jnp.bfloat16)
        query_cols.append(
            jnp.dot(score_grad, key_part, preferred_element_type=jnp.float32).astype(jnp.bfloat16)
        )
        key_local_cols.append(contract_rows(score_grad[:, :tok_rows], query_part))
        key_coarse_cols.append(contract_rows(score_grad[:, tok_rows:], query_part))
        value_local_cols.append(contract_rows(prob_low[:, :tok_rows], grad_part))
        value_coarse_cols.append(contract_rows(prob_low[:, tok_rows:], grad_part))
    attended = jnp.concatenate(attended_cols, axis=1)
    query_grad = jnp.concatenate(query_cols, axis=1)
    key_local = jnp.concatenate(key_local_cols, axis=1)
    value_local = jnp.concatenate(value_local_cols, axis=1)
    key_coarse = jnp.concatenate(key_coarse_cols, axis=1)
    value_coarse = jnp.concatenate(value_coarse_cols, axis=1)
    partial_out = contract_cols(attended, out_weight)
    output = lax.psum_scatter(
        partial_out.astype(jnp.bfloat16), "head", scatter_dimension=1, tiled=True
    )
    coarse_key_terms = [
        key_coarse[level * BLOCK : (level + 1) * BLOCK] for level in range(level_count)
    ]
    coarse_value_terms = [
        value_coarse[level * BLOCK : (level + 1) * BLOCK] for level in range(level_count)
    ]
    key_share = [None] * level_count
    value_share = [None] * level_count
    key_blocks = [
        coarse_key_terms[level].reshape(1 << level, row_counts[level], columns)
        for level in range(level_count)
    ]
    value_blocks = [
        coarse_value_terms[level].reshape(1 << level, row_counts[level], columns)
        for level in range(level_count)
    ]
    for step in range(level_count):
        my_bit = my_index >> step & 1
        key_sends = [key_blocks[step].reshape(-1, columns)]
        value_sends = [value_blocks[step].reshape(-1, columns)]
        key_keeps = []
        value_keeps = []
        counts = [row_counts[step]]
        for level in range(step + 1, level_count):
            paired_keys = key_blocks[level].reshape(-1, 2, row_counts[level], columns)
            paired_values = value_blocks[level].reshape(-1, 2, row_counts[level], columns)
            key_keeps.append(lax.dynamic_index_in_dim(paired_keys, my_bit, 1, keepdims=False))
            value_keeps.append(lax.dynamic_index_in_dim(paired_values, my_bit, 1, keepdims=False))
            key_sends.append(
                lax.dynamic_index_in_dim(paired_keys, 1 - my_bit, 1, keepdims=False).reshape(
                    -1, columns
                )
            )
            value_sends.append(
                lax.dynamic_index_in_dim(paired_values, 1 - my_bit, 1, keepdims=False).reshape(
                    -1, columns
                )
            )
            counts.append(key_sends[-1].shape[0])
        key_pack = jnp.concatenate(key_sends, axis=0)
        value_pack = jnp.concatenate(value_sends, axis=0)
        got_keys, got_values = (
            from_partner(key_pack.astype(jnp.bfloat16), "seq", step).astype(key_pack.dtype),
            from_partner(value_pack.astype(jnp.bfloat16), "seq", step).astype(value_pack.dtype),
        )
        key_parts = split_rows(got_keys, counts)
        value_parts = split_rows(got_values, counts)
        key_share[step] = key_parts[0]
        value_share[step] = value_parts[0]
        for level in range(step + 1, level_count):
            kept_keys = key_keeps[level - step - 1]
            kept_values = value_keeps[level - step - 1]
            key_blocks[level] = kept_keys + key_parts[level - step].reshape(kept_keys.shape)
            value_blocks[level] = kept_values + value_parts[level - step].reshape(kept_values.shape)
    key_sum = key_local
    value_sum = value_local
    for level in range(level_count):
        spread_shape = (row_counts[level], run_lengths[level], columns)
        key_part = jnp.broadcast_to(
            (key_share[level] / run_lengths[level])[:, None, :], spread_shape
        )
        value_part = jnp.broadcast_to(value_share[level][:, None, :], spread_shape)
        key_sum = key_sum + key_part.reshape(tok_rows, columns)
        value_sum = value_sum + value_part.reshape(tok_rows, columns)
    return (output, query_grad, key_sum.astype(jnp.bfloat16), value_sum.astype(jnp.bfloat16))


def solution(mesh):
    placed = (
        P("seq", "head"),
        P("seq", "head"),
        P("seq", "head"),
        P(None, "head"),
        P("seq", "head"),
    )
    return jax.shard_map(
        on_device,
        mesh=mesh,
        in_specs=placed,
        out_specs=(P("seq", "head"), P("seq", "head"), P("seq", "head"), P("seq", "head")),
        check_vma=False,
    )
```

profile of v0, /device:TPU:0, one launch (start us, length us, event | category | flops | bytes accessed | tf_op | source)
XLA Modules:
  0.0 210.1 jit_solution(6395635746020733649)
XLA Ops:
  7.2 1.1 bitcast_reduce_fusion.1
  8.3 1.1 reshape.215
  9.5 1.4 reshape.214
  12.7 2.9 %collective-permute-start = (bf16[240,1024]{1,0:T(8,128)(2,1)}, bf16[240,1024]{1,0:T(8,128)(2,1)S(1)}, u32[]{:S(2)}, u32[]{:S(2)}) collective-permute-start(bf16[240,1024]{1,0:T(8,128)(2,1)} %pad_maximum_fusion.2), channel_id=1, source_target_pairs={{0,2},{2,0},{4,6},{6,4},{8,10},{10,8},{12,14},{14,12},{16,18},{18,... | collective-permute-start | bytes 1474568 | tf_op jit(solution)/shard_map/ppermute | solution.py:13
  18.2 2.3 %all_gather.3 = bf16[128,2048]{1,0:T(8,128)(2,1)S(1)} all-gather(bf16[128,1024]{1,0:T(8,128)(2,1)S(1)} %copy-done.35), channel_id=1, replica_groups=mesh['seq'=16,'head'=2] {'head'}, dimensions={1}, use_global_device_ids=true | all-gather | bytes 786432 | tf_op jit(solution)/shard_map/all_gather | solution.py:83
  20.5 3.0 %convolution_convert_fusion.1 = bf16[128,1024]{1,0:T(8,128)(2,1)S(1)} fusion(bf16[128,2048]{1,0:T(8,128)(2,1)S(1)} %all_gather.3, bf16[2048,1024]{1,0:T(8,128)(2,1)} %param.8), kind=kOutput, calls=%fused_computation.17 | convolution fusion | flops 537001984 | bytes 4980736 | tf_op jit(solution)/shard_map/dot_general | solution.py:82
  24.2 3.7 %collective-permute-done = bf16[240,1024]{1,0:T(8,128)(2,1)S(1)} collective-permute-done((bf16[240,1024]{1,0:T(8,128)(2,1)}, bf16[240,1024]{1,0:T(8,128)(2,1)S(1)}, u32[]{:S(2)}, u32[]{:S(2)}) %collective-permute-start) | collective-permute-done | bytes 491552 | tf_op jit(solution)/shard_map/ppermute | solution.py:13
  28.1 2.2 %collective-permute-start.1 = (bf16[224,1024]{1,0:T(8,128)(2,1)S(1)}, bf16[224,1024]{1,0:T(8,128)(2,1)S(1)}, u32[]{:S(2)}, u32[]{:S(2)}) collective-permute-start(bf16[224,1024]{1,0:T(8,128)(2,1)S(1)} %pad_maximum_fusion.4), channel_id=1, source_target_pairs={{0,4},{2,6},{4,0},{6,2},{8,12},{10,14},{12,8},{14,10},{16,20},{18,... | collective-permute-start | bytes 1376264 | tf_op jit(solution)/shard_map/ppermute | solution.py:13
  30.2 7.4 %collective-permute-done.4 = bf16[240,1024]{1,0:T(8,128)(2,1)S(1)} collective-permute-done((bf16[240,1024]{1,0:T(8,128)(2,1)}, bf16[240,1024]{1,0:T(8,128)(2,1)S(1)}, u32[]{:S(2)}, u32[]{:S(2)}) %collective-permute-start.4) | collective-permute-done | bytes 491552 | tf_op jit(solution)/shard_map/ppermute | solution.py:13
  37.8 1.8 collective-permute-start.5
  39.9 1.6 collective-permute-start.2
  41.5 8.1 %collective-permute-done.5 = bf16[224,1024]{1,0:T(8,128)(2,1)S(1)} collective-permute-done((bf16[224,1024]{1,0:T(8,128)(2,1)S(1)}, bf16[224,1024]{1,0:T(8,128)(2,1)S(1)}, u32[]{:S(2)}, u32[]{:S(2)}) %collective-permute-start.5) | collective-permute-done | bytes 458784 | tf_op jit(solution)/shard_map/ppermute | solution.py:13
  49.7 1.6 collective-permute-start.6
  51.4 2.7 %collective-permute-start.3 = (bf16[128,1024]{1,0:T(8,128)(2,1)S(1)}, bf16[128,1024]{1,0:T(8,128)(2,1)S(1)}, u32[]{:S(2)}, u32[]{:S(2)}) collective-permute-start(bf16[128,1024]{1,0:T(8,128)(2,1)S(1)} %maximum_select_fusion.2), channel_id=1, source_target_pairs={{0,16},{2,18},{4,20},{6,22},{8,24},{10,26},{12,28},{14,30},{16,0},... | collective-permute-start | bytes 786440 | tf_op jit(solution)/shard_map/ppermute | solution.py:13
  54.1 10.7 %collective-permute-done.6 = bf16[192,1024]{1,0:T(8,128)(2,1)S(1)} collective-permute-done((bf16[192,1024]{1,0:T(8,128)(2,1)S(1)}, bf16[192,1024]{1,0:T(8,128)(2,1)S(1)}, u32[]{:S(2)}, u32[]{:S(2)}) %collective-permute-start.6) | collective-permute-done | bytes 393248 | tf_op jit(solution)/shard_map/ppermute | solution.py:13
  64.9 1.4 collective-permute-start.7
  68.8 8.8 %collective-permute-done.7 = bf16[128,1024]{1,0:T(8,128)(2,1)S(1)} collective-permute-done((bf16[128,1024]{1,0:T(8,128)(2,1)S(1)}, bf16[128,1024]{1,0:T(8,128)(2,1)S(1)}, u32[]{:S(2)}, u32[]{:S(2)}) %collective-permute-start.7) | collective-permute-done | bytes 262176 | tf_op jit(solution)/shard_map/ppermute | solution.py:13
  93.9 2.3 %convolution_convert_fusion = bf16[128,2048]{1,0:T(8,128)(2,1)} fusion(bf16[128,1024]{0,1:T(8,128)(2,1)S(1)} %fusion.8, bf16[2048,1024]{1,0:T(8,128)(2,1)S(1)} %copy-done), kind=kOutput, calls=%fused_computation | convolution fusion | flops 537133056 | bytes 4980736 | tf_op jit(solution)/shard_map/dot_general | solution.py:47
  96.3 1.9 fusion.6
  98.2 1.9 fusion.5
  100.1 1.9 fusion.4
  101.9 2.0 fusion.3
  103.9 1.9 fusion.2
  105.8 1.9 fusion.1
  107.7 1.8 fusion
  109.5 1.5 convolution_dynamic-update-slice_fusion.30
  111.0 1.5 convolution_dynamic-update-slice_fusion.29
  112.5 1.5 convolution_dynamic-update-slice_fusion.28
  114.1 1.5 convolution_dynamic-update-slice_fusion.27
  115.6 1.6 convolution_dynamic-update-slice_fusion.26
  117.1 1.0 copy.292
  118.1 1.0 copy.295
  125.8 1.2 pad_maximum_fusion
  127.0 1.1 copy.298
  128.9 1.4 collective-permute-start.12
  131.0 1.5 convolution_dynamic-update-slice_fusion.25
  133.4 1.0 copy.307
  135.5 1.5 convolution_dynamic-update-slice_fusion.24
  137.0 9.7 %collective-permute-done.12 = bf16[320,1024]{1,0:T(8,128)(2,1)} collective-permute-done((bf16[320,1024]{1,0:T(8,128)(2,1)S(1)}, bf16[320,1024]{1,0:T(8,128)(2,1)}, u32[]{:S(2)}, u32[]{:S(2)}) %collective-permute-start.12) | collective-permute-done | bytes 655392 | tf_op jit(solution)/shard_map/ppermute | solution.py:13
  146.8 1.4 copy.306
  148.3 1.1 fusion.196
  149.4 9.0 %collective-permute-done.8 = bf16[320,1024]{1,0:T(8,128)(2,1)} collective-permute-done((bf16[320,1024]{1,0:T(8,128)(2,1)}, bf16[320,1024]{1,0:T(8,128)(2,1)}, u32[]{:S(2)}, u32[]{:S(2)}) %collective-permute-start.8) | collective-permute-done | bytes 655392 | tf_op jit(solution)/shard_map/ppermute | solution.py:13
  158.4 1.0 fusion.197
  160.3 1.3 convert_element_type.218
  161.6 1.1 copy-done.4
  163.4 1.6 collective-permute-start.9
  165.2 2.0 copy.311
  167.2 1.3 copy.310
  168.6 1.1 bitcast_add_fusion.1
  169.9 1.1 bitcast_add_fusion
  171.2 1.1 fusion.66
  174.0 1.0 convert_element_type.219
  175.7 1.3 collective-permute-start.10
  177.6 1.4 collective-permute-done.13
  179.8 1.0 copy.314
  181.7 1.2 copy.315
  185.7 2.0 collective-permute-start.14
  188.6 1.7 collective-permute-done.14
  190.4 3.6 %collective-permute-start.15 = (bf16[16,1024]{1,0:T(8,128)(2,1)S(1)}, bf16[16,1024]{1,0:T(8,128)(2,1)S(1)}, u32[]{:S(2)}, u32[]{:S(2)}) collective-permute-start(bf16[16,1024]{1,0:T(8,128)(2,1)S(1)} %fusion.126), channel_id=1, source_target_pairs={{0,16},{2,18},{4,20},{6,22},{8,24},{10,26},{12,28},{14,30},{16,0},... | collective-permute-start | bytes 98312 | tf_op jit(solution)/shard_map/ppermute | solution.py:13
  194.5 1.0 reshape.242
  195.5 2.1 copy.317
  197.7 1.0 copy.318
  198.7 1.6 fusion.21
  201.2 2.1 fusion.25
  (282 shorter events, 46.1 us)
Async XLA Ops:
  7.2 196.1 %reduce-scatter.2.cloned.1.call-start = ((), (), s32[]{:S(2)}) async-start(), calls=%async_computation.1 | async-start | bytes 786432 | tf_op jit(solution)/shard_map/reduce_scatter | solution.py:124
  9.5 2.4 %copy-start.1 = (bf16[128,1024]{1,0:T(8,128)(2,1)S(1)}, bf16[128,1024]{1,0:T(8,128)(2,1)}, u32[]{:S(2)}) copy-start(bf16[128,1024]{1,0:T(8,128)(2,1)} %param.6) | copy-start | bytes 786436
  11.2 4.5 %copy-start.2 = (bf16[128,1024]{1,0:T(8,128)(2,1)S(1)}, bf16[128,1024]{1,0:T(8,128)(2,1)}, u32[]{:S(2)}) copy-start(bf16[128,1024]{1,0:T(8,128)(2,1)} %param.7) | copy-start | bytes 786436
  12.7 15.2 %collective-permute-start = (bf16[240,1024]{1,0:T(8,128)(2,1)}, bf16[240,1024]{1,0:T(8,128)(2,1)S(1)}, u32[]{:S(2)}, u32[]{:S(2)}) collective-permute-start(bf16[240,1024]{1,0:T(8,128)(2,1)} %pad_maximum_fusion.2), channel_id=1, source_target_pairs={{0,2},{2,0},{4,6},{6,4},{8,10},{10,8},{12,14},{14,12},{16,18},{18,... | collective-permute-start | bytes 1474568 | tf_op jit(solution)/shard_map/ppermute | solution.py:13
  16.3 1.8 copy-start.35
  18.2 19.4 %collective-permute-start.4 = (bf16[240,1024]{1,0:T(8,128)(2,1)}, bf16[240,1024]{1,0:T(8,128)(2,1)S(1)}, u32[]{:S(2)}, u32[]{:S(2)}) collective-permute-start(bf16[240,1024]{1,0:T(8,128)(2,1)} %pad_maximum_fusion.3), channel_id=1, source_target_pairs={{0,2},{2,0},{4,6},{6,4},{8,10},{10,8},{12,14},{14,12},{16,18},{18,... | collective-permute-start | bytes 1474568 | tf_op jit(solution)/shard_map/ppermute | solution.py:13
  28.1 11.6 %collective-permute-start.1 = (bf16[224,1024]{1,0:T(8,128)(2,1)S(1)}, bf16[224,1024]{1,0:T(8,128)(2,1)S(1)}, u32[]{:S(2)}, u32[]{:S(2)}) collective-permute-start(bf16[224,1024]{1,0:T(8,128)(2,1)S(1)} %pad_maximum_fusion.4), channel_id=1, source_target_pairs={{0,4},{2,6},{4,0},{6,2},{8,12},{10,14},{12,8},{14,10},{16,20},{18,... | collective-permute-start | bytes 1376264 | tf_op jit(solution)/shard_map/ppermute | solution.py:13
  37.6 2.0 copy-start.37
  37.8 11.8 %collective-permute-start.5 = (bf16[224,1024]{1,0:T(8,128)(2,1)S(1)}, bf16[224,1024]{1,0:T(8,128)(2,1)S(1)}, u32[]{:S(2)}, u32[]{:S(2)}) collective-permute-start(bf16[224,1024]{1,0:T(8,128)(2,1)S(1)} %pad_maximum_fusion.5), channel_id=1, source_target_pairs={{0,4},{2,6},{4,0},{6,2},{8,12},{10,14},{12,8},{14,10},{16,20},{18,... | collective-permute-start | bytes 1376264 | tf_op jit(solution)/shard_map/ppermute | solution.py:13
  39.9 11.5 %collective-permute-start.2 = (bf16[192,1024]{1,0:T(8,128)(2,1)S(1)}, bf16[192,1024]{1,0:T(8,128)(2,1)S(1)}, u32[]{:S(2)}, u32[]{:S(2)}) collective-permute-start(bf16[192,1024]{1,0:T(8,128)(2,1)S(1)} %pad_maximum_fusion.6), channel_id=1, source_target_pairs={{0,8},{2,10},{4,12},{6,14},{8,0},{10,2},{12,4},{14,6},{16,24},{18,... | collective-permute-start | bytes 1179656 | tf_op jit(solution)/shard_map/ppermute | solution.py:13
  49.7 15.1 %collective-permute-start.6 = (bf16[192,1024]{1,0:T(8,128)(2,1)S(1)}, bf16[192,1024]{1,0:T(8,128)(2,1)S(1)}, u32[]{:S(2)}, u32[]{:S(2)}) collective-permute-start(bf16[192,1024]{1,0:T(8,128)(2,1)S(1)} %pad_maximum_fusion.7), channel_id=1, source_target_pairs={{0,8},{2,10},{4,12},{6,14},{8,0},{10,2},{12,4},{14,6},{16,24},{18,... | collective-permute-start | bytes 1179656 | tf_op jit(solution)/shard_map/ppermute | solution.py:13
  51.4 14.9 %copy-start.6 = (bf16[128,1024]{1,0:T(8,128)(2,1)S(1)}, bf16[128,1024]{1,0:T(8,128)(2,1)}, u32[]{:S(2)}) copy-start(bf16[128,1024]{1,0:T(8,128)(2,1)} %param.5) | copy-start | bytes 786436
  51.4 14.8 %collective-permute-start.3 = (bf16[128,1024]{1,0:T(8,128)(2,1)S(1)}, bf16[128,1024]{1,0:T(8,128)(2,1)S(1)}, u32[]{:S(2)}, u32[]{:S(2)}) collective-permute-start(bf16[128,1024]{1,0:T(8,128)(2,1)S(1)} %maximum_select_fusion.2), channel_id=1, source_target_pairs={{0,16},{2,18},{4,20},{6,22},{8,24},{10,26},{12,28},{14,30},{16,0},... | collective-permute-start | bytes 786440 | tf_op jit(solution)/shard_map/ppermute | solution.py:13
  64.9 12.8 %collective-permute-start.7 = (bf16[128,1024]{1,0:T(8,128)(2,1)S(1)}, bf16[128,1024]{1,0:T(8,128)(2,1)S(1)}, u32[]{:S(2)}, u32[]{:S(2)}) collective-permute-start(bf16[128,1024]{1,0:T(8,128)(2,1)S(1)} %maximum_select_fusion.5), channel_id=1, source_target_pairs={{0,16},{2,18},{4,20},{6,22},{8,24},{10,26},{12,28},{14,30},{16,0},... | collective-permute-start | bytes 786440 | tf_op jit(solution)/shard_map/ppermute | solution.py:13
  66.3 15.1 %copy-start.10 = (bf16[640,1024]{1,0:T(8,128)(2,1)}, bf16[640,1024]{1,0:T(8,128)(2,1)S(1)}, u32[]{:S(2)}) copy-start(bf16[640,1024]{1,0:T(8,128)(2,1)S(1)} %constant_dynamic-update-slice_fusion) | copy-start | bytes 3932164
  83.5 0.7 copy-start.26
  83.6 0.8 copy-start.27
  83.7 0.9 copy-start.28
  83.8 1.1 copy-start.29
  83.9 1.2 copy-start.30
  84.0 1.6 copy-start.23
  84.1 1.7 copy-start.25
  88.6 5.3 %copy-start = (bf16[2048,1024]{1,0:T(8,128)(2,1)S(1)}, bf16[2048,1024]{1,0:T(8,128)(2,1)}, u32[]{:S(2)}) copy-start(bf16[2048,1024]{1,0:T(8,128)(2,1)} %param.8) | copy-start | bytes 12582916
  91.0 0.8 copy-start.22
  96.2 11.5 %copy-start.24 = (bf16[128,640]{0,1:T(8,128)(2,1)S(1)}, bf16[128,640]{0,1:T(8,128)(2,1)}, u32[]{:S(2)}) copy-start(bf16[128,640]{0,1:T(8,128)(2,1)} %copy-done.23) | copy-start | bytes 491524
  118.1 2.0 copy-start.8
  119.2 1.2 copy-start.11
  127.0 1.3 copy-start.15
  127.0 1.3 copy-start.16
  128.7 3.9 %copy-start.36 = (bf16[128,1024]{0,1:T(8,128)(2,1)S(1)}, bf16[128,1024]{0,1:T(8,128)(2,1)}, u32[]{:S(2)}) copy-start(bf16[128,1024]{0,1:T(8,128)(2,1)} %fusion) | copy-start | bytes 786436
  128.9 17.8 %collective-permute-start.12 = (bf16[320,1024]{1,0:T(8,128)(2,1)S(1)}, bf16[320,1024]{1,0:T(8,128)(2,1)}, u32[]{:S(2)}, u32[]{:S(2)}) collective-permute-start(bf16[320,1024]{1,0:T(8,128)(2,1)S(1)} %copy.305), channel_id=1, source_target_pairs={{0,2},{2,0},{4,6},{6,4},{8,10},{10,8},{12,14},{14,12},{16,18},{18,... | collective-permute-start | bytes 1966088 | tf_op jit(solution)/shard_map/ppermute | solution.py:13
  130.4 28.0 %collective-permute-start.8 = (bf16[320,1024]{1,0:T(8,128)(2,1)}, bf16[320,1024]{1,0:T(8,128)(2,1)}, u32[]{:S(2)}, u32[]{:S(2)}) collective-permute-start(bf16[320,1024]{1,0:T(8,128)(2,1)} %copy.298), channel_id=1, source_target_pairs={{0,2},{2,0},{4,6},{6,4},{8,10},{10,8},{12,14},{14,12},{16,18},{18,... | collective-permute-start | bytes 1966088 | tf_op jit(solution)/shard_map/ppermute | solution.py:13
  148.3 11.1 %copy-start.13 = (f32[128,1024]{1,0:T(8,128)S(1)}, f32[128,1024]{1,0:T(8,128)}, u32[]{:S(2)}) copy-start(f32[128,1024]{1,0:T(8,128)} %copy.294) | copy-start | bytes 1572868
  149.4 10.1 %copy-start.14 = (f32[4,1,16,1024]{3,2,1,0:T(8,128)S(1)}, f32[4,1,16,1024]{3,2,1,0:T(8,128)}, u32[]{:S(2)}) copy-start(f32[4,1,16,1024]{3,2,1,0:T(8,128)} %constant_dynamic-slice_fusion.4) | copy-start | bytes 786436
  159.5 0.7 copy-start.20
  159.5 0.7 copy-start.18
  159.6 3.1 %copy-start.12 = (f32[128,1024]{1,0:T(8,128)S(1)}, f32[128,1024]{1,0:T(8,128)}, u32[]{:S(2)}) copy-start(f32[128,1024]{1,0:T(8,128)} %copy.292) | copy-start | bytes 1572868
  160.3 4.7 %copy-start.9 = (f32[64,1024]{0,1:T(8,128)S(1)}, f32[64,1024]{0,1:T(8,128)}, u32[]{:S(2)}) copy-start(f32[64,1024]{0,1:T(8,128)} %get-tuple-element.30) | copy-start | bytes 786436
  161.6 1.1 copy-start.4
  163.4 9.6 %collective-permute-start.9 = (bf16[128,1024]{1,0:T(8,128)(2,1)}, bf16[128,1024]{1,0:T(8,128)(2,1)}, u32[]{:S(2)}, u32[]{:S(2)}) collective-permute-start(bf16[128,1024]{1,0:T(8,128)(2,1)} %pad_maximum_fusion.8), channel_id=1, source_target_pairs={{0,4},{2,6},{4,0},{6,2},{8,12},{10,14},{12,8},{14,10},{16,20},{18,... | collective-permute-start | bytes 786440 | tf_op jit(solution)/shard_map/ppermute | solution.py:13
  165.2 4.5 %copy-start.7 = (f32[1,1,64,1024]{2,3,1,0:T(8,128)S(1)}, f32[1,1,64,1024]{2,3,1,0:T(8,128)}, u32[]{:S(2)}) copy-start(f32[1,1,64,1024]{2,3,1,0:T(8,128)} %copy.307) | copy-start | bytes 786436
  168.5 1.4 copy-start.3
  169.7 1.3 copy-start.17
  171.0 2.9 %copy-start.19 = (f32[2,2,16,1024]{3,2,1,0:T(8,128)S(1)}, f32[2,2,16,1024]{3,2,1,0:T(8,128)}, u32[]{:S(2)}) copy-start(f32[2,2,16,1024]{3,2,1,0:T(8,128)} %copy-done.18) | copy-start | bytes 786436
  172.3 2.7 %copy-start.21 = (f32[2,32,1024]{2,1,0:T(8,128)S(1)}, f32[2,32,1024]{2,1,0:T(8,128)}, u32[]{:S(2)}) copy-start(f32[2,32,1024]{2,1,0:T(8,128)} %copy-done.20) | copy-start | bytes 786436
  172.6 6.4 %collective-permute-start.13 = (bf16[128,1024]{0,1:T(8,128)(2,1)S(1)}, bf16[128,1024]{0,1:T(8,128)(2,1)S(1)}, u32[]{:S(2)}, u32[]{:S(2)}) collective-permute-start(bf16[128,1024]{0,1:T(8,128)(2,1)S(1)} %pad_maximum_fusion.9), channel_id=1, source_target_pairs={{0,4},{2,6},{4,0},{6,2},{8,12},{10,14},{12,8},{14,10},{16,20},{18,... | collective-permute-start | bytes 786440 | tf_op jit(solution)/shard_map/ppermute | solution.py:13
  173.9 3.1 %copy-start.31 = (f32[2,16,1024]{2,1,0:T(8,128)}, f32[2,16,1024]{2,1,0:T(8,128)S(1)}, u32[]{:S(2)}) copy-start(f32[2,16,1024]{2,1,0:T(8,128)S(1)} %bitcast_add_fusion.5) | copy-start | bytes 393220
  175.7 12.0 %collective-permute-start.10 = (bf16[48,1024]{1,0:T(8,128)(2,1)}, bf16[48,1024]{1,0:T(8,128)(2,1)}, u32[]{:S(2)}, u32[]{:S(2)}) collective-permute-start(bf16[48,1024]{1,0:T(8,128)(2,1)} %pad_maximum_fusion.10), channel_id=1, source_target_pairs={{0,8},{2,10},{4,12},{6,14},{8,0},{10,2},{12,4},{14,6},{16,24},{18,... | collective-permute-start | bytes 294920 | tf_op jit(solution)/shard_map/ppermute | solution.py:13
  180.8 3.8 %copy-start.5 = (f32[2,32,1024]{1,2,0:T(8,128)S(1)}, f32[2,32,1024]{1,2,0:T(8,128)}, u32[]{:S(2)}) copy-start(f32[2,32,1024]{1,2,0:T(8,128)} %bitcast_add_fusion) | copy-start | bytes 786436
  183.9 0.7 copy-start.33
  184.6 9.4 %copy-start.32 = (f32[2,16,1024]{2,1,0:T(8,128)S(1)}, f32[2,16,1024]{2,1,0:T(8,128)}, u32[]{:S(2)}) copy-start(f32[2,16,1024]{2,1,0:T(8,128)} %copy-done.31) | copy-start | bytes 393220
  184.8 5.5 %copy-start.34 = (f32[2,16,1024]{2,1,0:T(8,128)S(1)}, f32[2,16,1024]{2,1,0:T(8,128)}, u32[]{:S(2)}) copy-start(f32[2,16,1024]{2,1,0:T(8,128)} %copy-done.33) | copy-start | bytes 393220
  185.7 4.6 %collective-permute-start.14 = (bf16[48,1024]{1,0:T(8,128)(2,1)S(1)}, bf16[48,1024]{1,0:T(8,128)(2,1)S(1)}, u32[]{:S(2)}, u32[]{:S(2)}) collective-permute-start(bf16[48,1024]{1,0:T(8,128)(2,1)S(1)} %pad_maximum_fusion.11), channel_id=1, source_target_pairs={{0,8},{2,10},{4,12},{6,14},{8,0},{10,2},{12,4},{14,6},{16,24},{18,... | collective-permute-start | bytes 294920 | tf_op jit(solution)/shard_map/ppermute | solution.py:13
  190.4 7.3 %collective-permute-start.15 = (bf16[16,1024]{1,0:T(8,128)(2,1)S(1)}, bf16[16,1024]{1,0:T(8,128)(2,1)S(1)}, u32[]{:S(2)}, u32[]{:S(2)}) collective-permute-start(bf16[16,1024]{1,0:T(8,128)(2,1)S(1)} %fusion.126), channel_id=1, source_target_pairs={{0,16},{2,18},{4,20},{6,22},{8,24},{10,26},{12,28},{14,30},{16,0},... | collective-permute-start | bytes 98312 | tf_op jit(solution)/shard_map/ppermute | solution.py:13
  194.0 7.2 %collective-permute-start.11 = (bf16[16,1024]{1,0:T(8,128)(2,1)S(1)}, bf16[16,1024]{1,0:T(8,128)(2,1)S(1)}, u32[]{:S(2)}, u32[]{:S(2)}) collective-permute-start(bf16[16,1024]{1,0:T(8,128)(2,1)S(1)} %fusion.127), channel_id=1, source_target_pairs={{0,16},{2,18},{4,20},{6,22},{8,24},{10,26},{12,28},{14,30},{16,0},... | collective-permute-start | bytes 98312 | tf_op jit(solution)/shard_map/ppermute | solution.py:13
Sparse Core Ops, SparseCore 0:
  96.4 8.4 reduce-scatter.1
where the time goes:
time: 211 us; the launch traced here: 210 us
  waiting for transfers between devices  60.4 us (29%)
  matrix products  42.6 us (20%)
  local copies, waits for them, and re-layouts  41.6 us (20%)
  starting transfers between devices  25.4 us (12%)
  other arithmetic  22.2 us (11%)
  between operations  15.5 us (7%)
  blocking collectives  2.35 us (1%)
    ppermute x16, waiting for transfers between devices, from_partner(): lax.ppermute(array, axis, [(i, i ^ 1 << bit) for i in range(lax.axis_size...  60.4 us
    ppermute x16, starting transfers between devices, from_partner(): lax.ppermute(array, axis, [(i, i ^ 1 << bit) for i in range(lax.axis_size...  25.4 us
    dot_general x32, matrix products, contract_rows(): lax.dot_general(left, right, (((0,), (0,)), ((), ())), preferred_element_...  16.7 us
    dot_general x8, matrix products, on_device(): jnp.dot(score_grad, key_part, preferred_element_type=jnp.float32)  14.1 us
    slice x22, local copies, waits for them, and re-layouts, split_rows(): pieces.append(packed[first:first + count])  7.59 us
    dot_general x17, matrix products, contract_cols(): lax.dot_general(left, right, (((1,), (1,)), ((), ())), preferred_element_...  6.59 us
    unnamed x88, local copies, waits for them, and re-layouts  6.44 us
    reshape x6, local copies, waits for them, and re-layouts, on_device(): value_sum = value_sum + value_part.reshape(tok_rows, columns)  5.49 us
  transfers between devices with their start and end apart: 17, of which 9 were waited for; matrix products, arithmetic and copies ran while one was open for 39% of the time, Pallas kernels for 0%

commit v1 on v0

v1 whole, which is shorter than its diff:
```python
import math

import jax
import jax.numpy as jnp
from jax import lax
from jax.experimental import pallas as pl
from jax.experimental.pallas import tpu as pltpu
from jax.sharding import PartitionSpec as P

HDIM = 128
BLOCK = 128
BF16 = jnp.bfloat16
F32 = jnp.float32
VMEM = pl.BlockSpec(memory_space=pltpu.VMEM)
SMEM = pl.BlockSpec(memory_space=pltpu.SMEM)


def swap_seq(array, mask):
    return lax.ppermute(array, "seq", [(i, i ^ mask) for i in range(lax.axis_size("seq"))])


def swap_head(array):
    return lax.ppermute(array, "head", [(0, 1), (1, 0)])


def mm(left, right):
    return jnp.dot(left, right, preferred_element_type=F32)


def mm_cols(left, right):
    return lax.dot_general(left, right, (((1,), (1,)), ((), ())), preferred_element_type=F32)


def mm_rows(left, right):
    return lax.dot_general(left, right, (((0,), (0,)), ((), ())), preferred_element_type=F32)


def pool_matrix(rows, shift):
    shape = (rows, rows << shift)
    row = lax.broadcasted_iota(jnp.int32, shape, 0)
    col = lax.broadcasted_iota(jnp.int32, shape, 1)
    return jnp.where(lax.shift_right_logical(col, shift) == row, 1.0, 0.0).astype(BF16)


def call(kernel, out_shape, operands, scratch=(), flops=0, vmem=24, specs=None):
    moved = sum(x.size * x.dtype.itemsize for x in operands)
    return pl.pallas_call(
        kernel,
        out_shape=out_shape,
        in_specs=specs or [VMEM] * len(operands),
        out_specs=jax.tree.map(lambda _: VMEM, out_shape),
        scratch_shapes=list(scratch),
        compiler_params=pltpu.CompilerParams(vmem_limit_bytes=vmem << 20),
        cost_estimate=pl.CostEstimate(flops=flops, bytes_accessed=moved, transcendentals=0),
    )(*operands)


def coarse_kernel(levels, k_ref, v_ref, out_ref):
    for place, level in enumerate(levels):
        shape = (16, BLOCK)
        row = lax.broadcasted_iota(jnp.int32, shape, 0)
        col = lax.broadcasted_iota(jnp.int32, shape, 1)
        pool = jnp.where(lax.shift_right_logical(col, level) == row, 1.0, 0.0).astype(BF16)
        keys = mm(pool, k_ref[...]) * (1.0 / (1 << level))
        out_ref[32 * place : 32 * place + 16, :] = keys.astype(BF16)
        out_ref[32 * place + 16 : 32 * place + 32, :] = mm(pool, v_ref[...]).astype(BF16)


def pack_kernel(heads, at_ref, q_ref, k_ref, v_ref, mine_ref, other_ref, w_ref, far_ref, *refs):
    out_refs, grad_ref = refs[:heads], refs[heads]
    low, core = at_ref[0], at_ref[1]
    half = mine_ref.shape[1]
    tok = q_ref.shape[0]
    first = pl.multiple_of(core * half, half)
    second = pl.multiple_of((1 - core) * half, half)
    total = mm(mine_ref[...], w_ref[pl.ds(first, half), :])
    total += mm(other_ref[...], w_ref[pl.ds(second, half), :])
    grad_ref[...] = total.astype(BF16)
    for mask in range(heads):
        col = pl.ds(pl.multiple_of((low ^ mask) * HDIM, HDIM), HDIM)
        out = out_refs[mask]
        out[0:tok, :] = q_ref[:, col]
        out[tok : 2 * tok, :] = k_ref[:, col]
        out[2 * tok : 3 * tok, :] = v_ref[:, col]
        out[3 * tok : 4 * tok, :] = grad_ref[:, col]
        out[4 * tok :, :] = far_ref[:, col]


def attend_kernel(heads, local_levels, far_levels, *refs):
    in_refs, out_refs = refs[:heads], refs[heads : 2 * heads]
    kl_ref, vl_ref, q_all, g_all, dk_ref, dv_ref, ck_ref, cv_ref, fk_ref, fv_ref = refs[2 * heads :]
    tok = BLOCK
    pairs = heads // 2
    inv_scale = 1.0 / math.sqrt(HDIM)
    to_exp2 = inv_scale * math.log2(math.e)
    for slab in range(heads):
        pair, row = slab // 2, (slab % 2) * tok
        q_all[pair, row : row + tok, :] = in_refs[slab][0:tok, :]
        kl_ref[pair, row : row + tok, :] = in_refs[slab][tok : 2 * tok, :]
        vl_ref[pair, row : row + tok, :] = in_refs[slab][2 * tok : 3 * tok, :]
        g_all[pair, row : row + tok, :] = in_refs[slab][3 * tok : 4 * tok, :]
        for place in range(far_levels):
            at = 4 * tok + 32 * place
            spot = 2 * tok + (local_levels - 1 + place) * BLOCK + 16 * slab
            fk, fv = in_refs[slab][at : at + 16, :], in_refs[slab][at + 16 : at + 32, :]
            for each in range(pairs):
                kl_ref[each, spot : spot + 16, :] = fk
                vl_ref[each, spot : spot + 16, :] = fv
    for level in range(1, local_levels):
        spot = 2 * tok + (level - 1) * BLOCK
        part = BLOCK >> level
        pool = pool_matrix(2 * part, level)
        for pair in range(pairs):
            keys = (mm(pool, kl_ref[pair, 0 : 2 * tok, :]) * (1.0 / (1 << level))).astype(BF16)
            values = mm(pool, vl_ref[pair, 0 : 2 * tok, :]).astype(BF16)
            group = pair >> (level - 1)
            inside = (pair & ((1 << (level - 1)) - 1)) * 2 * part
            at = spot + inside
            for each in range(pairs):
                if each >> (level - 1) == group ^ 1:
                    kl_ref[each, at : at + 2 * part, :] = keys
                    vl_ref[each, at : at + 2 * part, :] = values
    for pair in range(pairs):
        queries, grads = q_all[pair], g_all[pair]
        keys, values = kl_ref[pair], vl_ref[pair]
        scores = mm_cols(queries, keys)
        prob_grad = mm_cols(grads, values)
        top = jnp.max(scores, axis=1, keepdims=True)
        raised = jnp.exp2((scores - top) * to_exp2)
        inverse = 1.0 / jnp.sum(raised, axis=1, keepdims=True)
        prob = raised * inverse
        centre = jnp.sum(prob * prob_grad, axis=1, keepdims=True)
        prob_low = prob.astype(BF16)
        score_grad = (prob * ((prob_grad - centre) * inv_scale)).astype(BF16)
        attended = mm(prob_low, values).astype(BF16)
        query_grad = mm(score_grad, keys).astype(BF16)
        for side in range(2):
            rows = slice(side * tok, side * tok + tok)
            out_refs[2 * pair + side][0:tok, :] = attended[rows]
            out_refs[2 * pair + side][tok : 2 * tok, :] = query_grad[rows]
        key_terms = mm_rows(score_grad, queries)
        value_terms = mm_rows(prob_low, grads)
        dk_ref[pair] = key_terms[0 : 2 * tok]
        dv_ref[pair] = value_terms[0 : 2 * tok]
        for level in range(1, local_levels):
            group = (pair >> (level - 1)) ^ 1
            rows = slice(2 * tok + (level - 1) * BLOCK, 2 * tok + level * BLOCK)
            slot = (level - 1) * pairs + group
            if pair & ((1 << (level - 1)) - 1) == 0:
                ck_ref[slot] = key_terms[rows]
                cv_ref[slot] = value_terms[rows]
            else:
                ck_ref[slot] += key_terms[rows]
                cv_ref[slot] += value_terms[rows]
        for place in range(far_levels):
            start = 2 * tok + (local_levels - 1 + place) * BLOCK
            rows = slice(start, start + BLOCK)
            if pair == 0:
                fk_ref[place] = key_terms[rows]
                fv_ref[place] = value_terms[rows]
            else:
                fk_ref[place] += key_terms[rows]
                fv_ref[place] += value_terms[rows]
    for pair in range(pairs):
        key_sum, value_sum = dk_ref[pair], dv_ref[pair]
        for level in range(1, local_levels):
            part = BLOCK >> level
            pool = pool_matrix(2 * part, level)
            slot = (level - 1) * pairs + (pair >> (level - 1))
            inside = (pair & ((1 << (level - 1)) - 1)) * 2 * part
            rows = slice(inside, inside + 2 * part)
            key_sum += mm_rows(pool, (ck_ref[slot, rows, :] * (1.0 / (1 << level))).astype(BF16))
            value_sum += mm_rows(pool, cv_ref[slot, rows, :].astype(BF16))
        for side in range(2):
            rows = slice(side * tok, side * tok + tok)
            out_refs[2 * pair + side][2 * tok : 3 * tok, :] = key_sum[rows].astype(BF16)
            out_refs[2 * pair + side][3 * tok : 4 * tok, :] = value_sum[rows].astype(BF16)
    for slab in range(heads):
        for place in range(far_levels):
            at = 4 * tok + 32 * place
            rows = slice(16 * slab, 16 * slab + 16)
            out_refs[slab][at : at + 16, :] = fk_ref[place, rows, :].astype(BF16)
            out_refs[slab][at + 16 : at + 32, :] = fv_ref[place, rows, :].astype(BF16)


def unpack_kernel(heads, at_ref, w_ref, *refs):
    in_refs = refs[:heads]
    keep_ref, send_ref, dq_ref, dk_ref, dv_ref, far_ref, att_ref = refs[heads:]
    low, core = at_ref[0], at_ref[1]
    tok, half = dq_ref.shape
    for mask in range(heads):
        col = pl.ds(pl.multiple_of((low ^ mask) * HDIM, HDIM), HDIM)
        chunk = in_refs[mask]
        att_ref[:, col] = chunk[0:tok, :]
        dq_ref[:, col] = chunk[tok : 2 * tok, :]
        dk_ref[:, col] = chunk[2 * tok : 3 * tok, :]
        dv_ref[:, col] = chunk[3 * tok : 4 * tok, :]
        far_ref[:, col] = chunk[4 * tok :, :]
    first = pl.multiple_of(core * half, half)
    second = pl.multiple_of((1 - core) * half, half)
    send_ref[...] = mm_cols(att_ref[...], w_ref[pl.ds(second, half), :]).astype(BF16)
    keep_ref[...] = mm_cols(att_ref[...], w_ref[pl.ds(first, half), :])


def finish_kernel(levels, keep_ref, got_ref, dk_ref, dv_ref, far_ref, out_ref, key_ref, value_ref):
    out_ref[...] = (keep_ref[...] + got_ref[...].astype(F32)).astype(BF16)
    key_sum, value_sum = dk_ref[...].astype(F32), dv_ref[...].astype(F32)
    for place, level in enumerate(levels):
        shape = (16, BLOCK)
        row = lax.broadcasted_iota(jnp.int32, shape, 0)
        col = lax.broadcasted_iota(jnp.int32, shape, 1)
        pool = jnp.where(lax.shift_right_logical(col, level) == row, 1.0, 0.0).astype(BF16)
        at = 32 * place
        key_sum += mm_rows(pool, far_ref[at : at + 16, :]) * (1.0 / (1 << level))
        value_sum += mm_rows(pool, far_ref[at + 16 : at + 32, :])
    key_ref[...] = key_sum.astype(BF16)
    value_ref[...] = value_sum.astype(BF16)


def gather_far(pieces, levels, columns):
    held = {}
    for place, level in enumerate(levels):
        rows = BLOCK >> level
        block = pieces[32 * place : 32 * place + 32].reshape(2, 16, columns)
        held[level] = block[:, None, :rows]
    found = []
    for step in levels:
        sent = [held[level].reshape(-1, columns) for level in levels if level >= step]
        got = swap_seq(jnp.concatenate(sent, axis=0) if len(sent) > 1 else sent[0], 1 << step)
        first = 0
        for level in levels:
            if level < step:
                continue
            count = held[level].size // columns
            part = got[first : first + count].reshape(held[level].shape)
            first += count
            if level == step:
                found.append(part.reshape(32, columns))
            else:
                held[level] = jnp.concatenate([held[level], part], axis=1)
    return jnp.concatenate(found, axis=0) if len(found) > 1 else found[0]


def scatter_far(packed, levels, columns):
    blocks = {}
    for place, level in enumerate(levels):
        rows = BLOCK >> level
        block = packed[32 * place : 32 * place + 32]
        blocks[level] = block.reshape(2, 16 // rows, rows, columns)
    ready = {}
    for step in reversed(levels):
        sent, kept = [blocks[step].reshape(-1, columns)], {}
        for level in levels:
            if level > step:
                size = ready[level].shape[1] // 2
                kept[level] = ready[level][:, :size]
                sent.append(ready[level][:, size:].astype(BF16).reshape(-1, columns))
        got = swap_seq(jnp.concatenate(sent, axis=0) if len(sent) > 1 else sent[0], 1 << step)
        ready[step] = got[0 : blocks[step].size // columns].reshape(blocks[step].shape)
        first = blocks[step].size // columns
        for level in kept:
            count = kept[level].size // columns
            part = got[first : first + count].reshape(kept[level].shape)
            first += count
            ready[level] = kept[level].astype(F32) + part.astype(F32)
    shares = []
    for level in levels:
        share = ready[level].astype(BF16).reshape(2, -1, columns)
        pad = 16 - share.shape[1]
        if pad:
            share = jnp.pad(share, ((0, 0), (0, pad), (0, 0)))
        shares.append(share.reshape(32, columns))
    return jnp.concatenate(shares, axis=0) if len(shares) > 1 else shares[0]


def on_device(queries, key_tokens, value_tokens, out_weight, output_grad):
    tok, columns = queries.shape
    heads = columns // HDIM
    local_levels = heads.bit_length() - 1
    level_count = lax.axis_size("seq").bit_length() - 1
    far = list(range(local_levels, level_count))
    rows = 4 * tok + 32 * len(far)
    place = jnp.stack([lax.axis_index("seq") & (heads - 1), lax.axis_index("head")])
    place = place.astype(jnp.int32)

    def shape(dims, dtype=BF16):
        return jax.ShapeDtypeStruct(dims, dtype)

    other_grad = swap_head(output_grad)
    pieces = call(
        lambda *refs: coarse_kernel(far, *refs),
        shape((32 * len(far), columns)),
        (key_tokens, value_tokens),
    )
    far_rows = gather_far(pieces, far, columns)
    chunks = call(
        lambda *refs: pack_kernel(heads, *refs),
        [shape((rows, HDIM))] * heads,
        (place, queries, key_tokens, value_tokens, output_grad, other_grad, out_weight, far_rows),
        scratch=[pltpu.VMEM((tok, columns), BF16)],
        flops=4 * tok * columns * columns,
        specs=[SMEM] + [VMEM] * 7,
    )
    mine = [chunks[0]] + [swap_seq(chunks[mask], mask) for mask in range(1, heads)]
    list_rows = 2 * tok + (local_levels - 1 + len(far)) * BLOCK
    pairs = heads // 2
    back = call(
        lambda *refs: attend_kernel(heads, local_levels, len(far), *refs),
        [shape((rows, HDIM))] * heads,
        mine,
        scratch=[
            pltpu.VMEM((pairs, list_rows, HDIM), BF16),
            pltpu.VMEM((pairs, list_rows, HDIM), BF16),
            pltpu.VMEM((pairs, 2 * tok, HDIM), BF16),
            pltpu.VMEM((pairs, 2 * tok, HDIM), BF16),
            pltpu.VMEM((pairs, 2 * tok, HDIM), F32),
            pltpu.VMEM((pairs, 2 * tok, HDIM), F32),
            pltpu.VMEM(((local_levels - 1) * pairs, BLOCK, HDIM), F32),
            pltpu.VMEM(((local_levels - 1) * pairs, BLOCK, HDIM), F32),
            pltpu.VMEM((len(far), BLOCK, HDIM), F32),
            pltpu.VMEM((len(far), BLOCK, HDIM), F32),
        ],
        flops=12 * heads * tok * list_rows * HDIM,
    )
    home = [back[0]] + [swap_seq(back[mask], mask) for mask in range(1, heads)]
    wide = shape((tok, columns))
    keep, send, query_grad, key_part, value_part, far_part = call(
        lambda *refs: unpack_kernel(heads, *refs),
        [shape((tok, columns), F32), wide, wide, wide, wide, shape((32 * len(far), columns))],
        [place, out_weight] + home,
        scratch=[pltpu.VMEM((tok, columns), BF16)],
        flops=4 * tok * columns * columns,
        specs=[SMEM] + [VMEM] * (1 + heads),
    )
    got = swap_head(send)
    far_share = scatter_far(far_part, far, columns)
    output, key_grad, value_grad = call(
        lambda *refs: finish_kernel(far, *refs),
        [wide, wide, wide],
        (keep, got, key_part, value_part, far_share),
    )
    return output, query_grad, key_grad, value_grad


def solution(mesh):
    placed = P("seq", "head")
    return jax.shard_map(
        on_device,
        mesh=mesh,
        in_specs=(placed, placed, placed, P(None, "head"), placed),
        out_specs=(placed, placed, placed, placed),
        check_vma=False,
    )
```

time: 211 us -> 68.8 us (0.33)
  matrix products: 42.6 us -> 0 us
  waiting for transfers between devices: 60.4 us -> 23.5 us
  local copies, waits for them, and re-layouts: 41.6 us -> 7.89 us
  other arithmetic: 22.2 us -> 0.07 us
  between operations: 15.5 us -> 0.67 us
  Pallas kernels: 0 us -> 9.72 us
  blocking collectives: 2.35 us -> 0 us
    dot_general x66 -> x0, matrix products: 42.6 us -> none  [the longest x32 16.7 us: contract_rows(): lax.dot_general(left, right, (((0,), (0,)), ((), ())), preferred_element_...]
    ppermute x16 -> x18, waiting for transfers between devices: 60.4 us -> 23.5 us  [the longest x16 23.5 us: swap_seq(): lax.ppermute(array, 'seq', [(i, i ^ mask) for i in range(lax.axis_size('s...]
    reshape x22 -> x0, local copies, waits for them, and re-layouts: 13.6 us -> none  [the longest x6 5.49 us: on_device(): value_sum = value_sum + value_part.reshape(tok_rows, columns)]
    slice x32 -> x0, local copies, waits for them, and re-layouts: 13.1 us -> none  [the longest x22 7.59 us: split_rows(): pieces.append(packed[first:first + count])]
    pallas_call x0 -> x5, Pallas kernels: none -> 9.72 us  [call(): pl.pallas_call(kernel, out_shape=out_shape, in_specs=specs or [VMEM] * le...]
    convert_element_type x30 -> x0, other arithmetic: 8.42 us -> none  [the longest x3 3.23 us: on_device(): from_partner(key_pack.astype(jnp.bfloat16), 'seq', step)]
    concatenate x12 -> x0, other arithmetic: 5.67 us -> none  [the longest x3 2.58 us: on_device(): key_pack = jnp.concatenate(key_sends, axis=0)]
    reduce_sum x14 -> x0, other arithmetic: 4.07 us -> none  [the longest x3 2.05 us: coarsen(): reduced = jnp.mean(grouped, axis=1)]
  transfers between devices with their start and end apart: 17 -> 18, of which waited for: 9 -> 11; matrix products, arithmetic and copies ran while one was open for 39% -> 0% of each run, Pallas kernels for 0% -> 0%
where the time goes in v1:
time: 68.8 us; the launch traced here: 68.4 us
  starting transfers between devices  26.6 us (39%)
  waiting for transfers between devices  23.5 us (34%)
  Pallas kernels  9.72 us (14%)
  local copies, waits for them, and re-layouts  7.89 us (11%)
    ppermute x16, starting transfers between devices, swap_seq(): lax.ppermute(array, 'seq', [(i, i ^ mask) for i in range(lax.axis_size('s...  26.1 us
    ppermute x16, waiting for transfers between devices, swap_seq(): lax.ppermute(array, 'seq', [(i, i ^ mask) for i in range(lax.axis_size('s...  23.5 us
    pallas_call x5, Pallas kernels, call(): pl.pallas_call(kernel, out_shape=out_shape, in_specs=specs or [VMEM] * le...  9.72 us
    unnamed x16, local copies, waits for them, and re-layouts  7.89 us
  transfers between devices with their start and end apart: 18, of which 11 were waited for; matrix products, arithmetic and copies ran while one was open for 0% of the time, Pallas kernels for 0%

profile of v1, /device:TPU:0, one launch (start us, length us, event | category | flops | bytes accessed | tf_op | source)
XLA Modules:
  0.0 68.4 jit_solution(17153681361658169622)
XLA Ops:
  0.6 0.5 collective-permute-start
  1.1 0.0 copy-start.2
  1.1 0.9 %copy-done.2 = bf16[128,1024]{1,0:T(8,128)(2,1)S(1)} copy-done((bf16[128,1024]{1,0:T(8,128)(2,1)S(1)}, bf16[128,1024]{1,0:T(8,128)(2,1)}, u32[]{:S(2)}) %copy-start.2) | copy-done | bytes 262168
  2.1 0.0 copy-start.4
  2.1 0.9 %copy-done.4 = bf16[128,1024]{1,0:T(8,128)(2,1)S(1)} copy-done((bf16[128,1024]{1,0:T(8,128)(2,1)S(1)}, bf16[128,1024]{1,0:T(8,128)(2,1)}, u32[]{:S(2)}) %copy-start.4) | copy-done | bytes 262168
  3.0 0.2 shard_map.84
  3.2 3.7 %collective-permute-start.1 = (bf16[32,1024]{1,0:T(8,128)(2,1)S(1)}, bf16[32,1024]{1,0:T(8,128)(2,1)S(1)}, u32[]{:S(2)}, u32[]{:S(2)}) collective-permute-start(bf16[32,1024]{1,0:T(8,128)(2,1)S(1)} %shard_map.84), channel_id=1, source_target_pairs={{0,16},{2,18},{4,20},{6,22},{8,24},{10,26},{12,28},{14,30},{16,0},... | collective-permute-start | bytes 196616 | tf_op jit(solution)/shard_map/ppermute | solution.py:19
  6.9 0.1 pad_add_fusion.refs_0_
  7.0 4.1 %collective-permute-done.1.refs_7_ = bf16[32,1024]{1,0:T(8,128)(2,1)S(1)} collective-permute-done((bf16[32,1024]{1,0:T(8,128)(2,1)S(1)}, bf16[32,1024]{1,0:T(8,128)(2,1)S(1)}, u32[]{:S(2)}, u32[]{:S(2)}) %collective-permute-start.1) | collective-permute-done | bytes 65568 | tf_op jit(solution)/shard_map/ppermute | solution.py:19
  11.0 0.0 collective-permute-done.refs_5_
  11.0 0.0 copy-start
  11.0 2.2 %copy-done = bf16[2048,1024]{1,0:T(8,128)(2,1)S(1)} copy-done((bf16[2048,1024]{1,0:T(8,128)(2,1)S(1)}, bf16[2048,1024]{1,0:T(8,128)(2,1)}, u32[]{:S(2)}) %copy-start) | copy-done | bytes 4194328
  13.2 0.0 copy-start.3
  13.2 0.9 %copy-done.3 = bf16[128,1024]{1,0:T(8,128)(2,1)S(1)} copy-done((bf16[128,1024]{1,0:T(8,128)(2,1)S(1)}, bf16[128,1024]{1,0:T(8,128)(2,1)}, u32[]{:S(2)}) %copy-start.3) | copy-done | bytes 262168
  14.2 0.0 copy-start.5
  14.2 0.9 %copy-done.5 = bf16[128,1024]{1,0:T(8,128)(2,1)S(1)} copy-done((bf16[128,1024]{1,0:T(8,128)(2,1)S(1)}, bf16[128,1024]{1,0:T(8,128)(2,1)}, u32[]{:S(2)}) %copy-start.5) | copy-done | bytes 262168
  15.1 0.0 copy-start.6
  15.1 0.9 %copy-done.6 = bf16[128,1024]{1,0:T(8,128)(2,1)S(1)} copy-done((bf16[128,1024]{1,0:T(8,128)(2,1)S(1)}, bf16[128,1024]{1,0:T(8,128)(2,1)}, u32[]{:S(2)}) %copy-start.6) | copy-done | bytes 262168
  16.1 0.0 copy-start.7
  16.1 0.9 %copy-done.7 = bf16[128,1024]{1,0:T(8,128)(2,1)S(1)} copy-done((bf16[128,1024]{1,0:T(8,128)(2,1)S(1)}, bf16[128,1024]{1,0:T(8,128)(2,1)}, u32[]{:S(2)}) %copy-start.7) | copy-done | bytes 262168
  17.0 0.0 copy-start.1
  17.0 1.5 %shard_map.85 = (bf16[544,128]{1,0:T(8,128)(2,1)S(1)}, bf16[544,128]{1,0:T(8,128)(2,1)S(1)}, bf16[544,128]{1,0:T(8,128)(2,1)S(1)}, bf16[544,128]{1,0:T(8,128)(2,...) custom-call(s32[2]{0:T(128)S(1)} %pad_add_fusion.refs_0_, ...), custom_call_target="tpu_custom_call" | custom-call | flops 536870912 | bytes 5570568 | tf_op jit(solution)/shard_map/pallas_call | solution.py:47
  18.5 1.6 %collective-permute-start.2 = (bf16[544,128]{1,0:T(8,128)(2,1)S(1)}, bf16[544,128]{1,0:T(8,128)(2,1)S(1)}, u32[]{:S(2)}, u32[]{:S(2)}) collective-permute-start(bf16[544,128]{1,0:T(8,128)(2,1)S(1)} %get-tuple-element.30), channel_id=1, source_target_pairs={{0,2},{2,0},{4,6},{6,4},{8,10},{10,8},{12,14},{14,12},{16,18},{18,... | collective-permute-start | bytes 417800 | tf_op jit(solution)/shard_map/ppermute | solution.py:19
  20.1 1.5 %collective-permute-start.3 = (bf16[544,128]{1,0:T(8,128)(2,1)S(1)}, bf16[544,128]{1,0:T(8,128)(2,1)S(1)}, u32[]{:S(2)}, u32[]{:S(2)}) collective-permute-start(bf16[544,128]{1,0:T(8,128)(2,1)S(1)} %get-tuple-element.31), channel_id=1, source_target_pairs={{0,4},{2,6},{4,0},{6,2},{8,12},{10,14},{12,8},{14,10},{16,20},{18,... | collective-permute-start | bytes 417800 | tf_op jit(solution)/shard_map/ppermute | solution.py:19
  21.6 0.4 collective-permute-start.4
  22.1 0.7 %collective-permute-start.5 = (bf16[544,128]{1,0:T(8,128)(2,1)S(1)}, bf16[544,128]{1,0:T(8,128)(2,1)S(1)}, u32[]{:S(2)}, u32[]{:S(2)}) collective-permute-start(bf16[544,128]{1,0:T(8,128)(2,1)S(1)} %get-tuple-element.33), channel_id=1, source_target_pairs={{0,8},{2,10},{4,12},{6,14},{8,0},{10,2},{12,4},{14,6},{16,24},{18,... | collective-permute-start | bytes 417800 | tf_op jit(solution)/shard_map/ppermute | solution.py:19
  22.8 2.3 %collective-permute-start.6 = (bf16[544,128]{1,0:T(8,128)(2,1)S(1)}, bf16[544,128]{1,0:T(8,128)(2,1)S(1)}, u32[]{:S(2)}, u32[]{:S(2)}) collective-permute-start(bf16[544,128]{1,0:T(8,128)(2,1)S(1)} %get-tuple-element.34), channel_id=1, source_target_pairs={{0,10},{2,8},{4,14},{6,12},{8,2},{10,0},{12,6},{14,4},{16,26},{18,... | collective-permute-start | bytes 417800 | tf_op jit(solution)/shard_map/ppermute | solution.py:19
  25.1 0.1 collective-permute-done.2.refs_1_
  25.1 1.6 %collective-permute-start.7 = (bf16[544,128]{1,0:T(8,128)(2,1)S(1)}, bf16[544,128]{1,0:T(8,128)(2,1)S(1)}, u32[]{:S(2)}, u32[]{:S(2)}) collective-permute-start(bf16[544,128]{1,0:T(8,128)(2,1)S(1)} %get-tuple-element.35), channel_id=1, source_target_pairs={{0,12},{2,14},{4,8},{6,10},{8,4},{10,6},{12,0},{14,2},{16,28},{18,... | collective-permute-start | bytes 417800 | tf_op jit(solution)/shard_map/ppermute | solution.py:19
  26.7 0.0 collective-permute-done.3.refs_2_
  26.7 2.0 %collective-permute-start.8 = (bf16[544,128]{1,0:T(8,128)(2,1)S(1)}, bf16[544,128]{1,0:T(8,128)(2,1)S(1)}, u32[]{:S(2)}, u32[]{:S(2)}) collective-permute-start(bf16[544,128]{1,0:T(8,128)(2,1)S(1)} %get-tuple-element.36), channel_id=1, source_target_pairs={{0,14},{2,12},{4,10},{6,8},{8,6},{10,4},{12,2},{14,0},{16,30},{18,... | collective-permute-start | bytes 417800 | tf_op jit(solution)/shard_map/ppermute | solution.py:19
  28.7 0.5 collective-permute-done.4.refs_3_
  29.2 0.0 collective-permute-done.5.refs_4_
  29.2 3.4 %collective-permute-done.6.refs_5_ = bf16[544,128]{1,0:T(8,128)(2,1)S(1)} collective-permute-done((bf16[544,128]{1,0:T(8,128)(2,1)S(1)}, bf16[544,128]{1,0:T(8,128)(2,1)S(1)}, u32[]{:S(2)}, u32[]{:S(2)}) %collective-permute-start.6) | collective-permute-done | bytes 139296 | tf_op jit(solution)/shard_map/ppermute | solution.py:19
  32.6 2.5 %collective-permute-done.7.refs_6_ = bf16[544,128]{1,0:T(8,128)(2,1)S(1)} collective-permute-done((bf16[544,128]{1,0:T(8,128)(2,1)S(1)}, bf16[544,128]{1,0:T(8,128)(2,1)S(1)}, u32[]{:S(2)}, u32[]{:S(2)}) %collective-permute-start.7) | collective-permute-done | bytes 139296 | tf_op jit(solution)/shard_map/ppermute | solution.py:19
  35.2 1.7 %collective-permute-done.8.refs_7_ = bf16[544,128]{1,0:T(8,128)(2,1)S(1)} collective-permute-done((bf16[544,128]{1,0:T(8,128)(2,1)S(1)}, bf16[544,128]{1,0:T(8,128)(2,1)S(1)}, u32[]{:S(2)}, u32[]{:S(2)}) %collective-permute-start.8) | collective-permute-done | bytes 139296 | tf_op jit(solution)/shard_map/ppermute | solution.py:19
  36.9 4.2 %shard_map.86 = (bf16[544,128]{1,0:T(8,128)(2,1)S(1)}, bf16[544,128]{1,0:T(8,128)(2,1)S(1)}, bf16[544,128]{1,0:T(8,128)(2,1)S(1)}, bf16[544,128]{1,0:T(8,128)(2,...) custom-call(bf16[544,128]{1,0:T(8,128)(2,1)S(1)} %get-tuple-element., ...), custom_call_target="tpu_custom_call" | custom-call | flops 1006632960 | bytes 1114112 | tf_op jit(solution)/shard_map/pallas_call | solution.py:47
  41.0 1.4 %collective-permute-start.9 = (bf16[544,128]{1,0:T(8,128)(2,1)S(1)}, bf16[544,128]{1,0:T(8,128)(2,1)S(1)}, u32[]{:S(2)}, u32[]{:S(2)}) collective-permute-start(bf16[544,128]{1,0:T(8,128)(2,1)S(1)} %get-tuple-element.38), channel_id=1, source_target_pairs={{0,2},{2,0},{4,6},{6,4},{8,10},{10,8},{12,14},{14,12},{16,18},{18,... | collective-permute-start | bytes 417800 | tf_op jit(solution)/shard_map/ppermute | solution.py:19
  42.5 0.5 collective-permute-start.10
  43.0 1.6 %collective-permute-start.11 = (bf16[544,128]{1,0:T(8,128)(2,1)S(1)}, bf16[544,128]{1,0:T(8,128)(2,1)S(1)}, u32[]{:S(2)}, u32[]{:S(2)}) collective-permute-start(bf16[544,128]{1,0:T(8,128)(2,1)S(1)} %get-tuple-element.40), channel_id=1, source_target_pairs={{0,6},{2,4},{4,2},{6,0},{8,14},{10,12},{12,10},{14,8},{16,22},{18,... | collective-permute-start | bytes 417800 | tf_op jit(solution)/shard_map/ppermute | solution.py:19
  44.6 1.6 %collective-permute-start.12 = (bf16[544,128]{1,0:T(8,128)(2,1)S(1)}, bf16[544,128]{1,0:T(8,128)(2,1)S(1)}, u32[]{:S(2)}, u32[]{:S(2)}) collective-permute-start(bf16[544,128]{1,0:T(8,128)(2,1)S(1)} %get-tuple-element.41), channel_id=1, source_target_pairs={{0,8},{2,10},{4,12},{6,14},{8,0},{10,2},{12,4},{14,6},{16,24},{18,... | collective-permute-start | bytes 417800 | tf_op jit(solution)/shard_map/ppermute | solution.py:19
  46.2 1.2 %collective-permute-start.13 = (bf16[544,128]{1,0:T(8,128)(2,1)S(1)}, bf16[544,128]{1,0:T(8,128)(2,1)S(1)}, u32[]{:S(2)}, u32[]{:S(2)}) collective-permute-start(bf16[544,128]{1,0:T(8,128)(2,1)S(1)} %get-tuple-element.42), channel_id=1, source_target_pairs={{0,10},{2,8},{4,14},{6,12},{8,2},{10,0},{12,6},{14,4},{16,26},{18,... | collective-permute-start | bytes 417800 | tf_op jit(solution)/shard_map/ppermute | solution.py:19
  47.4 1.3 %collective-permute-done.9.refs_3_ = bf16[544,128]{1,0:T(8,128)(2,1)S(1)} collective-permute-done((bf16[544,128]{1,0:T(8,128)(2,1)S(1)}, bf16[544,128]{1,0:T(8,128)(2,1)S(1)}, u32[]{:S(2)}, u32[]{:S(2)}) %collective-permute-start.9) | collective-permute-done | bytes 139296 | tf_op jit(solution)/shard_map/ppermute | solution.py:19
  48.7 0.4 collective-permute-start.14
  49.2 0.0 collective-permute-done.10.refs_4_
  49.2 2.5 %collective-permute-start.15 = (bf16[544,128]{1,0:T(8,128)(2,1)S(1)}, bf16[544,128]{1,0:T(8,128)(2,1)S(1)}, u32[]{:S(2)}, u32[]{:S(2)}) collective-permute-start(bf16[544,128]{1,0:T(8,128)(2,1)S(1)} %get-tuple-element.44), channel_id=1, source_target_pairs={{0,14},{2,12},{4,10},{6,8},{8,6},{10,4},{12,2},{14,0},{16,30},{18,... | collective-permute-start | bytes 417800 | tf_op jit(solution)/shard_map/ppermute | solution.py:19
  51.7 0.0 collective-permute-done.11.refs_5_
  51.7 0.0 collective-permute-done.12.refs_6_
  51.7 2.7 %collective-permute-done.13.refs_7_ = bf16[544,128]{1,0:T(8,128)(2,1)S(1)} collective-permute-done((bf16[544,128]{1,0:T(8,128)(2,1)S(1)}, bf16[544,128]{1,0:T(8,128)(2,1)S(1)}, u32[]{:S(2)}, u32[]{:S(2)}) %collective-permute-start.13) | collective-permute-done | bytes 139296 | tf_op jit(solution)/shard_map/ppermute | solution.py:19
  54.5 0.9 %collective-permute-done.14.refs_8_ = bf16[544,128]{1,0:T(8,128)(2,1)S(1)} collective-permute-done((bf16[544,128]{1,0:T(8,128)(2,1)S(1)}, bf16[544,128]{1,0:T(8,128)(2,1)S(1)}, u32[]{:S(2)}, u32[]{:S(2)}) %collective-permute-start.14) | collective-permute-done | bytes 139296 | tf_op jit(solution)/shard_map/ppermute | solution.py:19
  55.3 2.1 %collective-permute-done.15.refs_9_ = bf16[544,128]{1,0:T(8,128)(2,1)S(1)} collective-permute-done((bf16[544,128]{1,0:T(8,128)(2,1)S(1)}, bf16[544,128]{1,0:T(8,128)(2,1)S(1)}, u32[]{:S(2)}, u32[]{:S(2)}) %collective-permute-start.15) | collective-permute-done | bytes 139296 | tf_op jit(solution)/shard_map/ppermute | solution.py:19
  57.4 0.0 copy-done.1
  57.4 2.8 %shard_map.87 = (f32[128,1024]{1,0:T(8,128)S(1)}, bf16[128,1024]{1,0:T(8,128)(2,1)S(1)}, bf16[128,1024]{1,0:T(8,128)(2,1)}, bf16[128,1024]{1,0:T(8,128)(2,1)S(1)...) custom-call(s32[2]{0:T(128)S(1)} %pad_add_fusion.refs_0_, bf16[2048,1024]{1,0:T(8,128)(2,1)S(1)} %copy-done.1, ...), custom_call_target="tpu_custom_call" | custom-call | flops 536870912 | bytes 5308424 | tf_op jit(solution)/shard_map/pallas_call | solution.py:47
  60.2 0.0 collective-permute-start.16
  60.2 3.0 %collective-permute-start.17 = (bf16[32,1024]{1,0:T(8,128)(2,1)S(1)}, bf16[32,1024]{1,0:T(8,128)(2,1)S(1)}, u32[]{:S(2)}, u32[]{:S(2)}) collective-permute-start(bf16[32,1024]{1,0:T(8,128)(2,1)S(1)} %get-tuple-element.49), channel_id=1, source_target_pairs={{0,16},{2,18},{4,20},{6,22},{8,24},{10,26},{12,28},{14,30},{16,0},... | collective-permute-start | bytes 196616 | tf_op jit(solution)/shard_map/ppermute | solution.py:19
  63.1 4.2 %collective-permute-done.17.refs_4_ = bf16[32,1024]{1,0:T(8,128)(2,1)S(1)} collective-permute-done((bf16[32,1024]{1,0:T(8,128)(2,1)S(1)}, bf16[32,1024]{1,0:T(8,128)(2,1)S(1)}, u32[]{:S(2)}, u32[]{:S(2)}) %collective-permute-start.17) | collective-permute-done | bytes 65568 | tf_op jit(solution)/shard_map/ppermute | solution.py:19
  67.3 0.0 collective-permute-done.16.refs_1_
  67.3 1.1 %shard_map.88 = (bf16[128,1024]{1,0:T(8,128)(2,1)}, bf16[128,1024]{1,0:T(8,128)(2,1)}, bf16[128,1024]{1,0:T(8,128)(2,1)}) custom-call(f32[128,1024]{1,0:T(8,128)S(1)} %get-tuple-element.45.refs_0_, bf16[128,1024]{1,0:T(8,128)(2,1)S(1)} %collective-permute-done.16.refs_1_, bf16[128,1024]{1,0:T(8,128)(2,1)S(1)} %get-tuple-element.47.refs_2_, ...), custom_call_target="tpu_custom_call" | custom-call | bytes 1376256 | tf_op jit(solution)/shard_map/pallas_call | solution.py:47
Async XLA Ops:
  0.6 10.4 %collective-permute-start = (bf16[128,1024]{1,0:T(8,128)(2,1)}, bf16[128,1024]{1,0:T(8,128)(2,1)S(1)}, u32[]{:S(2)}, u32[]{:S(2)}) collective-permute-start(bf16[128,1024]{1,0:T(8,128)(2,1)} %refs_4_.1), channel_id=1, source_target_pairs={{0,1},{1,0},{2,3},{3,2},{4,5},{5,4},{6,7},{7,6},{8,9},{9,8},{10,11... | collective-permute-start | bytes 786440 | tf_op jit(solution)/shard_map/ppermute | solution.py:23
  1.1 0.9 %copy-start.2 = (bf16[128,1024]{1,0:T(8,128)(2,1)S(1)}, bf16[128,1024]{1,0:T(8,128)(2,1)}, u32[]{:S(2)}) copy-start(bf16[128,1024]{1,0:T(8,128)(2,1)} %refs_2_.1) | copy-start | bytes 786436
  2.1 0.9 %copy-start.4 = (bf16[128,1024]{1,0:T(8,128)(2,1)S(1)}, bf16[128,1024]{1,0:T(8,128)(2,1)}, u32[]{:S(2)}) copy-start(bf16[128,1024]{1,0:T(8,128)(2,1)} %refs_3_.1) | copy-start | bytes 786436
  3.2 7.8 %collective-permute-start.1 = (bf16[32,1024]{1,0:T(8,128)(2,1)S(1)}, bf16[32,1024]{1,0:T(8,128)(2,1)S(1)}, u32[]{:S(2)}, u32[]{:S(2)}) collective-permute-start(bf16[32,1024]{1,0:T(8,128)(2,1)S(1)} %shard_map.84), channel_id=1, source_target_pairs={{0,16},{2,18},{4,20},{6,22},{8,24},{10,26},{12,28},{14,30},{16,0},... | collective-permute-start | bytes 196616 | tf_op jit(solution)/shard_map/ppermute | solution.py:19
  11.0 2.2 %copy-start = (bf16[2048,1024]{1,0:T(8,128)(2,1)S(1)}, bf16[2048,1024]{1,0:T(8,128)(2,1)}, u32[]{:S(2)}) copy-start(bf16[2048,1024]{1,0:T(8,128)(2,1)} %refs_1_.5) | copy-start | bytes 12582916
  13.2 0.9 %copy-start.3 = (bf16[128,1024]{1,0:T(8,128)(2,1)S(1)}, bf16[128,1024]{1,0:T(8,128)(2,1)}, u32[]{:S(2)}) copy-start(bf16[128,1024]{1,0:T(8,128)(2,1)} %refs_2_.1) | copy-start | bytes 786436
  14.2 0.9 %copy-start.5 = (bf16[128,1024]{1,0:T(8,128)(2,1)S(1)}, bf16[128,1024]{1,0:T(8,128)(2,1)}, u32[]{:S(2)}) copy-start(bf16[128,1024]{1,0:T(8,128)(2,1)} %refs_3_.1) | copy-start | bytes 786436
  15.1 0.9 %copy-start.6 = (bf16[128,1024]{1,0:T(8,128)(2,1)S(1)}, bf16[128,1024]{1,0:T(8,128)(2,1)}, u32[]{:S(2)}) copy-start(bf16[128,1024]{1,0:T(8,128)(2,1)} %refs_1_.4) | copy-start | bytes 786436
  16.1 0.9 %copy-start.7 = (bf16[128,1024]{1,0:T(8,128)(2,1)S(1)}, bf16[128,1024]{1,0:T(8,128)(2,1)}, u32[]{:S(2)}) copy-start(bf16[128,1024]{1,0:T(8,128)(2,1)} %refs_4_.1) | copy-start | bytes 786436
  17.0 40.4 %copy-start.1 = (bf16[2048,1024]{1,0:T(8,128)(2,1)S(1)}, bf16[2048,1024]{1,0:T(8,128)(2,1)}, u32[]{:S(2)}) copy-start(bf16[2048,1024]{1,0:T(8,128)(2,1)} %refs_1_.5) | copy-start | bytes 12582916
  18.5 6.6 %collective-permute-start.2 = (bf16[544,128]{1,0:T(8,128)(2,1)S(1)}, bf16[544,128]{1,0:T(8,128)(2,1)S(1)}, u32[]{:S(2)}, u32[]{:S(2)}) collective-permute-start(bf16[544,128]{1,0:T(8,128)(2,1)S(1)} %get-tuple-element.30), channel_id=1, source_target_pairs={{0,2},{2,0},{4,6},{6,4},{8,10},{10,8},{12,14},{14,12},{16,18},{18,... | collective-permute-start | bytes 417800 | tf_op jit(solution)/shard_map/ppermute | solution.py:19
  20.1 6.6 %collective-permute-start.3 = (bf16[544,128]{1,0:T(8,128)(2,1)S(1)}, bf16[544,128]{1,0:T(8,128)(2,1)S(1)}, u32[]{:S(2)}, u32[]{:S(2)}) collective-permute-start(bf16[544,128]{1,0:T(8,128)(2,1)S(1)} %get-tuple-element.31), channel_id=1, source_target_pairs={{0,4},{2,6},{4,0},{6,2},{8,12},{10,14},{12,8},{14,10},{16,20},{18,... | collective-permute-start | bytes 417800 | tf_op jit(solution)/shard_map/ppermute | solution.py:19
  21.6 7.6 %collective-permute-start.4 = (bf16[544,128]{1,0:T(8,128)(2,1)S(1)}, bf16[544,128]{1,0:T(8,128)(2,1)S(1)}, u32[]{:S(2)}, u32[]{:S(2)}) collective-permute-start(bf16[544,128]{1,0:T(8,128)(2,1)S(1)} %get-tuple-element.32), channel_id=1, source_target_pairs={{0,6},{2,4},{4,2},{6,0},{8,14},{10,12},{12,10},{14,8},{16,22},{18,... | collective-permute-start | bytes 417800 | tf_op jit(solution)/shard_map/ppermute | solution.py:19
  22.1 7.1 %collective-permute-start.5 = (bf16[544,128]{1,0:T(8,128)(2,1)S(1)}, bf16[544,128]{1,0:T(8,128)(2,1)S(1)}, u32[]{:S(2)}, u32[]{:S(2)}) collective-permute-start(bf16[544,128]{1,0:T(8,128)(2,1)S(1)} %get-tuple-element.33), channel_id=1, source_target_pairs={{0,8},{2,10},{4,12},{6,14},{8,0},{10,2},{12,4},{14,6},{16,24},{18,... | collective-permute-start | bytes 417800 | tf_op jit(solution)/shard_map/ppermute | solution.py:19
  22.8 9.8 %collective-permute-start.6 = (bf16[544,128]{1,0:T(8,128)(2,1)S(1)}, bf16[544,128]{1,0:T(8,128)(2,1)S(1)}, u32[]{:S(2)}, u32[]{:S(2)}) collective-permute-start(bf16[544,128]{1,0:T(8,128)(2,1)S(1)} %get-tuple-element.34), channel_id=1, source_target_pairs={{0,10},{2,8},{4,14},{6,12},{8,2},{10,0},{12,6},{14,4},{16,26},{18,... | collective-permute-start | bytes 417800 | tf_op jit(solution)/shard_map/ppermute | solution.py:19
  25.1 10.0 %collective-permute-start.7 = (bf16[544,128]{1,0:T(8,128)(2,1)S(1)}, bf16[544,128]{1,0:T(8,128)(2,1)S(1)}, u32[]{:S(2)}, u32[]{:S(2)}) collective-permute-start(bf16[544,128]{1,0:T(8,128)(2,1)S(1)} %get-tuple-element.35), channel_id=1, source_target_pairs={{0,12},{2,14},{4,8},{6,10},{8,4},{10,6},{12,0},{14,2},{16,28},{18,... | collective-permute-start | bytes 417800 | tf_op jit(solution)/shard_map/ppermute | solution.py:19
  26.7 10.2 %collective-permute-start.8 = (bf16[544,128]{1,0:T(8,128)(2,1)S(1)}, bf16[544,128]{1,0:T(8,128)(2,1)S(1)}, u32[]{:S(2)}, u32[]{:S(2)}) collective-permute-start(bf16[544,128]{1,0:T(8,128)(2,1)S(1)} %get-tuple-element.36), channel_id=1, source_target_pairs={{0,14},{2,12},{4,10},{6,8},{8,6},{10,4},{12,2},{14,0},{16,30},{18,... | collective-permute-start | bytes 417800 | tf_op jit(solution)/shard_map/ppermute | solution.py:19
  41.0 7.7 %collective-permute-start.9 = (bf16[544,128]{1,0:T(8,128)(2,1)S(1)}, bf16[544,128]{1,0:T(8,128)(2,1)S(1)}, u32[]{:S(2)}, u32[]{:S(2)}) collective-permute-start(bf16[544,128]{1,0:T(8,128)(2,1)S(1)} %get-tuple-element.38), channel_id=1, source_target_pairs={{0,2},{2,0},{4,6},{6,4},{8,10},{10,8},{12,14},{14,12},{16,18},{18,... | collective-permute-start | bytes 417800 | tf_op jit(solution)/shard_map/ppermute | solution.py:19
  42.5 6.7 %collective-permute-start.10 = (bf16[544,128]{1,0:T(8,128)(2,1)S(1)}, bf16[544,128]{1,0:T(8,128)(2,1)S(1)}, u32[]{:S(2)}, u32[]{:S(2)}) collective-permute-start(bf16[544,128]{1,0:T(8,128)(2,1)S(1)} %get-tuple-element.39), channel_id=1, source_target_pairs={{0,4},{2,6},{4,0},{6,2},{8,12},{10,14},{12,8},{14,10},{16,20},{18,... | collective-permute-start | bytes 417800 | tf_op jit(solution)/shard_map/ppermute | solution.py:19
  43.0 8.7 %collective-permute-start.11 = (bf16[544,128]{1,0:T(8,128)(2,1)S(1)}, bf16[544,128]{1,0:T(8,128)(2,1)S(1)}, u32[]{:S(2)}, u32[]{:S(2)}) collective-permute-start(bf16[544,128]{1,0:T(8,128)(2,1)S(1)} %get-tuple-element.40), channel_id=1, source_target_pairs={{0,6},{2,4},{4,2},{6,0},{8,14},{10,12},{12,10},{14,8},{16,22},{18,... | collective-permute-start | bytes 417800 | tf_op jit(solution)/shard_map/ppermute | solution.py:19
  44.6 7.1 %collective-permute-start.12 = (bf16[544,128]{1,0:T(8,128)(2,1)S(1)}, bf16[544,128]{1,0:T(8,128)(2,1)S(1)}, u32[]{:S(2)}, u32[]{:S(2)}) collective-permute-start(bf16[544,128]{1,0:T(8,128)(2,1)S(1)} %get-tuple-element.41), channel_id=1, source_target_pairs={{0,8},{2,10},{4,12},{6,14},{8,0},{10,2},{12,4},{14,6},{16,24},{18,... | collective-permute-start | bytes 417800 | tf_op jit(solution)/shard_map/ppermute | solution.py:19
  46.2 8.3 %collective-permute-start.13 = (bf16[544,128]{1,0:T(8,128)(2,1)S(1)}, bf16[544,128]{1,0:T(8,128)(2,1)S(1)}, u32[]{:S(2)}, u32[]{:S(2)}) collective-permute-start(bf16[544,128]{1,0:T(8,128)(2,1)S(1)} %get-tuple-element.42), channel_id=1, source_target_pairs={{0,10},{2,8},{4,14},{6,12},{8,2},{10,0},{12,6},{14,4},{16,26},{18,... | collective-permute-start | bytes 417800 | tf_op jit(solution)/shard_map/ppermute | solution.py:19
  48.7 6.6 %collective-permute-start.14 = (bf16[544,128]{1,0:T(8,128)(2,1)S(1)}, bf16[544,128]{1,0:T(8,128)(2,1)S(1)}, u32[]{:S(2)}, u32[]{:S(2)}) collective-permute-start(bf16[544,128]{1,0:T(8,128)(2,1)S(1)} %get-tuple-element.43), channel_id=1, source_target_pairs={{0,12},{2,14},{4,8},{6,10},{8,4},{10,6},{12,0},{14,2},{16,28},{18,... | collective-permute-start | bytes 417800 | tf_op jit(solution)/shard_map/ppermute | solution.py:19
  49.2 8.2 %collective-permute-start.15 = (bf16[544,128]{1,0:T(8,128)(2,1)S(1)}, bf16[544,128]{1,0:T(8,128)(2,1)S(1)}, u32[]{:S(2)}, u32[]{:S(2)}) collective-permute-start(bf16[544,128]{1,0:T(8,128)(2,1)S(1)} %get-tuple-element.44), channel_id=1, source_target_pairs={{0,14},{2,12},{4,10},{6,8},{8,6},{10,4},{12,2},{14,0},{16,30},{18,... | collective-permute-start | bytes 417800 | tf_op jit(solution)/shard_map/ppermute | solution.py:19
  60.2 7.1 %collective-permute-start.16 = (bf16[128,1024]{1,0:T(8,128)(2,1)S(1)}, bf16[128,1024]{1,0:T(8,128)(2,1)S(1)}, u32[]{:S(2)}, u32[]{:S(2)}) collective-permute-start(bf16[128,1024]{1,0:T(8,128)(2,1)S(1)} %get-tuple-element.46), channel_id=1, source_target_pairs={{0,1},{1,0},{2,3},{3,2},{4,5},{5,4},{6,7},{7,6},{8,9},{9,8},{10,11... | collective-permute-start | bytes 786440 | tf_op jit(solution)/shard_map/ppermute | solution.py:23
  60.2 7.1 %collective-permute-start.17 = (bf16[32,1024]{1,0:T(8,128)(2,1)S(1)}, bf16[32,1024]{1,0:T(8,128)(2,1)S(1)}, u32[]{:S(2)}, u32[]{:S(2)}) collective-permute-start(bf16[32,1024]{1,0:T(8,128)(2,1)S(1)} %get-tuple-element.49), channel_id=1, source_target_pairs={{0,16},{2,18},{4,20},{6,22},{8,24},{10,26},{12,28},{14,30},{16,0},... | collective-permute-start | bytes 196616 | tf_op jit(solution)/shard_map/ppermute | solution.py:19

commit v2 on v1

v2 whole, which is shorter than its diff:
```python
import math

import jax
import jax.numpy as jnp
from jax import lax
from jax.experimental import pallas as pl
from jax.experimental.pallas import tpu as pltpu
from jax.sharding import PartitionSpec as P

HDIM = 128
BLOCK = 128
BF16 = jnp.bfloat16
F32 = jnp.float32
VMEM = pl.BlockSpec(memory_space=pltpu.VMEM)
SMEM = pl.BlockSpec(memory_space=pltpu.SMEM)
HBM = pl.BlockSpec(memory_space=pltpu.HBM)


def swap_seq(array, mask):
    return lax.ppermute(array, "seq", [(i, i ^ mask) for i in range(lax.axis_size("seq"))])


def swap_head(array):
    return lax.ppermute(array, "head", [(0, 1), (1, 0)])


def mm(left, right):
    return jnp.dot(left, right, preferred_element_type=F32)


def mm_cols(left, right):
    return lax.dot_general(left, right, (((1,), (1,)), ((), ())), preferred_element_type=F32)


def mm_rows(left, right):
    return lax.dot_general(left, right, (((0,), (0,)), ((), ())), preferred_element_type=F32)


def pool_matrix(rows, shift):
    shape = (rows, rows << shift)
    row = lax.broadcasted_iota(jnp.int32, shape, 0)
    col = lax.broadcasted_iota(jnp.int32, shape, 1)
    return jnp.where(lax.shift_right_logical(col, shift) == row, 1.0, 0.0).astype(BF16)


def call(kernel, out_shape, operands, scratch=(), flops=0, vmem=24, specs=None, free=False, outs=VMEM):
    specs = specs or [VMEM] * len(operands)
    operands = [
        pltpu.with_memory_space_constraint(x, pltpu.HBM) if spec is HBM else x
        for x, spec in zip(operands, specs)
    ]
    moved = 0 if free else sum(x.size * x.dtype.itemsize for x in operands)
    return pl.pallas_call(
        kernel,
        out_shape=out_shape,
        in_specs=specs,
        out_specs=jax.tree.map(lambda _: outs, out_shape),
        scratch_shapes=list(scratch),
        compiler_params=pltpu.CompilerParams(vmem_limit_bytes=vmem << 20),
        cost_estimate=pl.CostEstimate(flops=flops, bytes_accessed=moved, transcendentals=0),
    )(*operands)


def level_pool(rows, level):
    row = lax.broadcasted_iota(jnp.int32, (rows, BLOCK), 0)
    col = lax.broadcasted_iota(jnp.int32, (rows, BLOCK), 1)
    return jnp.where(lax.shift_right_logical(col, level) == row, 1.0, 0.0).astype(BF16)


def col_block(low, mask, width):
    return pl.ds(pl.multiple_of((low ^ mask) * width, width), width)


def piece_rows(level):
    return max(16, BLOCK >> level)


def split_kernel(slots, at_ref, q_hbm, k_hbm, v_hbm, *refs):
    chunk_refs, sems = refs[:slots], refs[slots]
    low = at_ref[0]
    tok, width = BLOCK, chunk_refs[0].shape[1]
    copies = []
    for place, source in enumerate((q_hbm, k_hbm, v_hbm)):
        for mask in range(slots):
            copy = pltpu.make_async_copy(
                source.at[:, col_block(low, mask, width)],
                chunk_refs[mask].at[pl.ds(place * tok, tok), :],
                sems.at[place * slots + mask],
            )
            copy.start()
            copies.append(copy)
    for copy in copies:
        copy.wait()


def coarse_kernel(levels, k_hbm, v_hbm, *refs):
    piece_refs, (k_ref, v_ref, sems) = refs[: len(levels)], refs[len(levels) :]
    copies = [
        pltpu.make_async_copy(k_hbm, k_ref, sems.at[0]),
        pltpu.make_async_copy(v_hbm, v_ref, sems.at[1]),
    ]
    for copy in copies:
        copy.start()
    for copy in copies:
        copy.wait()
    for level, piece in zip(levels, piece_refs):
        rows = piece_rows(level)
        pool = level_pool(rows, level)
        piece[0:rows, :] = (mm(pool, k_ref[...]) * (1.0 / (1 << level))).astype(BF16)
        piece[rows:, :] = mm(pool, v_ref[...]).astype(BF16)


def grad_kernel(at_ref, mine_ref, w_ref, other_ref, out_ref):
    core = at_ref[1]
    half = mine_ref.shape[1]
    first = pl.multiple_of(core * half, half)
    second = pl.multiple_of((1 - core) * half, half)
    total = mm(mine_ref[...], w_ref[pl.ds(first, half), :])
    total += mm(other_ref[...], w_ref[pl.ds(second, half), :])
    out_ref[...] = total.astype(BF16)


def second_kernel(slots, entries, at_ref, grad_ref, *refs):
    far_refs, out_refs = refs[: len(entries)], refs[len(entries) :]
    low = at_ref[0]
    tok, width = BLOCK, out_refs[0].shape[1]
    for mask in range(slots):
        cols = col_block(low, mask, width)
        out_refs[mask][0:tok, :] = grad_ref[:, cols]
        for (place, part, rows), far_ref in zip(entries, far_refs):
            for kind in range(2):
                at = tok + 64 * place + 32 * kind + part * rows
                source = far_ref[kind * rows : kind * rows + rows, cols]
                out_refs[mask][at : at + rows, :] = source


def attend_kernel(slots, far_levels, entries, *refs):
    first_refs, second_refs = refs[:slots], refs[slots : 2 * slots]
    far_refs, refs = refs[2 * slots : 2 * slots + len(entries)], refs[2 * slots + len(entries) :]
    dk_ref, dv_ref, kl_ref, vl_ref, prob_ref, grad_ref = refs[:6]
    q_all, g_all, ck_ref, cv_ref, fk_ref, fv_ref = refs[6:]
    tok = BLOCK
    pairs = slots // 2
    inv_scale = 1.0 / math.sqrt(HDIM)
    to_exp2 = inv_scale * math.log2(math.e)
    near, far = 2 * tok, 3 * tok
    for slab in range(slots):
        pair, row = slab // 2, (slab % 2) * tok
        q_all[pair, row : row + tok, :] = first_refs[slab][0:tok, :]
        kl_ref[pair, row : row + tok, :] = first_refs[slab][tok : 2 * tok, :]
        vl_ref[pair, row : row + tok, :] = first_refs[slab][2 * tok : 3 * tok, :]
        g_all[pair, row : row + tok, :] = second_refs[slab][0:tok, :]
        for place in range(far_levels):
            at = tok + 64 * place
            spot = far + place * BLOCK + 32 * slab
            for each in range(pairs):
                kl_ref[each, spot : spot + 32, :] = second_refs[slab][at : at + 32, :]
                vl_ref[each, spot : spot + 32, :] = second_refs[slab][at + 32 : at + 64, :]
    pool = pool_matrix(BLOCK, 1)
    for pair in range(pairs):
        kl_ref[pair ^ 1, near:far, :] = (mm(pool, kl_ref[pair, 0:near, :]) * 0.5).astype(BF16)
        vl_ref[pair ^ 1, near:far, :] = mm(pool, vl_ref[pair, 0:near, :]).astype(BF16)
    for pair in range(pairs):
        for head in range(2):
            lanes = slice(head * HDIM, head * HDIM + HDIM)
            queries, grads = q_all[pair, :, lanes], g_all[pair, :, lanes]
            keys, values = kl_ref[pair, :, lanes], vl_ref[pair, :, lanes]
            scores = mm_cols(queries, keys)
            prob_grad = mm_cols(grads, values)
            top = jnp.max(scores, axis=1, keepdims=True)
            raised = jnp.exp2((scores - top) * to_exp2)
            inverse = 1.0 / jnp.sum(raised, axis=1, keepdims=True)
            prob = raised * inverse
            centre = jnp.sum(prob * prob_grad, axis=1, keepdims=True)
            prob_low = prob.astype(BF16)
            score_grad = (prob * ((prob_grad - centre) * inv_scale)).astype(BF16)
            prob_ref[2 * pair + head] = prob_low
            grad_ref[2 * pair + head] = score_grad
            key_terms = mm_rows(score_grad, queries)
            value_terms = mm_rows(prob_low, grads)
            for terms, local, level1, distant in (
                (key_terms, dk_ref, ck_ref, fk_ref),
                (value_terms, dv_ref, cv_ref, fv_ref),
            ):
                local[pair * near : pair * near + near, lanes] = terms[0:near]
                level1[pair ^ 1, :, lanes] = terms[near:far].astype(BF16)
                if pair == 0:
                    distant[:, lanes] = terms[far:]
                else:
                    distant[:, lanes] += terms[far:]
    for pair in range(pairs):
        rows = slice(pair * near, pair * near + near)
        dk_ref[rows, :] += mm_rows(pool, ck_ref[pair]) * 0.5
        dv_ref[rows, :] += mm_rows(pool, cv_ref[pair])
    for (place, part, count), out_ref in zip(entries, far_refs):
        for kind, total in enumerate((fk_ref, fv_ref)):
            for slab in range(slots):
                start = place * BLOCK + 32 * slab + part * count
                at = (kind * slots + slab) * count
                out_ref[at : at + count, :] = total[start : start + count, :].astype(BF16)


def reduce_kernel(slots, kl_ref, vl_ref, prob_ref, grad_ref, *refs):
    home_refs, query_refs = refs[:slots], refs[slots:]
    tok = BLOCK
    for pair in range(slots // 2):
        for head in range(2):
            lanes = slice(head * HDIM, head * HDIM + HDIM)
            attended = mm(prob_ref[2 * pair + head], vl_ref[pair, :, lanes]).astype(BF16)
            query_grad = mm(grad_ref[2 * pair + head], kl_ref[pair, :, lanes]).astype(BF16)
            for side in range(2):
                rows = slice(side * tok, side * tok + tok)
                home_refs[2 * pair + side][0:tok, lanes] = attended[rows]
                query_refs[2 * pair + side][:, lanes] = query_grad[rows]


def merge_kernel(slots, levels, dk_ref, dv_ref, *refs):
    query_refs, refs = refs[:slots], refs[slots:]
    far_refs, out_refs = refs[: len(levels)], refs[len(levels) :]
    tok = BLOCK
    for slab in range(slots):
        rows = slice(slab * tok, slab * tok + tok)
        key_sum, value_sum = dk_ref[rows, :], dv_ref[rows, :]
        for level, far_ref in zip(levels, far_refs):
            count = piece_rows(level)
            pool = level_pool(count, level)
            mine = far_ref[slab * count : slab * count + count, :]
            key_sum += mm_rows(pool, mine) * (1.0 / (1 << level))
            at = (slots + slab) * count
            value_sum += mm_rows(pool, far_ref[at : at + count, :])
        out_refs[slab][0:tok, :] = query_refs[slab][...]
        out_refs[slab][tok : 2 * tok, :] = key_sum.astype(BF16)
        out_refs[slab][2 * tok :, :] = value_sum.astype(BF16)


def collect_kernel(slots, at_ref, *refs):
    in_refs, att_ref = refs[:slots], refs[slots]
    low = at_ref[0]
    tok, width = BLOCK, in_refs[0].shape[1]
    for mask in range(slots):
        att_ref[:, col_block(low, mask, width)] = in_refs[mask][0:tok, :]


def project_kernel(at_ref, att_ref, w_ref, keep_ref, *send_refs):
    core = at_ref[1]
    half = att_ref.shape[1]
    part = half // 2
    for place in range(2):
        other = pl.multiple_of((1 - core) * half + place * part, part)
        send = mm_cols(att_ref[...], w_ref[pl.ds(other, part), :])
        send_refs[place][...] = send.astype(BF16)
    first = pl.multiple_of(core * half, half)
    keep_ref[...] = mm_cols(att_ref[...], w_ref[pl.ds(first, half), :])


def add_kernel(keep_ref, left_ref, right_ref, out_ref):
    part = left_ref.shape[1]
    for place, got_ref in enumerate((left_ref, right_ref)):
        cols = slice(place * part, place * part + part)
        out_ref[:, cols] = (keep_ref[:, cols] + got_ref[...].astype(F32)).astype(BF16)


def place_kernel(slots, blocks, at_ref, *refs):
    in_refs, out_refs, sems = refs[:slots], refs[slots:-1], refs[-1]
    low = at_ref[0]
    tok, width = BLOCK, in_refs[0].shape[1]
    copies = []
    for place, block in enumerate(blocks):
        for mask in range(slots):
            copy = pltpu.make_async_copy(
                in_refs[mask].at[pl.ds(block * tok, tok), :],
                out_refs[place].at[:, col_block(low, mask, width)],
                sems.at[place * slots + mask],
            )
            copy.start()
            copies.append(copy)
    for copy in copies:
        copy.wait()


def straight(levels, slots):
    return all((slots << place) * 4 <= 32 for place in range(len(levels)))


def far_entries(levels, slots):
    entries, masks = [], []
    for place, level in enumerate(levels):
        if not straight(levels, slots):
            entries.append((place, 0, 32))
            continue
        for part in range(1 << place):
            entries.append((place, part, BLOCK >> level))
            masks.append(1 << level ^ part * slots)
    return entries, masks


def gather_far(pieces, levels, slots):
    columns = pieces[0].shape[1]
    if straight(levels, slots):
        entries, masks = far_entries(levels, slots)
        return [swap_seq(pieces[entry[0]], mask) for entry, mask in zip(entries, masks)]
    held = {}
    for place, level in enumerate(levels):
        block = pieces[place].reshape(2, piece_rows(level), columns)
        held[level] = block[:, None, : BLOCK >> level]
    found = []
    for step in levels:
        sent = [held[level].reshape(-1, columns) for level in levels if level >= step]
        got = swap_seq(jnp.concatenate(sent, axis=0), 1 << step)
        first = 0
        for level in levels:
            if level < step:
                continue
            count = held[level].size // columns
            part = got[first : first + count].reshape(held[level].shape)
            first += count
            if level == step:
                found.append(part.reshape(64, columns))
            else:
                held[level] = jnp.concatenate([held[level], part], axis=1)
    return found


def scatter_far(packed, levels, slots):
    width = packed[0].shape[1]
    if straight(levels, slots):
        entries, masks = far_entries(levels, slots)
        shares = [swap_seq(array, mask) for array, mask in zip(packed, masks)]
        return shares, [levels[entry[0]] for entry in entries]
    blocks = {}
    for place, level in enumerate(levels):
        rows = BLOCK >> level
        blocks[level] = packed[place].reshape(2 * slots, 32 // rows, rows, width)
    ready = {}
    for step in reversed(levels):
        sent, kept = [blocks[step].reshape(-1, width)], {}
        for level in levels:
            if level > step:
                size = ready[level].shape[1] // 2
                kept[level] = ready[level][:, :size]
                sent.append(ready[level][:, size:].astype(BF16).reshape(-1, width))
        got = swap_seq(jnp.concatenate(sent, axis=0), 1 << step)
        first = blocks[step].size // width
        ready[step] = got[0:first].reshape(blocks[step].shape)
        for level in kept:
            count = kept[level].size // width
            part = got[first : first + count].reshape(kept[level].shape)
            first += count
            ready[level] = kept[level].astype(F32) + part.astype(F32)
    shares = []
    for level in levels:
        share = ready[level].astype(BF16).reshape(2 * slots, -1, width)
        pad = piece_rows(level) - share.shape[1]
        if pad:
            share = jnp.pad(share, ((0, 0), (0, pad), (0, 0)))
        shares.append(share.reshape(-1, width))
    return shares, list(levels)


def on_device(queries, key_tokens, value_tokens, out_weight, output_grad):
    tok, columns = queries.shape
    heads = columns // HDIM
    slots = heads // 2
    width = columns // slots
    local_levels = slots.bit_length() - 1
    level_count = lax.axis_size("seq").bit_length() - 1
    far = list(range(local_levels, level_count))
    far_rows = 64 * len(far)
    list_rows = 3 * tok + BLOCK * len(far)
    entries, _ = far_entries(far, slots)
    place = jnp.stack([lax.axis_index("seq") & (slots - 1), lax.axis_index("head")])
    place = place.astype(jnp.int32)

    def shape(dims, dtype=BF16):
        return jax.ShapeDtypeStruct(dims, dtype)

    def over(rows):
        return [shape((rows, width))] * slots

    def exchange(chunks):
        got = {0: chunks[0]}
        for mask in sorted(range(1, slots), key=lambda mask: (mask + 1) % 2):
            got[mask] = swap_seq(chunks[mask], mask)
        return [got[mask] for mask in range(slots)]

    other_grad = swap_head(output_grad)
    pieces = call(
        lambda *refs: coarse_kernel(far, *refs),
        [shape((2 * piece_rows(level), columns)) for level in far],
        (key_tokens, value_tokens),
        scratch=[pltpu.VMEM((tok, columns), BF16)] * 2 + [pltpu.SemaphoreType.DMA((2,))],
        specs=[HBM] * 2,
        vmem=8,
    )
    pieces, later, other_grad = lax.optimization_barrier((pieces, place, other_grad))
    far_got = gather_far(pieces, far, slots)
    chunks = call(
        lambda *refs: split_kernel(slots, *refs),
        over(3 * tok),
        (later, queries, key_tokens, value_tokens),
        scratch=[pltpu.SemaphoreType.DMA((3 * slots,))],
        flops=6 * 10**9,
        specs=[SMEM] + [HBM] * 3,
        vmem=8,
    )
    first = exchange(chunks)
    grads = call(
        grad_kernel,
        shape((tok, columns)),
        [place, output_grad, out_weight, other_grad],
        flops=4 * tok * columns * columns,
        specs=[SMEM] + [VMEM] * 3,
        vmem=16,
    )
    chunks = call(
        lambda *refs: second_kernel(slots, entries, *refs),
        over(tok + far_rows),
        [place, grads] + far_got,
        specs=[SMEM] + [VMEM] * (1 + len(far_got)),
        vmem=8,
    )
    second = exchange(chunks)
    pairs = slots // 2
    lists = [shape((pairs, list_rows, width))] * 2
    made = call(
        lambda *refs: attend_kernel(slots, len(far), entries, *refs),
        [shape((2 * slots * rows, width)) for _, _, rows in entries]
        + [shape((slots * tok, width), F32)] * 2
        + lists
        + [shape((slots, 2 * tok, list_rows))] * 2,
        first + second,
        scratch=[
            pltpu.VMEM((pairs, 2 * tok, width), BF16),
            pltpu.VMEM((pairs, 2 * tok, width), BF16),
            pltpu.VMEM((pairs, BLOCK, width), BF16),
            pltpu.VMEM((pairs, BLOCK, width), BF16),
            pltpu.VMEM((BLOCK * len(far), width), F32),
            pltpu.VMEM((BLOCK * len(far), width), F32),
        ],
        flops=8 * heads * tok * list_rows * HDIM,
    )
    shares, share_levels = scatter_far(made[: len(entries)], far, slots)
    key_sum, value_sum, *made = made[len(entries) :]
    made = call(
        lambda *refs: reduce_kernel(slots, *refs),
        over(tok) + over(tok),
        made,
        flops=6 * 10**9,
        vmem=16,
    )
    home = exchange(made[:slots])
    chunks = call(
        lambda *refs: merge_kernel(slots, share_levels, *refs),
        over(3 * tok),
        [key_sum, value_sum] + list(made[slots:]) + shares,
        vmem=8,
    )
    last = exchange(chunks)
    wide = shape((tok, columns))
    attended = call(
        lambda *refs: collect_kernel(slots, *refs),
        wide,
        [place] + home,
        specs=[SMEM] + [VMEM] * slots,
        vmem=8,
    )
    keep, *send = call(
        project_kernel,
        [shape((tok, columns), F32)] + [shape((tok, columns // 2))] * 2,
        [place, attended, out_weight],
        flops=4 * 10**9,
        specs=[SMEM, VMEM, VMEM],
        vmem=16,
    )
    got = [swap_head(part) for part in send]
    output = call(add_kernel, wide, [keep] + got, vmem=8)

    def put(chunks, blocks):
        return call(
            lambda *refs: place_kernel(slots, blocks, *refs),
            [wide] * len(blocks),
            [place] + chunks,
            scratch=[pltpu.SemaphoreType.DMA((len(blocks) * slots,))],
            specs=[SMEM] + [VMEM] * slots,
            vmem=8,
            free=True,
            outs=HBM,
        )

    query_grad, key_grad, value_grad = put(last, (0, 1, 2))
    return output, query_grad, key_grad, value_grad


def solution(mesh):
    placed = P("seq", "head")
    return jax.shard_map(
        on_device,
        mesh=mesh,
        in_specs=(placed, placed, placed, P(None, "head"), placed),
        out_specs=(placed, placed, placed, placed),
        check_vma=False,
    )
```

time: 68.8 us -> 56.5 us (0.82)
  waiting for transfers between devices: 23.5 us -> 14.1 us
  local copies, waits for them, and re-layouts: 7.89 us -> 0.01 us
  Pallas kernels: 9.72 us -> 15.3 us
    ppermute x16 -> x18, waiting for transfers between devices: 23.5 us -> 13.1 us  [swap_seq(): lax.ppermute(array, 'seq', [(i, i ^ mask) for i in range(lax.axis_size('s...]
    unnamed x16 -> x4, local copies, waits for them, and re-layouts: 7.89 us -> 0.01 us
    pallas_call x5 -> x11, Pallas kernels: 9.72 us -> 15.3 us  [call(): pl.pallas_call(kernel, out_shape=out_shape, in_specs=specs, out_specs=jax...]
    ppermute x2 -> x3, waiting for transfers between devices: 0.01 us -> 1.03 us  [swap_head(): return lax.ppermute(array, 'head', [(0, 1), (1, 0)])]
    ppermute x16 -> x18, starting transfers between devices: 26.1 us -> 25.1 us  [swap_seq(): lax.ppermute(array, 'seq', [(i, i ^ mask) for i in range(lax.axis_size('s...]
  transfers between devices with their start and end apart: 18 -> 21, of which waited for: 11 -> 9; matrix products, arithmetic and copies ran while one was open for 0% -> 0% of each run, Pallas kernels for 0% -> 12%
where the time goes in v2:
time: 56.5 us; the launch traced here: 56.4 us
  starting transfers between devices  26.2 us (46%)
  Pallas kernels  15.3 us (27%)
  waiting for transfers between devices  14.1 us (25%)
  between operations  0.74 us (1%)
    ppermute x18, starting transfers between devices, swap_seq(): lax.ppermute(array, 'seq', [(i, i ^ mask) for i in range(lax.axis_size('s...  25.1 us
    pallas_call x11, Pallas kernels, call(): pl.pallas_call(kernel, out_shape=out_shape, in_specs=specs, out_specs=jax...  15.3 us
    ppermute x18, waiting for transfers between devices, swap_seq(): lax.ppermute(array, 'seq', [(i, i ^ mask) for i in range(lax.axis_size('s...  13.1 us
  transfers between devices with their start and end apart: 21, of which 9 were waited for; matrix products, arithmetic and copies ran while one was open for 0% of the time, Pallas kernels for 12%

profile of v2, /device:TPU:0, one launch (start us, length us, event | category | flops | bytes accessed | tf_op | source)
XLA Modules:
  0.0 56.4 jit_solution(17319154066390941022)
XLA Ops:
  0.6 0.5 collective-permute-start
  1.1 1.3 %shard_map.84 = (bf16[64,1024]{1,0:T(8,128)(2,1)S(1)}, bf16[32,1024]{1,0:T(8,128)(2,1)S(1)}) custom-call(bf16[128,1024]{1,0:T(8,128)(2,1)} %refs_2_.1, bf16[128,1024]{1,0:T(8,128)(2,1)} %refs_3_.1), custom_call_target="tpu_custom_call" | custom-call | bytes 524288 | tf_op jit(solution)/shard_map/pallas_call | solution.py:53
  2.5 0.1 pad_add_fusion.refs_0_.at_ref
  2.6 0.0 collective-permute-done.other_ref
  2.6 0.0 copy-start
  2.6 0.0 copy-start.1
  2.6 2.1 %shard_map.85 = (bf16[384,256]{1,0:T(8,128)(2,1)S(1)}, bf16[384,256]{1,0:T(8,128)(2,1)S(1)}, bf16[384,256]{1,0:T(8,128)(2,1)S(1)}, bf16[384,256]{1,0:T(8,128)(2,1)S(1)}) custom-call(s32[2]{0:T(128)S(1)} %pad_add_fusion.refs_0_.at_ref, bf16[128,1024]{1,0:T(8,128)(2,1)} %refs_1_.3, bf16[128,1024]{1,0:T(8,128)(2,1)} %refs_2_.1, bf16[128,1024]{1,0:T(8,128)(2,1)} %refs_3_.1), custom_call_target="tpu_custom_call" | custom-call | flops 6000000000 | bytes 786440 | tf_op jit(solution)/shard_map/pallas_call | solution.py:53
  4.6 2.9 %collective-permute-start.1 = (bf16[384,256]{1,0:T(8,128)(2,1)S(1)}, bf16[384,256]{1,0:T(8,128)(2,1)S(1)}, u32[]{:S(2)}, u32[]{:S(2)}) collective-permute-start(bf16[384,256]{1,0:T(8,128)(2,1)S(1)} %get-tuple-element.49), channel_id=1, source_target_pairs={{0,2},{2,0},{4,6},{6,4},{8,10},{10,8},{12,14},{14,12},{16,18},{18,... | collective-permute-start | bytes 589832 | tf_op jit(solution)/shard_map/ppermute | solution.py:20
  7.5 1.6 %collective-permute-start.4 = (bf16[64,1024]{1,0:T(8,128)(2,1)S(1)}, bf16[64,1024]{1,0:T(8,128)(2,1)S(1)}, u32[]{:S(2)}, u32[]{:S(2)}) collective-permute-start(bf16[64,1024]{1,0:T(8,128)(2,1)S(1)} %get-tuple-element.53), channel_id=1, source_target_pairs={{0,8},{2,10},{4,12},{6,14},{8,0},{10,2},{12,4},{14,6},{16,24},{18,... | collective-permute-start | bytes 393224 | tf_op jit(solution)/shard_map/ppermute | solution.py:20
  9.1 2.5 %collective-permute-start.6 = (bf16[32,1024]{1,0:T(8,128)(2,1)S(1)}, bf16[32,1024]{1,0:T(8,128)(2,1)S(1)}, u32[]{:S(2)}, u32[]{:S(2)}) collective-permute-start(bf16[32,1024]{1,0:T(8,128)(2,1)S(1)} %get-tuple-element.54), channel_id=1, source_target_pairs={{0,24},{2,26},{4,28},{6,30},{8,16},{10,18},{12,20},{14,22},{16,8},... | collective-permute-start | bytes 196616 | tf_op jit(solution)/shard_map/ppermute | solution.py:20
  11.6 0.1 collective-permute-start.5
  11.7 1.5 %collective-permute-start.2 = (bf16[384,256]{1,0:T(8,128)(2,1)S(1)}, bf16[384,256]{1,0:T(8,128)(2,1)S(1)}, u32[]{:S(2)}, u32[]{:S(2)}) collective-permute-start(bf16[384,256]{1,0:T(8,128)(2,1)S(1)} %get-tuple-element.50), channel_id=1, source_target_pairs={{0,4},{2,6},{4,0},{6,2},{8,12},{10,14},{12,8},{14,10},{16,20},{18,... | collective-permute-start | bytes 589832 | tf_op jit(solution)/shard_map/ppermute | solution.py:20
  13.2 3.8 %collective-permute-done.6.refs_4_ = bf16[32,1024]{1,0:T(8,128)(2,1)S(1)} collective-permute-done((bf16[32,1024]{1,0:T(8,128)(2,1)S(1)}, bf16[32,1024]{1,0:T(8,128)(2,1)S(1)}, u32[]{:S(2)}, u32[]{:S(2)}) %collective-permute-start.6) | collective-permute-done | bytes 65568 | tf_op jit(solution)/shard_map/ppermute | solution.py:20
  17.1 1.5 %collective-permute-start.3 = (bf16[384,256]{1,0:T(8,128)(2,1)S(1)}, bf16[384,256]{1,0:T(8,128)(2,1)S(1)}, u32[]{:S(2)}, u32[]{:S(2)}) collective-permute-start(bf16[384,256]{1,0:T(8,128)(2,1)S(1)} %get-tuple-element.51), channel_id=1, source_target_pairs={{0,6},{2,4},{4,2},{6,0},{8,14},{10,12},{12,10},{14,8},{16,22},{18,... | collective-permute-start | bytes 589832 | tf_op jit(solution)/shard_map/ppermute | solution.py:20
  18.6 0.0 copy-done
  18.6 0.0 copy-done.1
  18.6 1.3 %shard_map.86.refs_1_ = bf16[128,1024]{1,0:T(8,128)(2,1)S(1)} custom-call(s32[2]{0:T(128)S(1)} %pad_add_fusion.refs_0_.at_ref, bf16[128,1024]{1,0:T(8,128)(2,1)S(1)} %copy-done.1, bf16[2048,1024]{1,0:T(8,128)(2,1)S(1)} %copy-done, bf16[128,1024]{1,0:T(8,128)(2,1)S(1)} %collective-permute-done.other_ref), custom_call_target="tpu_custom_call" | custom-call | flops 536870912 | bytes 4718600 | tf_op jit(solution)/shard_map/pallas_call | solution.py:53
  19.8 0.0 collective-permute-done.5.refs_3_
  19.8 0.0 collective-permute-done.4.refs_2_
  19.9 0.6 %shard_map.87 = (bf16[256,256]{1,0:T(8,128)(2,1)S(1)}, bf16[256,256]{1,0:T(8,128)(2,1)S(1)}, bf16[256,256]{1,0:T(8,128)(2,1)S(1)}, bf16[256,256]{1,0:T(8,128)(2,1)S(1)}) custom-call(s32[2]{0:T(128)S(1)} %pad_add_fusion.refs_0_.at_ref, bf16[128,1024]{1,0:T(8,128)(2,1)S(1)} %shard_map.86.refs_1_, bf16[64,1024]{1,0:T(8,128)(2,1)S(1)} %collective-permute-done.4.refs_2_, ...), custom_call_target="tpu_custom_call" | custom-call | bytes 524296 | tf_op jit(solution)/shard_map/pallas_call | solution.py:53
  20.5 1.6 %collective-permute-start.7 = (bf16[256,256]{1,0:T(8,128)(2,1)S(1)}, bf16[256,256]{1,0:T(8,128)(2,1)S(1)}, u32[]{:S(2)}, u32[]{:S(2)}) collective-permute-start(bf16[256,256]{1,0:T(8,128)(2,1)S(1)} %get-tuple-element.56), channel_id=1, source_target_pairs={{0,2},{2,0},{4,6},{6,4},{8,10},{10,8},{12,14},{14,12},{16,18},{18,... | collective-permute-start | bytes 393224 | tf_op jit(solution)/shard_map/ppermute | solution.py:20
  22.0 0.5 collective-permute-start.8
  22.5 0.0 collective-permute-done.1.refs_1_
  22.5 1.5 %collective-permute-start.9 = (bf16[256,256]{1,0:T(8,128)(2,1)S(1)}, bf16[256,256]{1,0:T(8,128)(2,1)S(1)}, u32[]{:S(2)}, u32[]{:S(2)}) collective-permute-start(bf16[256,256]{1,0:T(8,128)(2,1)S(1)} %get-tuple-element.58), channel_id=1, source_target_pairs={{0,6},{2,4},{4,2},{6,0},{8,14},{10,12},{12,10},{14,8},{16,22},{18,... | collective-permute-start | bytes 393224 | tf_op jit(solution)/shard_map/ppermute | solution.py:20
  24.0 0.0 collective-permute-done.2.refs_2_
  24.0 1.3 %collective-permute-done.3.refs_3_ = bf16[384,256]{1,0:T(8,128)(2,1)S(1)} collective-permute-done((bf16[384,256]{1,0:T(8,128)(2,1)S(1)}, bf16[384,256]{1,0:T(8,128)(2,1)S(1)}, u32[]{:S(2)}, u32[]{:S(2)}) %collective-permute-start.3) | collective-permute-done | bytes 196640 | tf_op jit(solution)/shard_map/ppermute | solution.py:20
  25.4 1.7 %collective-permute-done.7.refs_5_ = bf16[256,256]{1,0:T(8,128)(2,1)S(1)} collective-permute-done((bf16[256,256]{1,0:T(8,128)(2,1)S(1)}, bf16[256,256]{1,0:T(8,128)(2,1)S(1)}, u32[]{:S(2)}, u32[]{:S(2)}) %collective-permute-start.7) | collective-permute-done | bytes 131104 | tf_op jit(solution)/shard_map/ppermute | solution.py:20
  27.1 2.4 %collective-permute-done.8.refs_6_ = bf16[256,256]{1,0:T(8,128)(2,1)S(1)} collective-permute-done((bf16[256,256]{1,0:T(8,128)(2,1)S(1)}, bf16[256,256]{1,0:T(8,128)(2,1)S(1)}, u32[]{:S(2)}, u32[]{:S(2)}) %collective-permute-start.8) | collective-permute-done | bytes 131104 | tf_op jit(solution)/shard_map/ppermute | solution.py:20
  29.5 0.0 collective-permute-done.9.refs_7_
  29.5 3.7 %shard_map.88 = (bf16[256,256]{1,0:T(8,128)(2,1)S(1)}, bf16[128,256]{1,0:T(8,128)(2,1)S(1)}, bf16[128,256]{1,0:T(8,128)(2,1)S(1)}, f32[512,256]{1,0:T(8,128)S(1)...) custom-call(bf16[384,256]{1,0:T(8,128)(2,1)S(1)} %get-tuple-element., ...), custom_call_target="tpu_custom_call" | custom-call | flops 671088640 | bytes 1310720 | tf_op jit(solution)/shard_map/pallas_call | solution.py:53
  33.2 0.8 %shard_map.89 = (bf16[128,256]{1,0:T(8,128)(2,1)S(1)}, bf16[128,256]{1,0:T(8,128)(2,1)S(1)}, bf16[128,256]{1,0:T(8,128)(2,1)S(1)}, bf16[128,256]{1,0:T(8,128)(2,...) custom-call(bf16[2,640,256]{2,1,0:T(8,128)(2,1)S(1)} %get-tuple-elem, ...), custom_call_target="tpu_custom_call" | custom-call | flops 6000000000 | bytes 3932160 | tf_op jit(solution)/shard_map/pallas_call | solution.py:53
  34.0 0.5 collective-permute-start.10
  34.5 0.0 collective-permute-start.15
  34.5 1.4 %collective-permute-start.11 = (bf16[128,256]{1,0:T(8,128)(2,1)S(1)}, bf16[128,256]{1,0:T(8,128)(2,1)S(1)}, u32[]{:S(2)}, u32[]{:S(2)}) collective-permute-start(bf16[128,256]{1,0:T(8,128)(2,1)S(1)} %get-tuple-element.65), channel_id=1, source_target_pairs={{0,4},{2,6},{4,0},{6,2},{8,12},{10,14},{12,8},{14,10},{16,20},{18,... | collective-permute-start | bytes 196616 | tf_op jit(solution)/shard_map/ppermute | solution.py:20
  35.9 1.7 %collective-permute-start.12 = (bf16[128,256]{1,0:T(8,128)(2,1)S(1)}, bf16[128,256]{1,0:T(8,128)(2,1)S(1)}, u32[]{:S(2)}, u32[]{:S(2)}) collective-permute-start(bf16[128,256]{1,0:T(8,128)(2,1)S(1)} %get-tuple-element.66), channel_id=1, source_target_pairs={{0,6},{2,4},{4,2},{6,0},{8,14},{10,12},{12,10},{14,8},{16,22},{18,... | collective-permute-start | bytes 196616 | tf_op jit(solution)/shard_map/ppermute | solution.py:20
  37.6 2.1 %collective-permute-start.16 = (bf16[128,256]{1,0:T(8,128)(2,1)S(1)}, bf16[128,256]{1,0:T(8,128)(2,1)S(1)}, u32[]{:S(2)}, u32[]{:S(2)}) collective-permute-start(bf16[128,256]{1,0:T(8,128)(2,1)S(1)} %get-tuple-element.77), channel_id=1, source_target_pairs={{0,16},{2,18},{4,20},{6,22},{8,24},{10,26},{12,28},{14,30},{16,0},... | collective-permute-start | bytes 196616 | tf_op jit(solution)/shard_map/ppermute | solution.py:20
  39.6 0.0 collective-permute-done.10.refs_2_
  39.6 2.3 %collective-permute-start.17 = (bf16[128,256]{1,0:T(8,128)(2,1)S(1)}, bf16[128,256]{1,0:T(8,128)(2,1)S(1)}, u32[]{:S(2)}, u32[]{:S(2)}) collective-permute-start(bf16[128,256]{1,0:T(8,128)(2,1)S(1)} %get-tuple-element.78), channel_id=1, source_target_pairs={{0,24},{2,26},{4,28},{6,30},{8,16},{10,18},{12,20},{14,22},{16,8},... | collective-permute-start | bytes 196616 | tf_op jit(solution)/shard_map/ppermute | solution.py:20
  41.9 0.0 collective-permute-done.11.refs_3_
  42.0 0.0 collective-permute-done.12.refs_4_
  42.0 0.6 %shard_map.90.att_ref = bf16[128,1024]{1,0:T(8,128)(2,1)S(1)} custom-call(s32[2]{0:T(128)S(1)} %pad_add_fusion.refs_0_.at_ref, bf16[128,256]{1,0:T(8,128)(2,1)S(1)} %get-tuple-element.63.refs_1_, bf16[128,256]{1,0:T(8,128)(2,1)S(1)} %collective-permute-done.10.refs_2_, bf16[128,256]{1,0:T(8,128)(2,1)S(1)} %collective-permute-done.11.refs_3_, ...), custom_call_target="tpu_custom_call" | custom-call | bytes 262152 | tf_op jit(solution)/shard_map/pallas_call | solution.py:53
  42.5 0.7 %collective-permute-done.16.refs_7_ = bf16[128,256]{1,0:T(8,128)(2,1)S(1)} collective-permute-done((bf16[128,256]{1,0:T(8,128)(2,1)S(1)}, bf16[128,256]{1,0:T(8,128)(2,1)S(1)}, u32[]{:S(2)}, u32[]{:S(2)}) %collective-permute-start.16) | collective-permute-done | bytes 65568 | tf_op jit(solution)/shard_map/ppermute | solution.py:20
  43.2 2.5 %collective-permute-done.17.refs_8_ = bf16[128,256]{1,0:T(8,128)(2,1)S(1)} collective-permute-done((bf16[128,256]{1,0:T(8,128)(2,1)S(1)}, bf16[128,256]{1,0:T(8,128)(2,1)S(1)}, u32[]{:S(2)}, u32[]{:S(2)}) %collective-permute-start.17) | collective-permute-done | bytes 65568 | tf_op jit(solution)/shard_map/ppermute | solution.py:20
  45.7 0.0 collective-permute-done.15.refs_6_
  45.7 0.6 %shard_map.93 = (bf16[384,256]{1,0:T(8,128)(2,1)S(1)}, bf16[384,256]{1,0:T(8,128)(2,1)S(1)}, bf16[384,256]{1,0:T(8,128)(2,1)S(1)}, bf16[384,256]{1,0:T(8,128)(2,1)S(1)}) custom-call(f32[512,256]{1,0:T(8,128)S(1)} %get-tuple-element.70.refs_0_, f32[512,256]{1,0:T(8,128)S(1)} %get-tuple-element.71.refs_1_, bf16[128,256]{1,0:T(8,128)(2,1)S(1)} %get-tuple-element.72.refs_2_, ...), custom_call_target="tpu_custom_call" | custom-call | bytes 1572864 | tf_op jit(solution)/shard_map/pallas_call | solution.py:53
  46.3 0.5 collective-permute-start.18
  46.8 1.5 %collective-permute-start.19 = (bf16[384,256]{1,0:T(8,128)(2,1)S(1)}, bf16[384,256]{1,0:T(8,128)(2,1)S(1)}, u32[]{:S(2)}, u32[]{:S(2)}) collective-permute-start(bf16[384,256]{1,0:T(8,128)(2,1)S(1)} %get-tuple-element.81), channel_id=1, source_target_pairs={{0,4},{2,6},{4,0},{6,2},{8,12},{10,14},{12,8},{14,10},{16,20},{18,... | collective-permute-start | bytes 589832 | tf_op jit(solution)/shard_map/ppermute | solution.py:20
  48.3 1.5 %collective-permute-start.20 = (bf16[384,256]{1,0:T(8,128)(2,1)S(1)}, bf16[384,256]{1,0:T(8,128)(2,1)S(1)}, u32[]{:S(2)}, u32[]{:S(2)}) collective-permute-start(bf16[384,256]{1,0:T(8,128)(2,1)S(1)} %get-tuple-element.82), channel_id=1, source_target_pairs={{0,6},{2,4},{4,2},{6,0},{8,14},{10,12},{12,10},{14,8},{16,22},{18,... | collective-permute-start | bytes 589832 | tf_op jit(solution)/shard_map/ppermute | solution.py:20
  49.8 2.1 %shard_map.91 = (f32[128,1024]{1,0:T(8,128)S(1)}, bf16[128,512]{1,0:T(8,128)(2,1)S(1)}, bf16[128,512]{1,0:T(8,128)(2,1)S(1)}) custom-call(s32[2]{0:T(128)S(1)} %pad_add_fusion.refs_0_.at_ref, bf16[128,1024]{1,0:T(8,128)(2,1)S(1)} %shard_map.90.att_ref, bf16[2048,1024]{1,0:T(8,128)(2,1)S(1)} %copy-done), custom_call_target="tpu_custom_call" | custom-call | flops 4000000000 | bytes 4456456 | tf_op jit(solution)/shard_map/pallas_call | solution.py:53
  51.9 0.1 collective-permute-start.13
  52.0 0.5 collective-permute-start.14
  52.5 0.8 %collective-permute-done.13.left_ref = bf16[128,512]{1,0:T(8,128)(2,1)S(1)} collective-permute-done((bf16[128,512]{1,0:T(8,128)(2,1)S(1)}, bf16[128,512]{1,0:T(8,128)(2,1)S(1)}, u32[]{:S(2)}, u32[]{:S(2)}) %collective-permute-start.13) | collective-permute-done | bytes 131104 | tf_op jit(solution)/shard_map/ppermute | solution.py:24
  53.3 0.2 collective-permute-done.14.right_ref
  53.5 0.8 %shard_map.92 = bf16[128,1024]{1,0:T(8,128)(2,1)} custom-call(f32[128,1024]{1,0:T(8,128)S(1)} %get-tuple-element.67.keep_ref, bf16[128,512]{1,0:T(8,128)(2,1)S(1)} %collective-permute-done.13.left_ref, bf16[128,512]{1,0:T(8,128)(2,1)S(1)} %collective-permute-done.14.right_ref), custom_call_target="tpu_custom_call" | custom-call | bytes 786432 | tf_op jit(solution)/shard_map/pallas_call | solution.py:53
  54.3 0.0 collective-permute-done.18.refs_2_
  54.3 0.0 collective-permute-done.19.refs_3_
  54.3 0.6 %collective-permute-done.20.refs_4_ = bf16[384,256]{1,0:T(8,128)(2,1)S(1)} collective-permute-done((bf16[384,256]{1,0:T(8,128)(2,1)S(1)}, bf16[384,256]{1,0:T(8,128)(2,1)S(1)}, u32[]{:S(2)}, u32[]{:S(2)}) %collective-permute-start.20) | collective-permute-done | bytes 196640 | tf_op jit(solution)/shard_map/ppermute | solution.py:20
  54.9 1.5 %shard_map.94 = (bf16[128,1024]{1,0:T(8,128)(2,1)}, bf16[128,1024]{1,0:T(8,128)(2,1)}, bf16[128,1024]{1,0:T(8,128)(2,1)}) custom-call(s32[2]{0:T(128)S(1)} %pad_add_fusion.refs_0_.at_ref, bf16[384,256]{1,0:T(8,128)(2,1)S(1)} %get-tuple-element.79.refs_1_, bf16[384,256]{1,0:T(8,128)(2,1)S(1)} %collective-permute-done.18.refs_2_, ...), custom_call_target="tpu_custom_call" | custom-call | tf_op jit(solution)/shard_map/pallas_call | solution.py:53
Async XLA Ops:
  0.6 1.9 %collective-permute-start = (bf16[128,1024]{1,0:T(8,128)(2,1)}, bf16[128,1024]{1,0:T(8,128)(2,1)S(1)}, u32[]{:S(2)}, u32[]{:S(2)}) collective-permute-start(bf16[128,1024]{1,0:T(8,128)(2,1)} %mine_ref.1), channel_id=1, source_target_pairs={{0,1},{1,0},{2,3},{3,2},{4,5},{5,4},{6,7},{7,6},{8,9},{9,8},{10,11... | collective-permute-start | bytes 786440 | tf_op jit(solution)/shard_map/ppermute | solution.py:24
  2.6 16.0 %copy-start = (bf16[2048,1024]{1,0:T(8,128)(2,1)S(1)}, bf16[2048,1024]{1,0:T(8,128)(2,1)}, u32[]{:S(2)}) copy-start(bf16[2048,1024]{1,0:T(8,128)(2,1)} %w_ref.3) | copy-start | bytes 12582916
  2.6 16.0 %copy-start.1 = (bf16[128,1024]{1,0:T(8,128)(2,1)S(1)}, bf16[128,1024]{1,0:T(8,128)(2,1)}, u32[]{:S(2)}) copy-start(bf16[128,1024]{1,0:T(8,128)(2,1)} %mine_ref.1) | copy-start | bytes 786436
  4.6 17.9 %collective-permute-start.1 = (bf16[384,256]{1,0:T(8,128)(2,1)S(1)}, bf16[384,256]{1,0:T(8,128)(2,1)S(1)}, u32[]{:S(2)}, u32[]{:S(2)}) collective-permute-start(bf16[384,256]{1,0:T(8,128)(2,1)S(1)} %get-tuple-element.49), channel_id=1, source_target_pairs={{0,2},{2,0},{4,6},{6,4},{8,10},{10,8},{12,14},{14,12},{16,18},{18,... | collective-permute-start | bytes 589832 | tf_op jit(solution)/shard_map/ppermute | solution.py:20
  7.5 12.3 %collective-permute-start.4 = (bf16[64,1024]{1,0:T(8,128)(2,1)S(1)}, bf16[64,1024]{1,0:T(8,128)(2,1)S(1)}, u32[]{:S(2)}, u32[]{:S(2)}) collective-permute-start(bf16[64,1024]{1,0:T(8,128)(2,1)S(1)} %get-tuple-element.53), channel_id=1, source_target_pairs={{0,8},{2,10},{4,12},{6,14},{8,0},{10,2},{12,4},{14,6},{16,24},{18,... | collective-permute-start | bytes 393224 | tf_op jit(solution)/shard_map/ppermute | solution.py:20
  9.1 8.0 %collective-permute-start.6 = (bf16[32,1024]{1,0:T(8,128)(2,1)S(1)}, bf16[32,1024]{1,0:T(8,128)(2,1)S(1)}, u32[]{:S(2)}, u32[]{:S(2)}) collective-permute-start(bf16[32,1024]{1,0:T(8,128)(2,1)S(1)} %get-tuple-element.54), channel_id=1, source_target_pairs={{0,24},{2,26},{4,28},{6,30},{8,16},{10,18},{12,20},{14,22},{16,8},... | collective-permute-start | bytes 196616 | tf_op jit(solution)/shard_map/ppermute | solution.py:20
  11.6 8.2 %collective-permute-start.5 = (bf16[32,1024]{1,0:T(8,128)(2,1)S(1)}, bf16[32,1024]{1,0:T(8,128)(2,1)S(1)}, u32[]{:S(2)}, u32[]{:S(2)}) collective-permute-start(bf16[32,1024]{1,0:T(8,128)(2,1)S(1)} %get-tuple-element.54), channel_id=1, source_target_pairs={{0,16},{2,18},{4,20},{6,22},{8,24},{10,26},{12,28},{14,30},{16,0},... | collective-permute-start | bytes 196616 | tf_op jit(solution)/shard_map/ppermute | solution.py:20
  11.7 12.3 %collective-permute-start.2 = (bf16[384,256]{1,0:T(8,128)(2,1)S(1)}, bf16[384,256]{1,0:T(8,128)(2,1)S(1)}, u32[]{:S(2)}, u32[]{:S(2)}) collective-permute-start(bf16[384,256]{1,0:T(8,128)(2,1)S(1)} %get-tuple-element.50), channel_id=1, source_target_pairs={{0,4},{2,6},{4,0},{6,2},{8,12},{10,14},{12,8},{14,10},{16,20},{18,... | collective-permute-start | bytes 589832 | tf_op jit(solution)/shard_map/ppermute | solution.py:20
  17.1 8.3 %collective-permute-start.3 = (bf16[384,256]{1,0:T(8,128)(2,1)S(1)}, bf16[384,256]{1,0:T(8,128)(2,1)S(1)}, u32[]{:S(2)}, u32[]{:S(2)}) collective-permute-start(bf16[384,256]{1,0:T(8,128)(2,1)S(1)} %get-tuple-element.51), channel_id=1, source_target_pairs={{0,6},{2,4},{4,2},{6,0},{8,14},{10,12},{12,10},{14,8},{16,22},{18,... | collective-permute-start | bytes 589832 | tf_op jit(solution)/shard_map/ppermute | solution.py:20
  20.5 6.6 %collective-permute-start.7 = (bf16[256,256]{1,0:T(8,128)(2,1)S(1)}, bf16[256,256]{1,0:T(8,128)(2,1)S(1)}, u32[]{:S(2)}, u32[]{:S(2)}) collective-permute-start(bf16[256,256]{1,0:T(8,128)(2,1)S(1)} %get-tuple-element.56), channel_id=1, source_target_pairs={{0,2},{2,0},{4,6},{6,4},{8,10},{10,8},{12,14},{14,12},{16,18},{18,... | collective-permute-start | bytes 393224 | tf_op jit(solution)/shard_map/ppermute | solution.py:20
  22.0 7.4 %collective-permute-start.8 = (bf16[256,256]{1,0:T(8,128)(2,1)S(1)}, bf16[256,256]{1,0:T(8,128)(2,1)S(1)}, u32[]{:S(2)}, u32[]{:S(2)}) collective-permute-start(bf16[256,256]{1,0:T(8,128)(2,1)S(1)} %get-tuple-element.57), channel_id=1, source_target_pairs={{0,4},{2,6},{4,0},{6,2},{8,12},{10,14},{12,8},{14,10},{16,20},{18,... | collective-permute-start | bytes 393224 | tf_op jit(solution)/shard_map/ppermute | solution.py:20
  22.5 6.9 %collective-permute-start.9 = (bf16[256,256]{1,0:T(8,128)(2,1)S(1)}, bf16[256,256]{1,0:T(8,128)(2,1)S(1)}, u32[]{:S(2)}, u32[]{:S(2)}) collective-permute-start(bf16[256,256]{1,0:T(8,128)(2,1)S(1)} %get-tuple-element.58), channel_id=1, source_target_pairs={{0,6},{2,4},{4,2},{6,0},{8,14},{10,12},{12,10},{14,8},{16,22},{18,... | collective-permute-start | bytes 393224 | tf_op jit(solution)/shard_map/ppermute | solution.py:20
  34.0 5.6 %collective-permute-start.10 = (bf16[128,256]{1,0:T(8,128)(2,1)S(1)}, bf16[128,256]{1,0:T(8,128)(2,1)S(1)}, u32[]{:S(2)}, u32[]{:S(2)}) collective-permute-start(bf16[128,256]{1,0:T(8,128)(2,1)S(1)} %get-tuple-element.64), channel_id=1, source_target_pairs={{0,2},{2,0},{4,6},{6,4},{8,10},{10,8},{12,14},{14,12},{16,18},{18,... | collective-permute-start | bytes 196616 | tf_op jit(solution)/shard_map/ppermute | solution.py:20
  34.5 11.1 %collective-permute-start.15 = (bf16[256,256]{1,0:T(8,128)(2,1)S(1)}, bf16[256,256]{1,0:T(8,128)(2,1)S(1)}, u32[]{:S(2)}, u32[]{:S(2)}) collective-permute-start(bf16[256,256]{1,0:T(8,128)(2,1)S(1)} %get-tuple-element.76), channel_id=1, source_target_pairs={{0,8},{2,10},{4,12},{6,14},{8,0},{10,2},{12,4},{14,6},{16,24},{18,... | collective-permute-start | bytes 393224 | tf_op jit(solution)/shard_map/ppermute | solution.py:20
  34.5 7.4 %collective-permute-start.11 = (bf16[128,256]{1,0:T(8,128)(2,1)S(1)}, bf16[128,256]{1,0:T(8,128)(2,1)S(1)}, u32[]{:S(2)}, u32[]{:S(2)}) collective-permute-start(bf16[128,256]{1,0:T(8,128)(2,1)S(1)} %get-tuple-element.65), channel_id=1, source_target_pairs={{0,4},{2,6},{4,0},{6,2},{8,12},{10,14},{12,8},{14,10},{16,20},{18,... | collective-permute-start | bytes 196616 | tf_op jit(solution)/shard_map/ppermute | solution.py:20
  35.9 6.1 %collective-permute-start.12 = (bf16[128,256]{1,0:T(8,128)(2,1)S(1)}, bf16[128,256]{1,0:T(8,128)(2,1)S(1)}, u32[]{:S(2)}, u32[]{:S(2)}) collective-permute-start(bf16[128,256]{1,0:T(8,128)(2,1)S(1)} %get-tuple-element.66), channel_id=1, source_target_pairs={{0,6},{2,4},{4,2},{6,0},{8,14},{10,12},{12,10},{14,8},{16,22},{18,... | collective-permute-start | bytes 196616 | tf_op jit(solution)/shard_map/ppermute | solution.py:20
  37.6 5.6 %collective-permute-start.16 = (bf16[128,256]{1,0:T(8,128)(2,1)S(1)}, bf16[128,256]{1,0:T(8,128)(2,1)S(1)}, u32[]{:S(2)}, u32[]{:S(2)}) collective-permute-start(bf16[128,256]{1,0:T(8,128)(2,1)S(1)} %get-tuple-element.77), channel_id=1, source_target_pairs={{0,16},{2,18},{4,20},{6,22},{8,24},{10,26},{12,28},{14,30},{16,0},... | collective-permute-start | bytes 196616 | tf_op jit(solution)/shard_map/ppermute | solution.py:20
  39.6 6.1 %collective-permute-start.17 = (bf16[128,256]{1,0:T(8,128)(2,1)S(1)}, bf16[128,256]{1,0:T(8,128)(2,1)S(1)}, u32[]{:S(2)}, u32[]{:S(2)}) collective-permute-start(bf16[128,256]{1,0:T(8,128)(2,1)S(1)} %get-tuple-element.78), channel_id=1, source_target_pairs={{0,24},{2,26},{4,28},{6,30},{8,16},{10,18},{12,20},{14,22},{16,8},... | collective-permute-start | bytes 196616 | tf_op jit(solution)/shard_map/ppermute | solution.py:20
  46.3 8.0 %collective-permute-start.18 = (bf16[384,256]{1,0:T(8,128)(2,1)S(1)}, bf16[384,256]{1,0:T(8,128)(2,1)S(1)}, u32[]{:S(2)}, u32[]{:S(2)}) collective-permute-start(bf16[384,256]{1,0:T(8,128)(2,1)S(1)} %get-tuple-element.80), channel_id=1, source_target_pairs={{0,2},{2,0},{4,6},{6,4},{8,10},{10,8},{12,14},{14,12},{16,18},{18,... | collective-permute-start | bytes 589832 | tf_op jit(solution)/shard_map/ppermute | solution.py:20
  46.8 7.5 %collective-permute-start.19 = (bf16[384,256]{1,0:T(8,128)(2,1)S(1)}, bf16[384,256]{1,0:T(8,128)(2,1)S(1)}, u32[]{:S(2)}, u32[]{:S(2)}) collective-permute-start(bf16[384,256]{1,0:T(8,128)(2,1)S(1)} %get-tuple-element.81), channel_id=1, source_target_pairs={{0,4},{2,6},{4,0},{6,2},{8,12},{10,14},{12,8},{14,10},{16,20},{18,... | collective-permute-start | bytes 589832 | tf_op jit(solution)/shard_map/ppermute | solution.py:20
  48.3 6.6 %collective-permute-start.20 = (bf16[384,256]{1,0:T(8,128)(2,1)S(1)}, bf16[384,256]{1,0:T(8,128)(2,1)S(1)}, u32[]{:S(2)}, u32[]{:S(2)}) collective-permute-start(bf16[384,256]{1,0:T(8,128)(2,1)S(1)} %get-tuple-element.82), channel_id=1, source_target_pairs={{0,6},{2,4},{4,2},{6,0},{8,14},{10,12},{12,10},{14,8},{16,22},{18,... | collective-permute-start | bytes 589832 | tf_op jit(solution)/shard_map/ppermute | solution.py:20
  51.9 1.4 %collective-permute-start.13 = (bf16[128,512]{1,0:T(8,128)(2,1)S(1)}, bf16[128,512]{1,0:T(8,128)(2,1)S(1)}, u32[]{:S(2)}, u32[]{:S(2)}) collective-permute-start(bf16[128,512]{1,0:T(8,128)(2,1)S(1)} %get-tuple-element.68), channel_id=1, source_target_pairs={{0,1},{1,0},{2,3},{3,2},{4,5},{5,4},{6,7},{7,6},{8,9},{9,8},{10,11... | collective-permute-start | bytes 393224 | tf_op jit(solution)/shard_map/ppermute | solution.py:24
  52.0 1.5 %collective-permute-start.14 = (bf16[128,512]{1,0:T(8,128)(2,1)S(1)}, bf16[128,512]{1,0:T(8,128)(2,1)S(1)}, u32[]{:S(2)}, u32[]{:S(2)}) collective-permute-start(bf16[128,512]{1,0:T(8,128)(2,1)S(1)} %get-tuple-element.69), channel_id=1, source_target_pairs={{0,1},{1,0},{2,3},{3,2},{4,5},{5,4},{6,7},{7,6},{8,9},{9,8},{10,11... | collective-permute-start | bytes 393224 | tf_op jit(solution)/shard_map/ppermute | solution.py:24

commit v3 on v2

--- a/solution.py
+++ b/solution.py
@@ -8,6 +8,7 @@
 from jax.sharding import PartitionSpec as P
 
 HDIM = 128
+ORDER = (0, 1, 3, 2)
 BLOCK = 128
 BF16 = jnp.bfloat16
 F32 = jnp.float32
@@ -61,6 +62,10 @@
     )(*operands)
 
 
+def by_mask(refs):
+    return [refs[ORDER.index(mask)] for mask in range(len(refs))]
+
+
 def level_pool(rows, level):
     row = lax.broadcasted_iota(jnp.int32, (rows, BLOCK), 0)
     col = lax.broadcasted_iota(jnp.int32, (rows, BLOCK), 1)
@@ -75,12 +80,12 @@
     return max(16, BLOCK >> level)
 
 
-def split_kernel(slots, at_ref, q_hbm, k_hbm, v_hbm, *refs):
-    chunk_refs, sems = refs[:slots], refs[slots]
+def split_kernel(slots, levels, at_ref, q_hbm, k_hbm, v_hbm, *refs):
+    piece_refs, chunk_refs, sems = refs[: len(levels)], refs[len(levels) : -1], refs[-1]
     low = at_ref[0]
     tok, width = BLOCK, chunk_refs[0].shape[1]
     copies = []
-    for place, source in enumerate((q_hbm, k_hbm, v_hbm)):
+    for place, source in ((1, k_hbm), (2, v_hbm), (0, q_hbm)):
         for mask in range(slots):
             copy = pltpu.make_async_copy(
                 source.at[:, col_block(low, mask, width)],
@@ -89,25 +94,18 @@
             )
             copy.start()
             copies.append(copy)
-    for copy in copies:
-        copy.wait()
-
-
-def coarse_kernel(levels, k_hbm, v_hbm, *refs):
-    piece_refs, (k_ref, v_ref, sems) = refs[: len(levels)], refs[len(levels) :]
-    copies = [
-        pltpu.make_async_copy(k_hbm, k_ref, sems.at[0]),
-        pltpu.make_async_copy(v_hbm, v_ref, sems.at[1]),
-    ]
-    for copy in copies:
-        copy.start()
-    for copy in copies:
+    for copy in copies[: 2 * slots]:
         copy.wait()
     for level, piece in zip(levels, piece_refs):
         rows = piece_rows(level)
         pool = level_pool(rows, level)
-        piece[0:rows, :] = (mm(pool, k_ref[...]) * (1.0 / (1 << level))).astype(BF16)
-        piece[rows:, :] = mm(pool, v_ref[...]).astype(BF16)
+        for mask in range(slots):
+            cols = col_block(low, mask, width)
+            keys = mm(pool, chunk_refs[mask][tok : 2 * tok, :]) * (1.0 / (1 << level))
+            piece[0:rows, cols] = keys.astype(BF16)
+            piece[rows:, cols] = mm(pool, chunk_refs[mask][2 * tok : 3 * tok, :]).astype(BF16)
+    for copy in copies[2 * slots :]:
+        copy.wait()
 
 
 def grad_kernel(at_ref, mine_ref, w_ref, other_ref, out_ref):
@@ -135,10 +133,10 @@
 
 
 def attend_kernel(slots, far_levels, entries, *refs):
-    first_refs, second_refs = refs[:slots], refs[slots : 2 * slots]
-    far_refs, refs = refs[2 * slots : 2 * slots + len(entries)], refs[2 * slots + len(entries) :]
-    dk_ref, dv_ref, kl_ref, vl_ref, prob_ref, grad_ref = refs[:6]
-    q_all, g_all, ck_ref, cv_ref, fk_ref, fv_ref = refs[6:]
+    first_refs, second_refs = by_mask(refs[:slots]), by_mask(refs[slots : 2 * slots])
+    refs = refs[2 * slots :]
+    far_refs, refs = refs[: len(entries)], refs[len(entries) :]
+    kl_ref, vl_ref, q_all, g_all, prob_ref, grad_ref, fk_ref, fv_ref = refs
     tok = BLOCK
     pairs = slots // 2
     inv_scale = 1.0 / math.sqrt(HDIM)
@@ -148,7 +146,7 @@
         pair, row = slab // 2, (slab % 2) * tok
         q_all[pair, row : row + tok, :] = first_refs[slab][0:tok, :]
         kl_ref[pair, row : row + tok, :] = first_refs[slab][tok : 2 * tok, :]
-        vl_ref[pair, row : row + tok, :] = first_refs[slab][2 * tok : 3 * tok, :]
+        vl_ref[pair, row : row + tok, :] = first_refs[slab][2 * tok :, :]
         g_all[pair, row : row + tok, :] = second_refs[slab][0:tok, :]
         for place in range(far_levels):
             at = tok + 64 * place
@@ -176,46 +174,53 @@
             score_grad = (prob * ((prob_grad - centre) * inv_scale)).astype(BF16)
             prob_ref[2 * pair + head] = prob_low
             grad_ref[2 * pair + head] = score_grad
-            key_terms = mm_rows(score_grad, queries)
-            value_terms = mm_rows(prob_low, grads)
-            for terms, local, level1, distant in (
-                (key_terms, dk_ref, ck_ref, fk_ref),
-                (value_terms, dv_ref, cv_ref, fv_ref),
+            key_terms = mm_rows(score_grad[:, far:], queries)
+            value_terms = mm_rows(prob_low[:, far:], grads)
+            if pair == 0:
+                fk_ref[:, lanes] = key_terms
+                fv_ref[:, lanes] = value_terms
+            else:
+                fk_ref[:, lanes] += key_terms
+                fv_ref[:, lanes] += value_terms
+    for (place, part, rows), out_ref in zip(entries, far_refs):
+        for kind, total in enumerate((fk_ref, fv_ref)):
+            for slab in range(slots):
+                start = place * BLOCK + 32 * slab + part * rows
+                at = (kind * slots + slab) * rows
+                out_ref[at : at + rows, :] = total[start : start + rows, :].astype(BF16)
+
+
+def reduce_kernel(slots, kl_ref, vl_ref, q_all, g_all, prob_ref, grad_ref, *refs):
+    home_refs, (dk_ref, dv_ref, ck_ref, cv_ref) = refs[:slots], refs[slots:]
+    tok = BLOCK
+    pairs = slots // 2
+    near, far = 2 * tok, 3 * tok
+    for pair in range(pairs):
+        for head in range(2):
+            lanes = slice(head * HDIM, head * HDIM + HDIM)
+            unit = 2 * pair + head
+            attended = mm(prob_ref[unit], vl_ref[pair, :, lanes]).astype(BF16)
+            query_grad = mm(grad_ref[unit], kl_ref[pair, :, lanes]).astype(BF16)
+            for side in range(2):
+                rows = slice(side * tok, side * tok + tok)
+                home_refs[2 * pair + side][0:tok, lanes] = attended[rows]
+                home_refs[2 * pair + side][tok:, lanes] = query_grad[rows]
+            key_terms = mm_rows(grad_ref[unit, :, 0:far], q_all[pair, :, lanes])
+            value_terms = mm_rows(prob_ref[unit, :, 0:far], g_all[pair, :, lanes])
+            for terms, local, level1 in (
+                (key_terms, dk_ref, ck_ref),
+                (value_terms, dv_ref, cv_ref),
             ):
                 local[pair * near : pair * near + near, lanes] = terms[0:near]
-                level1[pair ^ 1, :, lanes] = terms[near:far].astype(BF16)
-                if pair == 0:
-                    distant[:, lanes] = terms[far:]
-                else:
-                    distant[:, lanes] += terms[far:]
+                level1[pair ^ 1, :, lanes] = terms[near:].astype(BF16)
+    pool = pool_matrix(BLOCK, 1)
     for pair in range(pairs):
         rows = slice(pair * near, pair * near + near)
         dk_ref[rows, :] += mm_rows(pool, ck_ref[pair]) * 0.5
         dv_ref[rows, :] += mm_rows(pool, cv_ref[pair])
-    for (place, part, count), out_ref in zip(entries, far_refs):
-        for kind, total in enumerate((fk_ref, fv_ref)):
-            for slab in range(slots):
-                start = place * BLOCK + 32 * slab + part * count
-                at = (kind * slots + slab) * count
-                out_ref[at : at + count, :] = total[start : start + count, :].astype(BF16)
-
-
-def reduce_kernel(slots, kl_ref, vl_ref, prob_ref, grad_ref, *refs):
-    home_refs, query_refs = refs[:slots], refs[slots:]
-    tok = BLOCK
-    for pair in range(slots // 2):
-        for head in range(2):
-            lanes = slice(head * HDIM, head * HDIM + HDIM)
-            attended = mm(prob_ref[2 * pair + head], vl_ref[pair, :, lanes]).astype(BF16)
-            query_grad = mm(grad_ref[2 * pair + head], kl_ref[pair, :, lanes]).astype(BF16)
-            for side in range(2):
-                rows = slice(side * tok, side * tok + tok)
-                home_refs[2 * pair + side][0:tok, lanes] = attended[rows]
-                query_refs[2 * pair + side][:, lanes] = query_grad[rows]
 
 
 def merge_kernel(slots, levels, dk_ref, dv_ref, *refs):
-    query_refs, refs = refs[:slots], refs[slots:]
     far_refs, out_refs = refs[: len(levels)], refs[len(levels) :]
     tok = BLOCK
     for slab in range(slots):
@@ -228,13 +233,12 @@
             key_sum += mm_rows(pool, mine) * (1.0 / (1 << level))
             at = (slots + slab) * count
             value_sum += mm_rows(pool, far_ref[at : at + count, :])
-        out_refs[slab][0:tok, :] = query_refs[slab][...]
-        out_refs[slab][tok : 2 * tok, :] = key_sum.astype(BF16)
-        out_refs[slab][2 * tok :, :] = value_sum.astype(BF16)
+        out_refs[slab][0:tok, :] = key_sum.astype(BF16)
+        out_refs[slab][tok:, :] = value_sum.astype(BF16)
 
 
 def collect_kernel(slots, at_ref, *refs):
-    in_refs, att_ref = refs[:slots], refs[slots]
+    in_refs, att_ref = by_mask(refs[:slots]), refs[slots]
     low = at_ref[0]
     tok, width = BLOCK, in_refs[0].shape[1]
     for mask in range(slots):
@@ -244,24 +248,24 @@
 def project_kernel(at_ref, att_ref, w_ref, keep_ref, *send_refs):
     core = at_ref[1]
     half = att_ref.shape[1]
-    part = half // 2
-    for place in range(2):
+    part = half // len(send_refs)
+    for place, send_ref in enumerate(send_refs):
         other = pl.multiple_of((1 - core) * half + place * part, part)
-        send = mm_cols(att_ref[...], w_ref[pl.ds(other, part), :])
-        send_refs[place][...] = send.astype(BF16)
+        send_ref[...] = mm_cols(att_ref[...], w_ref[pl.ds(other, part), :]).astype(BF16)
     first = pl.multiple_of(core * half, half)
     keep_ref[...] = mm_cols(att_ref[...], w_ref[pl.ds(first, half), :])
 
 
-def add_kernel(keep_ref, left_ref, right_ref, out_ref):
-    part = left_ref.shape[1]
-    for place, got_ref in enumerate((left_ref, right_ref)):
+def add_kernel(keep_ref, *refs):
+    got_refs, out_ref = refs[:-1], refs[-1]
+    part = got_refs[0].shape[1]
+    for place, got_ref in enumerate(got_refs):
         cols = slice(place * part, place * part + part)
         out_ref[:, cols] = (keep_ref[:, cols] + got_ref[...].astype(F32)).astype(BF16)
 
 
 def place_kernel(slots, blocks, at_ref, *refs):
-    in_refs, out_refs, sems = refs[:slots], refs[slots:-1], refs[-1]
+    in_refs, out_refs, sems = by_mask(refs[:slots]), refs[slots:-1], refs[-1]
     low = at_ref[0]
     tok, width = BLOCK, in_refs[0].shape[1]
     copies = []
@@ -378,32 +382,21 @@
         return [shape((rows, width))] * slots
 
     def exchange(chunks):
-        got = {0: chunks[0]}
-        for mask in sorted(range(1, slots), key=lambda mask: (mask + 1) % 2):
-            got[mask] = swap_seq(chunks[mask], mask)
-        return [got[mask] for mask in range(slots)]
+        moved = [chunks[0]] + [swap_seq(chunks[mask], mask) for mask in range(1, slots)]
+        return [moved[mask] for mask in ORDER]
 
     other_grad = swap_head(output_grad)
-    pieces = call(
-        lambda *refs: coarse_kernel(far, *refs),
-        [shape((2 * piece_rows(level), columns)) for level in far],
-        (key_tokens, value_tokens),
-        scratch=[pltpu.VMEM((tok, columns), BF16)] * 2 + [pltpu.SemaphoreType.DMA((2,))],
-        specs=[HBM] * 2,
-        vmem=8,
-    )
-    pieces, later, other_grad = lax.optimization_barrier((pieces, place, other_grad))
-    far_got = gather_far(pieces, far, slots)
-    chunks = call(
-        lambda *refs: split_kernel(slots, *refs),
-        over(3 * tok),
-        (later, queries, key_tokens, value_tokens),
+    made = call(
+        lambda *refs: split_kernel(slots, far, *refs),
+        [shape((2 * piece_rows(level), columns)) for level in far] + over(3 * tok),
+        (place, queries, key_tokens, value_tokens),
         scratch=[pltpu.SemaphoreType.DMA((3 * slots,))],
         flops=6 * 10**9,
         specs=[SMEM] + [HBM] * 3,
         vmem=8,
     )
-    first = exchange(chunks)
+    pieces, chunks = made[: len(far)], list(made[len(far) :])
+    far_got = gather_far(pieces, far, slots)
     grads = call(
         grad_kernel,
         shape((tok, columns)),
@@ -412,6 +405,12 @@
         specs=[SMEM] + [VMEM] * 3,
         vmem=16,
     )
+    first = {0: chunks[0]}
+    for mask in ORDER[1:]:
+        if mask == ORDER[-1]:
+            chunks[mask], grads, first[1] = lax.optimization_barrier((chunks[mask], grads, first[1]))
+        first[mask] = swap_seq(chunks[mask], mask)
+    first = [first[mask] for mask in ORDER]
     chunks = call(
         lambda *refs: second_kernel(slots, entries, *refs),
         over(tok + far_rows),
@@ -421,40 +420,34 @@
     )
     second = exchange(chunks)
     pairs = slots // 2
-    lists = [shape((pairs, list_rows, width))] * 2
     made = call(
         lambda *refs: attend_kernel(slots, len(far), entries, *refs),
         [shape((2 * slots * rows, width)) for _, _, rows in entries]
-        + [shape((slots * tok, width), F32)] * 2
-        + lists
+        + [shape((pairs, list_rows, width))] * 2
+        + [shape((pairs, 2 * tok, width))] * 2
         + [shape((slots, 2 * tok, list_rows))] * 2,
         first + second,
-        scratch=[
-            pltpu.VMEM((pairs, 2 * tok, width), BF16),
-            pltpu.VMEM((pairs, 2 * tok, width), BF16),
-            pltpu.VMEM((pairs, BLOCK, width), BF16),
-            pltpu.VMEM((pairs, BLOCK, width), BF16),
-            pltpu.VMEM((BLOCK * len(far), width), F32),
-            pltpu.VMEM((BLOCK * len(far), width), F32),
-        ],
-        flops=8 * heads * tok * list_rows * HDIM,
+        scratch=[pltpu.VMEM((BLOCK * len(far), width), F32)] * 2,
+        flops=6 * heads * tok * list_rows * HDIM,
     )
     shares, share_levels = scatter_far(made[: len(entries)], far, slots)
-    key_sum, value_sum, *made = made[len(entries) :]
-    made = call(
+    *made, key_sum, value_sum = call(
         lambda *refs: reduce_kernel(slots, *refs),
-        over(tok) + over(tok),
-        made,
+        over(2 * tok) + [shape((slots * tok, width), F32)] * 2,
+        made[len(entries) :],
+        scratch=[pltpu.VMEM((pairs, BLOCK, width), BF16)] * 2,
         flops=6 * 10**9,
         vmem=16,
     )
-    home = exchange(made[:slots])
+    made[2], *shares[1:] = lax.optimization_barrier((made[2], *shares[1:]))
+    home = exchange(made)
     chunks = call(
         lambda *refs: merge_kernel(slots, share_levels, *refs),
-        over(3 * tok),
-        [key_sum, value_sum] + list(made[slots:]) + shares,
+        over(2 * tok),
+        [key_sum, value_sum] + shares,
         vmem=8,
     )
+    home, _ = lax.optimization_barrier((home, chunks))
     last = exchange(chunks)
     wide = shape((tok, columns))
     attended = call(
@@ -475,7 +468,7 @@
     got = [swap_head(part) for part in send]
     output = call(add_kernel, wide, [keep] + got, vmem=8)
 
-    def put(chunks, blocks):
+    def put(chunks, blocks, flops):
         return call(
             lambda *refs: place_kernel(slots, blocks, *refs),
             [wide] * len(blocks),
@@ -484,10 +477,12 @@
             specs=[SMEM] + [VMEM] * slots,
             vmem=8,
             free=True,
+            flops=flops,
             outs=HBM,
         )
 
-    query_grad, key_grad, value_grad = put(last, (0, 1, 2))
+    (query_grad,) = put(home, (1,), 4 * 10**9)
+    key_grad, value_grad = put(last, (0, 1), 0)
     return output, query_grad, key_grad, value_grad
 
 

time: 56.5 us -> 55.3 us (0.979)
  starting transfers between devices: 26.2 us -> 24.9 us
    ppermute x18, starting transfers between devices: 25.1 us -> 23.8 us  [swap_seq(): lax.ppermute(array, 'seq', [(i, i ^ mask) for i in range(lax.axis_size('s...]
    ppermute x3, waiting for transfers between devices: 1.03 us -> 0.01 us  [swap_head(): return lax.ppermute(array, 'head', [(0, 1), (1, 0)])]
    ppermute x18, waiting for transfers between devices: 13.1 us -> 14.1 us  [swap_seq(): lax.ppermute(array, 'seq', [(i, i ^ mask) for i in range(lax.axis_size('s...]
  transfers between devices with their start and end apart: 21 -> 21, of which waited for: 9 -> 7; matrix products, arithmetic and copies ran while one was open for 0% -> 0% of each run, Pallas kernels for 12% -> 21%
where the time goes in v3:
time: 55.3 us; the launch traced here: 55.2 us
  starting transfers between devices  24.9 us (45%)
  Pallas kernels  15.3 us (28%)
  waiting for transfers between devices  14.1 us (25%)
  between operations  0.78 us (1%)
    ppermute x18, starting transfers between devices, swap_seq(): lax.ppermute(array, 'seq', [(i, i ^ mask) for i in range(lax.axis_size('s...  23.8 us
    pallas_call x11, Pallas kernels, call(): pl.pallas_call(kernel, out_shape=out_shape, in_specs=specs, out_specs=jax...  15.3 us
    ppermute x18, waiting for transfers between devices, swap_seq(): lax.ppermute(array, 'seq', [(i, i ^ mask) for i in range(lax.axis_size('s...  14.1 us
  transfers between devices with their start and end apart: 21, of which 7 were waited for; matrix products, arithmetic and copies ran while one was open for 0% of the time, Pallas kernels for 21%

profile of v3, /device:TPU:0, one launch (start us, length us, event | category | flops | bytes accessed | tf_op | source)
XLA Modules:
  0.0 55.2 jit_solution(8644973113706181536)
XLA Ops:
  0.6 0.5 collective-permute-start
  1.1 0.1 pad_add_fusion.refs_0_.at_ref
  1.2 0.0 copy-start
  1.2 0.0 copy-start.1
  1.2 2.3 %shard_map.84 = (bf16[64,1024]{1,0:T(8,128)(2,1)S(1)}, bf16[32,1024]{1,0:T(8,128)(2,1)S(1)}, bf16[384,256]{1,0:T(8,128)(2,1)S(1)}, bf16[384,256]{1,0:T(8,128)(2,...) custom-call(s32[2]{0:T(128)S(1)} %pad_add_fusion.refs_0_.at_ref, bf16[128,1024]{1,0:T(8,128)(2,1)} %refs_1_.1, ...), custom_call_target="tpu_custom_call" | custom-call | flops 6000000000 | bytes 786440 | tf_op jit(solution)/shard_map/pallas_call | solution.py:54
  3.5 2.6 %collective-permute-start.1 = (bf16[384,256]{1,0:T(8,128)(2,1)S(1)}, bf16[384,256]{1,0:T(8,128)(2,1)S(1)}, u32[]{:S(2)}, u32[]{:S(2)}) collective-permute-start(bf16[384,256]{1,0:T(8,128)(2,1)S(1)} %get-tuple-element.50), channel_id=1, source_target_pairs={{0,2},{2,0},{4,6},{6,4},{8,10},{10,8},{12,14},{14,12},{16,18},{18,... | collective-permute-start | bytes 589832 | tf_op jit(solution)/shard_map/ppermute | solution.py:21
  6.1 1.6 %collective-permute-start.4 = (bf16[64,1024]{1,0:T(8,128)(2,1)S(1)}, bf16[64,1024]{1,0:T(8,128)(2,1)S(1)}, u32[]{:S(2)}, u32[]{:S(2)}) collective-permute-start(bf16[64,1024]{1,0:T(8,128)(2,1)S(1)} %get-tuple-element.55), channel_id=1, source_target_pairs={{0,8},{2,10},{4,12},{6,14},{8,0},{10,2},{12,4},{14,6},{16,24},{18,... | collective-permute-start | bytes 393224 | tf_op jit(solution)/shard_map/ppermute | solution.py:21
  7.6 2.5 %collective-permute-start.6 = (bf16[32,1024]{1,0:T(8,128)(2,1)S(1)}, bf16[32,1024]{1,0:T(8,128)(2,1)S(1)}, u32[]{:S(2)}, u32[]{:S(2)}) collective-permute-start(bf16[32,1024]{1,0:T(8,128)(2,1)S(1)} %get-tuple-element.56), channel_id=1, source_target_pairs={{0,24},{2,26},{4,28},{6,30},{8,16},{10,18},{12,20},{14,22},{16,8},... | collective-permute-start | bytes 196616 | tf_op jit(solution)/shard_map/ppermute | solution.py:21
  10.1 0.1 collective-permute-start.5
  10.2 0.0 collective-permute-done.other_ref
  10.2 1.5 %collective-permute-start.2 = (bf16[384,256]{1,0:T(8,128)(2,1)S(1)}, bf16[384,256]{1,0:T(8,128)(2,1)S(1)}, u32[]{:S(2)}, u32[]{:S(2)}) collective-permute-start(bf16[384,256]{1,0:T(8,128)(2,1)S(1)} %get-tuple-element.52), channel_id=1, source_target_pairs={{0,6},{2,4},{4,2},{6,0},{8,14},{10,12},{12,10},{14,8},{16,22},{18,... | collective-permute-start | bytes 589832 | tf_op jit(solution)/shard_map/ppermute | solution.py:21
  11.7 0.0 copy-done
  11.7 0.0 copy-done.1
  11.7 1.3 %shard_map.85.refs_1_ = bf16[128,1024]{1,0:T(8,128)(2,1)S(1)} custom-call(s32[2]{0:T(128)S(1)} %pad_add_fusion.refs_0_.at_ref, bf16[128,1024]{1,0:T(8,128)(2,1)S(1)} %copy-done.1, bf16[2048,1024]{1,0:T(8,128)(2,1)S(1)} %copy-done, bf16[128,1024]{1,0:T(8,128)(2,1)S(1)} %collective-permute-done.other_ref), custom_call_target="tpu_custom_call" | custom-call | flops 536870912 | bytes 4718600 | tf_op jit(solution)/shard_map/pallas_call | solution.py:54
  13.0 0.0 collective-permute-done.1.refs_1_
  13.0 0.6 %collective-permute-start.3 = (bf16[384,256]{1,0:T(8,128)(2,1)S(1)}, bf16[384,256]{1,0:T(8,128)(2,1)S(1)}, u32[]{:S(2)}, u32[]{:S(2)}) collective-permute-start(bf16[384,256]{1,0:T(8,128)(2,1)S(1)} %get-tuple-element.53), channel_id=1, source_target_pairs={{0,4},{2,6},{4,0},{6,2},{8,12},{10,14},{12,8},{14,10},{16,20},{18,... | collective-permute-start | bytes 589832 | tf_op jit(solution)/shard_map/ppermute | solution.py:21
  13.6 2.3 %collective-permute-done.6.refs_4_ = bf16[32,1024]{1,0:T(8,128)(2,1)S(1)} collective-permute-done((bf16[32,1024]{1,0:T(8,128)(2,1)S(1)}, bf16[32,1024]{1,0:T(8,128)(2,1)S(1)}, u32[]{:S(2)}, u32[]{:S(2)}) %collective-permute-start.6) | collective-permute-done | bytes 65568 | tf_op jit(solution)/shard_map/ppermute | solution.py:21
  15.9 1.4 %collective-permute-done.5.refs_3_ = bf16[32,1024]{1,0:T(8,128)(2,1)S(1)} collective-permute-done((bf16[32,1024]{1,0:T(8,128)(2,1)S(1)}, bf16[32,1024]{1,0:T(8,128)(2,1)S(1)}, u32[]{:S(2)}, u32[]{:S(2)}) %collective-permute-start.5) | collective-permute-done | bytes 65568 | tf_op jit(solution)/shard_map/ppermute | solution.py:21
  17.3 0.0 collective-permute-done.4.refs_2_
  17.3 0.6 %shard_map.86 = (bf16[256,256]{1,0:T(8,128)(2,1)S(1)}, bf16[256,256]{1,0:T(8,128)(2,1)S(1)}, bf16[256,256]{1,0:T(8,128)(2,1)S(1)}, bf16[256,256]{1,0:T(8,128)(2,1)S(1)}) custom-call(s32[2]{0:T(128)S(1)} %pad_add_fusion.refs_0_.at_ref, bf16[128,1024]{1,0:T(8,128)(2,1)S(1)} %shard_map.85.refs_1_, bf16[64,1024]{1,0:T(8,128)(2,1)S(1)} %collective-permute-done.4.refs_2_, ...), custom_call_target="tpu_custom_call" | custom-call | bytes 524296 | tf_op jit(solution)/shard_map/pallas_call | solution.py:54
  18.0 0.6 %collective-permute-start.7 = (bf16[256,256]{1,0:T(8,128)(2,1)S(1)}, bf16[256,256]{1,0:T(8,128)(2,1)S(1)}, u32[]{:S(2)}, u32[]{:S(2)}) collective-permute-start(bf16[256,256]{1,0:T(8,128)(2,1)S(1)} %get-tuple-element.58), channel_id=1, source_target_pairs={{0,2},{2,0},{4,6},{6,4},{8,10},{10,8},{12,14},{14,12},{16,18},{18,... | collective-permute-start | bytes 393224 | tf_op jit(solution)/shard_map/ppermute | solution.py:21
  18.6 2.4 %collective-permute-start.8 = (bf16[256,256]{1,0:T(8,128)(2,1)S(1)}, bf16[256,256]{1,0:T(8,128)(2,1)S(1)}, u32[]{:S(2)}, u32[]{:S(2)}) collective-permute-start(bf16[256,256]{1,0:T(8,128)(2,1)S(1)} %get-tuple-element.59), channel_id=1, source_target_pairs={{0,6},{2,4},{4,2},{6,0},{8,14},{10,12},{12,10},{14,8},{16,22},{18,... | collective-permute-start | bytes 393224 | tf_op jit(solution)/shard_map/ppermute | solution.py:21
  21.0 0.5 collective-permute-start.9
  21.5 0.0 collective-permute-done.2.refs_2_
  21.5 2.7 %collective-permute-done.7.refs_5_ = bf16[256,256]{1,0:T(8,128)(2,1)S(1)} collective-permute-done((bf16[256,256]{1,0:T(8,128)(2,1)S(1)}, bf16[256,256]{1,0:T(8,128)(2,1)S(1)}, u32[]{:S(2)}, u32[]{:S(2)}) %collective-permute-start.7) | collective-permute-done | bytes 131104 | tf_op jit(solution)/shard_map/ppermute | solution.py:21
  24.3 2.4 %collective-permute-done.8.refs_6_ = bf16[256,256]{1,0:T(8,128)(2,1)S(1)} collective-permute-done((bf16[256,256]{1,0:T(8,128)(2,1)S(1)}, bf16[256,256]{1,0:T(8,128)(2,1)S(1)}, u32[]{:S(2)}, u32[]{:S(2)}) %collective-permute-start.8) | collective-permute-done | bytes 131104 | tf_op jit(solution)/shard_map/ppermute | solution.py:21
  26.7 1.3 %collective-permute-done.9.refs_7_ = bf16[256,256]{1,0:T(8,128)(2,1)S(1)} collective-permute-done((bf16[256,256]{1,0:T(8,128)(2,1)S(1)}, bf16[256,256]{1,0:T(8,128)(2,1)S(1)}, u32[]{:S(2)}, u32[]{:S(2)}) %collective-permute-start.9) | collective-permute-done | bytes 131104 | tf_op jit(solution)/shard_map/ppermute | solution.py:21
  28.0 0.0 collective-permute-done.3.refs_3_
  28.0 3.0 %shard_map.87 = (bf16[256,256]{1,0:T(8,128)(2,1)S(1)}, bf16[128,256]{1,0:T(8,128)(2,1)S(1)}, bf16[128,256]{1,0:T(8,128)(2,1)S(1)}, bf16[2,640,256]{2,1,0:T(8,128...) custom-call(bf16[384,256]{1,0:T(8,128)(2,1)S(1)} %get-tuple-element., ...), custom_call_target="tpu_custom_call" | custom-call | flops 503316480 | bytes 1310720 | tf_op jit(solution)/shard_map/pallas_call | solution.py:54
  31.0 2.0 %collective-permute-start.12 = (bf16[128,256]{1,0:T(8,128)(2,1)S(1)}, bf16[128,256]{1,0:T(8,128)(2,1)S(1)}, u32[]{:S(2)}, u32[]{:S(2)}) collective-permute-start(bf16[128,256]{1,0:T(8,128)(2,1)S(1)} %get-tuple-element.71), channel_id=1, source_target_pairs={{0,16},{2,18},{4,20},{6,22},{8,24},{10,26},{12,28},{14,30},{16,0},... | collective-permute-start | bytes 196616 | tf_op jit(solution)/shard_map/ppermute | solution.py:21
  33.1 1.3 %collective-permute-start.13 = (bf16[128,256]{1,0:T(8,128)(2,1)S(1)}, bf16[128,256]{1,0:T(8,128)(2,1)S(1)}, u32[]{:S(2)}, u32[]{:S(2)}) collective-permute-start(bf16[128,256]{1,0:T(8,128)(2,1)S(1)} %get-tuple-element.72), channel_id=1, source_target_pairs={{0,24},{2,26},{4,28},{6,30},{8,16},{10,18},{12,20},{14,22},{16,8},... | collective-permute-start | bytes 196616 | tf_op jit(solution)/shard_map/ppermute | solution.py:21
  34.4 0.2 collective-permute-start.15
  34.6 1.5 %shard_map.88 = (bf16[256,256]{1,0:T(8,128)(2,1)S(1)}, bf16[256,256]{1,0:T(8,128)(2,1)S(1)}, bf16[256,256]{1,0:T(8,128)(2,1)S(1)}, bf16[256,256]{1,0:T(8,128)(2,...) custom-call(bf16[2,640,256]{2,1,0:T(8,128)(2,1)S(1)} %get-tuple-element.61.refs_0_, ...), custom_call_target="tpu_custom_call" | custom-call | flops 6000000000 | bytes 4456448 | tf_op jit(solution)/shard_map/pallas_call | solution.py:54
  36.1 1.1 %collective-permute-start.10 = (bf16[256,256]{1,0:T(8,128)(2,1)S(1)}, bf16[256,256]{1,0:T(8,128)(2,1)S(1)}, u32[]{:S(2)}, u32[]{:S(2)}) collective-permute-start(bf16[256,256]{1,0:T(8,128)(2,1)S(1)} %get-tuple-element.68), channel_id=1, source_target_pairs={{0,2},{2,0},{4,6},{6,4},{8,10},{10,8},{12,14},{14,12},{16,18},{18,... | collective-permute-start | bytes 393224 | tf_op jit(solution)/shard_map/ppermute | solution.py:21
  37.2 1.8 %collective-permute-start.11 = (bf16[256,256]{1,0:T(8,128)(2,1)S(1)}, bf16[256,256]{1,0:T(8,128)(2,1)S(1)}, u32[]{:S(2)}, u32[]{:S(2)}) collective-permute-start(bf16[256,256]{1,0:T(8,128)(2,1)S(1)} %get-tuple-element.69), channel_id=1, source_target_pairs={{0,6},{2,4},{4,2},{6,0},{8,14},{10,12},{12,10},{14,8},{16,22},{18,... | collective-permute-start | bytes 393224 | tf_op jit(solution)/shard_map/ppermute | solution.py:21
  39.0 0.0 collective-permute-done.12.refs_3_
  39.0 0.9 %collective-permute-done.13.refs_4_ = bf16[128,256]{1,0:T(8,128)(2,1)S(1)} collective-permute-done((bf16[128,256]{1,0:T(8,128)(2,1)S(1)}, bf16[128,256]{1,0:T(8,128)(2,1)S(1)}, u32[]{:S(2)}, u32[]{:S(2)}) %collective-permute-start.13) | collective-permute-done | bytes 65568 | tf_op jit(solution)/shard_map/ppermute | solution.py:21
  39.9 1.5 %collective-permute-start.14 = (bf16[256,256]{1,0:T(8,128)(2,1)S(1)}, bf16[256,256]{1,0:T(8,128)(2,1)S(1)}, u32[]{:S(2)}, u32[]{:S(2)}) collective-permute-start(bf16[256,256]{1,0:T(8,128)(2,1)S(1)} %get-tuple-element.73), channel_id=1, source_target_pairs={{0,4},{2,6},{4,0},{6,2},{8,12},{10,14},{12,8},{14,10},{16,20},{18,... | collective-permute-start | bytes 393224 | tf_op jit(solution)/shard_map/ppermute | solution.py:21
  41.4 0.0 collective-permute-done.15.refs_2_
  41.4 0.6 %shard_map.89 = (bf16[256,256]{1,0:T(8,128)(2,1)S(1)}, bf16[256,256]{1,0:T(8,128)(2,1)S(1)}, bf16[256,256]{1,0:T(8,128)(2,1)S(1)}, bf16[256,256]{1,0:T(8,128)(2,1)S(1)}) custom-call(f32[512,256]{1,0:T(8,128)S(1)} %get-tuple-element.74.refs_0_, f32[512,256]{1,0:T(8,128)S(1)} %get-tuple-element.75.refs_1_, ...), custom_call_target="tpu_custom_call" | custom-call | bytes 1310720 | tf_op jit(solution)/shard_map/pallas_call | solution.py:54
  42.0 0.8 %collective-permute-start.18 = (bf16[256,256]{1,0:T(8,128)(2,1)S(1)}, bf16[256,256]{1,0:T(8,128)(2,1)S(1)}, u32[]{:S(2)}, u32[]{:S(2)}) collective-permute-start(bf16[256,256]{1,0:T(8,128)(2,1)S(1)} %get-tuple-element.80), channel_id=1, source_target_pairs={{0,2},{2,0},{4,6},{6,4},{8,10},{10,8},{12,14},{14,12},{16,18},{18,... | collective-permute-start | bytes 393224 | tf_op jit(solution)/shard_map/ppermute | solution.py:21
  42.8 1.1 %collective-permute-start.20 = (bf16[256,256]{1,0:T(8,128)(2,1)S(1)}, bf16[256,256]{1,0:T(8,128)(2,1)S(1)}, u32[]{:S(2)}, u32[]{:S(2)}) collective-permute-start(bf16[256,256]{1,0:T(8,128)(2,1)S(1)} %get-tuple-element.81), channel_id=1, source_target_pairs={{0,4},{2,6},{4,0},{6,2},{8,12},{10,14},{12,8},{14,10},{16,20},{18,... | collective-permute-start | bytes 393224 | tf_op jit(solution)/shard_map/ppermute | solution.py:21
  43.9 0.0 collective-permute-done.10.refs_2_
  43.9 1.6 %collective-permute-start.19 = (bf16[256,256]{1,0:T(8,128)(2,1)S(1)}, bf16[256,256]{1,0:T(8,128)(2,1)S(1)}, u32[]{:S(2)}, u32[]{:S(2)}) collective-permute-start(bf16[256,256]{1,0:T(8,128)(2,1)S(1)} %get-tuple-element.82), channel_id=1, source_target_pairs={{0,6},{2,4},{4,2},{6,0},{8,14},{10,12},{12,10},{14,8},{16,22},{18,... | collective-permute-start | bytes 393224 | tf_op jit(solution)/shard_map/ppermute | solution.py:21
  45.5 0.0 collective-permute-done.11.refs_3_
  45.6 2.9 %collective-permute-done.14.refs_4_ = bf16[256,256]{1,0:T(8,128)(2,1)S(1)} collective-permute-done((bf16[256,256]{1,0:T(8,128)(2,1)S(1)}, bf16[256,256]{1,0:T(8,128)(2,1)S(1)}, u32[]{:S(2)}, u32[]{:S(2)}) %collective-permute-start.14) | collective-permute-done | bytes 131104 | tf_op jit(solution)/shard_map/ppermute | solution.py:21
  48.5 0.6 %shard_map.90.att_ref = bf16[128,1024]{1,0:T(8,128)(2,1)S(1)} custom-call(s32[2]{0:T(128)S(1)} %pad_add_fusion.refs_0_.at_ref, bf16[256,256]{1,0:T(8,128)(2,1)S(1)} %get-tuple-element.83.refs_1_, bf16[256,256]{1,0:T(8,128)(2,1)S(1)} %collective-permute-done.10.refs_2_, bf16[256,256]{1,0:T(8,128)(2,1)S(1)} %collective-permute-done.11.refs_3_, ...), custom_call_target="tpu_custom_call" | custom-call | bytes 524296 | tf_op jit(solution)/shard_map/pallas_call | solution.py:54
  49.1 2.1 %shard_map.91 = (f32[128,1024]{1,0:T(8,128)S(1)}, bf16[128,512]{1,0:T(8,128)(2,1)S(1)}, bf16[128,512]{1,0:T(8,128)(2,1)S(1)}) custom-call(s32[2]{0:T(128)S(1)} %pad_add_fusion.refs_0_.at_ref, bf16[128,1024]{1,0:T(8,128)(2,1)S(1)} %shard_map.90.att_ref, bf16[2048,1024]{1,0:T(8,128)(2,1)S(1)} %copy-done), custom_call_target="tpu_custom_call" | custom-call | flops 4000000000 | bytes 4456456 | tf_op jit(solution)/shard_map/pallas_call | solution.py:54
  51.1 0.1 collective-permute-start.16
  51.2 0.5 collective-permute-start.17
  51.7 1.3 %shard_map.93 = bf16[128,1024]{1,0:T(8,128)(2,1)} custom-call(s32[2]{0:T(128)S(1)} %pad_add_fusion.refs_0_.at_ref, bf16[256,256]{1,0:T(8,128)(2,1)S(1)} %get-tuple-element.83.refs_1_, bf16[256,256]{1,0:T(8,128)(2,1)S(1)} %collective-permute-done.10.refs_2_, bf16[256,256]{1,0:T(8,128)(2,1)S(1)} %collective-permute-done.11.refs_3_, ...), custom_call_target="tpu_custom_call" | custom-call | flops 4000000000 | tf_op jit(solution)/shard_map/pallas_call | solution.py:54
  53.0 0.0 collective-permute-done.18.refs_2_
  53.0 0.0 collective-permute-done.20.refs_4_
  53.0 0.0 collective-permute-done.19.refs_3_
  53.0 1.4 %shard_map.94 = (bf16[128,1024]{1,0:T(8,128)(2,1)}, bf16[128,1024]{1,0:T(8,128)(2,1)}) custom-call(s32[2]{0:T(128)S(1)} %pad_add_fusion.refs_0_.at_ref, bf16[256,256]{1,0:T(8,128)(2,1)S(1)} %get-tuple-element.79.refs_1_, bf16[256,256]{1,0:T(8,128)(2,1)S(1)} %collective-permute-done.18.refs_2_, bf16[256,256]{1,0:T(8,128)(2,1)S(1)} %collective-permute-done.19.refs_3_, ...), custom_call_target="tpu_custom_call" | custom-call | tf_op jit(solution)/shard_map/pallas_call | solution.py:54
  54.4 0.0 collective-permute-done.16.refs_0_
  54.4 0.0 collective-permute-done.17.refs_1_
  54.4 0.7 %shard_map.92 = bf16[128,1024]{1,0:T(8,128)(2,1)} custom-call(f32[128,1024]{1,0:T(8,128)S(1)} %get-tuple-element.87.keep_ref, bf16[128,512]{1,0:T(8,128)(2,1)S(1)} %collective-permute-done.16.refs_0_, bf16[128,512]{1,0:T(8,128)(2,1)S(1)} %collective-permute-done.17.refs_1_), custom_call_target="tpu_custom_call" | custom-call | bytes 786432 | tf_op jit(solution)/shard_map/pallas_call | solution.py:54
Async XLA Ops:
  0.6 9.6 %collective-permute-start = (bf16[128,1024]{1,0:T(8,128)(2,1)}, bf16[128,1024]{1,0:T(8,128)(2,1)S(1)}, u32[]{:S(2)}, u32[]{:S(2)}) collective-permute-start(bf16[128,1024]{1,0:T(8,128)(2,1)} %mine_ref.1), channel_id=1, source_target_pairs={{0,1},{1,0},{2,3},{3,2},{4,5},{5,4},{6,7},{7,6},{8,9},{9,8},{10,11... | collective-permute-start | bytes 786440 | tf_op jit(solution)/shard_map/ppermute | solution.py:25
  1.2 10.5 %copy-start = (bf16[2048,1024]{1,0:T(8,128)(2,1)S(1)}, bf16[2048,1024]{1,0:T(8,128)(2,1)}, u32[]{:S(2)}) copy-start(bf16[2048,1024]{1,0:T(8,128)(2,1)} %w_ref.3) | copy-start | bytes 12582916
  1.2 10.5 %copy-start.1 = (bf16[128,1024]{1,0:T(8,128)(2,1)S(1)}, bf16[128,1024]{1,0:T(8,128)(2,1)}, u32[]{:S(2)}) copy-start(bf16[128,1024]{1,0:T(8,128)(2,1)} %mine_ref.1) | copy-start | bytes 786436
  3.5 9.5 %collective-permute-start.1 = (bf16[384,256]{1,0:T(8,128)(2,1)S(1)}, bf16[384,256]{1,0:T(8,128)(2,1)S(1)}, u32[]{:S(2)}, u32[]{:S(2)}) collective-permute-start(bf16[384,256]{1,0:T(8,128)(2,1)S(1)} %get-tuple-element.50), channel_id=1, source_target_pairs={{0,2},{2,0},{4,6},{6,4},{8,10},{10,8},{12,14},{14,12},{16,18},{18,... | collective-permute-start | bytes 589832 | tf_op jit(solution)/shard_map/ppermute | solution.py:21
  6.1 11.3 %collective-permute-start.4 = (bf16[64,1024]{1,0:T(8,128)(2,1)S(1)}, bf16[64,1024]{1,0:T(8,128)(2,1)S(1)}, u32[]{:S(2)}, u32[]{:S(2)}) collective-permute-start(bf16[64,1024]{1,0:T(8,128)(2,1)S(1)} %get-tuple-element.55), channel_id=1, source_target_pairs={{0,8},{2,10},{4,12},{6,14},{8,0},{10,2},{12,4},{14,6},{16,24},{18,... | collective-permute-start | bytes 393224 | tf_op jit(solution)/shard_map/ppermute | solution.py:21
  7.6 8.3 %collective-permute-start.6 = (bf16[32,1024]{1,0:T(8,128)(2,1)S(1)}, bf16[32,1024]{1,0:T(8,128)(2,1)S(1)}, u32[]{:S(2)}, u32[]{:S(2)}) collective-permute-start(bf16[32,1024]{1,0:T(8,128)(2,1)S(1)} %get-tuple-element.56), channel_id=1, source_target_pairs={{0,24},{2,26},{4,28},{6,30},{8,16},{10,18},{12,20},{14,22},{16,8},... | collective-permute-start | bytes 196616 | tf_op jit(solution)/shard_map/ppermute | solution.py:21
  10.1 7.2 %collective-permute-start.5 = (bf16[32,1024]{1,0:T(8,128)(2,1)S(1)}, bf16[32,1024]{1,0:T(8,128)(2,1)S(1)}, u32[]{:S(2)}, u32[]{:S(2)}) collective-permute-start(bf16[32,1024]{1,0:T(8,128)(2,1)S(1)} %get-tuple-element.56), channel_id=1, source_target_pairs={{0,16},{2,18},{4,20},{6,22},{8,24},{10,26},{12,28},{14,30},{16,0},... | collective-permute-start | bytes 196616 | tf_op jit(solution)/shard_map/ppermute | solution.py:21
  10.2 11.3 %collective-permute-start.2 = (bf16[384,256]{1,0:T(8,128)(2,1)S(1)}, bf16[384,256]{1,0:T(8,128)(2,1)S(1)}, u32[]{:S(2)}, u32[]{:S(2)}) collective-permute-start(bf16[384,256]{1,0:T(8,128)(2,1)S(1)} %get-tuple-element.52), channel_id=1, source_target_pairs={{0,6},{2,4},{4,2},{6,0},{8,14},{10,12},{12,10},{14,8},{16,22},{18,... | collective-permute-start | bytes 589832 | tf_op jit(solution)/shard_map/ppermute | solution.py:21
  13.0 15.0 %collective-permute-start.3 = (bf16[384,256]{1,0:T(8,128)(2,1)S(1)}, bf16[384,256]{1,0:T(8,128)(2,1)S(1)}, u32[]{:S(2)}, u32[]{:S(2)}) collective-permute-start(bf16[384,256]{1,0:T(8,128)(2,1)S(1)} %get-tuple-element.53), channel_id=1, source_target_pairs={{0,4},{2,6},{4,0},{6,2},{8,12},{10,14},{12,8},{14,10},{16,20},{18,... | collective-permute-start | bytes 589832 | tf_op jit(solution)/shard_map/ppermute | solution.py:21
  18.0 6.3 %collective-permute-start.7 = (bf16[256,256]{1,0:T(8,128)(2,1)S(1)}, bf16[256,256]{1,0:T(8,128)(2,1)S(1)}, u32[]{:S(2)}, u32[]{:S(2)}) collective-permute-start(bf16[256,256]{1,0:T(8,128)(2,1)S(1)} %get-tuple-element.58), channel_id=1, source_target_pairs={{0,2},{2,0},{4,6},{6,4},{8,10},{10,8},{12,14},{14,12},{16,18},{18,... | collective-permute-start | bytes 393224 | tf_op jit(solution)/shard_map/ppermute | solution.py:21
  18.6 8.1 %collective-permute-start.8 = (bf16[256,256]{1,0:T(8,128)(2,1)S(1)}, bf16[256,256]{1,0:T(8,128)(2,1)S(1)}, u32[]{:S(2)}, u32[]{:S(2)}) collective-permute-start(bf16[256,256]{1,0:T(8,128)(2,1)S(1)} %get-tuple-element.59), channel_id=1, source_target_pairs={{0,6},{2,4},{4,2},{6,0},{8,14},{10,12},{12,10},{14,8},{16,22},{18,... | collective-permute-start | bytes 393224 | tf_op jit(solution)/shard_map/ppermute | solution.py:21
  21.0 7.0 %collective-permute-start.9 = (bf16[256,256]{1,0:T(8,128)(2,1)S(1)}, bf16[256,256]{1,0:T(8,128)(2,1)S(1)}, u32[]{:S(2)}, u32[]{:S(2)}) collective-permute-start(bf16[256,256]{1,0:T(8,128)(2,1)S(1)} %get-tuple-element.60), channel_id=1, source_target_pairs={{0,4},{2,6},{4,0},{6,2},{8,12},{10,14},{12,8},{14,10},{16,20},{18,... | collective-permute-start | bytes 393224 | tf_op jit(solution)/shard_map/ppermute | solution.py:21
  31.0 8.0 %collective-permute-start.12 = (bf16[128,256]{1,0:T(8,128)(2,1)S(1)}, bf16[128,256]{1,0:T(8,128)(2,1)S(1)}, u32[]{:S(2)}, u32[]{:S(2)}) collective-permute-start(bf16[128,256]{1,0:T(8,128)(2,1)S(1)} %get-tuple-element.71), channel_id=1, source_target_pairs={{0,16},{2,18},{4,20},{6,22},{8,24},{10,26},{12,28},{14,30},{16,0},... | collective-permute-start | bytes 196616 | tf_op jit(solution)/shard_map/ppermute | solution.py:21
  33.1 6.8 %collective-permute-start.13 = (bf16[128,256]{1,0:T(8,128)(2,1)S(1)}, bf16[128,256]{1,0:T(8,128)(2,1)S(1)}, u32[]{:S(2)}, u32[]{:S(2)}) collective-permute-start(bf16[128,256]{1,0:T(8,128)(2,1)S(1)} %get-tuple-element.72), channel_id=1, source_target_pairs={{0,24},{2,26},{4,28},{6,30},{8,16},{10,18},{12,20},{14,22},{16,8},... | collective-permute-start | bytes 196616 | tf_op jit(solution)/shard_map/ppermute | solution.py:21
  34.4 7.0 %collective-permute-start.15 = (bf16[256,256]{1,0:T(8,128)(2,1)S(1)}, bf16[256,256]{1,0:T(8,128)(2,1)S(1)}, u32[]{:S(2)}, u32[]{:S(2)}) collective-permute-start(bf16[256,256]{1,0:T(8,128)(2,1)S(1)} %get-tuple-element.76), channel_id=1, source_target_pairs={{0,8},{2,10},{4,12},{6,14},{8,0},{10,2},{12,4},{14,6},{16,24},{18,... | collective-permute-start | bytes 393224 | tf_op jit(solution)/shard_map/ppermute | solution.py:21
  36.1 7.8 %collective-permute-start.10 = (bf16[256,256]{1,0:T(8,128)(2,1)S(1)}, bf16[256,256]{1,0:T(8,128)(2,1)S(1)}, u32[]{:S(2)}, u32[]{:S(2)}) collective-permute-start(bf16[256,256]{1,0:T(8,128)(2,1)S(1)} %get-tuple-element.68), channel_id=1, source_target_pairs={{0,2},{2,0},{4,6},{6,4},{8,10},{10,8},{12,14},{14,12},{16,18},{18,... | collective-permute-start | bytes 393224 | tf_op jit(solution)/shard_map/ppermute | solution.py:21
  37.2 8.3 %collective-permute-start.11 = (bf16[256,256]{1,0:T(8,128)(2,1)S(1)}, bf16[256,256]{1,0:T(8,128)(2,1)S(1)}, u32[]{:S(2)}, u32[]{:S(2)}) collective-permute-start(bf16[256,256]{1,0:T(8,128)(2,1)S(1)} %get-tuple-element.69), channel_id=1, source_target_pairs={{0,6},{2,4},{4,2},{6,0},{8,14},{10,12},{12,10},{14,8},{16,22},{18,... | collective-permute-start | bytes 393224 | tf_op jit(solution)/shard_map/ppermute | solution.py:21
  39.9 8.6 %collective-permute-start.14 = (bf16[256,256]{1,0:T(8,128)(2,1)S(1)}, bf16[256,256]{1,0:T(8,128)(2,1)S(1)}, u32[]{:S(2)}, u32[]{:S(2)}) collective-permute-start(bf16[256,256]{1,0:T(8,128)(2,1)S(1)} %get-tuple-element.73), channel_id=1, source_target_pairs={{0,4},{2,6},{4,0},{6,2},{8,12},{10,14},{12,8},{14,10},{16,20},{18,... | collective-permute-start | bytes 393224 | tf_op jit(solution)/shard_map/ppermute | solution.py:21
  42.0 11.0 %collective-permute-start.18 = (bf16[256,256]{1,0:T(8,128)(2,1)S(1)}, bf16[256,256]{1,0:T(8,128)(2,1)S(1)}, u32[]{:S(2)}, u32[]{:S(2)}) collective-permute-start(bf16[256,256]{1,0:T(8,128)(2,1)S(1)} %get-tuple-element.80), channel_id=1, source_target_pairs={{0,2},{2,0},{4,6},{6,4},{8,10},{10,8},{12,14},{14,12},{16,18},{18,... | collective-permute-start | bytes 393224 | tf_op jit(solution)/shard_map/ppermute | solution.py:21
  42.8 10.2 %collective-permute-start.20 = (bf16[256,256]{1,0:T(8,128)(2,1)S(1)}, bf16[256,256]{1,0:T(8,128)(2,1)S(1)}, u32[]{:S(2)}, u32[]{:S(2)}) collective-permute-start(bf16[256,256]{1,0:T(8,128)(2,1)S(1)} %get-tuple-element.81), channel_id=1, source_target_pairs={{0,4},{2,6},{4,0},{6,2},{8,12},{10,14},{12,8},{14,10},{16,20},{18,... | collective-permute-start | bytes 393224 | tf_op jit(solution)/shard_map/ppermute | solution.py:21
  43.9 9.1 %collective-permute-start.19 = (bf16[256,256]{1,0:T(8,128)(2,1)S(1)}, bf16[256,256]{1,0:T(8,128)(2,1)S(1)}, u32[]{:S(2)}, u32[]{:S(2)}) collective-permute-start(bf16[256,256]{1,0:T(8,128)(2,1)S(1)} %get-tuple-element.82), channel_id=1, source_target_pairs={{0,6},{2,4},{4,2},{6,0},{8,14},{10,12},{12,10},{14,8},{16,22},{18,... | collective-permute-start | bytes 393224 | tf_op jit(solution)/shard_map/ppermute | solution.py:21
  51.1 3.3 %collective-permute-start.16 = (bf16[128,512]{1,0:T(8,128)(2,1)S(1)}, bf16[128,512]{1,0:T(8,128)(2,1)S(1)}, u32[]{:S(2)}, u32[]{:S(2)}) collective-permute-start(bf16[128,512]{1,0:T(8,128)(2,1)S(1)} %get-tuple-element.88), channel_id=1, source_target_pairs={{0,1},{1,0},{2,3},{3,2},{4,5},{5,4},{6,7},{7,6},{8,9},{9,8},{10,11... | collective-permute-start | bytes 393224 | tf_op jit(solution)/shard_map/ppermute | solution.py:25
  51.2 3.2 %collective-permute-start.17 = (bf16[128,512]{1,0:T(8,128)(2,1)S(1)}, bf16[128,512]{1,0:T(8,128)(2,1)S(1)}, u32[]{:S(2)}, u32[]{:S(2)}) collective-permute-start(bf16[128,512]{1,0:T(8,128)(2,1)S(1)} %get-tuple-element.89), channel_id=1, source_target_pairs={{0,1},{1,0},{2,3},{3,2},{4,5},{5,4},{6,7},{7,6},{8,9},{9,8},{10,11... | collective-permute-start | bytes 393224 | tf_op jit(solution)/shard_map/ppermute | solution.py:25

commit v4 on v3

--- a/solution.py
+++ b/solution.py
@@ -8,7 +8,7 @@
 from jax.sharding import PartitionSpec as P
 
 HDIM = 128
-ORDER = (0, 1, 3, 2)
+ORDER = (0, 1, 2, 3)
 BLOCK = 128
 BF16 = jnp.bfloat16
 F32 = jnp.float32
@@ -44,18 +44,18 @@
     return jnp.where(lax.shift_right_logical(col, shift) == row, 1.0, 0.0).astype(BF16)
 
 
-def call(kernel, out_shape, operands, scratch=(), flops=0, vmem=24, specs=None, free=False, outs=VMEM):
+def call(kernel, out_shape, operands, scratch=(), flops=0, vmem=24, specs=None, outs=VMEM):
     specs = specs or [VMEM] * len(operands)
     operands = [
         pltpu.with_memory_space_constraint(x, pltpu.HBM) if spec is HBM else x
         for x, spec in zip(operands, specs)
     ]
-    moved = 0 if free else sum(x.size * x.dtype.itemsize for x in operands)
+    moved = sum(x.size * x.dtype.itemsize for x in operands)
     return pl.pallas_call(
         kernel,
         out_shape=out_shape,
         in_specs=specs,
-        out_specs=jax.tree.map(lambda _: outs, out_shape),
+        out_specs=outs if isinstance(outs, list) else jax.tree.map(lambda _: outs, out_shape),
         scratch_shapes=list(scratch),
         compiler_params=pltpu.CompilerParams(vmem_limit_bytes=vmem << 20),
         cost_estimate=pl.CostEstimate(flops=flops, bytes_accessed=moved, transcendentals=0),
@@ -81,31 +81,29 @@
 
 
 def split_kernel(slots, levels, at_ref, q_hbm, k_hbm, v_hbm, *refs):
-    piece_refs, chunk_refs, sems = refs[: len(levels)], refs[len(levels) : -1], refs[-1]
+    piece_refs, refs = refs[: len(levels)], refs[len(levels) :]
+    chunk_refs, (q_ref, k_ref, v_ref, sems) = refs[:slots], refs[slots:]
     low = at_ref[0]
     tok, width = BLOCK, chunk_refs[0].shape[1]
-    copies = []
-    for place, source in ((1, k_hbm), (2, v_hbm), (0, q_hbm)):
-        for mask in range(slots):
-            copy = pltpu.make_async_copy(
-                source.at[:, col_block(low, mask, width)],
-                chunk_refs[mask].at[pl.ds(place * tok, tok), :],
-                sems.at[place * slots + mask],
-            )
-            copy.start()
-            copies.append(copy)
-    for copy in copies[: 2 * slots]:
-        copy.wait()
+    held = (q_ref, k_ref, v_ref)
+    copies = [
+        pltpu.make_async_copy(source, held[place], sems.at[place])
+        for place, source in ((1, k_hbm), (2, v_hbm), (0, q_hbm))
+    ]
+    for copy in copies:
+        copy.start()
+    copies[0].wait()
+    copies[1].wait()
     for level, piece in zip(levels, piece_refs):
         rows = piece_rows(level)
         pool = level_pool(rows, level)
-        for mask in range(slots):
-            cols = col_block(low, mask, width)
-            keys = mm(pool, chunk_refs[mask][tok : 2 * tok, :]) * (1.0 / (1 << level))
-            piece[0:rows, cols] = keys.astype(BF16)
-            piece[rows:, cols] = mm(pool, chunk_refs[mask][2 * tok : 3 * tok, :]).astype(BF16)
-    for copy in copies[2 * slots :]:
-        copy.wait()
+        piece[0:rows, :] = (mm(pool, k_ref[...]) * (1.0 / (1 << level))).astype(BF16)
+        piece[rows:, :] = mm(pool, v_ref[...]).astype(BF16)
+    copies[2].wait()
+    for mask in range(slots):
+        cols = col_block(low, mask, width)
+        for place, source in enumerate(held):
+            chunk_refs[mask][place * tok : place * tok + tok, :] = source[:, cols]
 
 
 def grad_kernel(at_ref, mine_ref, w_ref, other_ref, out_ref):
@@ -136,7 +134,7 @@
     first_refs, second_refs = by_mask(refs[:slots]), by_mask(refs[slots : 2 * slots])
     refs = refs[2 * slots :]
     far_refs, refs = refs[: len(entries)], refs[len(entries) :]
-    kl_ref, vl_ref, q_all, g_all, prob_ref, grad_ref, fk_ref, fv_ref = refs
+    kl_ref, vl_ref, q_all, g_all, prob_ref, grad_ref, sum_ref, fk_ref, fv_ref = refs
     tok = BLOCK
     pairs = slots // 2
     inv_scale = 1.0 / math.sqrt(HDIM)
@@ -168,14 +166,18 @@
             top = jnp.max(scores, axis=1, keepdims=True)
             raised = jnp.exp2((scores - top) * to_exp2)
             inverse = 1.0 / jnp.sum(raised, axis=1, keepdims=True)
-            prob = raised * inverse
-            centre = jnp.sum(prob * prob_grad, axis=1, keepdims=True)
-            prob_low = prob.astype(BF16)
-            score_grad = (prob * ((prob_grad - centre) * inv_scale)).astype(BF16)
-            prob_ref[2 * pair + head] = prob_low
+            centre = jnp.sum(raised * prob_grad, axis=1, keepdims=True) * inverse
+            raised_low = raised.astype(BF16)
+            score_grad = (raised * (prob_grad - centre)).astype(BF16)
+            queries = (queries.astype(F32) * (inverse * inv_scale)).astype(BF16)
+            grads = (grads.astype(F32) * inverse).astype(BF16)
+            prob_ref[2 * pair + head] = raised_low
             grad_ref[2 * pair + head] = score_grad
+            sum_ref[2 * pair + head] = jnp.broadcast_to(inverse, (near, HDIM))
+            q_all[pair, :, lanes] = queries
+            g_all[pair, :, lanes] = grads
             key_terms = mm_rows(score_grad[:, far:], queries)
-            value_terms = mm_rows(prob_low[:, far:], grads)
+            value_terms = mm_rows(raised_low[:, far:], grads)
             if pair == 0:
                 fk_ref[:, lanes] = key_terms
                 fv_ref[:, lanes] = value_terms
@@ -190,8 +192,24 @@
                 out_ref[at : at + rows, :] = total[start : start + rows, :].astype(BF16)
 
 
-def reduce_kernel(slots, kl_ref, vl_ref, q_all, g_all, prob_ref, grad_ref, *refs):
-    home_refs, (dk_ref, dv_ref, ck_ref, cv_ref) = refs[:slots], refs[slots:]
+def reduce_kernel(slots, kl_ref, vl_ref, prob_ref, grad_ref, sum_ref, *home_refs):
+    tok = BLOCK
+    inv_scale = 1.0 / math.sqrt(HDIM)
+    for pair in range(slots // 2):
+        for head in range(2):
+            lanes = slice(head * HDIM, head * HDIM + HDIM)
+            unit = 2 * pair + head
+            inverse = sum_ref[unit]
+            attended = (mm(prob_ref[unit], vl_ref[pair, :, lanes]) * inverse).astype(BF16)
+            query_grad = mm(grad_ref[unit], kl_ref[pair, :, lanes]) * (inverse * inv_scale)
+            query_grad = query_grad.astype(BF16)
+            for side in range(2):
+                rows = slice(side * tok, side * tok + tok)
+                home_refs[2 * pair + side][0:tok, lanes] = attended[rows]
+                home_refs[2 * pair + side][tok:, lanes] = query_grad[rows]
+
+
+def local_kernel(slots, q_all, g_all, prob_ref, grad_ref, dk_ref, dv_ref, ck_ref, cv_ref):
     tok = BLOCK
     pairs = slots // 2
     near, far = 2 * tok, 3 * tok
@@ -199,12 +217,6 @@
         for head in range(2):
             lanes = slice(head * HDIM, head * HDIM + HDIM)
             unit = 2 * pair + head
-            attended = mm(prob_ref[unit], vl_ref[pair, :, lanes]).astype(BF16)
-            query_grad = mm(grad_ref[unit], kl_ref[pair, :, lanes]).astype(BF16)
-            for side in range(2):
-                rows = slice(side * tok, side * tok + tok)
-                home_refs[2 * pair + side][0:tok, lanes] = attended[rows]
-                home_refs[2 * pair + side][tok:, lanes] = query_grad[rows]
             key_terms = mm_rows(grad_ref[unit, :, 0:far], q_all[pair, :, lanes])
             value_terms = mm_rows(prob_ref[unit, :, 0:far], g_all[pair, :, lanes])
             for terms, local, level1 in (
@@ -237,47 +249,53 @@
         out_refs[slab][tok:, :] = value_sum.astype(BF16)
 
 
-def collect_kernel(slots, at_ref, *refs):
-    in_refs, att_ref = by_mask(refs[:slots]), refs[slots]
-    low = at_ref[0]
-    tok, width = BLOCK, in_refs[0].shape[1]
+def send_kernel(slots, at_ref, w_ref, *refs):
+    in_refs, att_ref, send_refs = by_mask(refs[:slots]), refs[slots], refs[slots + 1 :]
+    low, core = at_ref[0], at_ref[1]
+    tok, half = att_ref.shape
+    width = in_refs[0].shape[1]
     for mask in range(slots):
         att_ref[:, col_block(low, mask, width)] = in_refs[mask][0:tok, :]
-
-
-def project_kernel(at_ref, att_ref, w_ref, keep_ref, *send_refs):
-    core = at_ref[1]
-    half = att_ref.shape[1]
     part = half // len(send_refs)
     for place, send_ref in enumerate(send_refs):
         other = pl.multiple_of((1 - core) * half + place * part, part)
         send_ref[...] = mm_cols(att_ref[...], w_ref[pl.ds(other, part), :]).astype(BF16)
+
+
+def keep_kernel(slots, at_ref, w_ref, att_ref, *refs):
+    in_refs, (keep_ref, dq_hbm, dq_ref, sem) = by_mask(refs[:slots]), refs[slots:]
+    low, core = at_ref[0], at_ref[1]
+    tok, half = att_ref.shape
+    width = in_refs[0].shape[1]
+    for mask in range(slots):
+        dq_ref[:, col_block(low, mask, width)] = in_refs[mask][tok:, :]
+    copy = pltpu.make_async_copy(dq_ref, dq_hbm, sem)
+    copy.start()
     first = pl.multiple_of(core * half, half)
     keep_ref[...] = mm_cols(att_ref[...], w_ref[pl.ds(first, half), :])
-
-
-def add_kernel(keep_ref, *refs):
-    got_refs, out_ref = refs[:-1], refs[-1]
+    copy.wait()
+
+
+def finish_kernel(slots, at_ref, keep_ref, *refs):
+    in_refs, refs = by_mask(refs[:slots]), refs[slots:]
+    got_refs, refs = refs[:-7], refs[-7:]
+    hbm_refs, held_refs, sems = refs[:3], refs[3:6], refs[6]
+    low = at_ref[0]
+    tok, width = BLOCK, in_refs[0].shape[1]
+    copies = [
+        pltpu.make_async_copy(held_refs[place], hbm_refs[place], sems.at[place])
+        for place in range(3)
+    ]
+    for place in range(2):
+        for mask in range(slots):
+            rows = slice(place * tok, place * tok + tok)
+            held_refs[place][:, col_block(low, mask, width)] = in_refs[mask][rows, :]
+        copies[place].start()
     part = got_refs[0].shape[1]
     for place, got_ref in enumerate(got_refs):
         cols = slice(place * part, place * part + part)
-        out_ref[:, cols] = (keep_ref[:, cols] + got_ref[...].astype(F32)).astype(BF16)
-
-
-def place_kernel(slots, blocks, at_ref, *refs):
-    in_refs, out_refs, sems = by_mask(refs[:slots]), refs[slots:-1], refs[-1]
-    low = at_ref[0]
-    tok, width = BLOCK, in_refs[0].shape[1]
-    copies = []
-    for place, block in enumerate(blocks):
-        for mask in range(slots):
-            copy = pltpu.make_async_copy(
-                in_refs[mask].at[pl.ds(block * tok, tok), :],
-                out_refs[place].at[:, col_block(low, mask, width)],
-                sems.at[place * slots + mask],
-            )
-            copy.start()
-            copies.append(copy)
+        held_refs[2][:, cols] = (keep_ref[:, cols] + got_ref[...].astype(F32)).astype(BF16)
+    copies[2].start()
     for copy in copies:
         copy.wait()
 
@@ -385,17 +403,18 @@
         moved = [chunks[0]] + [swap_seq(chunks[mask], mask) for mask in range(1, slots)]
         return [moved[mask] for mask in ORDER]
 
-    other_grad = swap_head(output_grad)
     made = call(
         lambda *refs: split_kernel(slots, far, *refs),
         [shape((2 * piece_rows(level), columns)) for level in far] + over(3 * tok),
         (place, queries, key_tokens, value_tokens),
-        scratch=[pltpu.SemaphoreType.DMA((3 * slots,))],
+        scratch=[pltpu.VMEM((tok, columns), BF16)] * 3 + [pltpu.SemaphoreType.DMA((3,))],
         flops=6 * 10**9,
         specs=[SMEM] + [HBM] * 3,
         vmem=8,
     )
     pieces, chunks = made[: len(far)], list(made[len(far) :])
+    pieces, output_grad = lax.optimization_barrier((pieces, output_grad))
+    other_grad = swap_head(output_grad)
     far_got = gather_far(pieces, far, slots)
     grads = call(
         grad_kernel,
@@ -425,21 +444,32 @@
         [shape((2 * slots * rows, width)) for _, _, rows in entries]
         + [shape((pairs, list_rows, width))] * 2
         + [shape((pairs, 2 * tok, width))] * 2
-        + [shape((slots, 2 * tok, list_rows))] * 2,
+        + [shape((slots, 2 * tok, list_rows))] * 2
+        + [shape((slots, 2 * tok, HDIM), F32)],
         first + second,
         scratch=[pltpu.VMEM((BLOCK * len(far), width), F32)] * 2,
         flops=6 * heads * tok * list_rows * HDIM,
     )
     shares, share_levels = scatter_far(made[: len(entries)], far, slots)
-    *made, key_sum, value_sum = call(
+    key_list, value_list, asked, grads, probs, score_grads, sums = made[len(entries) :]
+    made = call(
         lambda *refs: reduce_kernel(slots, *refs),
-        over(2 * tok) + [shape((slots * tok, width), F32)] * 2,
-        made[len(entries) :],
-        scratch=[pltpu.VMEM((pairs, BLOCK, width), BF16)] * 2,
+        over(2 * tok),
+        [key_list, value_list, probs, score_grads, sums],
         flops=6 * 10**9,
         vmem=16,
     )
-    made[2], *shares[1:] = lax.optimization_barrier((made[2], *shares[1:]))
+    key_sum, value_sum = call(
+        lambda *refs: local_kernel(slots, *refs),
+        [shape((slots * tok, width), F32)] * 2,
+        [asked, grads, probs, score_grads],
+        scratch=[pltpu.VMEM((pairs, BLOCK, width), BF16)] * 2,
+        flops=4 * heads * tok * list_rows * HDIM,
+        vmem=16,
+    )
+    made = list(made)
+    late = ORDER[-1]
+    made[late], key_sum, *shares[1:] = lax.optimization_barrier((made[late], key_sum, *shares[1:]))
     home = exchange(made)
     chunks = call(
         lambda *refs: merge_kernel(slots, share_levels, *refs),
@@ -448,41 +478,38 @@
         vmem=8,
     )
     home, _ = lax.optimization_barrier((home, chunks))
+    chunks = list(chunks)
+    chunks[late], home[-1] = lax.optimization_barrier((chunks[late], home[-1]))
     last = exchange(chunks)
     wide = shape((tok, columns))
-    attended = call(
-        lambda *refs: collect_kernel(slots, *refs),
-        wide,
-        [place] + home,
-        specs=[SMEM] + [VMEM] * slots,
+    attended, *send = call(
+        lambda *refs: send_kernel(slots, *refs),
+        [wide] + [shape((tok, columns // 2))] * 2,
+        [place, out_weight] + home,
+        flops=2 * tok * columns * columns,
+        specs=[SMEM] + [VMEM] * (1 + slots),
+        vmem=16,
+    )
+    got = [swap_head(part) for part in send]
+    keep, query_grad = call(
+        lambda *refs: keep_kernel(slots, *refs),
+        [shape((tok, columns), F32), wide],
+        [place, out_weight, attended] + home,
+        scratch=[pltpu.VMEM((tok, columns), BF16), pltpu.SemaphoreType.DMA(())],
+        flops=4 * 10**9,
+        specs=[SMEM] + [VMEM] * (2 + slots),
+        outs=[VMEM, HBM],
+        vmem=16,
+    )
+    key_grad, value_grad, output = call(
+        lambda *refs: finish_kernel(slots, *refs),
+        [wide] * 3,
+        [place, keep] + last + got,
+        scratch=[pltpu.VMEM((tok, columns), BF16)] * 3 + [pltpu.SemaphoreType.DMA((3,))],
+        specs=[SMEM] + [VMEM] * (1 + slots + len(got)),
+        outs=HBM,
         vmem=8,
     )
-    keep, *send = call(
-        project_kernel,
-        [shape((tok, columns), F32)] + [shape((tok, columns // 2))] * 2,
-        [place, attended, out_weight],
-        flops=4 * 10**9,
-        specs=[SMEM, VMEM, VMEM],
-        vmem=16,
-    )
-    got = [swap_head(part) for part in send]
-    output = call(add_kernel, wide, [keep] + got, vmem=8)
-
-    def put(chunks, blocks, flops):
-        return call(
-            lambda *refs: place_kernel(slots, blocks, *refs),
-            [wide] * len(blocks),
-            [place] + chunks,
-            scratch=[pltpu.SemaphoreType.DMA((len(blocks) * slots,))],
-            specs=[SMEM] + [VMEM] * slots,
-            vmem=8,
-            free=True,
-            flops=flops,
-            outs=HBM,
-        )
-
-    (query_grad,) = put(home, (1,), 4 * 10**9)
-    key_grad, value_grad = put(last, (0, 1), 0)
     return output, query_grad, key_grad, value_grad
 
 

time: 55.3 us -> 53 us (0.958)
  waiting for transfers between devices: 14.1 us -> 12.7 us
  Pallas kernels: 15.3 us -> 14.2 us
    ppermute x18, waiting for transfers between devices: 14.1 us -> 12.7 us  [swap_seq(): lax.ppermute(array, 'seq', [(i, i ^ mask) for i in range(lax.axis_size('s...]
    pallas_call x11 -> x10, Pallas kernels: 15.3 us -> 14.2 us  [call(): pl.pallas_call(kernel, out_shape=out_shape, in_specs=specs, out_specs=out...]
  transfers between devices with their start and end apart: 21 -> 21, of which waited for: 7 -> 9; matrix products, arithmetic and copies ran while one was open for 0% -> 0% of each run, Pallas kernels for 21% -> 14%
where the time goes in v4:
time: 53 us; the launch traced here: 52.8 us
  starting transfers between devices  25.1 us (47%)
  Pallas kernels  14.2 us (27%)
  waiting for transfers between devices  12.7 us (24%)
  between operations  0.77 us (1%)
    ppermute x18, starting transfers between devices, swap_seq(): lax.ppermute(array, 'seq', [(i, i ^ mask) for i in range(lax.axis_size('s...  24 us
    pallas_call x10, Pallas kernels, call(): pl.pallas_call(kernel, out_shape=out_shape, in_specs=specs, out_specs=out...  14.2 us
    ppermute x18, waiting for transfers between devices, swap_seq(): lax.ppermute(array, 'seq', [(i, i ^ mask) for i in range(lax.axis_size('s...  12.7 us
    ppermute x3, starting transfers between devices, swap_head(): return lax.ppermute(array, 'head', [(0, 1), (1, 0)])  1.08 us
  transfers between devices with their start and end apart: 21, of which 9 were waited for; matrix products, arithmetic and copies ran while one was open for 0% of the time, Pallas kernels for 14%

profile of v4, /device:TPU:0, one launch (start us, length us, event | category | flops | bytes accessed | tf_op | source)
XLA Modules:
  0.0 52.8 jit_solution(15762535741299129825)
XLA Ops:
  0.6 0.1 pad_add_fusion.refs_0_.at_ref
  0.7 0.0 copy-start.1
  0.7 0.0 copy-start
  0.7 2.2 %shard_map.84 = (bf16[64,1024]{1,0:T(8,128)(2,1)S(1)}, bf16[32,1024]{1,0:T(8,128)(2,1)S(1)}, bf16[384,256]{1,0:T(8,128)(2,1)S(1)}, bf16[384,256]{1,0:T(8,128)(2,...) custom-call(s32[2]{0:T(128)S(1)} %pad_add_fusion.refs_0_.at_ref, bf16[128,1024]{1,0:T(8,128)(2,1)} %refs_1_.3, ...), custom_call_target="tpu_custom_call" | custom-call | flops 6000000000 | bytes 786440 | tf_op jit(solution)/shard_map/pallas_call | solution.py:54
  3.0 0.0 copy-done.1
  3.0 0.5 collective-permute-start
  3.5 2.6 %collective-permute-start.1 = (bf16[384,256]{1,0:T(8,128)(2,1)S(1)}, bf16[384,256]{1,0:T(8,128)(2,1)S(1)}, u32[]{:S(2)}, u32[]{:S(2)}) collective-permute-start(bf16[384,256]{1,0:T(8,128)(2,1)S(1)} %get-tuple-element.63), channel_id=1, source_target_pairs={{0,2},{2,0},{4,6},{6,4},{8,10},{10,8},{12,14},{14,12},{16,18},{18,... | collective-permute-start | bytes 589832 | tf_op jit(solution)/shard_map/ppermute | solution.py:21
  6.1 1.6 %collective-permute-start.4 = (bf16[64,1024]{1,0:T(8,128)(2,1)S(1)}, bf16[64,1024]{1,0:T(8,128)(2,1)S(1)}, u32[]{:S(2)}, u32[]{:S(2)}) collective-permute-start(bf16[64,1024]{1,0:T(8,128)(2,1)S(1)} %get-tuple-element.68), channel_id=1, source_target_pairs={{0,8},{2,10},{4,12},{6,14},{8,0},{10,2},{12,4},{14,6},{16,24},{18,... | collective-permute-start | bytes 393224 | tf_op jit(solution)/shard_map/ppermute | solution.py:21
  7.6 2.5 %collective-permute-start.6 = (bf16[32,1024]{1,0:T(8,128)(2,1)S(1)}, bf16[32,1024]{1,0:T(8,128)(2,1)S(1)}, u32[]{:S(2)}, u32[]{:S(2)}) collective-permute-start(bf16[32,1024]{1,0:T(8,128)(2,1)S(1)} %get-tuple-element.69), channel_id=1, source_target_pairs={{0,24},{2,26},{4,28},{6,30},{8,16},{10,18},{12,20},{14,22},{16,8},... | collective-permute-start | bytes 196616 | tf_op jit(solution)/shard_map/ppermute | solution.py:21
  10.1 0.1 collective-permute-start.5
  10.2 0.0 collective-permute-done.other_ref
  10.2 1.5 %collective-permute-start.2 = (bf16[384,256]{1,0:T(8,128)(2,1)S(1)}, bf16[384,256]{1,0:T(8,128)(2,1)S(1)}, u32[]{:S(2)}, u32[]{:S(2)}) collective-permute-start(bf16[384,256]{1,0:T(8,128)(2,1)S(1)} %get-tuple-element.65), channel_id=1, source_target_pairs={{0,4},{2,6},{4,0},{6,2},{8,12},{10,14},{12,8},{14,10},{16,20},{18,... | collective-permute-start | bytes 589832 | tf_op jit(solution)/shard_map/ppermute | solution.py:21
  11.8 0.0 copy-done
  11.8 1.3 %shard_map.85.refs_1_ = bf16[128,1024]{1,0:T(8,128)(2,1)S(1)} custom-call(s32[2]{0:T(128)S(1)} %pad_add_fusion.refs_0_.at_ref, bf16[128,1024]{1,0:T(8,128)(2,1)S(1)} %copy-done.1, bf16[2048,1024]{1,0:T(8,128)(2,1)S(1)} %copy-done, bf16[128,1024]{1,0:T(8,128)(2,1)S(1)} %collective-permute-done.other_ref), custom_call_target="tpu_custom_call" | custom-call | flops 536870912 | bytes 4718600 | tf_op jit(solution)/shard_map/pallas_call | solution.py:54
  13.0 0.0 collective-permute-done.1.refs_1_
  13.0 1.2 %collective-permute-start.3 = (bf16[384,256]{1,0:T(8,128)(2,1)S(1)}, bf16[384,256]{1,0:T(8,128)(2,1)S(1)}, u32[]{:S(2)}, u32[]{:S(2)}) collective-permute-start(bf16[384,256]{1,0:T(8,128)(2,1)S(1)} %get-tuple-element.66), channel_id=1, source_target_pairs={{0,6},{2,4},{4,2},{6,0},{8,14},{10,12},{12,10},{14,8},{16,22},{18,... | collective-permute-start | bytes 589832 | tf_op jit(solution)/shard_map/ppermute | solution.py:21
  14.3 1.6 %collective-permute-done.6.refs_4_ = bf16[32,1024]{1,0:T(8,128)(2,1)S(1)} collective-permute-done((bf16[32,1024]{1,0:T(8,128)(2,1)S(1)}, bf16[32,1024]{1,0:T(8,128)(2,1)S(1)}, u32[]{:S(2)}, u32[]{:S(2)}) %collective-permute-start.6) | collective-permute-done | bytes 65568 | tf_op jit(solution)/shard_map/ppermute | solution.py:21
  15.9 1.4 %collective-permute-done.5.refs_3_ = bf16[32,1024]{1,0:T(8,128)(2,1)S(1)} collective-permute-done((bf16[32,1024]{1,0:T(8,128)(2,1)S(1)}, bf16[32,1024]{1,0:T(8,128)(2,1)S(1)}, u32[]{:S(2)}, u32[]{:S(2)}) %collective-permute-start.5) | collective-permute-done | bytes 65568 | tf_op jit(solution)/shard_map/ppermute | solution.py:21
  17.3 0.0 collective-permute-done.4.refs_2_
  17.3 0.6 %shard_map.86 = (bf16[256,256]{1,0:T(8,128)(2,1)S(1)}, bf16[256,256]{1,0:T(8,128)(2,1)S(1)}, bf16[256,256]{1,0:T(8,128)(2,1)S(1)}, bf16[256,256]{1,0:T(8,128)(2,1)S(1)}) custom-call(s32[2]{0:T(128)S(1)} %pad_add_fusion.refs_0_.at_ref, bf16[128,1024]{1,0:T(8,128)(2,1)S(1)} %shard_map.85.refs_1_, bf16[64,1024]{1,0:T(8,128)(2,1)S(1)} %collective-permute-done.4.refs_2_, ...), custom_call_target="tpu_custom_call" | custom-call | bytes 524296 | tf_op jit(solution)/shard_map/pallas_call | solution.py:54
  17.9 0.6 %collective-permute-start.7 = (bf16[256,256]{1,0:T(8,128)(2,1)S(1)}, bf16[256,256]{1,0:T(8,128)(2,1)S(1)}, u32[]{:S(2)}, u32[]{:S(2)}) collective-permute-start(bf16[256,256]{1,0:T(8,128)(2,1)S(1)} %get-tuple-element.71), channel_id=1, source_target_pairs={{0,2},{2,0},{4,6},{6,4},{8,10},{10,8},{12,14},{14,12},{16,18},{18,... | collective-permute-start | bytes 393224 | tf_op jit(solution)/shard_map/ppermute | solution.py:21
  18.5 1.5 %collective-permute-start.8 = (bf16[256,256]{1,0:T(8,128)(2,1)S(1)}, bf16[256,256]{1,0:T(8,128)(2,1)S(1)}, u32[]{:S(2)}, u32[]{:S(2)}) collective-permute-start(bf16[256,256]{1,0:T(8,128)(2,1)S(1)} %get-tuple-element.72), channel_id=1, source_target_pairs={{0,4},{2,6},{4,0},{6,2},{8,12},{10,14},{12,8},{14,10},{16,20},{18,... | collective-permute-start | bytes 393224 | tf_op jit(solution)/shard_map/ppermute | solution.py:21
  20.0 1.4 %collective-permute-start.9 = (bf16[256,256]{1,0:T(8,128)(2,1)S(1)}, bf16[256,256]{1,0:T(8,128)(2,1)S(1)}, u32[]{:S(2)}, u32[]{:S(2)}) collective-permute-start(bf16[256,256]{1,0:T(8,128)(2,1)S(1)} %get-tuple-element.73), channel_id=1, source_target_pairs={{0,6},{2,4},{4,2},{6,0},{8,14},{10,12},{12,10},{14,8},{16,22},{18,... | collective-permute-start | bytes 393224 | tf_op jit(solution)/shard_map/ppermute | solution.py:21
  21.4 1.3 %collective-permute-done.2.refs_2_ = bf16[384,256]{1,0:T(8,128)(2,1)S(1)} collective-permute-done((bf16[384,256]{1,0:T(8,128)(2,1)S(1)}, bf16[384,256]{1,0:T(8,128)(2,1)S(1)}, u32[]{:S(2)}, u32[]{:S(2)}) %collective-permute-start.2) | collective-permute-done | bytes 196640 | tf_op jit(solution)/shard_map/ppermute | solution.py:21
  22.7 0.8 %collective-permute-done.7.refs_5_ = bf16[256,256]{1,0:T(8,128)(2,1)S(1)} collective-permute-done((bf16[256,256]{1,0:T(8,128)(2,1)S(1)}, bf16[256,256]{1,0:T(8,128)(2,1)S(1)}, u32[]{:S(2)}, u32[]{:S(2)}) %collective-permute-start.7) | collective-permute-done | bytes 131104 | tf_op jit(solution)/shard_map/ppermute | solution.py:21
  23.5 3.0 %collective-permute-done.8.refs_6_ = bf16[256,256]{1,0:T(8,128)(2,1)S(1)} collective-permute-done((bf16[256,256]{1,0:T(8,128)(2,1)S(1)}, bf16[256,256]{1,0:T(8,128)(2,1)S(1)}, u32[]{:S(2)}, u32[]{:S(2)}) %collective-permute-start.8) | collective-permute-done | bytes 131104 | tf_op jit(solution)/shard_map/ppermute | solution.py:21
  26.5 0.0 collective-permute-done.9.refs_7_
  26.5 0.0 collective-permute-done.3.refs_3_
  26.5 2.9 %shard_map.87 = (bf16[256,256]{1,0:T(8,128)(2,1)S(1)}, bf16[128,256]{1,0:T(8,128)(2,1)S(1)}, bf16[128,256]{1,0:T(8,128)(2,1)S(1)}, bf16[2,640,256]{2,1,0:T(8,128...) custom-call(bf16[384,256]{1,0:T(8,128)(2,1)S(1)} %get-tuple-element., ...), custom_call_target="tpu_custom_call" | custom-call | flops 503316480 | bytes 1310720 | tf_op jit(solution)/shard_map/pallas_call | solution.py:54
  29.4 2.6 %collective-permute-start.12 = (bf16[128,256]{1,0:T(8,128)(2,1)S(1)}, bf16[128,256]{1,0:T(8,128)(2,1)S(1)}, u32[]{:S(2)}, u32[]{:S(2)}) collective-permute-start(bf16[128,256]{1,0:T(8,128)(2,1)S(1)} %get-tuple-element.86), channel_id=1, source_target_pairs={{0,16},{2,18},{4,20},{6,22},{8,24},{10,26},{12,28},{14,30},{16,0},... | collective-permute-start | bytes 196616 | tf_op jit(solution)/shard_map/ppermute | solution.py:21
  32.0 1.4 %collective-permute-start.13 = (bf16[128,256]{1,0:T(8,128)(2,1)S(1)}, bf16[128,256]{1,0:T(8,128)(2,1)S(1)}, u32[]{:S(2)}, u32[]{:S(2)}) collective-permute-start(bf16[128,256]{1,0:T(8,128)(2,1)S(1)} %get-tuple-element.87), channel_id=1, source_target_pairs={{0,24},{2,26},{4,28},{6,30},{8,16},{10,18},{12,20},{14,22},{16,8},... | collective-permute-start | bytes 196616 | tf_op jit(solution)/shard_map/ppermute | solution.py:21
  33.4 0.8 %shard_map.88 = (bf16[256,256]{1,0:T(8,128)(2,1)S(1)}, bf16[256,256]{1,0:T(8,128)(2,1)S(1)}, bf16[256,256]{1,0:T(8,128)(2,1)S(1)}, bf16[256,256]{1,0:T(8,128)(2,1)S(1)}) custom-call(bf16[2,640,256]{2,1,0:T(8,128)(2,1)S(1)} %get-tuple-element.74.refs_0_, bf16[2,640,256]{2,1,0:T(8,128)(2,1)S(1)} %get-tuple-element.75.refs_1_, ...), custom_call_target="tpu_custom_call" | custom-call | flops 6000000000 | bytes 4456448 | tf_op jit(solution)/shard_map/pallas_call | solution.py:54
  34.2 0.6 %collective-permute-start.10 = (bf16[256,256]{1,0:T(8,128)(2,1)S(1)}, bf16[256,256]{1,0:T(8,128)(2,1)S(1)}, u32[]{:S(2)}, u32[]{:S(2)}) collective-permute-start(bf16[256,256]{1,0:T(8,128)(2,1)S(1)} %get-tuple-element.80), channel_id=1, source_target_pairs={{0,2},{2,0},{4,6},{6,4},{8,10},{10,8},{12,14},{14,12},{16,18},{18,... | collective-permute-start | bytes 393224 | tf_op jit(solution)/shard_map/ppermute | solution.py:21
  34.8 1.5 %collective-permute-start.11 = (bf16[256,256]{1,0:T(8,128)(2,1)S(1)}, bf16[256,256]{1,0:T(8,128)(2,1)S(1)}, u32[]{:S(2)}, u32[]{:S(2)}) collective-permute-start(bf16[256,256]{1,0:T(8,128)(2,1)S(1)} %get-tuple-element.81), channel_id=1, source_target_pairs={{0,4},{2,6},{4,0},{6,2},{8,12},{10,14},{12,8},{14,10},{16,20},{18,... | collective-permute-start | bytes 393224 | tf_op jit(solution)/shard_map/ppermute | solution.py:21
  36.3 0.0 collective-permute-start.15
  36.3 0.9 %shard_map.89 = (f32[512,256]{1,0:T(8,128)S(1)}, f32[512,256]{1,0:T(8,128)S(1)}) custom-call(bf16[2,256,256]{2,1,0:T(8,128)(2,1)S(1)} %get-tuple-element.83.refs_0_, bf16[2,256,256]{2,1,0:T(8,128)(2,1)S(1)} %get-tuple-element.84.refs_1_, bf16[4,256,640]{2,1,0:T(8,128)(2,1)S(1)} %get-tuple-element.76.refs_2_, bf16[4,256,640]{2,1,0:T(8,128)(2,1)S(1)} %get-tuple-element.77.refs_3_), custom_call_target="tpu_custom_call" | custom-call | flops 335544320 | bytes 3145728 | tf_op jit(solution)/shard_map/pallas_call | solution.py:54
  37.2 0.0 collective-permute-done.12.refs_3_
  37.2 1.0 %collective-permute-done.13.refs_4_ = bf16[128,256]{1,0:T(8,128)(2,1)S(1)} collective-permute-done((bf16[128,256]{1,0:T(8,128)(2,1)S(1)}, bf16[128,256]{1,0:T(8,128)(2,1)S(1)}, u32[]{:S(2)}, u32[]{:S(2)}) %collective-permute-start.13) | collective-permute-done | bytes 65568 | tf_op jit(solution)/shard_map/ppermute | solution.py:21
  38.2 1.5 %collective-permute-start.14 = (bf16[256,256]{1,0:T(8,128)(2,1)S(1)}, bf16[256,256]{1,0:T(8,128)(2,1)S(1)}, u32[]{:S(2)}, u32[]{:S(2)}) collective-permute-start(bf16[256,256]{1,0:T(8,128)(2,1)S(1)} %get-tuple-element.88), channel_id=1, source_target_pairs={{0,6},{2,4},{4,2},{6,0},{8,14},{10,12},{12,10},{14,8},{16,22},{18,... | collective-permute-start | bytes 393224 | tf_op jit(solution)/shard_map/ppermute | solution.py:21
  39.7 1.6 %collective-permute-done.15.refs_2_ = bf16[256,256]{1,0:T(8,128)(2,1)S(1)} collective-permute-done((bf16[256,256]{1,0:T(8,128)(2,1)S(1)}, bf16[256,256]{1,0:T(8,128)(2,1)S(1)}, u32[]{:S(2)}, u32[]{:S(2)}) %collective-permute-start.15) | collective-permute-done | bytes 131104 | tf_op jit(solution)/shard_map/ppermute | solution.py:21
  41.3 0.6 %shard_map.90 = (bf16[256,256]{1,0:T(8,128)(2,1)S(1)}, bf16[256,256]{1,0:T(8,128)(2,1)S(1)}, bf16[256,256]{1,0:T(8,128)(2,1)S(1)}, bf16[256,256]{1,0:T(8,128)(2,1)S(1)}) custom-call(f32[512,256]{1,0:T(8,128)S(1)} %get-tuple-element.89.refs_0_, f32[512,256]{1,0:T(8,128)S(1)} %get-tuple-element.90.refs_1_, ...), custom_call_target="tpu_custom_call" | custom-call | bytes 1310720 | tf_op jit(solution)/shard_map/pallas_call | solution.py:54
  41.9 1.6 %collective-permute-start.16 = (bf16[256,256]{1,0:T(8,128)(2,1)S(1)}, bf16[256,256]{1,0:T(8,128)(2,1)S(1)}, u32[]{:S(2)}, u32[]{:S(2)}) collective-permute-start(bf16[256,256]{1,0:T(8,128)(2,1)S(1)} %get-tuple-element.95), channel_id=1, source_target_pairs={{0,2},{2,0},{4,6},{6,4},{8,10},{10,8},{12,14},{14,12},{16,18},{18,... | collective-permute-start | bytes 393224 | tf_op jit(solution)/shard_map/ppermute | solution.py:21
  43.4 0.5 collective-permute-start.17
  43.9 0.0 collective-permute-done.10.refs_3_.refs_4_
  44.0 0.0 collective-permute-done.11.refs_4_.refs_5_
  44.0 1.5 %collective-permute-done.14.refs_5_.refs_6_ = bf16[256,256]{1,0:T(8,128)(2,1)S(1)} collective-permute-done((bf16[256,256]{1,0:T(8,128)(2,1)S(1)}, bf16[256,256]{1,0:T(8,128)(2,1)S(1)}, u32[]{:S(2)}, u32[]{:S(2)}) %collective-permute-start.14) | collective-permute-done | bytes 131104 | tf_op jit(solution)/shard_map/ppermute | solution.py:21
  45.4 1.3 %collective-permute-start.18 = (bf16[256,256]{1,0:T(8,128)(2,1)S(1)}, bf16[256,256]{1,0:T(8,128)(2,1)S(1)}, u32[]{:S(2)}, u32[]{:S(2)}) collective-permute-start(bf16[256,256]{1,0:T(8,128)(2,1)S(1)} %get-tuple-element.105), channel_id=1, source_target_pairs={{0,6},{2,4},{4,2},{6,0},{8,14},{10,12},{12,10},{14,8},{16,22},{18,... | collective-permute-start | bytes 393224 | tf_op jit(solution)/shard_map/ppermute | solution.py:21
  46.8 1.4 %shard_map.91 = (bf16[128,1024]{1,0:T(8,128)(2,1)S(1)}, bf16[128,512]{1,0:T(8,128)(2,1)S(1)}, bf16[128,512]{1,0:T(8,128)(2,1)S(1)}) custom-call(s32[2]{0:T(128)S(1)} %pad_add_fusion.refs_0_.at_ref, bf16[2048,1024]{1,0:T(8,128)(2,1)S(1)} %copy-done, bf16[256,256]{1,0:T(8,128)(2,1)S(1)} %get-tuple-element.98.refs_2_.refs_3_, ...), custom_call_target="tpu_custom_call" | custom-call | flops 268435456 | bytes 4718600 | tf_op jit(solution)/shard_map/pallas_call | solution.py:54
  48.2 0.1 collective-permute-start.19
  48.3 0.5 collective-permute-start.20
  48.8 2.0 %shard_map.92 = (f32[128,1024]{1,0:T(8,128)S(1)}, bf16[128,1024]{1,0:T(8,128)(2,1)}) custom-call(s32[2]{0:T(128)S(1)} %pad_add_fusion.refs_0_.at_ref, bf16[2048,1024]{1,0:T(8,128)(2,1)S(1)} %copy-done, bf16[128,1024]{1,0:T(8,128)(2,1)S(1)} %get-tuple-element.103.refs_2_, bf16[256,256]{1,0:T(8,128)(2,1)S(1)} %get-tuple-element.98.refs_2_.refs_3_, ...), custom_call_target="tpu_custom_call" | custom-call | flops 4000000000 | bytes 4980744 | tf_op jit(solution)/shard_map/pallas_call | solution.py:54
  50.7 0.0 collective-permute-done.16.refs_3_
  50.7 0.0 collective-permute-done.17.refs_4_
  50.7 0.6 %collective-permute-done.18.refs_5_ = bf16[256,256]{1,0:T(8,128)(2,1)S(1)} collective-permute-done((bf16[256,256]{1,0:T(8,128)(2,1)S(1)}, bf16[256,256]{1,0:T(8,128)(2,1)S(1)}, u32[]{:S(2)}, u32[]{:S(2)}) %collective-permute-start.18) | collective-permute-done | bytes 131104 | tf_op jit(solution)/shard_map/ppermute | solution.py:21
  51.3 0.0 collective-permute-done.19.refs_6_
  51.3 0.0 collective-permute-done.20.refs_7_
  51.3 1.5 %shard_map.93 = (bf16[128,1024]{1,0:T(8,128)(2,1)}, bf16[128,1024]{1,0:T(8,128)(2,1)}, bf16[128,1024]{1,0:T(8,128)(2,1)}) custom-call(s32[2]{0:T(128)S(1)} %pad_add_fusion.refs_0_.at_ref, f32[128,1024]{1,0:T(8,128)S(1)} %get-tuple-element.104.refs_1_, bf16[256,256]{1,0:T(8,128)(2,1)S(1)} %get-tuple-element.94.refs_2_, ...), custom_call_target="tpu_custom_call" | custom-call | bytes 1310728 | tf_op jit(solution)/shard_map/pallas_call | solution.py:54
Async XLA Ops:
  0.7 2.3 %copy-start.1 = (bf16[128,1024]{1,0:T(8,128)(2,1)S(1)}, bf16[128,1024]{1,0:T(8,128)(2,1)}, u32[]{:S(2)}) copy-start(bf16[128,1024]{1,0:T(8,128)(2,1)} %mine_ref) | copy-start | bytes 786436
  0.7 11.0 %copy-start = (bf16[2048,1024]{1,0:T(8,128)(2,1)S(1)}, bf16[2048,1024]{1,0:T(8,128)(2,1)}, u32[]{:S(2)}) copy-start(bf16[2048,1024]{1,0:T(8,128)(2,1)} %refs_1_.5) | copy-start | bytes 12582916
  3.0 7.3 %collective-permute-start = (bf16[128,1024]{1,0:T(8,128)(2,1)S(1)}, bf16[128,1024]{1,0:T(8,128)(2,1)S(1)}, u32[]{:S(2)}, u32[]{:S(2)}) collective-permute-start(bf16[128,1024]{1,0:T(8,128)(2,1)S(1)} %copy-done.1), channel_id=1, source_target_pairs={{0,1},{1,0},{2,3},{3,2},{4,5},{5,4},{6,7},{7,6},{8,9},{9,8},{10,11... | collective-permute-start | bytes 786440 | tf_op jit(solution)/shard_map/ppermute | solution.py:25
  3.5 9.5 %collective-permute-start.1 = (bf16[384,256]{1,0:T(8,128)(2,1)S(1)}, bf16[384,256]{1,0:T(8,128)(2,1)S(1)}, u32[]{:S(2)}, u32[]{:S(2)}) collective-permute-start(bf16[384,256]{1,0:T(8,128)(2,1)S(1)} %get-tuple-element.63), channel_id=1, source_target_pairs={{0,2},{2,0},{4,6},{6,4},{8,10},{10,8},{12,14},{14,12},{16,18},{18,... | collective-permute-start | bytes 589832 | tf_op jit(solution)/shard_map/ppermute | solution.py:21
  6.1 11.2 %collective-permute-start.4 = (bf16[64,1024]{1,0:T(8,128)(2,1)S(1)}, bf16[64,1024]{1,0:T(8,128)(2,1)S(1)}, u32[]{:S(2)}, u32[]{:S(2)}) collective-permute-start(bf16[64,1024]{1,0:T(8,128)(2,1)S(1)} %get-tuple-element.68), channel_id=1, source_target_pairs={{0,8},{2,10},{4,12},{6,14},{8,0},{10,2},{12,4},{14,6},{16,24},{18,... | collective-permute-start | bytes 393224 | tf_op jit(solution)/shard_map/ppermute | solution.py:21
  7.6 8.2 %collective-permute-start.6 = (bf16[32,1024]{1,0:T(8,128)(2,1)S(1)}, bf16[32,1024]{1,0:T(8,128)(2,1)S(1)}, u32[]{:S(2)}, u32[]{:S(2)}) collective-permute-start(bf16[32,1024]{1,0:T(8,128)(2,1)S(1)} %get-tuple-element.69), channel_id=1, source_target_pairs={{0,24},{2,26},{4,28},{6,30},{8,16},{10,18},{12,20},{14,22},{16,8},... | collective-permute-start | bytes 196616 | tf_op jit(solution)/shard_map/ppermute | solution.py:21
  10.1 7.1 %collective-permute-start.5 = (bf16[32,1024]{1,0:T(8,128)(2,1)S(1)}, bf16[32,1024]{1,0:T(8,128)(2,1)S(1)}, u32[]{:S(2)}, u32[]{:S(2)}) collective-permute-start(bf16[32,1024]{1,0:T(8,128)(2,1)S(1)} %get-tuple-element.69), channel_id=1, source_target_pairs={{0,16},{2,18},{4,20},{6,22},{8,24},{10,26},{12,28},{14,30},{16,0},... | collective-permute-start | bytes 196616 | tf_op jit(solution)/shard_map/ppermute | solution.py:21
  10.2 12.5 %collective-permute-start.2 = (bf16[384,256]{1,0:T(8,128)(2,1)S(1)}, bf16[384,256]{1,0:T(8,128)(2,1)S(1)}, u32[]{:S(2)}, u32[]{:S(2)}) collective-permute-start(bf16[384,256]{1,0:T(8,128)(2,1)S(1)} %get-tuple-element.65), channel_id=1, source_target_pairs={{0,4},{2,6},{4,0},{6,2},{8,12},{10,14},{12,8},{14,10},{16,20},{18,... | collective-permute-start | bytes 589832 | tf_op jit(solution)/shard_map/ppermute | solution.py:21
  13.0 13.4 %collective-permute-start.3 = (bf16[384,256]{1,0:T(8,128)(2,1)S(1)}, bf16[384,256]{1,0:T(8,128)(2,1)S(1)}, u32[]{:S(2)}, u32[]{:S(2)}) collective-permute-start(bf16[384,256]{1,0:T(8,128)(2,1)S(1)} %get-tuple-element.66), channel_id=1, source_target_pairs={{0,6},{2,4},{4,2},{6,0},{8,14},{10,12},{12,10},{14,8},{16,22},{18,... | collective-permute-start | bytes 589832 | tf_op jit(solution)/shard_map/ppermute | solution.py:21
  17.9 5.6 %collective-permute-start.7 = (bf16[256,256]{1,0:T(8,128)(2,1)S(1)}, bf16[256,256]{1,0:T(8,128)(2,1)S(1)}, u32[]{:S(2)}, u32[]{:S(2)}) collective-permute-start(bf16[256,256]{1,0:T(8,128)(2,1)S(1)} %get-tuple-element.71), channel_id=1, source_target_pairs={{0,2},{2,0},{4,6},{6,4},{8,10},{10,8},{12,14},{14,12},{16,18},{18,... | collective-permute-start | bytes 393224 | tf_op jit(solution)/shard_map/ppermute | solution.py:21
  18.5 8.0 %collective-permute-start.8 = (bf16[256,256]{1,0:T(8,128)(2,1)S(1)}, bf16[256,256]{1,0:T(8,128)(2,1)S(1)}, u32[]{:S(2)}, u32[]{:S(2)}) collective-permute-start(bf16[256,256]{1,0:T(8,128)(2,1)S(1)} %get-tuple-element.72), channel_id=1, source_target_pairs={{0,4},{2,6},{4,0},{6,2},{8,12},{10,14},{12,8},{14,10},{16,20},{18,... | collective-permute-start | bytes 393224 | tf_op jit(solution)/shard_map/ppermute | solution.py:21
  20.0 6.5 %collective-permute-start.9 = (bf16[256,256]{1,0:T(8,128)(2,1)S(1)}, bf16[256,256]{1,0:T(8,128)(2,1)S(1)}, u32[]{:S(2)}, u32[]{:S(2)}) collective-permute-start(bf16[256,256]{1,0:T(8,128)(2,1)S(1)} %get-tuple-element.73), channel_id=1, source_target_pairs={{0,6},{2,4},{4,2},{6,0},{8,14},{10,12},{12,10},{14,8},{16,22},{18,... | collective-permute-start | bytes 393224 | tf_op jit(solution)/shard_map/ppermute | solution.py:21
  29.4 7.8 %collective-permute-start.12 = (bf16[128,256]{1,0:T(8,128)(2,1)S(1)}, bf16[128,256]{1,0:T(8,128)(2,1)S(1)}, u32[]{:S(2)}, u32[]{:S(2)}) collective-permute-start(bf16[128,256]{1,0:T(8,128)(2,1)S(1)} %get-tuple-element.86), channel_id=1, source_target_pairs={{0,16},{2,18},{4,20},{6,22},{8,24},{10,26},{12,28},{14,30},{16,0},... | collective-permute-start | bytes 196616 | tf_op jit(solution)/shard_map/ppermute | solution.py:21
  32.0 6.2 %collective-permute-start.13 = (bf16[128,256]{1,0:T(8,128)(2,1)S(1)}, bf16[128,256]{1,0:T(8,128)(2,1)S(1)}, u32[]{:S(2)}, u32[]{:S(2)}) collective-permute-start(bf16[128,256]{1,0:T(8,128)(2,1)S(1)} %get-tuple-element.87), channel_id=1, source_target_pairs={{0,24},{2,26},{4,28},{6,30},{8,16},{10,18},{12,20},{14,22},{16,8},... | collective-permute-start | bytes 196616 | tf_op jit(solution)/shard_map/ppermute | solution.py:21
  34.2 9.8 %collective-permute-start.10 = (bf16[256,256]{1,0:T(8,128)(2,1)S(1)}, bf16[256,256]{1,0:T(8,128)(2,1)S(1)}, u32[]{:S(2)}, u32[]{:S(2)}) collective-permute-start(bf16[256,256]{1,0:T(8,128)(2,1)S(1)} %get-tuple-element.80), channel_id=1, source_target_pairs={{0,2},{2,0},{4,6},{6,4},{8,10},{10,8},{12,14},{14,12},{16,18},{18,... | collective-permute-start | bytes 393224 | tf_op jit(solution)/shard_map/ppermute | solution.py:21
  34.8 9.2 %collective-permute-start.11 = (bf16[256,256]{1,0:T(8,128)(2,1)S(1)}, bf16[256,256]{1,0:T(8,128)(2,1)S(1)}, u32[]{:S(2)}, u32[]{:S(2)}) collective-permute-start(bf16[256,256]{1,0:T(8,128)(2,1)S(1)} %get-tuple-element.81), channel_id=1, source_target_pairs={{0,4},{2,6},{4,0},{6,2},{8,12},{10,14},{12,8},{14,10},{16,20},{18,... | collective-permute-start | bytes 393224 | tf_op jit(solution)/shard_map/ppermute | solution.py:21
  36.3 5.0 %collective-permute-start.15 = (bf16[256,256]{1,0:T(8,128)(2,1)S(1)}, bf16[256,256]{1,0:T(8,128)(2,1)S(1)}, u32[]{:S(2)}, u32[]{:S(2)}) collective-permute-start(bf16[256,256]{1,0:T(8,128)(2,1)S(1)} %get-tuple-element.91), channel_id=1, source_target_pairs={{0,8},{2,10},{4,12},{6,14},{8,0},{10,2},{12,4},{14,6},{16,24},{18,... | collective-permute-start | bytes 393224 | tf_op jit(solution)/shard_map/ppermute | solution.py:21
  38.2 7.3 %collective-permute-start.14 = (bf16[256,256]{1,0:T(8,128)(2,1)S(1)}, bf16[256,256]{1,0:T(8,128)(2,1)S(1)}, u32[]{:S(2)}, u32[]{:S(2)}) collective-permute-start(bf16[256,256]{1,0:T(8,128)(2,1)S(1)} %get-tuple-element.88), channel_id=1, source_target_pairs={{0,6},{2,4},{4,2},{6,0},{8,14},{10,12},{12,10},{14,8},{16,22},{18,... | collective-permute-start | bytes 393224 | tf_op jit(solution)/shard_map/ppermute | solution.py:21
  41.9 8.8 %collective-permute-start.16 = (bf16[256,256]{1,0:T(8,128)(2,1)S(1)}, bf16[256,256]{1,0:T(8,128)(2,1)S(1)}, u32[]{:S(2)}, u32[]{:S(2)}) collective-permute-start(bf16[256,256]{1,0:T(8,128)(2,1)S(1)} %get-tuple-element.95), channel_id=1, source_target_pairs={{0,2},{2,0},{4,6},{6,4},{8,10},{10,8},{12,14},{14,12},{16,18},{18,... | collective-permute-start | bytes 393224 | tf_op jit(solution)/shard_map/ppermute | solution.py:21
  43.4 7.3 %collective-permute-start.17 = (bf16[256,256]{1,0:T(8,128)(2,1)S(1)}, bf16[256,256]{1,0:T(8,128)(2,1)S(1)}, u32[]{:S(2)}, u32[]{:S(2)}) collective-permute-start(bf16[256,256]{1,0:T(8,128)(2,1)S(1)} %get-tuple-element.96), channel_id=1, source_target_pairs={{0,4},{2,6},{4,0},{6,2},{8,12},{10,14},{12,8},{14,10},{16,20},{18,... | collective-permute-start | bytes 393224 | tf_op jit(solution)/shard_map/ppermute | solution.py:21
  45.4 5.9 %collective-permute-start.18 = (bf16[256,256]{1,0:T(8,128)(2,1)S(1)}, bf16[256,256]{1,0:T(8,128)(2,1)S(1)}, u32[]{:S(2)}, u32[]{:S(2)}) collective-permute-start(bf16[256,256]{1,0:T(8,128)(2,1)S(1)} %get-tuple-element.105), channel_id=1, source_target_pairs={{0,6},{2,4},{4,2},{6,0},{8,14},{10,12},{12,10},{14,8},{16,22},{18,... | collective-permute-start | bytes 393224 | tf_op jit(solution)/shard_map/ppermute | solution.py:21
  48.2 3.1 %collective-permute-start.19 = (bf16[128,512]{1,0:T(8,128)(2,1)S(1)}, bf16[128,512]{1,0:T(8,128)(2,1)S(1)}, u32[]{:S(2)}, u32[]{:S(2)}) collective-permute-start(bf16[128,512]{1,0:T(8,128)(2,1)S(1)} %get-tuple-element.106), channel_id=1, source_target_pairs={{0,1},{1,0},{2,3},{3,2},{4,5},{5,4},{6,7},{7,6},{8,9},{9,8},{10,11... | collective-permute-start | bytes 393224 | tf_op jit(solution)/shard_map/ppermute | solution.py:25
  48.3 3.1 %collective-permute-start.20 = (bf16[128,512]{1,0:T(8,128)(2,1)S(1)}, bf16[128,512]{1,0:T(8,128)(2,1)S(1)}, u32[]{:S(2)}, u32[]{:S(2)}) collective-permute-start(bf16[128,512]{1,0:T(8,128)(2,1)S(1)} %get-tuple-element.107), channel_id=1, source_target_pairs={{0,1},{1,0},{2,3},{3,2},{4,5},{5,4},{6,7},{7,6},{8,9},{9,8},{10,11... | collective-permute-start | bytes 393224 | tf_op jit(solution)/shard_map/ppermute | solution.py:25

commit v5 on v4

--- a/solution.py
+++ b/solution.py
@@ -55,7 +55,7 @@
         kernel,
         out_shape=out_shape,
         in_specs=specs,
-        out_specs=outs if isinstance(outs, list) else jax.tree.map(lambda _: outs, out_shape),
+        out_specs=jax.tree.map(lambda _: outs, out_shape),
         scratch_shapes=list(scratch),
         compiler_params=pltpu.CompilerParams(vmem_limit_bytes=vmem << 20),
         cost_estimate=pl.CostEstimate(flops=flops, bytes_accessed=moved, transcendentals=0),
@@ -80,60 +80,59 @@
     return max(16, BLOCK >> level)
 
 
-def split_kernel(slots, levels, at_ref, q_hbm, k_hbm, v_hbm, *refs):
-    piece_refs, refs = refs[: len(levels)], refs[len(levels) :]
-    chunk_refs, (q_ref, k_ref, v_ref, sems) = refs[:slots], refs[slots:]
+def token_kernel(slots, at_ref, k_hbm, v_hbm, *refs):
+    chunk_refs, (k_ref, v_ref, sems) = refs[:slots], refs[slots:]
     low = at_ref[0]
     tok, width = BLOCK, chunk_refs[0].shape[1]
-    held = (q_ref, k_ref, v_ref)
+    held = (k_ref, v_ref)
     copies = [
         pltpu.make_async_copy(source, held[place], sems.at[place])
-        for place, source in ((1, k_hbm), (2, v_hbm), (0, q_hbm))
+        for place, source in enumerate((k_hbm, v_hbm))
     ]
     for copy in copies:
         copy.start()
-    copies[0].wait()
-    copies[1].wait()
-    for level, piece in zip(levels, piece_refs):
-        rows = piece_rows(level)
-        pool = level_pool(rows, level)
-        piece[0:rows, :] = (mm(pool, k_ref[...]) * (1.0 / (1 << level))).astype(BF16)
-        piece[rows:, :] = mm(pool, v_ref[...]).astype(BF16)
-    copies[2].wait()
-    for mask in range(slots):
-        cols = col_block(low, mask, width)
-        for place, source in enumerate(held):
-            chunk_refs[mask][place * tok : place * tok + tok, :] = source[:, cols]
-
-
-def grad_kernel(at_ref, mine_ref, w_ref, other_ref, out_ref):
-    core = at_ref[1]
-    half = mine_ref.shape[1]
+    for place, source in enumerate(held):
+        copies[place].wait()
+        for mask in range(slots):
+            rows = slice(place * tok, place * tok + tok)
+            chunk_refs[mask][rows, :] = source[:, col_block(low, mask, width)]
+
+
+def query_kernel(slots, at_ref, q_ref, mine_ref, w_ref, other_ref, *refs):
+    chunk_refs, grad_ref = refs[:slots], refs[slots]
+    low, core = at_ref[0], at_ref[1]
+    tok, half = mine_ref.shape
+    width = chunk_refs[0].shape[1]
     first = pl.multiple_of(core * half, half)
     second = pl.multiple_of((1 - core) * half, half)
     total = mm(mine_ref[...], w_ref[pl.ds(first, half), :])
     total += mm(other_ref[...], w_ref[pl.ds(second, half), :])
-    out_ref[...] = total.astype(BF16)
-
-
-def second_kernel(slots, entries, at_ref, grad_ref, *refs):
-    far_refs, out_refs = refs[: len(entries)], refs[len(entries) :]
-    low = at_ref[0]
-    tok, width = BLOCK, out_refs[0].shape[1]
+    grad_ref[...] = total.astype(BF16)
     for mask in range(slots):
         cols = col_block(low, mask, width)
-        out_refs[mask][0:tok, :] = grad_ref[:, cols]
-        for (place, part, rows), far_ref in zip(entries, far_refs):
-            for kind in range(2):
-                at = tok + 64 * place + 32 * kind + part * rows
-                source = far_ref[kind * rows : kind * rows + rows, cols]
-                out_refs[mask][at : at + rows, :] = source
+        chunk_refs[mask][0:tok, :] = q_ref[:, cols]
+        chunk_refs[mask][tok:, :] = grad_ref[:, cols]
+
+
+def coarse_kernel(slots, levels, *refs):
+    in_refs, piece_refs = by_mask(refs[:slots]), refs[slots:]
+    tok = BLOCK
+    for level, piece in zip(levels, piece_refs):
+        rows = piece_rows(level)
+        pool = level_pool(rows, level)
+        for slab in range(slots):
+            at = slab * rows
+            keys = mm(pool, in_refs[slab][0:tok, :]) * (1.0 / (1 << level))
+            piece[at : at + rows, :] = keys.astype(BF16)
+            at = (slots + slab) * rows
+            piece[at : at + rows, :] = mm(pool, in_refs[slab][tok:, :]).astype(BF16)
 
 
 def attend_kernel(slots, far_levels, entries, *refs):
-    first_refs, second_refs = by_mask(refs[:slots]), by_mask(refs[slots : 2 * slots])
+    key_refs, query_refs = by_mask(refs[:slots]), by_mask(refs[slots : 2 * slots])
     refs = refs[2 * slots :]
-    far_refs, refs = refs[: len(entries)], refs[len(entries) :]
+    count = len(entries)
+    got_refs, far_refs, refs = refs[:count], refs[count : 2 * count], refs[2 * count :]
     kl_ref, vl_ref, q_all, g_all, prob_ref, grad_ref, sum_ref, fk_ref, fv_ref = refs
     tok = BLOCK
     pairs = slots // 2
@@ -142,16 +141,17 @@
     near, far = 2 * tok, 3 * tok
     for slab in range(slots):
         pair, row = slab // 2, (slab % 2) * tok
-        q_all[pair, row : row + tok, :] = first_refs[slab][0:tok, :]
-        kl_ref[pair, row : row + tok, :] = first_refs[slab][tok : 2 * tok, :]
-        vl_ref[pair, row : row + tok, :] = first_refs[slab][2 * tok :, :]
-        g_all[pair, row : row + tok, :] = second_refs[slab][0:tok, :]
-        for place in range(far_levels):
-            at = tok + 64 * place
-            spot = far + place * BLOCK + 32 * slab
-            for each in range(pairs):
-                kl_ref[each, spot : spot + 32, :] = second_refs[slab][at : at + 32, :]
-                vl_ref[each, spot : spot + 32, :] = second_refs[slab][at + 32 : at + 64, :]
+        q_all[pair, row : row + tok, :] = query_refs[slab][0:tok, :]
+        g_all[pair, row : row + tok, :] = query_refs[slab][tok:, :]
+        kl_ref[pair, row : row + tok, :] = key_refs[slab][0:tok, :]
+        vl_ref[pair, row : row + tok, :] = key_refs[slab][tok:, :]
+    for (place, part, rows), got_ref in zip(entries, got_refs):
+        for slab in range(slots):
+            spot = far + place * BLOCK + 32 * slab + part * rows
+            for kind, list_ref in enumerate((kl_ref, vl_ref)):
+                at = (kind * slots + slab) * rows
+                for pair in range(pairs):
+                    list_ref[pair, spot : spot + rows, :] = got_ref[at : at + rows, :]
     pool = pool_matrix(BLOCK, 1)
     for pair in range(pairs):
         kl_ref[pair ^ 1, near:far, :] = (mm(pool, kl_ref[pair, 0:near, :]) * 0.5).astype(BF16)
@@ -262,40 +262,32 @@
         send_ref[...] = mm_cols(att_ref[...], w_ref[pl.ds(other, part), :]).astype(BF16)
 
 
-def keep_kernel(slots, at_ref, w_ref, att_ref, *refs):
-    in_refs, (keep_ref, dq_hbm, dq_ref, sem) = by_mask(refs[:slots]), refs[slots:]
-    low, core = at_ref[0], at_ref[1]
-    tok, half = att_ref.shape
-    width = in_refs[0].shape[1]
-    for mask in range(slots):
-        dq_ref[:, col_block(low, mask, width)] = in_refs[mask][tok:, :]
-    copy = pltpu.make_async_copy(dq_ref, dq_hbm, sem)
-    copy.start()
-    first = pl.multiple_of(core * half, half)
+def keep_kernel(at_ref, w_ref, att_ref, keep_ref):
+    half = att_ref.shape[1]
+    first = pl.multiple_of(at_ref[1] * half, half)
     keep_ref[...] = mm_cols(att_ref[...], w_ref[pl.ds(first, half), :])
-    copy.wait()
 
 
 def finish_kernel(slots, at_ref, keep_ref, *refs):
-    in_refs, refs = by_mask(refs[:slots]), refs[slots:]
-    got_refs, refs = refs[:-7], refs[-7:]
-    hbm_refs, held_refs, sems = refs[:3], refs[3:6], refs[6]
+    home_refs, last_refs = by_mask(refs[:slots]), by_mask(refs[slots : 2 * slots])
+    got_refs, refs = refs[2 * slots : -9], refs[-9:]
+    hbm_refs, held_refs, sems = refs[:4], refs[4:8], refs[8]
     low = at_ref[0]
-    tok, width = BLOCK, in_refs[0].shape[1]
+    tok, width = BLOCK, home_refs[0].shape[1]
     copies = [
         pltpu.make_async_copy(held_refs[place], hbm_refs[place], sems.at[place])
-        for place in range(3)
+        for place in range(4)
     ]
-    for place in range(2):
+    for place, (in_refs, start) in enumerate(((home_refs, tok), (last_refs, 0), (last_refs, tok))):
         for mask in range(slots):
-            rows = slice(place * tok, place * tok + tok)
-            held_refs[place][:, col_block(low, mask, width)] = in_refs[mask][rows, :]
+            cols = col_block(low, mask, width)
+            held_refs[place][:, cols] = in_refs[mask][start : start + tok, :]
         copies[place].start()
     part = got_refs[0].shape[1]
     for place, got_ref in enumerate(got_refs):
         cols = slice(place * part, place * part + part)
-        held_refs[2][:, cols] = (keep_ref[:, cols] + got_ref[...].astype(F32)).astype(BF16)
-    copies[2].start()
+        held_refs[3][:, cols] = (keep_ref[:, cols] + got_ref[...].astype(F32)).astype(BF16)
+    copies[3].start()
     for copy in copies:
         copy.wait()
 
@@ -317,27 +309,27 @@
 
 
 def gather_far(pieces, levels, slots):
-    columns = pieces[0].shape[1]
+    width = pieces[0].shape[1]
     if straight(levels, slots):
         entries, masks = far_entries(levels, slots)
         return [swap_seq(pieces[entry[0]], mask) for entry, mask in zip(entries, masks)]
     held = {}
     for place, level in enumerate(levels):
-        block = pieces[place].reshape(2, piece_rows(level), columns)
+        block = pieces[place].reshape(2 * slots, piece_rows(level), width)
         held[level] = block[:, None, : BLOCK >> level]
     found = []
     for step in levels:
-        sent = [held[level].reshape(-1, columns) for level in levels if level >= step]
+        sent = [held[level].reshape(-1, width) for level in levels if level >= step]
         got = swap_seq(jnp.concatenate(sent, axis=0), 1 << step)
         first = 0
         for level in levels:
             if level < step:
                 continue
-            count = held[level].size // columns
+            count = held[level].size // width
             part = got[first : first + count].reshape(held[level].shape)
             first += count
             if level == step:
-                found.append(part.reshape(64, columns))
+                found.append(part.reshape(-1, width))
             else:
                 held[level] = jnp.concatenate([held[level], part], axis=1)
     return found
@@ -387,7 +379,6 @@
     local_levels = slots.bit_length() - 1
     level_count = lax.axis_size("seq").bit_length() - 1
     far = list(range(local_levels, level_count))
-    far_rows = 64 * len(far)
     list_rows = 3 * tok + BLOCK * len(far)
     entries, _ = far_entries(far, slots)
     place = jnp.stack([lax.axis_index("seq") & (slots - 1), lax.axis_index("head")])
@@ -403,41 +394,36 @@
         moved = [chunks[0]] + [swap_seq(chunks[mask], mask) for mask in range(1, slots)]
         return [moved[mask] for mask in ORDER]
 
-    made = call(
-        lambda *refs: split_kernel(slots, far, *refs),
-        [shape((2 * piece_rows(level), columns)) for level in far] + over(3 * tok),
-        (place, queries, key_tokens, value_tokens),
-        scratch=[pltpu.VMEM((tok, columns), BF16)] * 3 + [pltpu.SemaphoreType.DMA((3,))],
+    chunks = call(
+        lambda *refs: token_kernel(slots, *refs),
+        over(2 * tok),
+        (place, key_tokens, value_tokens),
+        scratch=[pltpu.VMEM((tok, columns), BF16)] * 2 + [pltpu.SemaphoreType.DMA((2,))],
         flops=6 * 10**9,
-        specs=[SMEM] + [HBM] * 3,
+        specs=[SMEM] + [HBM] * 2,
         vmem=8,
     )
-    pieces, chunks = made[: len(far)], list(made[len(far) :])
-    pieces, output_grad = lax.optimization_barrier((pieces, output_grad))
+    keys = exchange(chunks)
+    later, output_grad, *_ = lax.optimization_barrier((place, output_grad, *chunks))
     other_grad = swap_head(output_grad)
+    chunks = call(
+        lambda *refs: query_kernel(slots, *refs),
+        over(2 * tok),
+        [later, queries, output_grad, out_weight, other_grad],
+        scratch=[pltpu.VMEM((tok, columns), BF16)],
+        flops=6 * 10**9,
+        specs=[SMEM] + [VMEM] * 4,
+        vmem=16,
+    )
+    asked = exchange(chunks)
+    sources, *_ = lax.optimization_barrier((keys, asked[1]))
+    pieces = call(
+        lambda *refs: coarse_kernel(slots, far, *refs),
+        [shape((2 * slots * piece_rows(level), width)) for level in far],
+        sources,
+        vmem=8,
+    )
     far_got = gather_far(pieces, far, slots)
-    grads = call(
-        grad_kernel,
-        shape((tok, columns)),
-        [place, output_grad, out_weight, other_grad],
-        flops=4 * tok * columns * columns,
-        specs=[SMEM] + [VMEM] * 3,
-        vmem=16,
-    )
-    first = {0: chunks[0]}
-    for mask in ORDER[1:]:
-        if mask == ORDER[-1]:
-            chunks[mask], grads, first[1] = lax.optimization_barrier((chunks[mask], grads, first[1]))
-        first[mask] = swap_seq(chunks[mask], mask)
-    first = [first[mask] for mask in ORDER]
-    chunks = call(
-        lambda *refs: second_kernel(slots, entries, *refs),
-        over(tok + far_rows),
-        [place, grads] + far_got,
-        specs=[SMEM] + [VMEM] * (1 + len(far_got)),
-        vmem=8,
-    )
-    second = exchange(chunks)
     pairs = slots // 2
     made = call(
         lambda *refs: attend_kernel(slots, len(far), entries, *refs),
@@ -446,7 +432,7 @@
         + [shape((pairs, 2 * tok, width))] * 2
         + [shape((slots, 2 * tok, list_rows))] * 2
         + [shape((slots, 2 * tok, HDIM), F32)],
-        first + second,
+        keys + asked + far_got,
         scratch=[pltpu.VMEM((BLOCK * len(far), width), F32)] * 2,
         flops=6 * heads * tok * list_rows * HDIM,
     )
@@ -469,7 +455,7 @@
     )
     made = list(made)
     late = ORDER[-1]
-    made[late], key_sum, *shares[1:] = lax.optimization_barrier((made[late], key_sum, *shares[1:]))
+    made[late], key_sum, *shares = lax.optimization_barrier((made[late], key_sum, *shares))
     home = exchange(made)
     chunks = call(
         lambda *refs: merge_kernel(slots, share_levels, *refs),
@@ -479,7 +465,6 @@
     )
     home, _ = lax.optimization_barrier((home, chunks))
     chunks = list(chunks)
-    chunks[late], home[-1] = lax.optimization_barrier((chunks[late], home[-1]))
     last = exchange(chunks)
     wide = shape((tok, columns))
     attended, *send = call(
@@ -491,22 +476,20 @@
         vmem=16,
     )
     got = [swap_head(part) for part in send]
-    keep, query_grad = call(
-        lambda *refs: keep_kernel(slots, *refs),
-        [shape((tok, columns), F32), wide],
-        [place, out_weight, attended] + home,
-        scratch=[pltpu.VMEM((tok, columns), BF16), pltpu.SemaphoreType.DMA(())],
+    keep = call(
+        keep_kernel,
+        shape((tok, columns), F32),
+        [place, out_weight, attended],
         flops=4 * 10**9,
-        specs=[SMEM] + [VMEM] * (2 + slots),
-        outs=[VMEM, HBM],
+        specs=[SMEM, VMEM, VMEM],
         vmem=16,
     )
-    key_grad, value_grad, output = call(
+    query_grad, key_grad, value_grad, output = call(
         lambda *refs: finish_kernel(slots, *refs),
-        [wide] * 3,
-        [place, keep] + last + got,
-        scratch=[pltpu.VMEM((tok, columns), BF16)] * 3 + [pltpu.SemaphoreType.DMA((3,))],
-        specs=[SMEM] + [VMEM] * (1 + slots + len(got)),
+        [wide] * 4,
+        [place, keep] + home + last + got,
+        scratch=[pltpu.VMEM((tok, columns), BF16)] * 4 + [pltpu.SemaphoreType.DMA((4,))],
+        specs=[SMEM] + [VMEM] * (1 + 2 * slots + len(got)),
         outs=HBM,
         vmem=8,
     )

time: 53 us -> 50.7 us (0.957)
  waiting for transfers between devices: 12.7 us -> 10.3 us
  Pallas kernels: 14.2 us -> 13 us
  starting transfers between devices: 25.1 us -> 26.3 us
    ppermute x18, waiting for transfers between devices: 12.7 us -> 10.3 us  [swap_seq(): lax.ppermute(array, 'seq', [(i, i ^ mask) for i in range(lax.axis_size('s...]
    ppermute x18, starting transfers between devices: 24 us -> 25.3 us  [swap_seq(): lax.ppermute(array, 'seq', [(i, i ^ mask) for i in range(lax.axis_size('s...]
    pallas_call x10, Pallas kernels: 14.2 us -> 13 us  [call(): pl.pallas_call(kernel, out_shape=out_shape, in_specs=specs, out_specs=jax...]
  transfers between devices with their start and end apart: 21 -> 21, of which waited for: 9 -> 7; matrix products, arithmetic and copies ran while one was open for 0% -> 0% of each run, Pallas kernels for 14% -> 13%
where the time goes in v5:
time: 50.7 us; the launch traced here: 50.6 us
  starting transfers between devices  26.3 us (52%)
  Pallas kernels  13 us (26%)
  waiting for transfers between devices  10.3 us (20%)
  between operations  0.77 us (2%)
    ppermute x18, starting transfers between devices, swap_seq(): lax.ppermute(array, 'seq', [(i, i ^ mask) for i in range(lax.axis_size('s...  25.3 us
    pallas_call x10, Pallas kernels, call(): pl.pallas_call(kernel, out_shape=out_shape, in_specs=specs, out_specs=jax...  13 us
    ppermute x18, waiting for transfers between devices, swap_seq(): lax.ppermute(array, 'seq', [(i, i ^ mask) for i in range(lax.axis_size('s...  10.3 us
    ppermute x3, starting transfers between devices, swap_head(): return lax.ppermute(array, 'head', [(0, 1), (1, 0)])  1.09 us
  transfers between devices with their start and end apart: 21, of which 7 were waited for; matrix products, arithmetic and copies ran while one was open for 0% of the time, Pallas kernels for 13%

profile of v5, /device:TPU:0, one launch (start us, length us, event | category | flops | bytes accessed | tf_op | source)
XLA Modules:
  0.0 50.6 jit_solution(10133655500491760965)
XLA Ops:
  0.6 0.1 pad_add_fusion.refs_0_.at_ref
  0.7 0.0 copy-start.2
  0.7 0.0 copy-start
  0.7 0.0 copy-start.1
  0.7 1.9 %shard_map.84 = (bf16[256,256]{1,0:T(8,128)(2,1)S(1)}, bf16[256,256]{1,0:T(8,128)(2,1)S(1)}, bf16[256,256]{1,0:T(8,128)(2,1)S(1)}, bf16[256,256]{1,0:T(8,128)(2,1)S(1)}) custom-call(s32[2]{0:T(128)S(1)} %pad_add_fusion.refs_0_.at_ref, bf16[128,1024]{1,0:T(8,128)(2,1)} %refs_1_.3, bf16[128,1024]{1,0:T(8,128)(2,1)} %refs_2_.1), custom_call_target="tpu_custom_call" | custom-call | flops 6000000000 | bytes 524296 | tf_op jit(solution)/shard_map/pallas_call | solution.py:54
  2.6 0.0 copy-done.2
  2.6 0.5 %collective-permute-start.3 = (bf16[128,1024]{1,0:T(8,128)(2,1)S(1)}, bf16[128,1024]{1,0:T(8,128)(2,1)S(1)}, u32[]{:S(2)}, u32[]{:S(2)}) collective-permute-start(bf16[128,1024]{1,0:T(8,128)(2,1)S(1)} %copy-done.2), channel_id=1, source_target_pairs={{0,1},{1,0},{2,3},{3,2},{4,5},{5,4},{6,7},{7,6},{8,9},{9,8},{10,11... | collective-permute-start | bytes 786440 | tf_op jit(solution)/shard_map/ppermute | solution.py:25
  3.1 2.6 %collective-permute-start = (bf16[256,256]{1,0:T(8,128)(2,1)S(1)}, bf16[256,256]{1,0:T(8,128)(2,1)S(1)}, u32[]{:S(2)}, u32[]{:S(2)}) collective-permute-start(bf16[256,256]{1,0:T(8,128)(2,1)S(1)} %get-tuple-element.57), channel_id=1, source_target_pairs={{0,2},{2,0},{4,6},{6,4},{8,10},{10,8},{12,14},{14,12},{16,18},{18,... | collective-permute-start | bytes 393224 | tf_op jit(solution)/shard_map/ppermute | solution.py:21
  5.7 1.5 %collective-permute-start.1 = (bf16[256,256]{1,0:T(8,128)(2,1)S(1)}, bf16[256,256]{1,0:T(8,128)(2,1)S(1)}, u32[]{:S(2)}, u32[]{:S(2)}) collective-permute-start(bf16[256,256]{1,0:T(8,128)(2,1)S(1)} %get-tuple-element.58), channel_id=1, source_target_pairs={{0,4},{2,6},{4,0},{6,2},{8,12},{10,14},{12,8},{14,10},{16,20},{18,... | collective-permute-start | bytes 393224 | tf_op jit(solution)/shard_map/ppermute | solution.py:21
  7.2 0.0 collective-permute-start.2
  7.2 0.0 collective-permute-done.3.refs_4_
  7.2 0.0 copy-done
  7.3 0.0 copy-done.1
  7.3 1.3 %shard_map.85 = (bf16[256,256]{1,0:T(8,128)(2,1)S(1)}, bf16[256,256]{1,0:T(8,128)(2,1)S(1)}, bf16[256,256]{1,0:T(8,128)(2,1)S(1)}, bf16[256,256]{1,0:T(8,128)(2,1)S(1)}) custom-call(s32[2]{0:T(128)S(1)} %pad_add_fusion.refs_0_.at_ref, bf16[128,1024]{1,0:T(8,128)(2,1)S(1)} %copy-done.1, bf16[128,1024]{1,0:T(8,128)(2,1)S(1)} %copy-done.2, ...), custom_call_target="tpu_custom_call" | custom-call | flops 6000000000 | bytes 4980744 | tf_op jit(solution)/shard_map/pallas_call | solution.py:54
  8.6 2.0 %collective-permute-start.4 = (bf16[256,256]{1,0:T(8,128)(2,1)S(1)}, bf16[256,256]{1,0:T(8,128)(2,1)S(1)}, u32[]{:S(2)}, u32[]{:S(2)}) collective-permute-start(bf16[256,256]{1,0:T(8,128)(2,1)S(1)} %get-tuple-element.63), channel_id=1, source_target_pairs={{0,2},{2,0},{4,6},{6,4},{8,10},{10,8},{12,14},{14,12},{16,18},{18,... | collective-permute-start | bytes 393224 | tf_op jit(solution)/shard_map/ppermute | solution.py:21
  10.6 1.5 %collective-permute-start.5 = (bf16[256,256]{1,0:T(8,128)(2,1)S(1)}, bf16[256,256]{1,0:T(8,128)(2,1)S(1)}, u32[]{:S(2)}, u32[]{:S(2)}) collective-permute-start(bf16[256,256]{1,0:T(8,128)(2,1)S(1)} %get-tuple-element.64), channel_id=1, source_target_pairs={{0,4},{2,6},{4,0},{6,2},{8,12},{10,14},{12,8},{14,10},{16,20},{18,... | collective-permute-start | bytes 393224 | tf_op jit(solution)/shard_map/ppermute | solution.py:21
  12.1 0.0 collective-permute-done.refs_1_
  12.1 0.8 %collective-permute-start.6 = (bf16[256,256]{1,0:T(8,128)(2,1)S(1)}, bf16[256,256]{1,0:T(8,128)(2,1)S(1)}, u32[]{:S(2)}, u32[]{:S(2)}) collective-permute-start(bf16[256,256]{1,0:T(8,128)(2,1)S(1)} %get-tuple-element.65), channel_id=1, source_target_pairs={{0,6},{2,4},{4,2},{6,0},{8,14},{10,12},{12,10},{14,8},{16,22},{18,... | collective-permute-start | bytes 393224 | tf_op jit(solution)/shard_map/ppermute | solution.py:21
  13.0 0.8 %collective-permute-done.1.refs_2_ = bf16[256,256]{1,0:T(8,128)(2,1)S(1)} collective-permute-done((bf16[256,256]{1,0:T(8,128)(2,1)S(1)}, bf16[256,256]{1,0:T(8,128)(2,1)S(1)}, u32[]{:S(2)}, u32[]{:S(2)}) %collective-permute-start.1) | collective-permute-done | bytes 131104 | tf_op jit(solution)/shard_map/ppermute | solution.py:21
  13.8 0.8 %collective-permute-done.2.refs_3_ = bf16[256,256]{1,0:T(8,128)(2,1)S(1)} collective-permute-done((bf16[256,256]{1,0:T(8,128)(2,1)S(1)}, bf16[256,256]{1,0:T(8,128)(2,1)S(1)}, u32[]{:S(2)}, u32[]{:S(2)}) %collective-permute-start.2) | collective-permute-done | bytes 131104 | tf_op jit(solution)/shard_map/ppermute | solution.py:21
  14.6 1.9 %collective-permute-done.4.refs_5_ = bf16[256,256]{1,0:T(8,128)(2,1)S(1)} collective-permute-done((bf16[256,256]{1,0:T(8,128)(2,1)S(1)}, bf16[256,256]{1,0:T(8,128)(2,1)S(1)}, u32[]{:S(2)}, u32[]{:S(2)}) %collective-permute-start.4) | collective-permute-done | bytes 131104 | tf_op jit(solution)/shard_map/ppermute | solution.py:21
  16.4 0.3 shard_map.86
  16.7 1.6 %collective-permute-start.7 = (bf16[256,256]{1,0:T(8,128)(2,1)S(1)}, bf16[256,256]{1,0:T(8,128)(2,1)S(1)}, u32[]{:S(2)}, u32[]{:S(2)}) collective-permute-start(bf16[256,256]{1,0:T(8,128)(2,1)S(1)} %get-tuple-element.70), channel_id=1, source_target_pairs={{0,8},{2,10},{4,12},{6,14},{8,0},{10,2},{12,4},{14,6},{16,24},{18,... | collective-permute-start | bytes 393224 | tf_op jit(solution)/shard_map/ppermute | solution.py:21
  18.3 2.5 %collective-permute-start.9 = (bf16[128,256]{1,0:T(8,128)(2,1)S(1)}, bf16[128,256]{1,0:T(8,128)(2,1)S(1)}, u32[]{:S(2)}, u32[]{:S(2)}) collective-permute-start(bf16[128,256]{1,0:T(8,128)(2,1)S(1)} %get-tuple-element.71), channel_id=1, source_target_pairs={{0,24},{2,26},{4,28},{6,30},{8,16},{10,18},{12,20},{14,22},{16,8},... | collective-permute-start | bytes 196616 | tf_op jit(solution)/shard_map/ppermute | solution.py:21
  20.8 0.1 collective-permute-start.8
  20.9 0.0 collective-permute-done.5.refs_6_
  20.9 0.0 collective-permute-done.6.refs_7_
  20.9 4.3 %collective-permute-done.9.refs_10_ = bf16[128,256]{1,0:T(8,128)(2,1)S(1)} collective-permute-done((bf16[128,256]{1,0:T(8,128)(2,1)S(1)}, bf16[128,256]{1,0:T(8,128)(2,1)S(1)}, u32[]{:S(2)}, u32[]{:S(2)}) %collective-permute-start.9) | collective-permute-done | bytes 65568 | tf_op jit(solution)/shard_map/ppermute | solution.py:21
  25.2 1.4 %collective-permute-done.8.refs_9_ = bf16[128,256]{1,0:T(8,128)(2,1)S(1)} collective-permute-done((bf16[128,256]{1,0:T(8,128)(2,1)S(1)}, bf16[128,256]{1,0:T(8,128)(2,1)S(1)}, u32[]{:S(2)}, u32[]{:S(2)}) %collective-permute-start.8) | collective-permute-done | bytes 65568 | tf_op jit(solution)/shard_map/ppermute | solution.py:21
  26.6 0.0 collective-permute-done.7.refs_8_
  26.6 2.9 %shard_map.87 = (bf16[256,256]{1,0:T(8,128)(2,1)S(1)}, bf16[128,256]{1,0:T(8,128)(2,1)S(1)}, bf16[128,256]{1,0:T(8,128)(2,1)S(1)}, bf16[2,640,256]{2,1,0:T(8,128...) custom-call(bf16[256,256]{1,0:T(8,128)(2,1)S(1)} %get-tuple-element., ...), custom_call_target="tpu_custom_call" | custom-call | flops 503316480 | bytes 1310720 | tf_op jit(solution)/shard_map/pallas_call | solution.py:54
  29.6 0.5 %collective-permute-start.13 = (bf16[128,256]{1,0:T(8,128)(2,1)S(1)}, bf16[128,256]{1,0:T(8,128)(2,1)S(1)}, u32[]{:S(2)}, u32[]{:S(2)}) collective-permute-start(bf16[128,256]{1,0:T(8,128)(2,1)S(1)} %get-tuple-element.85), channel_id=1, source_target_pairs={{0,16},{2,18},{4,20},{6,22},{8,24},{10,26},{12,28},{14,30},{16,0},... | collective-permute-start | bytes 196616 | tf_op jit(solution)/shard_map/ppermute | solution.py:21
  30.1 1.9 %collective-permute-start.14 = (bf16[128,256]{1,0:T(8,128)(2,1)S(1)}, bf16[128,256]{1,0:T(8,128)(2,1)S(1)}, u32[]{:S(2)}, u32[]{:S(2)}) collective-permute-start(bf16[128,256]{1,0:T(8,128)(2,1)S(1)} %get-tuple-element.86), channel_id=1, source_target_pairs={{0,24},{2,26},{4,28},{6,30},{8,16},{10,18},{12,20},{14,22},{16,8},... | collective-permute-start | bytes 196616 | tf_op jit(solution)/shard_map/ppermute | solution.py:21
  32.0 1.1 %collective-permute-start.12 = (bf16[256,256]{1,0:T(8,128)(2,1)S(1)}, bf16[256,256]{1,0:T(8,128)(2,1)S(1)}, u32[]{:S(2)}, u32[]{:S(2)}) collective-permute-start(bf16[256,256]{1,0:T(8,128)(2,1)S(1)} %get-tuple-element.84), channel_id=1, source_target_pairs={{0,8},{2,10},{4,12},{6,14},{8,0},{10,2},{12,4},{14,6},{16,24},{18,... | collective-permute-start | bytes 393224 | tf_op jit(solution)/shard_map/ppermute | solution.py:21
  33.1 0.8 %shard_map.88 = (bf16[256,256]{1,0:T(8,128)(2,1)S(1)}, bf16[256,256]{1,0:T(8,128)(2,1)S(1)}, bf16[256,256]{1,0:T(8,128)(2,1)S(1)}, bf16[256,256]{1,0:T(8,128)(2,1)S(1)}) custom-call(bf16[2,640,256]{2,1,0:T(8,128)(2,1)S(1)} %get-tuple-element.72.refs_0_, bf16[2,640,256]{2,1,0:T(8,128)(2,1)S(1)} %get-tuple-element.73.refs_1_, ...), custom_call_target="tpu_custom_call" | custom-call | flops 6000000000 | bytes 4456448 | tf_op jit(solution)/shard_map/pallas_call | solution.py:54
  34.0 1.6 %collective-permute-start.10 = (bf16[256,256]{1,0:T(8,128)(2,1)S(1)}, bf16[256,256]{1,0:T(8,128)(2,1)S(1)}, u32[]{:S(2)}, u32[]{:S(2)}) collective-permute-start(bf16[256,256]{1,0:T(8,128)(2,1)S(1)} %get-tuple-element.78), channel_id=1, source_target_pairs={{0,2},{2,0},{4,6},{6,4},{8,10},{10,8},{12,14},{14,12},{16,18},{18,... | collective-permute-start | bytes 393224 | tf_op jit(solution)/shard_map/ppermute | solution.py:21
  35.6 1.5 %collective-permute-start.11 = (bf16[256,256]{1,0:T(8,128)(2,1)S(1)}, bf16[256,256]{1,0:T(8,128)(2,1)S(1)}, u32[]{:S(2)}, u32[]{:S(2)}) collective-permute-start(bf16[256,256]{1,0:T(8,128)(2,1)S(1)} %get-tuple-element.79), channel_id=1, source_target_pairs={{0,4},{2,6},{4,0},{6,2},{8,12},{10,14},{12,8},{14,10},{16,20},{18,... | collective-permute-start | bytes 393224 | tf_op jit(solution)/shard_map/ppermute | solution.py:21
  37.1 0.9 %shard_map.89 = (f32[512,256]{1,0:T(8,128)S(1)}, f32[512,256]{1,0:T(8,128)S(1)}) custom-call(bf16[2,256,256]{2,1,0:T(8,128)(2,1)S(1)} %get-tuple-element.81.refs_0_, bf16[2,256,256]{2,1,0:T(8,128)(2,1)S(1)} %get-tuple-element.82.refs_1_, bf16[4,256,640]{2,1,0:T(8,128)(2,1)S(1)} %get-tuple-element.74.refs_2_, bf16[4,256,640]{2,1,0:T(8,128)(2,1)S(1)} %get-tuple-element.75.refs_3_), custom_call_target="tpu_custom_call" | custom-call | flops 335544320 | bytes 3145728 | tf_op jit(solution)/shard_map/pallas_call | solution.py:54
  37.9 0.0 collective-permute-done.13.refs_3_
  38.0 0.0 collective-permute-done.14.refs_4_
  38.0 0.0 collective-permute-done.12.refs_2_
  38.0 2.4 %collective-permute-start.15 = (bf16[256,256]{1,0:T(8,128)(2,1)S(1)}, bf16[256,256]{1,0:T(8,128)(2,1)S(1)}, u32[]{:S(2)}, u32[]{:S(2)}) collective-permute-start(bf16[256,256]{1,0:T(8,128)(2,1)S(1)} %get-tuple-element.87), channel_id=1, source_target_pairs={{0,6},{2,4},{4,2},{6,0},{8,14},{10,12},{12,10},{14,8},{16,22},{18,... | collective-permute-start | bytes 393224 | tf_op jit(solution)/shard_map/ppermute | solution.py:21
  40.3 0.6 %shard_map.90 = (bf16[256,256]{1,0:T(8,128)(2,1)S(1)}, bf16[256,256]{1,0:T(8,128)(2,1)S(1)}, bf16[256,256]{1,0:T(8,128)(2,1)S(1)}, bf16[256,256]{1,0:T(8,128)(2,1)S(1)}) custom-call(f32[512,256]{1,0:T(8,128)S(1)} %get-tuple-element.88.refs_0_, f32[512,256]{1,0:T(8,128)S(1)} %get-tuple-element.89.refs_1_, ...), custom_call_target="tpu_custom_call" | custom-call | bytes 1310720 | tf_op jit(solution)/shard_map/pallas_call | solution.py:54
  40.9 0.4 collective-permute-start.16
  41.3 0.9 %collective-permute-start.17 = (bf16[256,256]{1,0:T(8,128)(2,1)S(1)}, bf16[256,256]{1,0:T(8,128)(2,1)S(1)}, u32[]{:S(2)}, u32[]{:S(2)}) collective-permute-start(bf16[256,256]{1,0:T(8,128)(2,1)S(1)} %get-tuple-element.95), channel_id=1, source_target_pairs={{0,4},{2,6},{4,0},{6,2},{8,12},{10,14},{12,8},{14,10},{16,20},{18,... | collective-permute-start | bytes 393224 | tf_op jit(solution)/shard_map/ppermute | solution.py:21
  42.2 0.0 collective-permute-done.10.refs_3_
  42.2 2.3 %collective-permute-start.18 = (bf16[256,256]{1,0:T(8,128)(2,1)S(1)}, bf16[256,256]{1,0:T(8,128)(2,1)S(1)}, u32[]{:S(2)}, u32[]{:S(2)}) collective-permute-start(bf16[256,256]{1,0:T(8,128)(2,1)S(1)} %get-tuple-element.96), channel_id=1, source_target_pairs={{0,6},{2,4},{4,2},{6,0},{8,14},{10,12},{12,10},{14,8},{16,22},{18,... | collective-permute-start | bytes 393224 | tf_op jit(solution)/shard_map/ppermute | solution.py:21
  44.5 0.0 collective-permute-done.11.refs_4_
  44.5 1.0 %collective-permute-done.15.refs_5_ = bf16[256,256]{1,0:T(8,128)(2,1)S(1)} collective-permute-done((bf16[256,256]{1,0:T(8,128)(2,1)S(1)}, bf16[256,256]{1,0:T(8,128)(2,1)S(1)}, u32[]{:S(2)}, u32[]{:S(2)}) %collective-permute-start.15) | collective-permute-done | bytes 131104 | tf_op jit(solution)/shard_map/ppermute | solution.py:21
  45.5 1.4 %shard_map.91 = (bf16[128,1024]{1,0:T(8,128)(2,1)S(1)}, bf16[128,512]{1,0:T(8,128)(2,1)S(1)}, bf16[128,512]{1,0:T(8,128)(2,1)S(1)}) custom-call(s32[2]{0:T(128)S(1)} %pad_add_fusion.refs_0_.at_ref, bf16[2048,1024]{1,0:T(8,128)(2,1)S(1)} %copy-done, bf16[256,256]{1,0:T(8,128)(2,1)S(1)} %get-tuple-element.97.refs_2_, ...), custom_call_target="tpu_custom_call" | custom-call | flops 268435456 | bytes 4718600 | tf_op jit(solution)/shard_map/pallas_call | solution.py:54
  46.9 0.1 collective-permute-start.19
  47.0 0.5 collective-permute-start.20
  47.5 1.4 %shard_map.92.refs_1_ = f32[128,1024]{1,0:T(8,128)S(1)} custom-call(s32[2]{0:T(128)S(1)} %pad_add_fusion.refs_0_.at_ref, bf16[2048,1024]{1,0:T(8,128)(2,1)S(1)} %copy-done, bf16[128,1024]{1,0:T(8,128)(2,1)S(1)} %get-tuple-element.101.att_ref), custom_call_target="tpu_custom_call" | custom-call | flops 4000000000 | bytes 4456456 | tf_op jit(solution)/shard_map/pallas_call | solution.py:54
  48.8 0.0 collective-permute-done.16.refs_7_
  48.8 0.1 collective-permute-done.17.refs_8_
  49.0 0.0 collective-permute-done.18.refs_9_
  49.0 0.0 collective-permute-done.19.refs_10_
  49.0 0.0 collective-permute-done.20.refs_11_
  49.0 1.6 %shard_map.93 = (bf16[128,1024]{1,0:T(8,128)(2,1)}, bf16[128,1024]{1,0:T(8,128)(2,1)}, bf16[128,1024]{1,0:T(8,128)(2,1)}, bf16[128,1024]{1,0:T(8,128)(2,1)}) custom-call(s32[2]{0:T(128)S(1)} %pad_add_fusion.refs_0_.at_ref, f32[128,1024]{1,0:T(8,128)S(1)} %shard_map.92.refs_1_, bf16[256,256]{1,0:T(8,128)(2,1)S(1)} %get-tuple-element.97.refs_2_, ...), custom_call_target="tpu_custom_call" | custom-call | bytes 1835016 | tf_op jit(solution)/shard_map/pallas_call | solution.py:54
Async XLA Ops:
  0.7 1.9 %copy-start.2 = (bf16[128,1024]{1,0:T(8,128)(2,1)S(1)}, bf16[128,1024]{1,0:T(8,128)(2,1)}, u32[]{:S(2)}) copy-start(bf16[128,1024]{1,0:T(8,128)(2,1)} %refs_2_.2) | copy-start | bytes 786436
  0.7 6.5 %copy-start = (bf16[2048,1024]{1,0:T(8,128)(2,1)S(1)}, bf16[2048,1024]{1,0:T(8,128)(2,1)}, u32[]{:S(2)}) copy-start(bf16[2048,1024]{1,0:T(8,128)(2,1)} %w_ref.1) | copy-start | bytes 12582916
  0.7 6.5 %copy-start.1 = (bf16[128,1024]{1,0:T(8,128)(2,1)S(1)}, bf16[128,1024]{1,0:T(8,128)(2,1)}, u32[]{:S(2)}) copy-start(bf16[128,1024]{1,0:T(8,128)(2,1)} %refs_1_.4) | copy-start | bytes 786436
  2.6 4.6 %collective-permute-start.3 = (bf16[128,1024]{1,0:T(8,128)(2,1)S(1)}, bf16[128,1024]{1,0:T(8,128)(2,1)S(1)}, u32[]{:S(2)}, u32[]{:S(2)}) collective-permute-start(bf16[128,1024]{1,0:T(8,128)(2,1)S(1)} %copy-done.2), channel_id=1, source_target_pairs={{0,1},{1,0},{2,3},{3,2},{4,5},{5,4},{6,7},{7,6},{8,9},{9,8},{10,11... | collective-permute-start | bytes 786440 | tf_op jit(solution)/shard_map/ppermute | solution.py:25
  3.1 9.0 %collective-permute-start = (bf16[256,256]{1,0:T(8,128)(2,1)S(1)}, bf16[256,256]{1,0:T(8,128)(2,1)S(1)}, u32[]{:S(2)}, u32[]{:S(2)}) collective-permute-start(bf16[256,256]{1,0:T(8,128)(2,1)S(1)} %get-tuple-element.57), channel_id=1, source_target_pairs={{0,2},{2,0},{4,6},{6,4},{8,10},{10,8},{12,14},{14,12},{16,18},{18,... | collective-permute-start | bytes 393224 | tf_op jit(solution)/shard_map/ppermute | solution.py:21
  5.7 8.1 %collective-permute-start.1 = (bf16[256,256]{1,0:T(8,128)(2,1)S(1)}, bf16[256,256]{1,0:T(8,128)(2,1)S(1)}, u32[]{:S(2)}, u32[]{:S(2)}) collective-permute-start(bf16[256,256]{1,0:T(8,128)(2,1)S(1)} %get-tuple-element.58), channel_id=1, source_target_pairs={{0,4},{2,6},{4,0},{6,2},{8,12},{10,14},{12,8},{14,10},{16,20},{18,... | collective-permute-start | bytes 393224 | tf_op jit(solution)/shard_map/ppermute | solution.py:21
  7.2 7.3 %collective-permute-start.2 = (bf16[256,256]{1,0:T(8,128)(2,1)S(1)}, bf16[256,256]{1,0:T(8,128)(2,1)S(1)}, u32[]{:S(2)}, u32[]{:S(2)}) collective-permute-start(bf16[256,256]{1,0:T(8,128)(2,1)S(1)} %get-tuple-element.59), channel_id=1, source_target_pairs={{0,6},{2,4},{4,2},{6,0},{8,14},{10,12},{12,10},{14,8},{16,22},{18,... | collective-permute-start | bytes 393224 | tf_op jit(solution)/shard_map/ppermute | solution.py:21
  8.6 7.8 %collective-permute-start.4 = (bf16[256,256]{1,0:T(8,128)(2,1)S(1)}, bf16[256,256]{1,0:T(8,128)(2,1)S(1)}, u32[]{:S(2)}, u32[]{:S(2)}) collective-permute-start(bf16[256,256]{1,0:T(8,128)(2,1)S(1)} %get-tuple-element.63), channel_id=1, source_target_pairs={{0,2},{2,0},{4,6},{6,4},{8,10},{10,8},{12,14},{14,12},{16,18},{18,... | collective-permute-start | bytes 393224 | tf_op jit(solution)/shard_map/ppermute | solution.py:21
  10.6 10.3 %collective-permute-start.5 = (bf16[256,256]{1,0:T(8,128)(2,1)S(1)}, bf16[256,256]{1,0:T(8,128)(2,1)S(1)}, u32[]{:S(2)}, u32[]{:S(2)}) collective-permute-start(bf16[256,256]{1,0:T(8,128)(2,1)S(1)} %get-tuple-element.64), channel_id=1, source_target_pairs={{0,4},{2,6},{4,0},{6,2},{8,12},{10,14},{12,8},{14,10},{16,20},{18,... | collective-permute-start | bytes 393224 | tf_op jit(solution)/shard_map/ppermute | solution.py:21
  12.1 8.8 %collective-permute-start.6 = (bf16[256,256]{1,0:T(8,128)(2,1)S(1)}, bf16[256,256]{1,0:T(8,128)(2,1)S(1)}, u32[]{:S(2)}, u32[]{:S(2)}) collective-permute-start(bf16[256,256]{1,0:T(8,128)(2,1)S(1)} %get-tuple-element.65), channel_id=1, source_target_pairs={{0,6},{2,4},{4,2},{6,0},{8,14},{10,12},{12,10},{14,8},{16,22},{18,... | collective-permute-start | bytes 393224 | tf_op jit(solution)/shard_map/ppermute | solution.py:21
  16.7 10.0 %collective-permute-start.7 = (bf16[256,256]{1,0:T(8,128)(2,1)S(1)}, bf16[256,256]{1,0:T(8,128)(2,1)S(1)}, u32[]{:S(2)}, u32[]{:S(2)}) collective-permute-start(bf16[256,256]{1,0:T(8,128)(2,1)S(1)} %get-tuple-element.70), channel_id=1, source_target_pairs={{0,8},{2,10},{4,12},{6,14},{8,0},{10,2},{12,4},{14,6},{16,24},{18,... | collective-permute-start | bytes 393224 | tf_op jit(solution)/shard_map/ppermute | solution.py:21
  18.3 6.9 %collective-permute-start.9 = (bf16[128,256]{1,0:T(8,128)(2,1)S(1)}, bf16[128,256]{1,0:T(8,128)(2,1)S(1)}, u32[]{:S(2)}, u32[]{:S(2)}) collective-permute-start(bf16[128,256]{1,0:T(8,128)(2,1)S(1)} %get-tuple-element.71), channel_id=1, source_target_pairs={{0,24},{2,26},{4,28},{6,30},{8,16},{10,18},{12,20},{14,22},{16,8},... | collective-permute-start | bytes 196616 | tf_op jit(solution)/shard_map/ppermute | solution.py:21
  20.8 5.9 %collective-permute-start.8 = (bf16[128,256]{1,0:T(8,128)(2,1)S(1)}, bf16[128,256]{1,0:T(8,128)(2,1)S(1)}, u32[]{:S(2)}, u32[]{:S(2)}) collective-permute-start(bf16[128,256]{1,0:T(8,128)(2,1)S(1)} %get-tuple-element.71), channel_id=1, source_target_pairs={{0,16},{2,18},{4,20},{6,22},{8,24},{10,26},{12,28},{14,30},{16,0},... | collective-permute-start | bytes 196616 | tf_op jit(solution)/shard_map/ppermute | solution.py:21
  29.6 8.4 %collective-permute-start.13 = (bf16[128,256]{1,0:T(8,128)(2,1)S(1)}, bf16[128,256]{1,0:T(8,128)(2,1)S(1)}, u32[]{:S(2)}, u32[]{:S(2)}) collective-permute-start(bf16[128,256]{1,0:T(8,128)(2,1)S(1)} %get-tuple-element.85), channel_id=1, source_target_pairs={{0,16},{2,18},{4,20},{6,22},{8,24},{10,26},{12,28},{14,30},{16,0},... | collective-permute-start | bytes 196616 | tf_op jit(solution)/shard_map/ppermute | solution.py:21
  30.1 7.9 %collective-permute-start.14 = (bf16[128,256]{1,0:T(8,128)(2,1)S(1)}, bf16[128,256]{1,0:T(8,128)(2,1)S(1)}, u32[]{:S(2)}, u32[]{:S(2)}) collective-permute-start(bf16[128,256]{1,0:T(8,128)(2,1)S(1)} %get-tuple-element.86), channel_id=1, source_target_pairs={{0,24},{2,26},{4,28},{6,30},{8,16},{10,18},{12,20},{14,22},{16,8},... | collective-permute-start | bytes 196616 | tf_op jit(solution)/shard_map/ppermute | solution.py:21
  32.0 6.0 %collective-permute-start.12 = (bf16[256,256]{1,0:T(8,128)(2,1)S(1)}, bf16[256,256]{1,0:T(8,128)(2,1)S(1)}, u32[]{:S(2)}, u32[]{:S(2)}) collective-permute-start(bf16[256,256]{1,0:T(8,128)(2,1)S(1)} %get-tuple-element.84), channel_id=1, source_target_pairs={{0,8},{2,10},{4,12},{6,14},{8,0},{10,2},{12,4},{14,6},{16,24},{18,... | collective-permute-start | bytes 393224 | tf_op jit(solution)/shard_map/ppermute | solution.py:21
  34.0 8.2 %collective-permute-start.10 = (bf16[256,256]{1,0:T(8,128)(2,1)S(1)}, bf16[256,256]{1,0:T(8,128)(2,1)S(1)}, u32[]{:S(2)}, u32[]{:S(2)}) collective-permute-start(bf16[256,256]{1,0:T(8,128)(2,1)S(1)} %get-tuple-element.78), channel_id=1, source_target_pairs={{0,2},{2,0},{4,6},{6,4},{8,10},{10,8},{12,14},{14,12},{16,18},{18,... | collective-permute-start | bytes 393224 | tf_op jit(solution)/shard_map/ppermute | solution.py:21
  35.6 8.9 %collective-permute-start.11 = (bf16[256,256]{1,0:T(8,128)(2,1)S(1)}, bf16[256,256]{1,0:T(8,128)(2,1)S(1)}, u32[]{:S(2)}, u32[]{:S(2)}) collective-permute-start(bf16[256,256]{1,0:T(8,128)(2,1)S(1)} %get-tuple-element.79), channel_id=1, source_target_pairs={{0,4},{2,6},{4,0},{6,2},{8,12},{10,14},{12,8},{14,10},{16,20},{18,... | collective-permute-start | bytes 393224 | tf_op jit(solution)/shard_map/ppermute | solution.py:21
  38.0 7.5 %collective-permute-start.15 = (bf16[256,256]{1,0:T(8,128)(2,1)S(1)}, bf16[256,256]{1,0:T(8,128)(2,1)S(1)}, u32[]{:S(2)}, u32[]{:S(2)}) collective-permute-start(bf16[256,256]{1,0:T(8,128)(2,1)S(1)} %get-tuple-element.87), channel_id=1, source_target_pairs={{0,6},{2,4},{4,2},{6,0},{8,14},{10,12},{12,10},{14,8},{16,22},{18,... | collective-permute-start | bytes 393224 | tf_op jit(solution)/shard_map/ppermute | solution.py:21
  40.9 7.9 %collective-permute-start.16 = (bf16[256,256]{1,0:T(8,128)(2,1)S(1)}, bf16[256,256]{1,0:T(8,128)(2,1)S(1)}, u32[]{:S(2)}, u32[]{:S(2)}) collective-permute-start(bf16[256,256]{1,0:T(8,128)(2,1)S(1)} %get-tuple-element.94), channel_id=1, source_target_pairs={{0,2},{2,0},{4,6},{6,4},{8,10},{10,8},{12,14},{14,12},{16,18},{18,... | collective-permute-start | bytes 393224 | tf_op jit(solution)/shard_map/ppermute | solution.py:21
  41.3 7.7 %collective-permute-start.17 = (bf16[256,256]{1,0:T(8,128)(2,1)S(1)}, bf16[256,256]{1,0:T(8,128)(2,1)S(1)}, u32[]{:S(2)}, u32[]{:S(2)}) collective-permute-start(bf16[256,256]{1,0:T(8,128)(2,1)S(1)} %get-tuple-element.95), channel_id=1, source_target_pairs={{0,4},{2,6},{4,0},{6,2},{8,12},{10,14},{12,8},{14,10},{16,20},{18,... | collective-permute-start | bytes 393224 | tf_op jit(solution)/shard_map/ppermute | solution.py:21
  42.2 6.7 %collective-permute-start.18 = (bf16[256,256]{1,0:T(8,128)(2,1)S(1)}, bf16[256,256]{1,0:T(8,128)(2,1)S(1)}, u32[]{:S(2)}, u32[]{:S(2)}) collective-permute-start(bf16[256,256]{1,0:T(8,128)(2,1)S(1)} %get-tuple-element.96), channel_id=1, source_target_pairs={{0,6},{2,4},{4,2},{6,0},{8,14},{10,12},{12,10},{14,8},{16,22},{18,... | collective-permute-start | bytes 393224 | tf_op jit(solution)/shard_map/ppermute | solution.py:21
  46.9 2.1 %collective-permute-start.19 = (bf16[128,512]{1,0:T(8,128)(2,1)S(1)}, bf16[128,512]{1,0:T(8,128)(2,1)S(1)}, u32[]{:S(2)}, u32[]{:S(2)}) collective-permute-start(bf16[128,512]{1,0:T(8,128)(2,1)S(1)} %get-tuple-element.102), channel_id=1, source_target_pairs={{0,1},{1,0},{2,3},{3,2},{4,5},{5,4},{6,7},{7,6},{8,9},{9,8},{10,11... | collective-permute-start | bytes 393224 | tf_op jit(solution)/shard_map/ppermute | solution.py:25
  47.0 2.0 %collective-permute-start.20 = (bf16[128,512]{1,0:T(8,128)(2,1)S(1)}, bf16[128,512]{1,0:T(8,128)(2,1)S(1)}, u32[]{:S(2)}, u32[]{:S(2)}) collective-permute-start(bf16[128,512]{1,0:T(8,128)(2,1)S(1)} %get-tuple-element.103), channel_id=1, source_target_pairs={{0,1},{1,0},{2,3},{3,2},{4,5},{5,4},{6,7},{7,6},{8,9},{9,8},{10,11... | collective-permute-start | bytes 393224 | tf_op jit(solution)/shard_map/ppermute | solution.py:25

commit v6 on v5

--- a/solution.py
+++ b/solution.py
@@ -44,13 +44,13 @@
     return jnp.where(lax.shift_right_logical(col, shift) == row, 1.0, 0.0).astype(BF16)
 
 
-def call(kernel, out_shape, operands, scratch=(), flops=0, vmem=24, specs=None, outs=VMEM):
+def call(kernel, out_shape, operands, scratch=(), flops=0, vmem=24, specs=None, outs=VMEM, free=False):
     specs = specs or [VMEM] * len(operands)
     operands = [
         pltpu.with_memory_space_constraint(x, pltpu.HBM) if spec is HBM else x
         for x, spec in zip(operands, specs)
     ]
-    moved = sum(x.size * x.dtype.itemsize for x in operands)
+    moved = 0 if free else sum(x.size * x.dtype.itemsize for x in operands)
     return pl.pallas_call(
         kernel,
         out_shape=out_shape,
@@ -80,22 +80,26 @@
     return max(16, BLOCK >> level)
 
 
-def token_kernel(slots, at_ref, k_hbm, v_hbm, *refs):
-    chunk_refs, (k_ref, v_ref, sems) = refs[:slots], refs[slots:]
-    low = at_ref[0]
-    tok, width = BLOCK, chunk_refs[0].shape[1]
-    held = (k_ref, v_ref)
+def load_kernel(*refs):
+    count = len(refs) // 2
+    sems = refs[-1]
     copies = [
-        pltpu.make_async_copy(source, held[place], sems.at[place])
-        for place, source in enumerate((k_hbm, v_hbm))
+        pltpu.make_async_copy(refs[place], refs[count + place], sems.at[place])
+        for place in range(count)
     ]
     for copy in copies:
         copy.start()
-    for place, source in enumerate(held):
-        copies[place].wait()
-        for mask in range(slots):
-            rows = slice(place * tok, place * tok + tok)
-            chunk_refs[mask][rows, :] = source[:, col_block(low, mask, width)]
+    for copy in copies:
+        copy.wait()
+
+
+def token_kernel(slots, at_ref, k_ref, v_ref, *chunk_refs):
+    low = at_ref[0]
+    tok, width = BLOCK, chunk_refs[0].shape[1]
+    for mask in range(slots):
+        cols = col_block(low, mask, width)
+        chunk_refs[mask][0:tok, :] = k_ref[:, cols]
+        chunk_refs[mask][tok:, :] = v_ref[:, cols]
 
 
 def query_kernel(slots, at_ref, q_ref, mine_ref, w_ref, other_ref, *refs):
@@ -249,6 +253,13 @@
         out_refs[slab][tok:, :] = value_sum.astype(BF16)
 
 
+def flip_kernel(w_ref, out_ref):
+    half = out_ref.shape[0]
+    for place in range(w_ref.shape[0] // half):
+        rows = slice(place * half, place * half + half)
+        out_ref[:, rows] = w_ref[rows, :].T
+
+
 def send_kernel(slots, at_ref, w_ref, *refs):
     in_refs, att_ref, send_refs = by_mask(refs[:slots]), refs[slots], refs[slots + 1 :]
     low, core = at_ref[0], at_ref[1]
@@ -259,35 +270,42 @@
     part = half // len(send_refs)
     for place, send_ref in enumerate(send_refs):
         other = pl.multiple_of((1 - core) * half + place * part, part)
-        send_ref[...] = mm_cols(att_ref[...], w_ref[pl.ds(other, part), :]).astype(BF16)
-
-
-def keep_kernel(at_ref, w_ref, att_ref, keep_ref):
-    half = att_ref.shape[1]
+        send_ref[...] = mm(att_ref[...], w_ref[:, pl.ds(other, part)]).astype(BF16)
+
+
+def keep_kernel(slots, at_ref, w_ref, att_ref, *refs):
+    home_refs, (keep_ref, dq_ref) = by_mask(refs[:slots]), refs[slots:]
+    tok, half = att_ref.shape
+    width = home_refs[0].shape[1]
+    for mask in range(slots):
+        dq_ref[:, col_block(at_ref[0], mask, width)] = home_refs[mask][tok:, :]
     first = pl.multiple_of(at_ref[1] * half, half)
-    keep_ref[...] = mm_cols(att_ref[...], w_ref[pl.ds(first, half), :])
-
-
-def finish_kernel(slots, at_ref, keep_ref, *refs):
-    home_refs, last_refs = by_mask(refs[:slots]), by_mask(refs[slots : 2 * slots])
-    got_refs, refs = refs[2 * slots : -9], refs[-9:]
-    hbm_refs, held_refs, sems = refs[:4], refs[4:8], refs[8]
-    low = at_ref[0]
-    tok, width = BLOCK, home_refs[0].shape[1]
-    copies = [
-        pltpu.make_async_copy(held_refs[place], hbm_refs[place], sems.at[place])
-        for place in range(4)
-    ]
-    for place, (in_refs, start) in enumerate(((home_refs, tok), (last_refs, 0), (last_refs, tok))):
-        for mask in range(slots):
-            cols = col_block(low, mask, width)
-            held_refs[place][:, cols] = in_refs[mask][start : start + tok, :]
-        copies[place].start()
+    keep_ref[...] = mm(att_ref[...], w_ref[:, pl.ds(first, half)])
+
+
+def add_kernel(keep_ref, *refs):
+    got_refs, out_ref = refs[:-1], refs[-1]
     part = got_refs[0].shape[1]
     for place, got_ref in enumerate(got_refs):
         cols = slice(place * part, place * part + part)
-        held_refs[3][:, cols] = (keep_ref[:, cols] + got_ref[...].astype(F32)).astype(BF16)
-    copies[3].start()
+        out_ref[:, cols] = (keep_ref[:, cols] + got_ref[...].astype(F32)).astype(BF16)
+
+
+def finish_kernel(slots, at_ref, out_ref, dq_ref, *refs):
+    last_refs, refs = by_mask(refs[:slots]), refs[slots:]
+    hbm_refs, (dk_ref, dv_ref, sems) = refs[:4], refs[4:]
+    tok, width = BLOCK, last_refs[0].shape[1]
+    copies = [
+        pltpu.make_async_copy(source, hbm_refs[place], sems.at[place])
+        for place, source in enumerate((out_ref, dq_ref, dk_ref, dv_ref))
+    ]
+    copies[0].start()
+    copies[1].start()
+    for place, held_ref in enumerate((dk_ref, dv_ref)):
+        rows = slice(place * tok, place * tok + tok)
+        for mask in range(slots):
+            held_ref[:, col_block(at_ref[0], mask, width)] = last_refs[mask][rows, :]
+        copies[2 + place].start()
     for copy in copies:
         copy.wait()
 
@@ -394,17 +412,24 @@
         moved = [chunks[0]] + [swap_seq(chunks[mask], mask) for mask in range(1, slots)]
         return [moved[mask] for mask in ORDER]
 
+    held = call(
+        load_kernel,
+        [shape((tok, columns))] * 2,
+        [key_tokens, value_tokens],
+        scratch=[pltpu.SemaphoreType.DMA((2,))],
+        specs=[HBM] * 2,
+        vmem=8,
+    )
     chunks = call(
         lambda *refs: token_kernel(slots, *refs),
         over(2 * tok),
-        (place, key_tokens, value_tokens),
-        scratch=[pltpu.VMEM((tok, columns), BF16)] * 2 + [pltpu.SemaphoreType.DMA((2,))],
+        [place] + list(held),
         flops=6 * 10**9,
-        specs=[SMEM] + [HBM] * 2,
+        specs=[SMEM] + [VMEM] * 2,
         vmem=8,
     )
     keys = exchange(chunks)
-    later, output_grad, *_ = lax.optimization_barrier((place, output_grad, *chunks))
+    later, *_ = lax.optimization_barrier((place, *chunks))
     other_grad = swap_head(output_grad)
     chunks = call(
         lambda *refs: query_kernel(slots, *refs),
@@ -416,7 +441,14 @@
         vmem=16,
     )
     asked = exchange(chunks)
-    sources, *_ = lax.optimization_barrier((keys, asked[1]))
+    flipped = call(
+        flip_kernel,
+        shape(out_weight.shape[::-1]),
+        [out_weight],
+        vmem=24,
+        free=True,
+    )
+    sources, flipped, *_ = lax.optimization_barrier((keys, flipped, asked[1]))
     pieces = call(
         lambda *refs: coarse_kernel(slots, far, *refs),
         [shape((2 * slots * piece_rows(level), width)) for level in far],
@@ -470,26 +502,27 @@
     attended, *send = call(
         lambda *refs: send_kernel(slots, *refs),
         [wide] + [shape((tok, columns // 2))] * 2,
-        [place, out_weight] + home,
+        [place, flipped] + home,
         flops=2 * tok * columns * columns,
         specs=[SMEM] + [VMEM] * (1 + slots),
         vmem=16,
     )
     got = [swap_head(part) for part in send]
-    keep = call(
-        keep_kernel,
-        shape((tok, columns), F32),
-        [place, out_weight, attended],
+    keep, query_grad = call(
+        lambda *refs: keep_kernel(slots, *refs),
+        [shape((tok, columns), F32), wide],
+        [place, flipped, attended] + home,
         flops=4 * 10**9,
-        specs=[SMEM, VMEM, VMEM],
+        specs=[SMEM] + [VMEM] * (2 + slots),
         vmem=16,
     )
-    query_grad, key_grad, value_grad, output = call(
+    output = call(add_kernel, wide, [keep] + got, vmem=8)
+    output, query_grad, key_grad, value_grad = call(
         lambda *refs: finish_kernel(slots, *refs),
         [wide] * 4,
-        [place, keep] + home + last + got,
-        scratch=[pltpu.VMEM((tok, columns), BF16)] * 4 + [pltpu.SemaphoreType.DMA((4,))],
-        specs=[SMEM] + [VMEM] * (1 + 2 * slots + len(got)),
+        [place, output, query_grad] + last,
+        scratch=[pltpu.VMEM((tok, columns), BF16)] * 2 + [pltpu.SemaphoreType.DMA((4,))],
+        specs=[SMEM] + [VMEM] * (2 + slots),
         outs=HBM,
         vmem=8,
     )

time: 50.7 us -> 50.2 us (level)
    pallas_call x10 -> x13, Pallas kernels: 13 us -> 13.3 us  [call(): pl.pallas_call(kernel, out_shape=out_shape, in_specs=specs, out_specs=jax...]
  transfers between devices with their start and end apart: 21 -> 21, of which waited for: 7 -> 8; matrix products, arithmetic and copies ran while one was open for 0% -> 0% of each run, Pallas kernels for 13% -> 18%
where the time goes in v6:
time: 50.2 us; the launch traced here: 50 us
  starting transfers between devices  25.9 us (52%)
  Pallas kernels  13.3 us (26%)
  waiting for transfers between devices  9.88 us (20%)
  between operations  0.82 us (2%)
    ppermute x18, starting transfers between devices, swap_seq(): lax.ppermute(array, 'seq', [(i, i ^ mask) for i in range(lax.axis_size('s...  24.8 us
    pallas_call x13, Pallas kernels, call(): pl.pallas_call(kernel, out_shape=out_shape, in_specs=specs, out_specs=jax...  13.3 us
    ppermute x18, waiting for transfers between devices, swap_seq(): lax.ppermute(array, 'seq', [(i, i ^ mask) for i in range(lax.axis_size('s...  9.87 us
    ppermute x3, starting transfers between devices, swap_head(): return lax.ppermute(array, 'head', [(0, 1), (1, 0)])  1.09 us
  transfers between devices with their start and end apart: 21, of which 8 were waited for; matrix products, arithmetic and copies ran while one was open for 0% of the time, Pallas kernels for 18%

profile of v6, /device:TPU:0, one launch (start us, length us, event | category | flops | bytes accessed | tf_op | source)
XLA Modules:
  0.0 50.0 jit_solution(12977246348634373343)
XLA Ops:
  0.6 0.5 %collective-permute-start.3 = (bf16[128,1024]{1,0:T(8,128)(2,1)}, bf16[128,1024]{1,0:T(8,128)(2,1)S(1)}, u32[]{:S(2)}, u32[]{:S(2)}) collective-permute-start(bf16[128,1024]{1,0:T(8,128)(2,1)} %refs_2_.1), channel_id=1, source_target_pairs={{0,1},{1,0},{2,3},{3,2},{4,5},{5,4},{6,7},{7,6},{8,9},{9,8},{10,11... | collective-permute-start | bytes 786440 | tf_op jit(solution)/shard_map/ppermute | solution.py:25
  1.1 0.1 pad_add_fusion.refs_0_
  1.2 1.0 %shard_map.84 = (bf16[128,1024]{1,0:T(8,128)(2,1)S(1)}, bf16[128,1024]{1,0:T(8,128)(2,1)S(1)}) custom-call(bf16[128,1024]{1,0:T(8,128)(2,1)} %refs_0_.1, bf16[128,1024]{1,0:T(8,128)(2,1)} %refs_1_.2), custom_call_target="tpu_custom_call" | custom-call | bytes 524288 | tf_op jit(solution)/shard_map/pallas_call | solution.py:54
  2.3 0.0 copy-start
  2.3 0.0 copy-start.1
  2.3 0.0 copy-start.2
  2.3 0.6 %shard_map.85 = (bf16[256,256]{1,0:T(8,128)(2,1)S(1)}, bf16[256,256]{1,0:T(8,128)(2,1)S(1)}, bf16[256,256]{1,0:T(8,128)(2,1)S(1)}, bf16[256,256]{1,0:T(8,128)(2,1)S(1)}) custom-call(s32[2]{0:T(128)S(1)} %pad_add_fusion.refs_0_, bf16[128,1024]{1,0:T(8,128)(2,1)S(1)} %get-tuple-element.56.refs_1_, bf16[128,1024]{1,0:T(8,128)(2,1)S(1)} %get-tuple-element.57.refs_2_), custom_call_target="tpu_custom_call" | custom-call | flops 6000000000 | bytes 524296 | tf_op jit(solution)/shard_map/pallas_call | solution.py:54
  2.9 2.6 %collective-permute-start = (bf16[256,256]{1,0:T(8,128)(2,1)S(1)}, bf16[256,256]{1,0:T(8,128)(2,1)S(1)}, u32[]{:S(2)}, u32[]{:S(2)}) collective-permute-start(bf16[256,256]{1,0:T(8,128)(2,1)S(1)} %get-tuple-element.59), channel_id=1, source_target_pairs={{0,2},{2,0},{4,6},{6,4},{8,10},{10,8},{12,14},{14,12},{16,18},{18,... | collective-permute-start | bytes 393224 | tf_op jit(solution)/shard_map/ppermute | solution.py:21
  5.5 1.5 %collective-permute-start.1 = (bf16[256,256]{1,0:T(8,128)(2,1)S(1)}, bf16[256,256]{1,0:T(8,128)(2,1)S(1)}, u32[]{:S(2)}, u32[]{:S(2)}) collective-permute-start(bf16[256,256]{1,0:T(8,128)(2,1)S(1)} %get-tuple-element.60), channel_id=1, source_target_pairs={{0,4},{2,6},{4,0},{6,2},{8,12},{10,14},{12,8},{14,10},{16,20},{18,... | collective-permute-start | bytes 393224 | tf_op jit(solution)/shard_map/ppermute | solution.py:21
  7.0 0.0 collective-permute-start.2
  7.1 0.0 collective-permute-done.3.refs_4_
  7.1 0.0 copy-done
  7.1 0.0 copy-done.1
  7.1 0.0 copy-done.2
  7.1 1.3 %shard_map.87 = (bf16[256,256]{1,0:T(8,128)(2,1)S(1)}, bf16[256,256]{1,0:T(8,128)(2,1)S(1)}, bf16[256,256]{1,0:T(8,128)(2,1)S(1)}, bf16[256,256]{1,0:T(8,128)(2,1)S(1)}) custom-call(s32[2]{0:T(128)S(1)} %pad_add_fusion.refs_0_, bf16[128,1024]{1,0:T(8,128)(2,1)S(1)} %copy-done.1, bf16[128,1024]{1,0:T(8,128)(2,1)S(1)} %copy-done.2, ...), custom_call_target="tpu_custom_call" | custom-call | flops 6000000000 | bytes 4980744 | tf_op jit(solution)/shard_map/pallas_call | solution.py:54
  8.4 2.0 %collective-permute-start.4 = (bf16[256,256]{1,0:T(8,128)(2,1)S(1)}, bf16[256,256]{1,0:T(8,128)(2,1)S(1)}, u32[]{:S(2)}, u32[]{:S(2)}) collective-permute-start(bf16[256,256]{1,0:T(8,128)(2,1)S(1)} %get-tuple-element.63), channel_id=1, source_target_pairs={{0,2},{2,0},{4,6},{6,4},{8,10},{10,8},{12,14},{14,12},{16,18},{18,... | collective-permute-start | bytes 393224 | tf_op jit(solution)/shard_map/ppermute | solution.py:21
  10.4 1.2 %shard_map.86.refs_1_ = bf16[1024,2048]{1,0:T(8,128)(2,1)S(1)} custom-call(bf16[2048,1024]{1,0:T(8,128)(2,1)S(1)} %copy-done), custom_call_target="tpu_custom_call" | custom-call | tf_op jit(solution)/shard_map/pallas_call | solution.py:54
  11.6 1.6 %collective-permute-start.5 = (bf16[256,256]{1,0:T(8,128)(2,1)S(1)}, bf16[256,256]{1,0:T(8,128)(2,1)S(1)}, u32[]{:S(2)}, u32[]{:S(2)}) collective-permute-start(bf16[256,256]{1,0:T(8,128)(2,1)S(1)} %get-tuple-element.66), channel_id=1, source_target_pairs={{0,4},{2,6},{4,0},{6,2},{8,12},{10,14},{12,8},{14,10},{16,20},{18,... | collective-permute-start | bytes 393224 | tf_op jit(solution)/shard_map/ppermute | solution.py:21
  13.2 0.0 collective-permute-done.refs_1_
  13.2 0.1 collective-permute-start.6
  13.3 0.1 collective-permute-done.1.refs_2_
  13.4 1.0 %collective-permute-done.2.refs_3_ = bf16[256,256]{1,0:T(8,128)(2,1)S(1)} collective-permute-done((bf16[256,256]{1,0:T(8,128)(2,1)S(1)}, bf16[256,256]{1,0:T(8,128)(2,1)S(1)}, u32[]{:S(2)}, u32[]{:S(2)}) %collective-permute-start.2) | collective-permute-done | bytes 131104 | tf_op jit(solution)/shard_map/ppermute | solution.py:21
  14.4 1.3 %collective-permute-done.4.refs_5_ = bf16[256,256]{1,0:T(8,128)(2,1)S(1)} collective-permute-done((bf16[256,256]{1,0:T(8,128)(2,1)S(1)}, bf16[256,256]{1,0:T(8,128)(2,1)S(1)}, u32[]{:S(2)}, u32[]{:S(2)}) %collective-permute-start.4) | collective-permute-done | bytes 131104 | tf_op jit(solution)/shard_map/ppermute | solution.py:21
  15.7 0.3 shard_map.88
  16.0 2.2 %collective-permute-start.7 = (bf16[256,256]{1,0:T(8,128)(2,1)S(1)}, bf16[256,256]{1,0:T(8,128)(2,1)S(1)}, u32[]{:S(2)}, u32[]{:S(2)}) collective-permute-start(bf16[256,256]{1,0:T(8,128)(2,1)S(1)} %get-tuple-element.72), channel_id=1, source_target_pairs={{0,8},{2,10},{4,12},{6,14},{8,0},{10,2},{12,4},{14,6},{16,24},{18,... | collective-permute-start | bytes 393224 | tf_op jit(solution)/shard_map/ppermute | solution.py:21
  18.2 2.5 %collective-permute-start.9 = (bf16[128,256]{1,0:T(8,128)(2,1)S(1)}, bf16[128,256]{1,0:T(8,128)(2,1)S(1)}, u32[]{:S(2)}, u32[]{:S(2)}) collective-permute-start(bf16[128,256]{1,0:T(8,128)(2,1)S(1)} %get-tuple-element.73), channel_id=1, source_target_pairs={{0,24},{2,26},{4,28},{6,30},{8,16},{10,18},{12,20},{14,22},{16,8},... | collective-permute-start | bytes 196616 | tf_op jit(solution)/shard_map/ppermute | solution.py:21
  20.6 0.1 collective-permute-start.8
  20.8 0.0 collective-permute-done.5.refs_6_
  20.8 0.0 collective-permute-done.6.refs_7_
  20.8 4.3 %collective-permute-done.9.refs_10_ = bf16[128,256]{1,0:T(8,128)(2,1)S(1)} collective-permute-done((bf16[128,256]{1,0:T(8,128)(2,1)S(1)}, bf16[128,256]{1,0:T(8,128)(2,1)S(1)}, u32[]{:S(2)}, u32[]{:S(2)}) %collective-permute-start.9) | collective-permute-done | bytes 65568 | tf_op jit(solution)/shard_map/ppermute | solution.py:21
  25.1 1.4 %collective-permute-done.8.refs_9_ = bf16[128,256]{1,0:T(8,128)(2,1)S(1)} collective-permute-done((bf16[128,256]{1,0:T(8,128)(2,1)S(1)}, bf16[128,256]{1,0:T(8,128)(2,1)S(1)}, u32[]{:S(2)}, u32[]{:S(2)}) %collective-permute-start.8) | collective-permute-done | bytes 65568 | tf_op jit(solution)/shard_map/ppermute | solution.py:21
  26.5 0.0 collective-permute-done.7.refs_8_
  26.5 2.9 %shard_map.89 = (bf16[256,256]{1,0:T(8,128)(2,1)S(1)}, bf16[128,256]{1,0:T(8,128)(2,1)S(1)}, bf16[128,256]{1,0:T(8,128)(2,1)S(1)}, bf16[2,640,256]{2,1,0:T(8,128...) custom-call(bf16[256,256]{1,0:T(8,128)(2,1)S(1)} %get-tuple-element., ...), custom_call_target="tpu_custom_call" | custom-call | flops 503316480 | bytes 1310720 | tf_op jit(solution)/shard_map/pallas_call | solution.py:54
  29.4 0.5 collective-permute-start.13
  29.9 1.9 %collective-permute-start.14 = (bf16[128,256]{1,0:T(8,128)(2,1)S(1)}, bf16[128,256]{1,0:T(8,128)(2,1)S(1)}, u32[]{:S(2)}, u32[]{:S(2)}) collective-permute-start(bf16[128,256]{1,0:T(8,128)(2,1)S(1)} %get-tuple-element.88), channel_id=1, source_target_pairs={{0,24},{2,26},{4,28},{6,30},{8,16},{10,18},{12,20},{14,22},{16,8},... | collective-permute-start | bytes 196616 | tf_op jit(solution)/shard_map/ppermute | solution.py:21
  31.8 1.2 %collective-permute-start.12 = (bf16[256,256]{1,0:T(8,128)(2,1)S(1)}, bf16[256,256]{1,0:T(8,128)(2,1)S(1)}, u32[]{:S(2)}, u32[]{:S(2)}) collective-permute-start(bf16[256,256]{1,0:T(8,128)(2,1)S(1)} %get-tuple-element.86), channel_id=1, source_target_pairs={{0,8},{2,10},{4,12},{6,14},{8,0},{10,2},{12,4},{14,6},{16,24},{18,... | collective-permute-start | bytes 393224 | tf_op jit(solution)/shard_map/ppermute | solution.py:21
  33.0 0.8 %shard_map.90 = (bf16[256,256]{1,0:T(8,128)(2,1)S(1)}, bf16[256,256]{1,0:T(8,128)(2,1)S(1)}, bf16[256,256]{1,0:T(8,128)(2,1)S(1)}, bf16[256,256]{1,0:T(8,128)(2,1)S(1)}) custom-call(bf16[2,640,256]{2,1,0:T(8,128)(2,1)S(1)} %get-tuple-element.74.refs_0_, bf16[2,640,256]{2,1,0:T(8,128)(2,1)S(1)} %get-tuple-element.75.refs_1_, ...), custom_call_target="tpu_custom_call" | custom-call | flops 6000000000 | bytes 4456448 | tf_op jit(solution)/shard_map/pallas_call | solution.py:54
  33.8 1.6 %collective-permute-start.10 = (bf16[256,256]{1,0:T(8,128)(2,1)S(1)}, bf16[256,256]{1,0:T(8,128)(2,1)S(1)}, u32[]{:S(2)}, u32[]{:S(2)}) collective-permute-start(bf16[256,256]{1,0:T(8,128)(2,1)S(1)} %get-tuple-element.80), channel_id=1, source_target_pairs={{0,2},{2,0},{4,6},{6,4},{8,10},{10,8},{12,14},{14,12},{16,18},{18,... | collective-permute-start | bytes 393224 | tf_op jit(solution)/shard_map/ppermute | solution.py:21
  35.4 1.5 %collective-permute-start.11 = (bf16[256,256]{1,0:T(8,128)(2,1)S(1)}, bf16[256,256]{1,0:T(8,128)(2,1)S(1)}, u32[]{:S(2)}, u32[]{:S(2)}) collective-permute-start(bf16[256,256]{1,0:T(8,128)(2,1)S(1)} %get-tuple-element.81), channel_id=1, source_target_pairs={{0,4},{2,6},{4,0},{6,2},{8,12},{10,14},{12,8},{14,10},{16,20},{18,... | collective-permute-start | bytes 393224 | tf_op jit(solution)/shard_map/ppermute | solution.py:21
  36.9 0.9 %shard_map.91 = (f32[512,256]{1,0:T(8,128)S(1)}, f32[512,256]{1,0:T(8,128)S(1)}) custom-call(bf16[2,256,256]{2,1,0:T(8,128)(2,1)S(1)} %get-tuple-element.83.refs_0_, bf16[2,256,256]{2,1,0:T(8,128)(2,1)S(1)} %get-tuple-element.84.refs_1_, bf16[4,256,640]{2,1,0:T(8,128)(2,1)S(1)} %get-tuple-element.76.refs_2_, bf16[4,256,640]{2,1,0:T(8,128)(2,1)S(1)} %get-tuple-element.77.refs_3_), custom_call_target="tpu_custom_call" | custom-call | flops 335544320 | bytes 3145728 | tf_op jit(solution)/shard_map/pallas_call | solution.py:54
  37.8 0.0 collective-permute-done.13.refs_3_
  37.8 0.0 collective-permute-done.14.refs_4_
  37.8 0.0 collective-permute-done.12.refs_2_
  37.8 2.1 %collective-permute-start.15 = (bf16[256,256]{1,0:T(8,128)(2,1)S(1)}, bf16[256,256]{1,0:T(8,128)(2,1)S(1)}, u32[]{:S(2)}, u32[]{:S(2)}) collective-permute-start(bf16[256,256]{1,0:T(8,128)(2,1)S(1)} %get-tuple-element.89), channel_id=1, source_target_pairs={{0,6},{2,4},{4,2},{6,0},{8,14},{10,12},{12,10},{14,8},{16,22},{18,... | collective-permute-start | bytes 393224 | tf_op jit(solution)/shard_map/ppermute | solution.py:21
  39.9 0.6 %shard_map.92 = (bf16[256,256]{1,0:T(8,128)(2,1)S(1)}, bf16[256,256]{1,0:T(8,128)(2,1)S(1)}, bf16[256,256]{1,0:T(8,128)(2,1)S(1)}, bf16[256,256]{1,0:T(8,128)(2,1)S(1)}) custom-call(f32[512,256]{1,0:T(8,128)S(1)} %get-tuple-element.90.refs_0_, f32[512,256]{1,0:T(8,128)S(1)} %get-tuple-element.91.refs_1_, ...), custom_call_target="tpu_custom_call" | custom-call | bytes 1310720 | tf_op jit(solution)/shard_map/pallas_call | solution.py:54
  40.5 0.6 %collective-permute-start.18 = (bf16[256,256]{1,0:T(8,128)(2,1)S(1)}, bf16[256,256]{1,0:T(8,128)(2,1)S(1)}, u32[]{:S(2)}, u32[]{:S(2)}) collective-permute-start(bf16[256,256]{1,0:T(8,128)(2,1)S(1)} %get-tuple-element.96), channel_id=1, source_target_pairs={{0,2},{2,0},{4,6},{6,4},{8,10},{10,8},{12,14},{14,12},{16,18},{18,... | collective-permute-start | bytes 393224 | tf_op jit(solution)/shard_map/ppermute | solution.py:21
  41.1 0.9 %collective-permute-start.19 = (bf16[256,256]{1,0:T(8,128)(2,1)S(1)}, bf16[256,256]{1,0:T(8,128)(2,1)S(1)}, u32[]{:S(2)}, u32[]{:S(2)}) collective-permute-start(bf16[256,256]{1,0:T(8,128)(2,1)S(1)} %get-tuple-element.97), channel_id=1, source_target_pairs={{0,4},{2,6},{4,0},{6,2},{8,12},{10,14},{12,8},{14,10},{16,20},{18,... | collective-permute-start | bytes 393224 | tf_op jit(solution)/shard_map/ppermute | solution.py:21
  42.1 0.0 collective-permute-done.10.refs_3_.refs_4_
  42.1 2.0 %collective-permute-start.20 = (bf16[256,256]{1,0:T(8,128)(2,1)S(1)}, bf16[256,256]{1,0:T(8,128)(2,1)S(1)}, u32[]{:S(2)}, u32[]{:S(2)}) collective-permute-start(bf16[256,256]{1,0:T(8,128)(2,1)S(1)} %get-tuple-element.98), channel_id=1, source_target_pairs={{0,6},{2,4},{4,2},{6,0},{8,14},{10,12},{12,10},{14,8},{16,22},{18,... | collective-permute-start | bytes 393224 | tf_op jit(solution)/shard_map/ppermute | solution.py:21
  44.1 0.4 collective-permute-done.11.refs_4_.refs_5_
  44.5 0.9 %collective-permute-done.15.refs_5_.refs_6_ = bf16[256,256]{1,0:T(8,128)(2,1)S(1)} collective-permute-done((bf16[256,256]{1,0:T(8,128)(2,1)S(1)}, bf16[256,256]{1,0:T(8,128)(2,1)S(1)}, u32[]{:S(2)}, u32[]{:S(2)}) %collective-permute-start.15) | collective-permute-done | bytes 131104 | tf_op jit(solution)/shard_map/ppermute | solution.py:21
  45.3 1.0 %shard_map.93 = (bf16[128,1024]{1,0:T(8,128)(2,1)S(1)}, bf16[128,512]{1,0:T(8,128)(2,1)S(1)}, bf16[128,512]{1,0:T(8,128)(2,1)S(1)}) custom-call(s32[2]{0:T(128)S(1)} %pad_add_fusion.refs_0_, bf16[1024,2048]{1,0:T(8,128)(2,1)S(1)} %shard_map.86.refs_1_, bf16[256,256]{1,0:T(8,128)(2,1)S(1)} %get-tuple-element.99.refs_2_.refs_3_, ...), custom_call_target="tpu_custom_call" | custom-call | flops 268435456 | bytes 4718600 | tf_op jit(solution)/shard_map/pallas_call | solution.py:54
  46.4 0.1 collective-permute-start.16
  46.5 0.5 collective-permute-start.17
  46.9 1.0 %shard_map.94 = (f32[128,1024]{1,0:T(8,128)S(1)}, bf16[128,1024]{1,0:T(8,128)(2,1)S(1)}) custom-call(s32[2]{0:T(128)S(1)} %pad_add_fusion.refs_0_, bf16[1024,2048]{1,0:T(8,128)(2,1)S(1)} %shard_map.86.refs_1_, bf16[128,1024]{1,0:T(8,128)(2,1)S(1)} %get-tuple-element.103.refs_2_, bf16[256,256]{1,0:T(8,128)(2,1)S(1)} %get-tuple-element.99.refs_2_.refs_3_, ...), custom_call_target="tpu_custom_call" | custom-call | flops 4000000000 | bytes 4980744 | tf_op jit(solution)/shard_map/pallas_call | solution.py:54
  48.0 0.0 collective-permute-done.16.refs_0_
  48.0 0.0 collective-permute-done.17.refs_1_
  48.0 0.1 shard_map.95.refs_1_
  48.0 0.0 collective-permute-done.18.refs_4_
  48.1 0.4 collective-permute-done.19.refs_5_
  48.5 0.0 collective-permute-done.20.refs_6_
  48.5 1.5 %shard_map.96 = (bf16[128,1024]{1,0:T(8,128)(2,1)}, bf16[128,1024]{1,0:T(8,128)(2,1)}, bf16[128,1024]{1,0:T(8,128)(2,1)}, bf16[128,1024]{1,0:T(8,128)(2,1)}) custom-call(s32[2]{0:T(128)S(1)} %pad_add_fusion.refs_0_, bf16[128,1024]{1,0:T(8,128)(2,1)S(1)} %shard_map.95.refs_1_, bf16[128,1024]{1,0:T(8,128)(2,1)S(1)} %get-tuple-element.107.refs_2_, ...), custom_call_target="tpu_custom_call" | custom-call | bytes 1048584 | tf_op jit(solution)/shard_map/pallas_call | solution.py:54
Async XLA Ops:
  0.6 6.4 %collective-permute-start.3 = (bf16[128,1024]{1,0:T(8,128)(2,1)}, bf16[128,1024]{1,0:T(8,128)(2,1)S(1)}, u32[]{:S(2)}, u32[]{:S(2)}) collective-permute-start(bf16[128,1024]{1,0:T(8,128)(2,1)} %refs_2_.1), channel_id=1, source_target_pairs={{0,1},{1,0},{2,3},{3,2},{4,5},{5,4},{6,7},{7,6},{8,9},{9,8},{10,11... | collective-permute-start | bytes 786440 | tf_op jit(solution)/shard_map/ppermute | solution.py:25
  2.3 4.8 %copy-start = (bf16[2048,1024]{1,0:T(8,128)(2,1)S(1)}, bf16[2048,1024]{1,0:T(8,128)(2,1)}, u32[]{:S(2)}) copy-start(bf16[2048,1024]{1,0:T(8,128)(2,1)} %refs_3_.1) | copy-start | bytes 12582916
  2.3 4.8 %copy-start.1 = (bf16[128,1024]{1,0:T(8,128)(2,1)S(1)}, bf16[128,1024]{1,0:T(8,128)(2,1)}, u32[]{:S(2)}) copy-start(bf16[128,1024]{1,0:T(8,128)(2,1)} %refs_1_.3) | copy-start | bytes 786436
  2.3 4.8 %copy-start.2 = (bf16[128,1024]{1,0:T(8,128)(2,1)S(1)}, bf16[128,1024]{1,0:T(8,128)(2,1)}, u32[]{:S(2)}) copy-start(bf16[128,1024]{1,0:T(8,128)(2,1)} %refs_2_.1) | copy-start | bytes 786436
  2.9 10.3 %collective-permute-start = (bf16[256,256]{1,0:T(8,128)(2,1)S(1)}, bf16[256,256]{1,0:T(8,128)(2,1)S(1)}, u32[]{:S(2)}, u32[]{:S(2)}) collective-permute-start(bf16[256,256]{1,0:T(8,128)(2,1)S(1)} %get-tuple-element.59), channel_id=1, source_target_pairs={{0,2},{2,0},{4,6},{6,4},{8,10},{10,8},{12,14},{14,12},{16,18},{18,... | collective-permute-start | bytes 393224 | tf_op jit(solution)/shard_map/ppermute | solution.py:21
  5.5 7.9 %collective-permute-start.1 = (bf16[256,256]{1,0:T(8,128)(2,1)S(1)}, bf16[256,256]{1,0:T(8,128)(2,1)S(1)}, u32[]{:S(2)}, u32[]{:S(2)}) collective-permute-start(bf16[256,256]{1,0:T(8,128)(2,1)S(1)} %get-tuple-element.60), channel_id=1, source_target_pairs={{0,4},{2,6},{4,0},{6,2},{8,12},{10,14},{12,8},{14,10},{16,20},{18,... | collective-permute-start | bytes 393224 | tf_op jit(solution)/shard_map/ppermute | solution.py:21
  7.0 7.4 %collective-permute-start.2 = (bf16[256,256]{1,0:T(8,128)(2,1)S(1)}, bf16[256,256]{1,0:T(8,128)(2,1)S(1)}, u32[]{:S(2)}, u32[]{:S(2)}) collective-permute-start(bf16[256,256]{1,0:T(8,128)(2,1)S(1)} %get-tuple-element.61), channel_id=1, source_target_pairs={{0,6},{2,4},{4,2},{6,0},{8,14},{10,12},{12,10},{14,8},{16,22},{18,... | collective-permute-start | bytes 393224 | tf_op jit(solution)/shard_map/ppermute | solution.py:21
  8.4 7.3 %collective-permute-start.4 = (bf16[256,256]{1,0:T(8,128)(2,1)S(1)}, bf16[256,256]{1,0:T(8,128)(2,1)S(1)}, u32[]{:S(2)}, u32[]{:S(2)}) collective-permute-start(bf16[256,256]{1,0:T(8,128)(2,1)S(1)} %get-tuple-element.63), channel_id=1, source_target_pairs={{0,2},{2,0},{4,6},{6,4},{8,10},{10,8},{12,14},{14,12},{16,18},{18,... | collective-permute-start | bytes 393224 | tf_op jit(solution)/shard_map/ppermute | solution.py:21
  11.6 9.1 %collective-permute-start.5 = (bf16[256,256]{1,0:T(8,128)(2,1)S(1)}, bf16[256,256]{1,0:T(8,128)(2,1)S(1)}, u32[]{:S(2)}, u32[]{:S(2)}) collective-permute-start(bf16[256,256]{1,0:T(8,128)(2,1)S(1)} %get-tuple-element.66), channel_id=1, source_target_pairs={{0,4},{2,6},{4,0},{6,2},{8,12},{10,14},{12,8},{14,10},{16,20},{18,... | collective-permute-start | bytes 393224 | tf_op jit(solution)/shard_map/ppermute | solution.py:21
  13.2 7.5 %collective-permute-start.6 = (bf16[256,256]{1,0:T(8,128)(2,1)S(1)}, bf16[256,256]{1,0:T(8,128)(2,1)S(1)}, u32[]{:S(2)}, u32[]{:S(2)}) collective-permute-start(bf16[256,256]{1,0:T(8,128)(2,1)S(1)} %get-tuple-element.67), channel_id=1, source_target_pairs={{0,6},{2,4},{4,2},{6,0},{8,14},{10,12},{12,10},{14,8},{16,22},{18,... | collective-permute-start | bytes 393224 | tf_op jit(solution)/shard_map/ppermute | solution.py:21
  16.0 10.5 %collective-permute-start.7 = (bf16[256,256]{1,0:T(8,128)(2,1)S(1)}, bf16[256,256]{1,0:T(8,128)(2,1)S(1)}, u32[]{:S(2)}, u32[]{:S(2)}) collective-permute-start(bf16[256,256]{1,0:T(8,128)(2,1)S(1)} %get-tuple-element.72), channel_id=1, source_target_pairs={{0,8},{2,10},{4,12},{6,14},{8,0},{10,2},{12,4},{14,6},{16,24},{18,... | collective-permute-start | bytes 393224 | tf_op jit(solution)/shard_map/ppermute | solution.py:21
  18.2 6.9 %collective-permute-start.9 = (bf16[128,256]{1,0:T(8,128)(2,1)S(1)}, bf16[128,256]{1,0:T(8,128)(2,1)S(1)}, u32[]{:S(2)}, u32[]{:S(2)}) collective-permute-start(bf16[128,256]{1,0:T(8,128)(2,1)S(1)} %get-tuple-element.73), channel_id=1, source_target_pairs={{0,24},{2,26},{4,28},{6,30},{8,16},{10,18},{12,20},{14,22},{16,8},... | collective-permute-start | bytes 196616 | tf_op jit(solution)/shard_map/ppermute | solution.py:21
  20.6 5.9 %collective-permute-start.8 = (bf16[128,256]{1,0:T(8,128)(2,1)S(1)}, bf16[128,256]{1,0:T(8,128)(2,1)S(1)}, u32[]{:S(2)}, u32[]{:S(2)}) collective-permute-start(bf16[128,256]{1,0:T(8,128)(2,1)S(1)} %get-tuple-element.73), channel_id=1, source_target_pairs={{0,16},{2,18},{4,20},{6,22},{8,24},{10,26},{12,28},{14,30},{16,0},... | collective-permute-start | bytes 196616 | tf_op jit(solution)/shard_map/ppermute | solution.py:21
  29.4 8.4 %collective-permute-start.13 = (bf16[128,256]{1,0:T(8,128)(2,1)S(1)}, bf16[128,256]{1,0:T(8,128)(2,1)S(1)}, u32[]{:S(2)}, u32[]{:S(2)}) collective-permute-start(bf16[128,256]{1,0:T(8,128)(2,1)S(1)} %get-tuple-element.87), channel_id=1, source_target_pairs={{0,16},{2,18},{4,20},{6,22},{8,24},{10,26},{12,28},{14,30},{16,0},... | collective-permute-start | bytes 196616 | tf_op jit(solution)/shard_map/ppermute | solution.py:21
  29.9 7.9 %collective-permute-start.14 = (bf16[128,256]{1,0:T(8,128)(2,1)S(1)}, bf16[128,256]{1,0:T(8,128)(2,1)S(1)}, u32[]{:S(2)}, u32[]{:S(2)}) collective-permute-start(bf16[128,256]{1,0:T(8,128)(2,1)S(1)} %get-tuple-element.88), channel_id=1, source_target_pairs={{0,24},{2,26},{4,28},{6,30},{8,16},{10,18},{12,20},{14,22},{16,8},... | collective-permute-start | bytes 196616 | tf_op jit(solution)/shard_map/ppermute | solution.py:21
  31.8 6.0 %collective-permute-start.12 = (bf16[256,256]{1,0:T(8,128)(2,1)S(1)}, bf16[256,256]{1,0:T(8,128)(2,1)S(1)}, u32[]{:S(2)}, u32[]{:S(2)}) collective-permute-start(bf16[256,256]{1,0:T(8,128)(2,1)S(1)} %get-tuple-element.86), channel_id=1, source_target_pairs={{0,8},{2,10},{4,12},{6,14},{8,0},{10,2},{12,4},{14,6},{16,24},{18,... | collective-permute-start | bytes 393224 | tf_op jit(solution)/shard_map/ppermute | solution.py:21
  33.8 8.2 %collective-permute-start.10 = (bf16[256,256]{1,0:T(8,128)(2,1)S(1)}, bf16[256,256]{1,0:T(8,128)(2,1)S(1)}, u32[]{:S(2)}, u32[]{:S(2)}) collective-permute-start(bf16[256,256]{1,0:T(8,128)(2,1)S(1)} %get-tuple-element.80), channel_id=1, source_target_pairs={{0,2},{2,0},{4,6},{6,4},{8,10},{10,8},{12,14},{14,12},{16,18},{18,... | collective-permute-start | bytes 393224 | tf_op jit(solution)/shard_map/ppermute | solution.py:21
  35.4 9.0 %collective-permute-start.11 = (bf16[256,256]{1,0:T(8,128)(2,1)S(1)}, bf16[256,256]{1,0:T(8,128)(2,1)S(1)}, u32[]{:S(2)}, u32[]{:S(2)}) collective-permute-start(bf16[256,256]{1,0:T(8,128)(2,1)S(1)} %get-tuple-element.81), channel_id=1, source_target_pairs={{0,4},{2,6},{4,0},{6,2},{8,12},{10,14},{12,8},{14,10},{16,20},{18,... | collective-permute-start | bytes 393224 | tf_op jit(solution)/shard_map/ppermute | solution.py:21
  37.8 7.5 %collective-permute-start.15 = (bf16[256,256]{1,0:T(8,128)(2,1)S(1)}, bf16[256,256]{1,0:T(8,128)(2,1)S(1)}, u32[]{:S(2)}, u32[]{:S(2)}) collective-permute-start(bf16[256,256]{1,0:T(8,128)(2,1)S(1)} %get-tuple-element.89), channel_id=1, source_target_pairs={{0,6},{2,4},{4,2},{6,0},{8,14},{10,12},{12,10},{14,8},{16,22},{18,... | collective-permute-start | bytes 393224 | tf_op jit(solution)/shard_map/ppermute | solution.py:21
  40.5 7.5 %collective-permute-start.18 = (bf16[256,256]{1,0:T(8,128)(2,1)S(1)}, bf16[256,256]{1,0:T(8,128)(2,1)S(1)}, u32[]{:S(2)}, u32[]{:S(2)}) collective-permute-start(bf16[256,256]{1,0:T(8,128)(2,1)S(1)} %get-tuple-element.96), channel_id=1, source_target_pairs={{0,2},{2,0},{4,6},{6,4},{8,10},{10,8},{12,14},{14,12},{16,18},{18,... | collective-permute-start | bytes 393224 | tf_op jit(solution)/shard_map/ppermute | solution.py:21
  41.1 7.4 %collective-permute-start.19 = (bf16[256,256]{1,0:T(8,128)(2,1)S(1)}, bf16[256,256]{1,0:T(8,128)(2,1)S(1)}, u32[]{:S(2)}, u32[]{:S(2)}) collective-permute-start(bf16[256,256]{1,0:T(8,128)(2,1)S(1)} %get-tuple-element.97), channel_id=1, source_target_pairs={{0,4},{2,6},{4,0},{6,2},{8,12},{10,14},{12,8},{14,10},{16,20},{18,... | collective-permute-start | bytes 393224 | tf_op jit(solution)/shard_map/ppermute | solution.py:21
  42.1 6.4 %collective-permute-start.20 = (bf16[256,256]{1,0:T(8,128)(2,1)S(1)}, bf16[256,256]{1,0:T(8,128)(2,1)S(1)}, u32[]{:S(2)}, u32[]{:S(2)}) collective-permute-start(bf16[256,256]{1,0:T(8,128)(2,1)S(1)} %get-tuple-element.98), channel_id=1, source_target_pairs={{0,6},{2,4},{4,2},{6,0},{8,14},{10,12},{12,10},{14,8},{16,22},{18,... | collective-permute-start | bytes 393224 | tf_op jit(solution)/shard_map/ppermute | solution.py:21
  46.4 1.6 %collective-permute-start.16 = (bf16[128,512]{1,0:T(8,128)(2,1)S(1)}, bf16[128,512]{1,0:T(8,128)(2,1)S(1)}, u32[]{:S(2)}, u32[]{:S(2)}) collective-permute-start(bf16[128,512]{1,0:T(8,128)(2,1)S(1)} %get-tuple-element.105), channel_id=1, source_target_pairs={{0,1},{1,0},{2,3},{3,2},{4,5},{5,4},{6,7},{7,6},{8,9},{9,8},{10,11... | collective-permute-start | bytes 393224 | tf_op jit(solution)/shard_map/ppermute | solution.py:25
  46.5 1.5 %collective-permute-start.17 = (bf16[128,512]{1,0:T(8,128)(2,1)S(1)}, bf16[128,512]{1,0:T(8,128)(2,1)S(1)}, u32[]{:S(2)}, u32[]{:S(2)}) collective-permute-start(bf16[128,512]{1,0:T(8,128)(2,1)S(1)} %get-tuple-element.106), channel_id=1, source_target_pairs={{0,1},{1,0},{2,3},{3,2},{4,5},{5,4},{6,7},{7,6},{8,9},{9,8},{10,11... | collective-permute-start | bytes 393224 | tf_op jit(solution)/shard_map/ppermute | solution.py:25

commit v7 on v6

--- a/solution.py
+++ b/solution.py
@@ -137,7 +137,7 @@
     refs = refs[2 * slots :]
     count = len(entries)
     got_refs, far_refs, refs = refs[:count], refs[count : 2 * count], refs[2 * count :]
-    kl_ref, vl_ref, q_all, g_all, prob_ref, grad_ref, sum_ref, fk_ref, fv_ref = refs
+    kl_ref, vl_ref, q_all, g_all, prob_ref, grad_ref, sum_ref = refs
     tok = BLOCK
     pairs = slots // 2
     inv_scale = 1.0 / math.sqrt(HDIM)
@@ -160,40 +160,42 @@
     for pair in range(pairs):
         kl_ref[pair ^ 1, near:far, :] = (mm(pool, kl_ref[pair, 0:near, :]) * 0.5).astype(BF16)
         vl_ref[pair ^ 1, near:far, :] = mm(pool, vl_ref[pair, 0:near, :]).astype(BF16)
-    for pair in range(pairs):
-        for head in range(2):
-            lanes = slice(head * HDIM, head * HDIM + HDIM)
-            queries, grads = q_all[pair, :, lanes], g_all[pair, :, lanes]
-            keys, values = kl_ref[pair, :, lanes], vl_ref[pair, :, lanes]
-            scores = mm_cols(queries, keys)
-            prob_grad = mm_cols(grads, values)
-            top = jnp.max(scores, axis=1, keepdims=True)
-            raised = jnp.exp2((scores - top) * to_exp2)
-            inverse = 1.0 / jnp.sum(raised, axis=1, keepdims=True)
-            centre = jnp.sum(raised * prob_grad, axis=1, keepdims=True) * inverse
-            raised_low = raised.astype(BF16)
-            score_grad = (raised * (prob_grad - centre)).astype(BF16)
-            queries = (queries.astype(F32) * (inverse * inv_scale)).astype(BF16)
-            grads = (grads.astype(F32) * inverse).astype(BF16)
-            prob_ref[2 * pair + head] = raised_low
-            grad_ref[2 * pair + head] = score_grad
-            sum_ref[2 * pair + head] = jnp.broadcast_to(inverse, (near, HDIM))
-            q_all[pair, :, lanes] = queries
-            g_all[pair, :, lanes] = grads
-            key_terms = mm_rows(score_grad[:, far:], queries)
-            value_terms = mm_rows(raised_low[:, far:], grads)
-            if pair == 0:
-                fk_ref[:, lanes] = key_terms
-                fv_ref[:, lanes] = value_terms
-            else:
-                fk_ref[:, lanes] += key_terms
-                fv_ref[:, lanes] += value_terms
-    for (place, part, rows), out_ref in zip(entries, far_refs):
-        for kind, total in enumerate((fk_ref, fv_ref)):
-            for slab in range(slots):
-                start = place * BLOCK + 32 * slab + part * rows
-                at = (kind * slots + slab) * rows
-                out_ref[at : at + rows, :] = total[start : start + rows, :].astype(BF16)
+
+    def products(unit):
+        pair, head = unit // 2, unit % 2
+        lanes = slice(head * HDIM, head * HDIM + HDIM)
+        scores = mm_cols(q_all[pair, :, lanes], kl_ref[pair, :, lanes])
+        return scores, mm_cols(g_all[pair, :, lanes], vl_ref[pair, :, lanes])
+
+    ready = products(0)
+    for unit in range(slots):
+        pair, head = unit // 2, unit % 2
+        lanes = slice(head * HDIM, head * HDIM + HDIM)
+        scores, prob_grad = ready
+        if unit + 1 < slots:
+            ready = products(unit + 1)
+        top = jnp.max(scores, axis=1, keepdims=True)
+        raised = jnp.exp2((scores - top) * to_exp2)
+        inverse = 1.0 / jnp.sum(raised, axis=1, keepdims=True)
+        centre = jnp.sum(raised * prob_grad, axis=1, keepdims=True) * inverse
+        prob_ref[unit] = raised.astype(BF16)
+        grad_ref[unit] = (raised * (prob_grad - centre)).astype(BF16)
+        sum_ref[unit] = jnp.broadcast_to(inverse, (near, HDIM))
+        queries = q_all[pair, :, lanes].astype(F32) * (inverse * inv_scale)
+        q_all[pair, :, lanes] = queries.astype(BF16)
+        g_all[pair, :, lanes] = (g_all[pair, :, lanes].astype(F32) * inverse).astype(BF16)
+    for head in range(2):
+        lanes = slice(head * HDIM, head * HDIM + HDIM)
+        units = [2 * pair + head for pair in range(pairs)]
+        for kind, (left_ref, right_ref) in enumerate(((grad_ref, q_all), (prob_ref, g_all))):
+            left = jnp.concatenate([left_ref[unit, :, far:] for unit in units], axis=0)
+            right = jnp.concatenate([right_ref[pair, :, lanes] for pair in range(pairs)], axis=0)
+            total = mm_rows(left, right).astype(BF16)
+            for (place, part, rows), out_ref in zip(entries, far_refs):
+                for slab in range(slots):
+                    start = place * BLOCK + 32 * slab + part * rows
+                    at = (kind * slots + slab) * rows
+                    out_ref[at : at + rows, lanes] = total[start : start + rows, :]
 
 
 def reduce_kernel(slots, kl_ref, vl_ref, prob_ref, grad_ref, sum_ref, *home_refs):
@@ -239,18 +241,25 @@
 def merge_kernel(slots, levels, dk_ref, dv_ref, *refs):
     far_refs, out_refs = refs[: len(levels)], refs[len(levels) :]
     tok = BLOCK
+    key_pools, value_pools = [], []
+    for level in levels:
+        count = piece_rows(level)
+        shape = (slots * count, slots * tok)
+        row = lax.broadcasted_iota(jnp.int32, shape, 0)
+        col = lax.broadcasted_iota(jnp.int32, shape, 1)
+        slab = lax.shift_right_logical(col, tok.bit_length() - 1)
+        held = slab * count + lax.shift_right_logical(col & (tok - 1), level)
+        key_pools.append(jnp.where(held == row, 1.0 / (1 << level), 0.0).astype(BF16))
+        value_pools.append(jnp.where(held == row, 1.0, 0.0).astype(BF16))
+    halves = [ref.shape[0] // 2 for ref in far_refs]
+    keys = jnp.concatenate([ref[:half, :] for ref, half in zip(far_refs, halves)], axis=0)
+    values = jnp.concatenate([ref[half:, :] for ref, half in zip(far_refs, halves)], axis=0)
+    key_sum = dk_ref[...] + mm_rows(jnp.concatenate(key_pools, axis=0), keys)
+    value_sum = dv_ref[...] + mm_rows(jnp.concatenate(value_pools, axis=0), values)
     for slab in range(slots):
         rows = slice(slab * tok, slab * tok + tok)
-        key_sum, value_sum = dk_ref[rows, :], dv_ref[rows, :]
-        for level, far_ref in zip(levels, far_refs):
-            count = piece_rows(level)
-            pool = level_pool(count, level)
-            mine = far_ref[slab * count : slab * count + count, :]
-            key_sum += mm_rows(pool, mine) * (1.0 / (1 << level))
-            at = (slots + slab) * count
-            value_sum += mm_rows(pool, far_ref[at : at + count, :])
-        out_refs[slab][0:tok, :] = key_sum.astype(BF16)
-        out_refs[slab][tok:, :] = value_sum.astype(BF16)
+        out_refs[slab][0:tok, :] = key_sum[rows].astype(BF16)
+        out_refs[slab][tok:, :] = value_sum[rows].astype(BF16)
 
 
 def flip_kernel(w_ref, out_ref):
@@ -465,7 +474,6 @@
         + [shape((slots, 2 * tok, list_rows))] * 2
         + [shape((slots, 2 * tok, HDIM), F32)],
         keys + asked + far_got,
-        scratch=[pltpu.VMEM((BLOCK * len(far), width), F32)] * 2,
         flops=6 * heads * tok * list_rows * HDIM,
     )
     shares, share_levels = scatter_far(made[: len(entries)], far, slots)

time: 50.2 us -> 49.6 us (0.988)
  Pallas kernels: 13.3 us -> 12.5 us
    pallas_call x13, Pallas kernels: 13.3 us -> 12.5 us  [call(): pl.pallas_call(kernel, out_shape=out_shape, in_specs=specs, out_specs=jax...]
  transfers between devices with their start and end apart: 21 -> 21, of which waited for: 8 -> 8; matrix products, arithmetic and copies ran while one was open for 0% -> 0% of each run, Pallas kernels for 18% -> 17%
where the time goes in v7:
time: 49.6 us; the launch traced here: 49.4 us
  starting transfers between devices  25.9 us (52%)
  Pallas kernels  12.5 us (25%)
  waiting for transfers between devices  10.1 us (20%)
  between operations  0.81 us (2%)
    ppermute x18, starting transfers between devices, swap_seq(): lax.ppermute(array, 'seq', [(i, i ^ mask) for i in range(lax.axis_size('s...  24.8 us
    pallas_call x13, Pallas kernels, call(): pl.pallas_call(kernel, out_shape=out_shape, in_specs=specs, out_specs=jax...  12.5 us
    ppermute x18, waiting for transfers between devices, swap_seq(): lax.ppermute(array, 'seq', [(i, i ^ mask) for i in range(lax.axis_size('s...  10.1 us
    ppermute x3, starting transfers between devices, swap_head(): return lax.ppermute(array, 'head', [(0, 1), (1, 0)])  1.09 us
  transfers between devices with their start and end apart: 21, of which 8 were waited for; matrix products, arithmetic and copies ran while one was open for 0% of the time, Pallas kernels for 17%

profile of v7, /device:TPU:0, one launch (start us, length us, event | category | flops | bytes accessed | tf_op | source)
XLA Modules:
  0.0 49.4 jit_solution(13732284014236998673)
XLA Ops:
  0.6 0.5 %collective-permute-start.3 = (bf16[128,1024]{1,0:T(8,128)(2,1)}, bf16[128,1024]{1,0:T(8,128)(2,1)S(1)}, u32[]{:S(2)}, u32[]{:S(2)}) collective-permute-start(bf16[128,1024]{1,0:T(8,128)(2,1)} %refs_2_.1), channel_id=1, source_target_pairs={{0,1},{1,0},{2,3},{3,2},{4,5},{5,4},{6,7},{7,6},{8,9},{9,8},{10,11... | collective-permute-start | bytes 786440 | tf_op jit(solution)/shard_map/ppermute | solution.py:25
  1.1 0.1 pad_add_fusion.refs_0_
  1.2 1.0 %shard_map.84 = (bf16[128,1024]{1,0:T(8,128)(2,1)S(1)}, bf16[128,1024]{1,0:T(8,128)(2,1)S(1)}) custom-call(bf16[128,1024]{1,0:T(8,128)(2,1)} %refs_0_.1, bf16[128,1024]{1,0:T(8,128)(2,1)} %refs_1_.2), custom_call_target="tpu_custom_call" | custom-call | bytes 524288 | tf_op jit(solution)/shard_map/pallas_call | solution.py:54
  2.3 0.0 copy-start
  2.3 0.0 copy-start.1
  2.3 0.0 copy-start.2
  2.3 0.6 %shard_map.85 = (bf16[256,256]{1,0:T(8,128)(2,1)S(1)}, bf16[256,256]{1,0:T(8,128)(2,1)S(1)}, bf16[256,256]{1,0:T(8,128)(2,1)S(1)}, bf16[256,256]{1,0:T(8,128)(2,1)S(1)}) custom-call(s32[2]{0:T(128)S(1)} %pad_add_fusion.refs_0_, bf16[128,1024]{1,0:T(8,128)(2,1)S(1)} %get-tuple-element.56.refs_1_, bf16[128,1024]{1,0:T(8,128)(2,1)S(1)} %get-tuple-element.57.refs_2_), custom_call_target="tpu_custom_call" | custom-call | flops 6000000000 | bytes 524296 | tf_op jit(solution)/shard_map/pallas_call | solution.py:54
  2.9 2.6 %collective-permute-start = (bf16[256,256]{1,0:T(8,128)(2,1)S(1)}, bf16[256,256]{1,0:T(8,128)(2,1)S(1)}, u32[]{:S(2)}, u32[]{:S(2)}) collective-permute-start(bf16[256,256]{1,0:T(8,128)(2,1)S(1)} %get-tuple-element.59), channel_id=1, source_target_pairs={{0,2},{2,0},{4,6},{6,4},{8,10},{10,8},{12,14},{14,12},{16,18},{18,... | collective-permute-start | bytes 393224 | tf_op jit(solution)/shard_map/ppermute | solution.py:21
  5.5 1.5 %collective-permute-start.1 = (bf16[256,256]{1,0:T(8,128)(2,1)S(1)}, bf16[256,256]{1,0:T(8,128)(2,1)S(1)}, u32[]{:S(2)}, u32[]{:S(2)}) collective-permute-start(bf16[256,256]{1,0:T(8,128)(2,1)S(1)} %get-tuple-element.60), channel_id=1, source_target_pairs={{0,4},{2,6},{4,0},{6,2},{8,12},{10,14},{12,8},{14,10},{16,20},{18,... | collective-permute-start | bytes 393224 | tf_op jit(solution)/shard_map/ppermute | solution.py:21
  7.0 0.0 collective-permute-start.2
  7.1 0.0 collective-permute-done.3.refs_4_
  7.1 0.0 copy-done
  7.1 0.0 copy-done.1
  7.1 0.0 copy-done.2
  7.1 1.3 %shard_map.87 = (bf16[256,256]{1,0:T(8,128)(2,1)S(1)}, bf16[256,256]{1,0:T(8,128)(2,1)S(1)}, bf16[256,256]{1,0:T(8,128)(2,1)S(1)}, bf16[256,256]{1,0:T(8,128)(2,1)S(1)}) custom-call(s32[2]{0:T(128)S(1)} %pad_add_fusion.refs_0_, bf16[128,1024]{1,0:T(8,128)(2,1)S(1)} %copy-done.1, bf16[128,1024]{1,0:T(8,128)(2,1)S(1)} %copy-done.2, ...), custom_call_target="tpu_custom_call" | custom-call | flops 6000000000 | bytes 4980744 | tf_op jit(solution)/shard_map/pallas_call | solution.py:54
  8.4 2.0 %collective-permute-start.4 = (bf16[256,256]{1,0:T(8,128)(2,1)S(1)}, bf16[256,256]{1,0:T(8,128)(2,1)S(1)}, u32[]{:S(2)}, u32[]{:S(2)}) collective-permute-start(bf16[256,256]{1,0:T(8,128)(2,1)S(1)} %get-tuple-element.63), channel_id=1, source_target_pairs={{0,2},{2,0},{4,6},{6,4},{8,10},{10,8},{12,14},{14,12},{16,18},{18,... | collective-permute-start | bytes 393224 | tf_op jit(solution)/shard_map/ppermute | solution.py:21
  10.4 1.2 %shard_map.86.refs_1_ = bf16[1024,2048]{1,0:T(8,128)(2,1)S(1)} custom-call(bf16[2048,1024]{1,0:T(8,128)(2,1)S(1)} %copy-done), custom_call_target="tpu_custom_call" | custom-call | tf_op jit(solution)/shard_map/pallas_call | solution.py:54
  11.6 1.6 %collective-permute-start.5 = (bf16[256,256]{1,0:T(8,128)(2,1)S(1)}, bf16[256,256]{1,0:T(8,128)(2,1)S(1)}, u32[]{:S(2)}, u32[]{:S(2)}) collective-permute-start(bf16[256,256]{1,0:T(8,128)(2,1)S(1)} %get-tuple-element.66), channel_id=1, source_target_pairs={{0,4},{2,6},{4,0},{6,2},{8,12},{10,14},{12,8},{14,10},{16,20},{18,... | collective-permute-start | bytes 393224 | tf_op jit(solution)/shard_map/ppermute | solution.py:21
  13.2 0.0 collective-permute-done.refs_1_
  13.2 0.1 collective-permute-start.6
  13.3 0.1 collective-permute-done.1.refs_2_
  13.4 1.0 %collective-permute-done.2.refs_3_ = bf16[256,256]{1,0:T(8,128)(2,1)S(1)} collective-permute-done((bf16[256,256]{1,0:T(8,128)(2,1)S(1)}, bf16[256,256]{1,0:T(8,128)(2,1)S(1)}, u32[]{:S(2)}, u32[]{:S(2)}) %collective-permute-start.2) | collective-permute-done | bytes 131104 | tf_op jit(solution)/shard_map/ppermute | solution.py:21
  14.4 1.3 %collective-permute-done.4.refs_5_ = bf16[256,256]{1,0:T(8,128)(2,1)S(1)} collective-permute-done((bf16[256,256]{1,0:T(8,128)(2,1)S(1)}, bf16[256,256]{1,0:T(8,128)(2,1)S(1)}, u32[]{:S(2)}, u32[]{:S(2)}) %collective-permute-start.4) | collective-permute-done | bytes 131104 | tf_op jit(solution)/shard_map/ppermute | solution.py:21
  15.7 0.3 shard_map.88
  16.0 2.2 %collective-permute-start.7 = (bf16[256,256]{1,0:T(8,128)(2,1)S(1)}, bf16[256,256]{1,0:T(8,128)(2,1)S(1)}, u32[]{:S(2)}, u32[]{:S(2)}) collective-permute-start(bf16[256,256]{1,0:T(8,128)(2,1)S(1)} %get-tuple-element.72), channel_id=1, source_target_pairs={{0,8},{2,10},{4,12},{6,14},{8,0},{10,2},{12,4},{14,6},{16,24},{18,... | collective-permute-start | bytes 393224 | tf_op jit(solution)/shard_map/ppermute | solution.py:21
  18.2 2.5 %collective-permute-start.9 = (bf16[128,256]{1,0:T(8,128)(2,1)S(1)}, bf16[128,256]{1,0:T(8,128)(2,1)S(1)}, u32[]{:S(2)}, u32[]{:S(2)}) collective-permute-start(bf16[128,256]{1,0:T(8,128)(2,1)S(1)} %get-tuple-element.73), channel_id=1, source_target_pairs={{0,24},{2,26},{4,28},{6,30},{8,16},{10,18},{12,20},{14,22},{16,8},... | collective-permute-start | bytes 196616 | tf_op jit(solution)/shard_map/ppermute | solution.py:21
  20.6 0.1 collective-permute-start.8
  20.8 0.0 collective-permute-done.5.refs_6_
  20.8 0.0 collective-permute-done.6.refs_7_
  20.8 4.3 %collective-permute-done.9.refs_10_ = bf16[128,256]{1,0:T(8,128)(2,1)S(1)} collective-permute-done((bf16[128,256]{1,0:T(8,128)(2,1)S(1)}, bf16[128,256]{1,0:T(8,128)(2,1)S(1)}, u32[]{:S(2)}, u32[]{:S(2)}) %collective-permute-start.9) | collective-permute-done | bytes 65568 | tf_op jit(solution)/shard_map/ppermute | solution.py:21
  25.1 1.4 %collective-permute-done.8.refs_9_ = bf16[128,256]{1,0:T(8,128)(2,1)S(1)} collective-permute-done((bf16[128,256]{1,0:T(8,128)(2,1)S(1)}, bf16[128,256]{1,0:T(8,128)(2,1)S(1)}, u32[]{:S(2)}, u32[]{:S(2)}) %collective-permute-start.8) | collective-permute-done | bytes 65568 | tf_op jit(solution)/shard_map/ppermute | solution.py:21
  26.5 0.0 collective-permute-done.7.refs_8_
  26.5 2.3 %shard_map.89 = (bf16[256,256]{1,0:T(8,128)(2,1)S(1)}, bf16[128,256]{1,0:T(8,128)(2,1)S(1)}, bf16[128,256]{1,0:T(8,128)(2,1)S(1)}, bf16[2,640,256]{2,1,0:T(8,128...) custom-call(bf16[256,256]{1,0:T(8,128)(2,1)S(1)} %get-tuple-element., ...), custom_call_target="tpu_custom_call" | custom-call | flops 503316480 | bytes 1310720 | tf_op jit(solution)/shard_map/pallas_call | solution.py:54
  28.8 0.5 collective-permute-start.13
  29.3 1.9 %collective-permute-start.14 = (bf16[128,256]{1,0:T(8,128)(2,1)S(1)}, bf16[128,256]{1,0:T(8,128)(2,1)S(1)}, u32[]{:S(2)}, u32[]{:S(2)}) collective-permute-start(bf16[128,256]{1,0:T(8,128)(2,1)S(1)} %get-tuple-element.88), channel_id=1, source_target_pairs={{0,24},{2,26},{4,28},{6,30},{8,16},{10,18},{12,20},{14,22},{16,8},... | collective-permute-start | bytes 196616 | tf_op jit(solution)/shard_map/ppermute | solution.py:21
  31.3 1.1 %collective-permute-start.12 = (bf16[256,256]{1,0:T(8,128)(2,1)S(1)}, bf16[256,256]{1,0:T(8,128)(2,1)S(1)}, u32[]{:S(2)}, u32[]{:S(2)}) collective-permute-start(bf16[256,256]{1,0:T(8,128)(2,1)S(1)} %get-tuple-element.86), channel_id=1, source_target_pairs={{0,8},{2,10},{4,12},{6,14},{8,0},{10,2},{12,4},{14,6},{16,24},{18,... | collective-permute-start | bytes 393224 | tf_op jit(solution)/shard_map/ppermute | solution.py:21
  32.4 0.8 %shard_map.90 = (bf16[256,256]{1,0:T(8,128)(2,1)S(1)}, bf16[256,256]{1,0:T(8,128)(2,1)S(1)}, bf16[256,256]{1,0:T(8,128)(2,1)S(1)}, bf16[256,256]{1,0:T(8,128)(2,1)S(1)}) custom-call(bf16[2,640,256]{2,1,0:T(8,128)(2,1)S(1)} %get-tuple-element.74.refs_0_, bf16[2,640,256]{2,1,0:T(8,128)(2,1)S(1)} %get-tuple-element.75.refs_1_, ...), custom_call_target="tpu_custom_call" | custom-call | flops 6000000000 | bytes 4456448 | tf_op jit(solution)/shard_map/pallas_call | solution.py:54
  33.2 1.6 %collective-permute-start.10 = (bf16[256,256]{1,0:T(8,128)(2,1)S(1)}, bf16[256,256]{1,0:T(8,128)(2,1)S(1)}, u32[]{:S(2)}, u32[]{:S(2)}) collective-permute-start(bf16[256,256]{1,0:T(8,128)(2,1)S(1)} %get-tuple-element.80), channel_id=1, source_target_pairs={{0,2},{2,0},{4,6},{6,4},{8,10},{10,8},{12,14},{14,12},{16,18},{18,... | collective-permute-start | bytes 393224 | tf_op jit(solution)/shard_map/ppermute | solution.py:21
  34.9 1.5 %collective-permute-start.11 = (bf16[256,256]{1,0:T(8,128)(2,1)S(1)}, bf16[256,256]{1,0:T(8,128)(2,1)S(1)}, u32[]{:S(2)}, u32[]{:S(2)}) collective-permute-start(bf16[256,256]{1,0:T(8,128)(2,1)S(1)} %get-tuple-element.81), channel_id=1, source_target_pairs={{0,4},{2,6},{4,0},{6,2},{8,12},{10,14},{12,8},{14,10},{16,20},{18,... | collective-permute-start | bytes 393224 | tf_op jit(solution)/shard_map/ppermute | solution.py:21
  36.3 0.9 %shard_map.91 = (f32[512,256]{1,0:T(8,128)S(1)}, f32[512,256]{1,0:T(8,128)S(1)}) custom-call(bf16[2,256,256]{2,1,0:T(8,128)(2,1)S(1)} %get-tuple-element.83.refs_0_, bf16[2,256,256]{2,1,0:T(8,128)(2,1)S(1)} %get-tuple-element.84.refs_1_, bf16[4,256,640]{2,1,0:T(8,128)(2,1)S(1)} %get-tuple-element.76.refs_2_, bf16[4,256,640]{2,1,0:T(8,128)(2,1)S(1)} %get-tuple-element.77.refs_3_), custom_call_target="tpu_custom_call" | custom-call | flops 335544320 | bytes 3145728 | tf_op jit(solution)/shard_map/pallas_call | solution.py:54
  37.2 0.0 collective-permute-done.13.refs_3_
  37.2 0.0 collective-permute-done.14.refs_4_
  37.2 0.0 collective-permute-done.12.refs_2_
  37.3 2.1 %collective-permute-start.15 = (bf16[256,256]{1,0:T(8,128)(2,1)S(1)}, bf16[256,256]{1,0:T(8,128)(2,1)S(1)}, u32[]{:S(2)}, u32[]{:S(2)}) collective-permute-start(bf16[256,256]{1,0:T(8,128)(2,1)S(1)} %get-tuple-element.89), channel_id=1, source_target_pairs={{0,6},{2,4},{4,2},{6,0},{8,14},{10,12},{12,10},{14,8},{16,22},{18,... | collective-permute-start | bytes 393224 | tf_op jit(solution)/shard_map/ppermute | solution.py:21
  39.3 0.4 shard_map.92
  39.7 0.6 %collective-permute-start.18 = (bf16[256,256]{1,0:T(8,128)(2,1)S(1)}, bf16[256,256]{1,0:T(8,128)(2,1)S(1)}, u32[]{:S(2)}, u32[]{:S(2)}) collective-permute-start(bf16[256,256]{1,0:T(8,128)(2,1)S(1)} %get-tuple-element.96), channel_id=1, source_target_pairs={{0,2},{2,0},{4,6},{6,4},{8,10},{10,8},{12,14},{14,12},{16,18},{18,... | collective-permute-start | bytes 393224 | tf_op jit(solution)/shard_map/ppermute | solution.py:21
  40.3 0.9 %collective-permute-start.19 = (bf16[256,256]{1,0:T(8,128)(2,1)S(1)}, bf16[256,256]{1,0:T(8,128)(2,1)S(1)}, u32[]{:S(2)}, u32[]{:S(2)}) collective-permute-start(bf16[256,256]{1,0:T(8,128)(2,1)S(1)} %get-tuple-element.97), channel_id=1, source_target_pairs={{0,4},{2,6},{4,0},{6,2},{8,12},{10,14},{12,8},{14,10},{16,20},{18,... | collective-permute-start | bytes 393224 | tf_op jit(solution)/shard_map/ppermute | solution.py:21
  41.2 0.0 collective-permute-done.10.refs_3_.refs_4_
  41.2 2.0 %collective-permute-start.20 = (bf16[256,256]{1,0:T(8,128)(2,1)S(1)}, bf16[256,256]{1,0:T(8,128)(2,1)S(1)}, u32[]{:S(2)}, u32[]{:S(2)}) collective-permute-start(bf16[256,256]{1,0:T(8,128)(2,1)S(1)} %get-tuple-element.98), channel_id=1, source_target_pairs={{0,6},{2,4},{4,2},{6,0},{8,14},{10,12},{12,10},{14,8},{16,22},{18,... | collective-permute-start | bytes 393224 | tf_op jit(solution)/shard_map/ppermute | solution.py:21
  43.3 0.6 %collective-permute-done.11.refs_4_.refs_5_ = bf16[256,256]{1,0:T(8,128)(2,1)S(1)} collective-permute-done((bf16[256,256]{1,0:T(8,128)(2,1)S(1)}, bf16[256,256]{1,0:T(8,128)(2,1)S(1)}, u32[]{:S(2)}, u32[]{:S(2)}) %collective-permute-start.11) | collective-permute-done | bytes 131104 | tf_op jit(solution)/shard_map/ppermute | solution.py:21
  43.9 0.9 %collective-permute-done.15.refs_5_.refs_6_ = bf16[256,256]{1,0:T(8,128)(2,1)S(1)} collective-permute-done((bf16[256,256]{1,0:T(8,128)(2,1)S(1)}, bf16[256,256]{1,0:T(8,128)(2,1)S(1)}, u32[]{:S(2)}, u32[]{:S(2)}) %collective-permute-start.15) | collective-permute-done | bytes 131104 | tf_op jit(solution)/shard_map/ppermute | solution.py:21
  44.8 1.0 %shard_map.93 = (bf16[128,1024]{1,0:T(8,128)(2,1)S(1)}, bf16[128,512]{1,0:T(8,128)(2,1)S(1)}, bf16[128,512]{1,0:T(8,128)(2,1)S(1)}) custom-call(s32[2]{0:T(128)S(1)} %pad_add_fusion.refs_0_, bf16[1024,2048]{1,0:T(8,128)(2,1)S(1)} %shard_map.86.refs_1_, bf16[256,256]{1,0:T(8,128)(2,1)S(1)} %get-tuple-element.99.refs_2_.refs_3_, ...), custom_call_target="tpu_custom_call" | custom-call | flops 268435456 | bytes 4718600 | tf_op jit(solution)/shard_map/pallas_call | solution.py:54
  45.8 0.1 collective-permute-start.16
  45.9 0.5 %collective-permute-start.17 = (bf16[128,512]{1,0:T(8,128)(2,1)S(1)}, bf16[128,512]{1,0:T(8,128)(2,1)S(1)}, u32[]{:S(2)}, u32[]{:S(2)}) collective-permute-start(bf16[128,512]{1,0:T(8,128)(2,1)S(1)} %get-tuple-element.106), channel_id=1, source_target_pairs={{0,1},{1,0},{2,3},{3,2},{4,5},{5,4},{6,7},{7,6},{8,9},{9,8},{10,11... | collective-permute-start | bytes 393224 | tf_op jit(solution)/shard_map/ppermute | solution.py:25
  46.4 1.0 %shard_map.94 = (f32[128,1024]{1,0:T(8,128)S(1)}, bf16[128,1024]{1,0:T(8,128)(2,1)S(1)}) custom-call(s32[2]{0:T(128)S(1)} %pad_add_fusion.refs_0_, bf16[1024,2048]{1,0:T(8,128)(2,1)S(1)} %shard_map.86.refs_1_, bf16[128,1024]{1,0:T(8,128)(2,1)S(1)} %get-tuple-element.103.refs_2_, bf16[256,256]{1,0:T(8,128)(2,1)S(1)} %get-tuple-element.99.refs_2_.refs_3_, ...), custom_call_target="tpu_custom_call" | custom-call | flops 4000000000 | bytes 4980744 | tf_op jit(solution)/shard_map/pallas_call | solution.py:54
  47.4 0.0 collective-permute-done.16.refs_0_
  47.4 0.0 collective-permute-done.17.refs_1_
  47.4 0.1 shard_map.95.refs_1_
  47.5 0.0 collective-permute-done.18.refs_4_
  47.5 0.4 collective-permute-done.19.refs_5_
  47.9 0.0 collective-permute-done.20.refs_6_
  47.9 1.5 %shard_map.96 = (bf16[128,1024]{1,0:T(8,128)(2,1)}, bf16[128,1024]{1,0:T(8,128)(2,1)}, bf16[128,1024]{1,0:T(8,128)(2,1)}, bf16[128,1024]{1,0:T(8,128)(2,1)}) custom-call(s32[2]{0:T(128)S(1)} %pad_add_fusion.refs_0_, bf16[128,1024]{1,0:T(8,128)(2,1)S(1)} %shard_map.95.refs_1_, bf16[128,1024]{1,0:T(8,128)(2,1)S(1)} %get-tuple-element.107.refs_2_, ...), custom_call_target="tpu_custom_call" | custom-call | bytes 1048584 | tf_op jit(solution)/shard_map/pallas_call | solution.py:54
Async XLA Ops:
  0.6 6.4 %collective-permute-start.3 = (bf16[128,1024]{1,0:T(8,128)(2,1)}, bf16[128,1024]{1,0:T(8,128)(2,1)S(1)}, u32[]{:S(2)}, u32[]{:S(2)}) collective-permute-start(bf16[128,1024]{1,0:T(8,128)(2,1)} %refs_2_.1), channel_id=1, source_target_pairs={{0,1},{1,0},{2,3},{3,2},{4,5},{5,4},{6,7},{7,6},{8,9},{9,8},{10,11... | collective-permute-start | bytes 786440 | tf_op jit(solution)/shard_map/ppermute | solution.py:25
  2.3 4.8 %copy-start = (bf16[2048,1024]{1,0:T(8,128)(2,1)S(1)}, bf16[2048,1024]{1,0:T(8,128)(2,1)}, u32[]{:S(2)}) copy-start(bf16[2048,1024]{1,0:T(8,128)(2,1)} %refs_3_.1) | copy-start | bytes 12582916
  2.3 4.8 %copy-start.1 = (bf16[128,1024]{1,0:T(8,128)(2,1)S(1)}, bf16[128,1024]{1,0:T(8,128)(2,1)}, u32[]{:S(2)}) copy-start(bf16[128,1024]{1,0:T(8,128)(2,1)} %refs_1_.3) | copy-start | bytes 786436
  2.3 4.8 %copy-start.2 = (bf16[128,1024]{1,0:T(8,128)(2,1)S(1)}, bf16[128,1024]{1,0:T(8,128)(2,1)}, u32[]{:S(2)}) copy-start(bf16[128,1024]{1,0:T(8,128)(2,1)} %refs_2_.1) | copy-start | bytes 786436
  2.9 10.3 %collective-permute-start = (bf16[256,256]{1,0:T(8,128)(2,1)S(1)}, bf16[256,256]{1,0:T(8,128)(2,1)S(1)}, u32[]{:S(2)}, u32[]{:S(2)}) collective-permute-start(bf16[256,256]{1,0:T(8,128)(2,1)S(1)} %get-tuple-element.59), channel_id=1, source_target_pairs={{0,2},{2,0},{4,6},{6,4},{8,10},{10,8},{12,14},{14,12},{16,18},{18,... | collective-permute-start | bytes 393224 | tf_op jit(solution)/shard_map/ppermute | solution.py:21
  5.5 7.9 %collective-permute-start.1 = (bf16[256,256]{1,0:T(8,128)(2,1)S(1)}, bf16[256,256]{1,0:T(8,128)(2,1)S(1)}, u32[]{:S(2)}, u32[]{:S(2)}) collective-permute-start(bf16[256,256]{1,0:T(8,128)(2,1)S(1)} %get-tuple-element.60), channel_id=1, source_target_pairs={{0,4},{2,6},{4,0},{6,2},{8,12},{10,14},{12,8},{14,10},{16,20},{18,... | collective-permute-start | bytes 393224 | tf_op jit(solution)/shard_map/ppermute | solution.py:21
  7.0 7.4 %collective-permute-start.2 = (bf16[256,256]{1,0:T(8,128)(2,1)S(1)}, bf16[256,256]{1,0:T(8,128)(2,1)S(1)}, u32[]{:S(2)}, u32[]{:S(2)}) collective-permute-start(bf16[256,256]{1,0:T(8,128)(2,1)S(1)} %get-tuple-element.61), channel_id=1, source_target_pairs={{0,6},{2,4},{4,2},{6,0},{8,14},{10,12},{12,10},{14,8},{16,22},{18,... | collective-permute-start | bytes 393224 | tf_op jit(solution)/shard_map/ppermute | solution.py:21
  8.4 7.3 %collective-permute-start.4 = (bf16[256,256]{1,0:T(8,128)(2,1)S(1)}, bf16[256,256]{1,0:T(8,128)(2,1)S(1)}, u32[]{:S(2)}, u32[]{:S(2)}) collective-permute-start(bf16[256,256]{1,0:T(8,128)(2,1)S(1)} %get-tuple-element.63), channel_id=1, source_target_pairs={{0,2},{2,0},{4,6},{6,4},{8,10},{10,8},{12,14},{14,12},{16,18},{18,... | collective-permute-start | bytes 393224 | tf_op jit(solution)/shard_map/ppermute | solution.py:21
  11.6 9.1 %collective-permute-start.5 = (bf16[256,256]{1,0:T(8,128)(2,1)S(1)}, bf16[256,256]{1,0:T(8,128)(2,1)S(1)}, u32[]{:S(2)}, u32[]{:S(2)}) collective-permute-start(bf16[256,256]{1,0:T(8,128)(2,1)S(1)} %get-tuple-element.66), channel_id=1, source_target_pairs={{0,4},{2,6},{4,0},{6,2},{8,12},{10,14},{12,8},{14,10},{16,20},{18,... | collective-permute-start | bytes 393224 | tf_op jit(solution)/shard_map/ppermute | solution.py:21
  13.2 7.5 %collective-permute-start.6 = (bf16[256,256]{1,0:T(8,128)(2,1)S(1)}, bf16[256,256]{1,0:T(8,128)(2,1)S(1)}, u32[]{:S(2)}, u32[]{:S(2)}) collective-permute-start(bf16[256,256]{1,0:T(8,128)(2,1)S(1)} %get-tuple-element.67), channel_id=1, source_target_pairs={{0,6},{2,4},{4,2},{6,0},{8,14},{10,12},{12,10},{14,8},{16,22},{18,... | collective-permute-start | bytes 393224 | tf_op jit(solution)/shard_map/ppermute | solution.py:21
  16.0 10.5 %collective-permute-start.7 = (bf16[256,256]{1,0:T(8,128)(2,1)S(1)}, bf16[256,256]{1,0:T(8,128)(2,1)S(1)}, u32[]{:S(2)}, u32[]{:S(2)}) collective-permute-start(bf16[256,256]{1,0:T(8,128)(2,1)S(1)} %get-tuple-element.72), channel_id=1, source_target_pairs={{0,8},{2,10},{4,12},{6,14},{8,0},{10,2},{12,4},{14,6},{16,24},{18,... | collective-permute-start | bytes 393224 | tf_op jit(solution)/shard_map/ppermute | solution.py:21
  18.2 6.9 %collective-permute-start.9 = (bf16[128,256]{1,0:T(8,128)(2,1)S(1)}, bf16[128,256]{1,0:T(8,128)(2,1)S(1)}, u32[]{:S(2)}, u32[]{:S(2)}) collective-permute-start(bf16[128,256]{1,0:T(8,128)(2,1)S(1)} %get-tuple-element.73), channel_id=1, source_target_pairs={{0,24},{2,26},{4,28},{6,30},{8,16},{10,18},{12,20},{14,22},{16,8},... | collective-permute-start | bytes 196616 | tf_op jit(solution)/shard_map/ppermute | solution.py:21
  20.6 5.9 %collective-permute-start.8 = (bf16[128,256]{1,0:T(8,128)(2,1)S(1)}, bf16[128,256]{1,0:T(8,128)(2,1)S(1)}, u32[]{:S(2)}, u32[]{:S(2)}) collective-permute-start(bf16[128,256]{1,0:T(8,128)(2,1)S(1)} %get-tuple-element.73), channel_id=1, source_target_pairs={{0,16},{2,18},{4,20},{6,22},{8,24},{10,26},{12,28},{14,30},{16,0},... | collective-permute-start | bytes 196616 | tf_op jit(solution)/shard_map/ppermute | solution.py:21
  28.8 8.4 %collective-permute-start.13 = (bf16[128,256]{1,0:T(8,128)(2,1)S(1)}, bf16[128,256]{1,0:T(8,128)(2,1)S(1)}, u32[]{:S(2)}, u32[]{:S(2)}) collective-permute-start(bf16[128,256]{1,0:T(8,128)(2,1)S(1)} %get-tuple-element.87), channel_id=1, source_target_pairs={{0,16},{2,18},{4,20},{6,22},{8,24},{10,26},{12,28},{14,30},{16,0},... | collective-permute-start | bytes 196616 | tf_op jit(solution)/shard_map/ppermute | solution.py:21
  29.3 7.9 %collective-permute-start.14 = (bf16[128,256]{1,0:T(8,128)(2,1)S(1)}, bf16[128,256]{1,0:T(8,128)(2,1)S(1)}, u32[]{:S(2)}, u32[]{:S(2)}) collective-permute-start(bf16[128,256]{1,0:T(8,128)(2,1)S(1)} %get-tuple-element.88), channel_id=1, source_target_pairs={{0,24},{2,26},{4,28},{6,30},{8,16},{10,18},{12,20},{14,22},{16,8},... | collective-permute-start | bytes 196616 | tf_op jit(solution)/shard_map/ppermute | solution.py:21
  31.3 6.0 %collective-permute-start.12 = (bf16[256,256]{1,0:T(8,128)(2,1)S(1)}, bf16[256,256]{1,0:T(8,128)(2,1)S(1)}, u32[]{:S(2)}, u32[]{:S(2)}) collective-permute-start(bf16[256,256]{1,0:T(8,128)(2,1)S(1)} %get-tuple-element.86), channel_id=1, source_target_pairs={{0,8},{2,10},{4,12},{6,14},{8,0},{10,2},{12,4},{14,6},{16,24},{18,... | collective-permute-start | bytes 393224 | tf_op jit(solution)/shard_map/ppermute | solution.py:21
  33.2 8.0 %collective-permute-start.10 = (bf16[256,256]{1,0:T(8,128)(2,1)S(1)}, bf16[256,256]{1,0:T(8,128)(2,1)S(1)}, u32[]{:S(2)}, u32[]{:S(2)}) collective-permute-start(bf16[256,256]{1,0:T(8,128)(2,1)S(1)} %get-tuple-element.80), channel_id=1, source_target_pairs={{0,2},{2,0},{4,6},{6,4},{8,10},{10,8},{12,14},{14,12},{16,18},{18,... | collective-permute-start | bytes 393224 | tf_op jit(solution)/shard_map/ppermute | solution.py:21
  34.9 9.0 %collective-permute-start.11 = (bf16[256,256]{1,0:T(8,128)(2,1)S(1)}, bf16[256,256]{1,0:T(8,128)(2,1)S(1)}, u32[]{:S(2)}, u32[]{:S(2)}) collective-permute-start(bf16[256,256]{1,0:T(8,128)(2,1)S(1)} %get-tuple-element.81), channel_id=1, source_target_pairs={{0,4},{2,6},{4,0},{6,2},{8,12},{10,14},{12,8},{14,10},{16,20},{18,... | collective-permute-start | bytes 393224 | tf_op jit(solution)/shard_map/ppermute | solution.py:21
  37.3 7.5 %collective-permute-start.15 = (bf16[256,256]{1,0:T(8,128)(2,1)S(1)}, bf16[256,256]{1,0:T(8,128)(2,1)S(1)}, u32[]{:S(2)}, u32[]{:S(2)}) collective-permute-start(bf16[256,256]{1,0:T(8,128)(2,1)S(1)} %get-tuple-element.89), channel_id=1, source_target_pairs={{0,6},{2,4},{4,2},{6,0},{8,14},{10,12},{12,10},{14,8},{16,22},{18,... | collective-permute-start | bytes 393224 | tf_op jit(solution)/shard_map/ppermute | solution.py:21
  39.7 7.8 %collective-permute-start.18 = (bf16[256,256]{1,0:T(8,128)(2,1)S(1)}, bf16[256,256]{1,0:T(8,128)(2,1)S(1)}, u32[]{:S(2)}, u32[]{:S(2)}) collective-permute-start(bf16[256,256]{1,0:T(8,128)(2,1)S(1)} %get-tuple-element.96), channel_id=1, source_target_pairs={{0,2},{2,0},{4,6},{6,4},{8,10},{10,8},{12,14},{14,12},{16,18},{18,... | collective-permute-start | bytes 393224 | tf_op jit(solution)/shard_map/ppermute | solution.py:21
  40.3 7.6 %collective-permute-start.19 = (bf16[256,256]{1,0:T(8,128)(2,1)S(1)}, bf16[256,256]{1,0:T(8,128)(2,1)S(1)}, u32[]{:S(2)}, u32[]{:S(2)}) collective-permute-start(bf16[256,256]{1,0:T(8,128)(2,1)S(1)} %get-tuple-element.97), channel_id=1, source_target_pairs={{0,4},{2,6},{4,0},{6,2},{8,12},{10,14},{12,8},{14,10},{16,20},{18,... | collective-permute-start | bytes 393224 | tf_op jit(solution)/shard_map/ppermute | solution.py:21
  41.2 6.7 %collective-permute-start.20 = (bf16[256,256]{1,0:T(8,128)(2,1)S(1)}, bf16[256,256]{1,0:T(8,128)(2,1)S(1)}, u32[]{:S(2)}, u32[]{:S(2)}) collective-permute-start(bf16[256,256]{1,0:T(8,128)(2,1)S(1)} %get-tuple-element.98), channel_id=1, source_target_pairs={{0,6},{2,4},{4,2},{6,0},{8,14},{10,12},{12,10},{14,8},{16,22},{18,... | collective-permute-start | bytes 393224 | tf_op jit(solution)/shard_map/ppermute | solution.py:21
  45.8 1.6 %collective-permute-start.16 = (bf16[128,512]{1,0:T(8,128)(2,1)S(1)}, bf16[128,512]{1,0:T(8,128)(2,1)S(1)}, u32[]{:S(2)}, u32[]{:S(2)}) collective-permute-start(bf16[128,512]{1,0:T(8,128)(2,1)S(1)} %get-tuple-element.105), channel_id=1, source_target_pairs={{0,1},{1,0},{2,3},{3,2},{4,5},{5,4},{6,7},{7,6},{8,9},{9,8},{10,11... | collective-permute-start | bytes 393224 | tf_op jit(solution)/shard_map/ppermute | solution.py:25
  45.9 1.5 %collective-permute-start.17 = (bf16[128,512]{1,0:T(8,128)(2,1)S(1)}, bf16[128,512]{1,0:T(8,128)(2,1)S(1)}, u32[]{:S(2)}, u32[]{:S(2)}) collective-permute-start(bf16[128,512]{1,0:T(8,128)(2,1)S(1)} %get-tuple-element.106), channel_id=1, source_target_pairs={{0,1},{1,0},{2,3},{3,2},{4,5},{5,4},{6,7},{7,6},{8,9},{9,8},{10,11... | collective-permute-start | bytes 393224 | tf_op jit(solution)/shard_map/ppermute | solution.py:25

commit v8 on v7

--- a/solution.py
+++ b/solution.py
@@ -509,7 +509,7 @@
     wide = shape((tok, columns))
     attended, *send = call(
         lambda *refs: send_kernel(slots, *refs),
-        [wide] + [shape((tok, columns // 2))] * 2,
+        [wide] + [shape((tok, columns))],
         [place, flipped] + home,
         flops=2 * tok * columns * columns,
         specs=[SMEM] + [VMEM] * (1 + slots),

time: 49.6 us -> 49.6 us (level)
  waiting for transfers between devices: 10.1 us -> 10.7 us
  starting transfers between devices: 25.9 us -> 25.4 us
    ppermute x3 -> x2, starting transfers between devices: 1.09 us -> 0.59 us  [swap_head(): return lax.ppermute(array, 'head', [(0, 1), (1, 0)])]
  transfers between devices with their start and end apart: 21 -> 20, of which waited for: 8 -> 9; matrix products, arithmetic and copies ran while one was open for 0% -> 0% of each run, Pallas kernels for 17% -> 17%
where the time goes in v8:
time: 49.6 us; the launch traced here: 49.4 us
  starting transfers between devices  25.4 us (51%)
  Pallas kernels  12.5 us (25%)
  waiting for transfers between devices  10.7 us (22%)
  between operations  0.8 us (2%)
    ppermute x18, starting transfers between devices, swap_seq(): lax.ppermute(array, 'seq', [(i, i ^ mask) for i in range(lax.axis_size('s...  24.8 us
    pallas_call x13, Pallas kernels, call(): pl.pallas_call(kernel, out_shape=out_shape, in_specs=specs, out_specs=jax...  12.5 us
    ppermute x18, waiting for transfers between devices, swap_seq(): lax.ppermute(array, 'seq', [(i, i ^ mask) for i in range(lax.axis_size('s...  10.1 us
  transfers between devices with their start and end apart: 20, of which 9 were waited for; matrix products, arithmetic and copies ran while one was open for 0% of the time, Pallas kernels for 17%

profile of v8, /device:TPU:0, one launch (start us, length us, event | category | flops | bytes accessed | tf_op | source)
XLA Modules:
  0.0 49.4 jit_solution(8716911454144720365)
XLA Ops:
  0.6 0.5 %collective-permute-start.3 = (bf16[128,1024]{1,0:T(8,128)(2,1)}, bf16[128,1024]{1,0:T(8,128)(2,1)S(1)}, u32[]{:S(2)}, u32[]{:S(2)}) collective-permute-start(bf16[128,1024]{1,0:T(8,128)(2,1)} %refs_2_.1), channel_id=1, source_target_pairs={{0,1},{1,0},{2,3},{3,2},{4,5},{5,4},{6,7},{7,6},{8,9},{9,8},{10,11... | collective-permute-start | bytes 786440 | tf_op jit(solution)/shard_map/ppermute | solution.py:25
  1.1 0.1 pad_add_fusion.refs_0_
  1.2 1.0 %shard_map.84 = (bf16[128,1024]{1,0:T(8,128)(2,1)S(1)}, bf16[128,1024]{1,0:T(8,128)(2,1)S(1)}) custom-call(bf16[128,1024]{1,0:T(8,128)(2,1)} %refs_0_.1, bf16[128,1024]{1,0:T(8,128)(2,1)} %refs_1_.2), custom_call_target="tpu_custom_call" | custom-call | bytes 524288 | tf_op jit(solution)/shard_map/pallas_call | solution.py:54
  2.3 0.0 copy-start
  2.3 0.0 copy-start.1
  2.3 0.0 copy-start.2
  2.3 0.6 %shard_map.85 = (bf16[256,256]{1,0:T(8,128)(2,1)S(1)}, bf16[256,256]{1,0:T(8,128)(2,1)S(1)}, bf16[256,256]{1,0:T(8,128)(2,1)S(1)}, bf16[256,256]{1,0:T(8,128)(2,1)S(1)}) custom-call(s32[2]{0:T(128)S(1)} %pad_add_fusion.refs_0_, bf16[128,1024]{1,0:T(8,128)(2,1)S(1)} %get-tuple-element.55.refs_1_, bf16[128,1024]{1,0:T(8,128)(2,1)S(1)} %get-tuple-element.56.refs_2_), custom_call_target="tpu_custom_call" | custom-call | flops 6000000000 | bytes 524296 | tf_op jit(solution)/shard_map/pallas_call | solution.py:54
  2.9 2.6 %collective-permute-start = (bf16[256,256]{1,0:T(8,128)(2,1)S(1)}, bf16[256,256]{1,0:T(8,128)(2,1)S(1)}, u32[]{:S(2)}, u32[]{:S(2)}) collective-permute-start(bf16[256,256]{1,0:T(8,128)(2,1)S(1)} %get-tuple-element.58), channel_id=1, source_target_pairs={{0,2},{2,0},{4,6},{6,4},{8,10},{10,8},{12,14},{14,12},{16,18},{18,... | collective-permute-start | bytes 393224 | tf_op jit(solution)/shard_map/ppermute | solution.py:21
  5.5 1.5 %collective-permute-start.1 = (bf16[256,256]{1,0:T(8,128)(2,1)S(1)}, bf16[256,256]{1,0:T(8,128)(2,1)S(1)}, u32[]{:S(2)}, u32[]{:S(2)}) collective-permute-start(bf16[256,256]{1,0:T(8,128)(2,1)S(1)} %get-tuple-element.59), channel_id=1, source_target_pairs={{0,4},{2,6},{4,0},{6,2},{8,12},{10,14},{12,8},{14,10},{16,20},{18,... | collective-permute-start | bytes 393224 | tf_op jit(solution)/shard_map/ppermute | solution.py:21
  7.0 0.0 collective-permute-start.2
  7.1 0.0 collective-permute-done.3.refs_4_
  7.1 0.0 copy-done
  7.1 0.0 copy-done.1
  7.1 0.0 copy-done.2
  7.1 1.3 %shard_map.87 = (bf16[256,256]{1,0:T(8,128)(2,1)S(1)}, bf16[256,256]{1,0:T(8,128)(2,1)S(1)}, bf16[256,256]{1,0:T(8,128)(2,1)S(1)}, bf16[256,256]{1,0:T(8,128)(2,1)S(1)}) custom-call(s32[2]{0:T(128)S(1)} %pad_add_fusion.refs_0_, bf16[128,1024]{1,0:T(8,128)(2,1)S(1)} %copy-done.1, bf16[128,1024]{1,0:T(8,128)(2,1)S(1)} %copy-done.2, ...), custom_call_target="tpu_custom_call" | custom-call | flops 6000000000 | bytes 4980744 | tf_op jit(solution)/shard_map/pallas_call | solution.py:54
  8.4 2.0 %collective-permute-start.4 = (bf16[256,256]{1,0:T(8,128)(2,1)S(1)}, bf16[256,256]{1,0:T(8,128)(2,1)S(1)}, u32[]{:S(2)}, u32[]{:S(2)}) collective-permute-start(bf16[256,256]{1,0:T(8,128)(2,1)S(1)} %get-tuple-element.62), channel_id=1, source_target_pairs={{0,2},{2,0},{4,6},{6,4},{8,10},{10,8},{12,14},{14,12},{16,18},{18,... | collective-permute-start | bytes 393224 | tf_op jit(solution)/shard_map/ppermute | solution.py:21
  10.4 1.2 %shard_map.86.refs_1_ = bf16[1024,2048]{1,0:T(8,128)(2,1)S(1)} custom-call(bf16[2048,1024]{1,0:T(8,128)(2,1)S(1)} %copy-done), custom_call_target="tpu_custom_call" | custom-call | tf_op jit(solution)/shard_map/pallas_call | solution.py:54
  11.6 1.6 %collective-permute-start.5 = (bf16[256,256]{1,0:T(8,128)(2,1)S(1)}, bf16[256,256]{1,0:T(8,128)(2,1)S(1)}, u32[]{:S(2)}, u32[]{:S(2)}) collective-permute-start(bf16[256,256]{1,0:T(8,128)(2,1)S(1)} %get-tuple-element.65), channel_id=1, source_target_pairs={{0,4},{2,6},{4,0},{6,2},{8,12},{10,14},{12,8},{14,10},{16,20},{18,... | collective-permute-start | bytes 393224 | tf_op jit(solution)/shard_map/ppermute | solution.py:21
  13.2 0.0 collective-permute-done.refs_1_
  13.2 0.1 collective-permute-start.6
  13.3 0.1 collective-permute-done.1.refs_2_
  13.4 1.0 %collective-permute-done.2.refs_3_ = bf16[256,256]{1,0:T(8,128)(2,1)S(1)} collective-permute-done((bf16[256,256]{1,0:T(8,128)(2,1)S(1)}, bf16[256,256]{1,0:T(8,128)(2,1)S(1)}, u32[]{:S(2)}, u32[]{:S(2)}) %collective-permute-start.2) | collective-permute-done | bytes 131104 | tf_op jit(solution)/shard_map/ppermute | solution.py:21
  14.4 1.3 %collective-permute-done.4.refs_5_ = bf16[256,256]{1,0:T(8,128)(2,1)S(1)} collective-permute-done((bf16[256,256]{1,0:T(8,128)(2,1)S(1)}, bf16[256,256]{1,0:T(8,128)(2,1)S(1)}, u32[]{:S(2)}, u32[]{:S(2)}) %collective-permute-start.4) | collective-permute-done | bytes 131104 | tf_op jit(solution)/shard_map/ppermute | solution.py:21
  15.7 0.3 shard_map.88
  16.0 2.2 %collective-permute-start.7 = (bf16[256,256]{1,0:T(8,128)(2,1)S(1)}, bf16[256,256]{1,0:T(8,128)(2,1)S(1)}, u32[]{:S(2)}, u32[]{:S(2)}) collective-permute-start(bf16[256,256]{1,0:T(8,128)(2,1)S(1)} %get-tuple-element.71), channel_id=1, source_target_pairs={{0,8},{2,10},{4,12},{6,14},{8,0},{10,2},{12,4},{14,6},{16,24},{18,... | collective-permute-start | bytes 393224 | tf_op jit(solution)/shard_map/ppermute | solution.py:21
  18.2 2.5 %collective-permute-start.9 = (bf16[128,256]{1,0:T(8,128)(2,1)S(1)}, bf16[128,256]{1,0:T(8,128)(2,1)S(1)}, u32[]{:S(2)}, u32[]{:S(2)}) collective-permute-start(bf16[128,256]{1,0:T(8,128)(2,1)S(1)} %get-tuple-element.72), channel_id=1, source_target_pairs={{0,24},{2,26},{4,28},{6,30},{8,16},{10,18},{12,20},{14,22},{16,8},... | collective-permute-start | bytes 196616 | tf_op jit(solution)/shard_map/ppermute | solution.py:21
  20.6 0.1 collective-permute-start.8
  20.8 0.0 collective-permute-done.5.refs_6_
  20.8 0.0 collective-permute-done.6.refs_7_
  20.8 4.3 %collective-permute-done.9.refs_10_ = bf16[128,256]{1,0:T(8,128)(2,1)S(1)} collective-permute-done((bf16[128,256]{1,0:T(8,128)(2,1)S(1)}, bf16[128,256]{1,0:T(8,128)(2,1)S(1)}, u32[]{:S(2)}, u32[]{:S(2)}) %collective-permute-start.9) | collective-permute-done | bytes 65568 | tf_op jit(solution)/shard_map/ppermute | solution.py:21
  25.1 1.4 %collective-permute-done.8.refs_9_ = bf16[128,256]{1,0:T(8,128)(2,1)S(1)} collective-permute-done((bf16[128,256]{1,0:T(8,128)(2,1)S(1)}, bf16[128,256]{1,0:T(8,128)(2,1)S(1)}, u32[]{:S(2)}, u32[]{:S(2)}) %collective-permute-start.8) | collective-permute-done | bytes 65568 | tf_op jit(solution)/shard_map/ppermute | solution.py:21
  26.5 0.0 collective-permute-done.7.refs_8_
  26.5 2.3 %shard_map.89 = (bf16[256,256]{1,0:T(8,128)(2,1)S(1)}, bf16[128,256]{1,0:T(8,128)(2,1)S(1)}, bf16[128,256]{1,0:T(8,128)(2,1)S(1)}, bf16[2,640,256]{2,1,0:T(8,128...) custom-call(bf16[256,256]{1,0:T(8,128)(2,1)S(1)} %get-tuple-element., ...), custom_call_target="tpu_custom_call" | custom-call | flops 503316480 | bytes 1310720 | tf_op jit(solution)/shard_map/pallas_call | solution.py:54
  28.8 0.5 collective-permute-start.13
  29.3 1.9 %collective-permute-start.14 = (bf16[128,256]{1,0:T(8,128)(2,1)S(1)}, bf16[128,256]{1,0:T(8,128)(2,1)S(1)}, u32[]{:S(2)}, u32[]{:S(2)}) collective-permute-start(bf16[128,256]{1,0:T(8,128)(2,1)S(1)} %get-tuple-element.87), channel_id=1, source_target_pairs={{0,24},{2,26},{4,28},{6,30},{8,16},{10,18},{12,20},{14,22},{16,8},... | collective-permute-start | bytes 196616 | tf_op jit(solution)/shard_map/ppermute | solution.py:21
  31.3 1.1 %collective-permute-start.12 = (bf16[256,256]{1,0:T(8,128)(2,1)S(1)}, bf16[256,256]{1,0:T(8,128)(2,1)S(1)}, u32[]{:S(2)}, u32[]{:S(2)}) collective-permute-start(bf16[256,256]{1,0:T(8,128)(2,1)S(1)} %get-tuple-element.85), channel_id=1, source_target_pairs={{0,8},{2,10},{4,12},{6,14},{8,0},{10,2},{12,4},{14,6},{16,24},{18,... | collective-permute-start | bytes 393224 | tf_op jit(solution)/shard_map/ppermute | solution.py:21
  32.4 0.8 %shard_map.90 = (bf16[256,256]{1,0:T(8,128)(2,1)S(1)}, bf16[256,256]{1,0:T(8,128)(2,1)S(1)}, bf16[256,256]{1,0:T(8,128)(2,1)S(1)}, bf16[256,256]{1,0:T(8,128)(2,1)S(1)}) custom-call(bf16[2,640,256]{2,1,0:T(8,128)(2,1)S(1)} %get-tuple-element.73.refs_0_, bf16[2,640,256]{2,1,0:T(8,128)(2,1)S(1)} %get-tuple-element.74.refs_1_, ...), custom_call_target="tpu_custom_call" | custom-call | flops 6000000000 | bytes 4456448 | tf_op jit(solution)/shard_map/pallas_call | solution.py:54
  33.2 1.6 %collective-permute-start.10 = (bf16[256,256]{1,0:T(8,128)(2,1)S(1)}, bf16[256,256]{1,0:T(8,128)(2,1)S(1)}, u32[]{:S(2)}, u32[]{:S(2)}) collective-permute-start(bf16[256,256]{1,0:T(8,128)(2,1)S(1)} %get-tuple-element.79), channel_id=1, source_target_pairs={{0,2},{2,0},{4,6},{6,4},{8,10},{10,8},{12,14},{14,12},{16,18},{18,... | collective-permute-start | bytes 393224 | tf_op jit(solution)/shard_map/ppermute | solution.py:21
  34.9 1.5 %collective-permute-start.11 = (bf16[256,256]{1,0:T(8,128)(2,1)S(1)}, bf16[256,256]{1,0:T(8,128)(2,1)S(1)}, u32[]{:S(2)}, u32[]{:S(2)}) collective-permute-start(bf16[256,256]{1,0:T(8,128)(2,1)S(1)} %get-tuple-element.80), channel_id=1, source_target_pairs={{0,4},{2,6},{4,0},{6,2},{8,12},{10,14},{12,8},{14,10},{16,20},{18,... | collective-permute-start | bytes 393224 | tf_op jit(solution)/shard_map/ppermute | solution.py:21
  36.3 0.9 %shard_map.91 = (f32[512,256]{1,0:T(8,128)S(1)}, f32[512,256]{1,0:T(8,128)S(1)}) custom-call(bf16[2,256,256]{2,1,0:T(8,128)(2,1)S(1)} %get-tuple-element.82.refs_0_, bf16[2,256,256]{2,1,0:T(8,128)(2,1)S(1)} %get-tuple-element.83.refs_1_, bf16[4,256,640]{2,1,0:T(8,128)(2,1)S(1)} %get-tuple-element.75.refs_2_, bf16[4,256,640]{2,1,0:T(8,128)(2,1)S(1)} %get-tuple-element.76.refs_3_), custom_call_target="tpu_custom_call" | custom-call | flops 335544320 | bytes 3145728 | tf_op jit(solution)/shard_map/pallas_call | solution.py:54
  37.2 0.0 collective-permute-done.13.refs_3_
  37.2 0.0 collective-permute-done.14.refs_4_
  37.2 0.0 collective-permute-done.12.refs_2_
  37.3 2.1 %collective-permute-start.15 = (bf16[256,256]{1,0:T(8,128)(2,1)S(1)}, bf16[256,256]{1,0:T(8,128)(2,1)S(1)}, u32[]{:S(2)}, u32[]{:S(2)}) collective-permute-start(bf16[256,256]{1,0:T(8,128)(2,1)S(1)} %get-tuple-element.88), channel_id=1, source_target_pairs={{0,6},{2,4},{4,2},{6,0},{8,14},{10,12},{12,10},{14,8},{16,22},{18,... | collective-permute-start | bytes 393224 | tf_op jit(solution)/shard_map/ppermute | solution.py:21
  39.3 0.4 shard_map.92
  39.7 0.6 %collective-permute-start.17 = (bf16[256,256]{1,0:T(8,128)(2,1)S(1)}, bf16[256,256]{1,0:T(8,128)(2,1)S(1)}, u32[]{:S(2)}, u32[]{:S(2)}) collective-permute-start(bf16[256,256]{1,0:T(8,128)(2,1)S(1)} %get-tuple-element.95), channel_id=1, source_target_pairs={{0,2},{2,0},{4,6},{6,4},{8,10},{10,8},{12,14},{14,12},{16,18},{18,... | collective-permute-start | bytes 393224 | tf_op jit(solution)/shard_map/ppermute | solution.py:21
  40.3 0.9 %collective-permute-start.18 = (bf16[256,256]{1,0:T(8,128)(2,1)S(1)}, bf16[256,256]{1,0:T(8,128)(2,1)S(1)}, u32[]{:S(2)}, u32[]{:S(2)}) collective-permute-start(bf16[256,256]{1,0:T(8,128)(2,1)S(1)} %get-tuple-element.96), channel_id=1, source_target_pairs={{0,4},{2,6},{4,0},{6,2},{8,12},{10,14},{12,8},{14,10},{16,20},{18,... | collective-permute-start | bytes 393224 | tf_op jit(solution)/shard_map/ppermute | solution.py:21
  41.2 0.0 collective-permute-done.10.refs_3_.refs_4_
  41.2 2.0 %collective-permute-start.19 = (bf16[256,256]{1,0:T(8,128)(2,1)S(1)}, bf16[256,256]{1,0:T(8,128)(2,1)S(1)}, u32[]{:S(2)}, u32[]{:S(2)}) collective-permute-start(bf16[256,256]{1,0:T(8,128)(2,1)S(1)} %get-tuple-element.97), channel_id=1, source_target_pairs={{0,6},{2,4},{4,2},{6,0},{8,14},{10,12},{12,10},{14,8},{16,22},{18,... | collective-permute-start | bytes 393224 | tf_op jit(solution)/shard_map/ppermute | solution.py:21
  43.3 0.6 %collective-permute-done.11.refs_4_.refs_5_ = bf16[256,256]{1,0:T(8,128)(2,1)S(1)} collective-permute-done((bf16[256,256]{1,0:T(8,128)(2,1)S(1)}, bf16[256,256]{1,0:T(8,128)(2,1)S(1)}, u32[]{:S(2)}, u32[]{:S(2)}) %collective-permute-start.11) | collective-permute-done | bytes 131104 | tf_op jit(solution)/shard_map/ppermute | solution.py:21
  43.9 0.9 %collective-permute-done.15.refs_5_.refs_6_ = bf16[256,256]{1,0:T(8,128)(2,1)S(1)} collective-permute-done((bf16[256,256]{1,0:T(8,128)(2,1)S(1)}, bf16[256,256]{1,0:T(8,128)(2,1)S(1)}, u32[]{:S(2)}, u32[]{:S(2)}) %collective-permute-start.15) | collective-permute-done | bytes 131104 | tf_op jit(solution)/shard_map/ppermute | solution.py:21
  44.8 1.0 %shard_map.93 = (bf16[128,1024]{1,0:T(8,128)(2,1)S(1)}, bf16[128,1024]{1,0:T(8,128)(2,1)S(1)}) custom-call(s32[2]{0:T(128)S(1)} %pad_add_fusion.refs_0_, bf16[1024,2048]{1,0:T(8,128)(2,1)S(1)} %shard_map.86.refs_1_, bf16[256,256]{1,0:T(8,128)(2,1)S(1)} %get-tuple-element.98.refs_2_.refs_3_, bf16[256,256]{1,0:T(8,128)(2,1)S(1)} %collective-permute-done.10.refs_3_.refs_4_, ...), custom_call_target="tpu_custom_call" | custom-call | flops 268435456 | bytes 4718600 | tf_op jit(solution)/shard_map/pallas_call | solution.py:54
  45.8 0.1 collective-permute-start.16
  45.8 1.0 %shard_map.94 = (f32[128,1024]{1,0:T(8,128)S(1)}, bf16[128,1024]{1,0:T(8,128)(2,1)S(1)}) custom-call(s32[2]{0:T(128)S(1)} %pad_add_fusion.refs_0_, bf16[1024,2048]{1,0:T(8,128)(2,1)S(1)} %shard_map.86.refs_1_, bf16[128,1024]{1,0:T(8,128)(2,1)S(1)} %get-tuple-element.102.refs_2_, bf16[256,256]{1,0:T(8,128)(2,1)S(1)} %get-tuple-element.98.refs_2_.refs_3_, ...), custom_call_target="tpu_custom_call" | custom-call | flops 4000000000 | bytes 4980744 | tf_op jit(solution)/shard_map/pallas_call | solution.py:54
  46.9 0.5 %collective-permute-done.16.refs_0_ = bf16[128,1024]{1,0:T(8,128)(2,1)S(1)} collective-permute-done((bf16[128,1024]{1,0:T(8,128)(2,1)S(1)}, bf16[128,1024]{1,0:T(8,128)(2,1)S(1)}, u32[]{:S(2)}, u32[]{:S(2)}) %collective-permute-start.16) | collective-permute-done | bytes 262176 | tf_op jit(solution)/shard_map/ppermute | solution.py:25
  47.4 0.1 shard_map.95.refs_1_
  47.4 0.0 collective-permute-done.17.refs_4_
  47.4 0.5 collective-permute-done.18.refs_5_
  47.9 0.0 collective-permute-done.19.refs_6_
  47.9 1.5 %shard_map.96 = (bf16[128,1024]{1,0:T(8,128)(2,1)}, bf16[128,1024]{1,0:T(8,128)(2,1)}, bf16[128,1024]{1,0:T(8,128)(2,1)}, bf16[128,1024]{1,0:T(8,128)(2,1)}) custom-call(s32[2]{0:T(128)S(1)} %pad_add_fusion.refs_0_, bf16[128,1024]{1,0:T(8,128)(2,1)S(1)} %shard_map.95.refs_1_, bf16[128,1024]{1,0:T(8,128)(2,1)S(1)} %get-tuple-element.105.refs_2_, ...), custom_call_target="tpu_custom_call" | custom-call | bytes 1048584 | tf_op jit(solution)/shard_map/pallas_call | solution.py:54
Async XLA Ops:
  0.6 6.4 %collective-permute-start.3 = (bf16[128,1024]{1,0:T(8,128)(2,1)}, bf16[128,1024]{1,0:T(8,128)(2,1)S(1)}, u32[]{:S(2)}, u32[]{:S(2)}) collective-permute-start(bf16[128,1024]{1,0:T(8,128)(2,1)} %refs_2_.1), channel_id=1, source_target_pairs={{0,1},{1,0},{2,3},{3,2},{4,5},{5,4},{6,7},{7,6},{8,9},{9,8},{10,11... | collective-permute-start | bytes 786440 | tf_op jit(solution)/shard_map/ppermute | solution.py:25
  2.3 4.8 %copy-start = (bf16[2048,1024]{1,0:T(8,128)(2,1)S(1)}, bf16[2048,1024]{1,0:T(8,128)(2,1)}, u32[]{:S(2)}) copy-start(bf16[2048,1024]{1,0:T(8,128)(2,1)} %refs_3_.1) | copy-start | bytes 12582916
  2.3 4.8 %copy-start.1 = (bf16[128,1024]{1,0:T(8,128)(2,1)S(1)}, bf16[128,1024]{1,0:T(8,128)(2,1)}, u32[]{:S(2)}) copy-start(bf16[128,1024]{1,0:T(8,128)(2,1)} %refs_1_.3) | copy-start | bytes 786436
  2.3 4.8 %copy-start.2 = (bf16[128,1024]{1,0:T(8,128)(2,1)S(1)}, bf16[128,1024]{1,0:T(8,128)(2,1)}, u32[]{:S(2)}) copy-start(bf16[128,1024]{1,0:T(8,128)(2,1)} %refs_2_.1) | copy-start | bytes 786436
  2.9 10.3 %collective-permute-start = (bf16[256,256]{1,0:T(8,128)(2,1)S(1)}, bf16[256,256]{1,0:T(8,128)(2,1)S(1)}, u32[]{:S(2)}, u32[]{:S(2)}) collective-permute-start(bf16[256,256]{1,0:T(8,128)(2,1)S(1)} %get-tuple-element.58), channel_id=1, source_target_pairs={{0,2},{2,0},{4,6},{6,4},{8,10},{10,8},{12,14},{14,12},{16,18},{18,... | collective-permute-start | bytes 393224 | tf_op jit(solution)/shard_map/ppermute | solution.py:21
  5.5 7.9 %collective-permute-start.1 = (bf16[256,256]{1,0:T(8,128)(2,1)S(1)}, bf16[256,256]{1,0:T(8,128)(2,1)S(1)}, u32[]{:S(2)}, u32[]{:S(2)}) collective-permute-start(bf16[256,256]{1,0:T(8,128)(2,1)S(1)} %get-tuple-element.59), channel_id=1, source_target_pairs={{0,4},{2,6},{4,0},{6,2},{8,12},{10,14},{12,8},{14,10},{16,20},{18,... | collective-permute-start | bytes 393224 | tf_op jit(solution)/shard_map/ppermute | solution.py:21
  7.0 7.4 %collective-permute-start.2 = (bf16[256,256]{1,0:T(8,128)(2,1)S(1)}, bf16[256,256]{1,0:T(8,128)(2,1)S(1)}, u32[]{:S(2)}, u32[]{:S(2)}) collective-permute-start(bf16[256,256]{1,0:T(8,128)(2,1)S(1)} %get-tuple-element.60), channel_id=1, source_target_pairs={{0,6},{2,4},{4,2},{6,0},{8,14},{10,12},{12,10},{14,8},{16,22},{18,... | collective-permute-start | bytes 393224 | tf_op jit(solution)/shard_map/ppermute | solution.py:21
  8.4 7.3 %collective-permute-start.4 = (bf16[256,256]{1,0:T(8,128)(2,1)S(1)}, bf16[256,256]{1,0:T(8,128)(2,1)S(1)}, u32[]{:S(2)}, u32[]{:S(2)}) collective-permute-start(bf16[256,256]{1,0:T(8,128)(2,1)S(1)} %get-tuple-element.62), channel_id=1, source_target_pairs={{0,2},{2,0},{4,6},{6,4},{8,10},{10,8},{12,14},{14,12},{16,18},{18,... | collective-permute-start | bytes 393224 | tf_op jit(solution)/shard_map/ppermute | solution.py:21
  11.6 9.1 %collective-permute-start.5 = (bf16[256,256]{1,0:T(8,128)(2,1)S(1)}, bf16[256,256]{1,0:T(8,128)(2,1)S(1)}, u32[]{:S(2)}, u32[]{:S(2)}) collective-permute-start(bf16[256,256]{1,0:T(8,128)(2,1)S(1)} %get-tuple-element.65), channel_id=1, source_target_pairs={{0,4},{2,6},{4,0},{6,2},{8,12},{10,14},{12,8},{14,10},{16,20},{18,... | collective-permute-start | bytes 393224 | tf_op jit(solution)/shard_map/ppermute | solution.py:21
  13.2 7.5 %collective-permute-start.6 = (bf16[256,256]{1,0:T(8,128)(2,1)S(1)}, bf16[256,256]{1,0:T(8,128)(2,1)S(1)}, u32[]{:S(2)}, u32[]{:S(2)}) collective-permute-start(bf16[256,256]{1,0:T(8,128)(2,1)S(1)} %get-tuple-element.66), channel_id=1, source_target_pairs={{0,6},{2,4},{4,2},{6,0},{8,14},{10,12},{12,10},{14,8},{16,22},{18,... | collective-permute-start | bytes 393224 | tf_op jit(solution)/shard_map/ppermute | solution.py:21
  16.0 10.5 %collective-permute-start.7 = (bf16[256,256]{1,0:T(8,128)(2,1)S(1)}, bf16[256,256]{1,0:T(8,128)(2,1)S(1)}, u32[]{:S(2)}, u32[]{:S(2)}) collective-permute-start(bf16[256,256]{1,0:T(8,128)(2,1)S(1)} %get-tuple-element.71), channel_id=1, source_target_pairs={{0,8},{2,10},{4,12},{6,14},{8,0},{10,2},{12,4},{14,6},{16,24},{18,... | collective-permute-start | bytes 393224 | tf_op jit(solution)/shard_map/ppermute | solution.py:21
  18.2 6.9 %collective-permute-start.9 = (bf16[128,256]{1,0:T(8,128)(2,1)S(1)}, bf16[128,256]{1,0:T(8,128)(2,1)S(1)}, u32[]{:S(2)}, u32[]{:S(2)}) collective-permute-start(bf16[128,256]{1,0:T(8,128)(2,1)S(1)} %get-tuple-element.72), channel_id=1, source_target_pairs={{0,24},{2,26},{4,28},{6,30},{8,16},{10,18},{12,20},{14,22},{16,8},... | collective-permute-start | bytes 196616 | tf_op jit(solution)/shard_map/ppermute | solution.py:21
  20.6 5.9 %collective-permute-start.8 = (bf16[128,256]{1,0:T(8,128)(2,1)S(1)}, bf16[128,256]{1,0:T(8,128)(2,1)S(1)}, u32[]{:S(2)}, u32[]{:S(2)}) collective-permute-start(bf16[128,256]{1,0:T(8,128)(2,1)S(1)} %get-tuple-element.72), channel_id=1, source_target_pairs={{0,16},{2,18},{4,20},{6,22},{8,24},{10,26},{12,28},{14,30},{16,0},... | collective-permute-start | bytes 196616 | tf_op jit(solution)/shard_map/ppermute | solution.py:21
  28.8 8.4 %collective-permute-start.13 = (bf16[128,256]{1,0:T(8,128)(2,1)S(1)}, bf16[128,256]{1,0:T(8,128)(2,1)S(1)}, u32[]{:S(2)}, u32[]{:S(2)}) collective-permute-start(bf16[128,256]{1,0:T(8,128)(2,1)S(1)} %get-tuple-element.86), channel_id=1, source_target_pairs={{0,16},{2,18},{4,20},{6,22},{8,24},{10,26},{12,28},{14,30},{16,0},... | collective-permute-start | bytes 196616 | tf_op jit(solution)/shard_map/ppermute | solution.py:21
  29.3 7.9 %collective-permute-start.14 = (bf16[128,256]{1,0:T(8,128)(2,1)S(1)}, bf16[128,256]{1,0:T(8,128)(2,1)S(1)}, u32[]{:S(2)}, u32[]{:S(2)}) collective-permute-start(bf16[128,256]{1,0:T(8,128)(2,1)S(1)} %get-tuple-element.87), channel_id=1, source_target_pairs={{0,24},{2,26},{4,28},{6,30},{8,16},{10,18},{12,20},{14,22},{16,8},... | collective-permute-start | bytes 196616 | tf_op jit(solution)/shard_map/ppermute | solution.py:21
  31.3 6.0 %collective-permute-start.12 = (bf16[256,256]{1,0:T(8,128)(2,1)S(1)}, bf16[256,256]{1,0:T(8,128)(2,1)S(1)}, u32[]{:S(2)}, u32[]{:S(2)}) collective-permute-start(bf16[256,256]{1,0:T(8,128)(2,1)S(1)} %get-tuple-element.85), channel_id=1, source_target_pairs={{0,8},{2,10},{4,12},{6,14},{8,0},{10,2},{12,4},{14,6},{16,24},{18,... | collective-permute-start | bytes 393224 | tf_op jit(solution)/shard_map/ppermute | solution.py:21
  33.2 8.0 %collective-permute-start.10 = (bf16[256,256]{1,0:T(8,128)(2,1)S(1)}, bf16[256,256]{1,0:T(8,128)(2,1)S(1)}, u32[]{:S(2)}, u32[]{:S(2)}) collective-permute-start(bf16[256,256]{1,0:T(8,128)(2,1)S(1)} %get-tuple-element.79), channel_id=1, source_target_pairs={{0,2},{2,0},{4,6},{6,4},{8,10},{10,8},{12,14},{14,12},{16,18},{18,... | collective-permute-start | bytes 393224 | tf_op jit(solution)/shard_map/ppermute | solution.py:21
  34.9 9.0 %collective-permute-start.11 = (bf16[256,256]{1,0:T(8,128)(2,1)S(1)}, bf16[256,256]{1,0:T(8,128)(2,1)S(1)}, u32[]{:S(2)}, u32[]{:S(2)}) collective-permute-start(bf16[256,256]{1,0:T(8,128)(2,1)S(1)} %get-tuple-element.80), channel_id=1, source_target_pairs={{0,4},{2,6},{4,0},{6,2},{8,12},{10,14},{12,8},{14,10},{16,20},{18,... | collective-permute-start | bytes 393224 | tf_op jit(solution)/shard_map/ppermute | solution.py:21
  37.3 7.5 %collective-permute-start.15 = (bf16[256,256]{1,0:T(8,128)(2,1)S(1)}, bf16[256,256]{1,0:T(8,128)(2,1)S(1)}, u32[]{:S(2)}, u32[]{:S(2)}) collective-permute-start(bf16[256,256]{1,0:T(8,128)(2,1)S(1)} %get-tuple-element.88), channel_id=1, source_target_pairs={{0,6},{2,4},{4,2},{6,0},{8,14},{10,12},{12,10},{14,8},{16,22},{18,... | collective-permute-start | bytes 393224 | tf_op jit(solution)/shard_map/ppermute | solution.py:21
  39.7 7.7 %collective-permute-start.17 = (bf16[256,256]{1,0:T(8,128)(2,1)S(1)}, bf16[256,256]{1,0:T(8,128)(2,1)S(1)}, u32[]{:S(2)}, u32[]{:S(2)}) collective-permute-start(bf16[256,256]{1,0:T(8,128)(2,1)S(1)} %get-tuple-element.95), channel_id=1, source_target_pairs={{0,2},{2,0},{4,6},{6,4},{8,10},{10,8},{12,14},{14,12},{16,18},{18,... | collective-permute-start | bytes 393224 | tf_op jit(solution)/shard_map/ppermute | solution.py:21
  40.3 7.6 %collective-permute-start.18 = (bf16[256,256]{1,0:T(8,128)(2,1)S(1)}, bf16[256,256]{1,0:T(8,128)(2,1)S(1)}, u32[]{:S(2)}, u32[]{:S(2)}) collective-permute-start(bf16[256,256]{1,0:T(8,128)(2,1)S(1)} %get-tuple-element.96), channel_id=1, source_target_pairs={{0,4},{2,6},{4,0},{6,2},{8,12},{10,14},{12,8},{14,10},{16,20},{18,... | collective-permute-start | bytes 393224 | tf_op jit(solution)/shard_map/ppermute | solution.py:21
  41.2 6.7 %collective-permute-start.19 = (bf16[256,256]{1,0:T(8,128)(2,1)S(1)}, bf16[256,256]{1,0:T(8,128)(2,1)S(1)}, u32[]{:S(2)}, u32[]{:S(2)}) collective-permute-start(bf16[256,256]{1,0:T(8,128)(2,1)S(1)} %get-tuple-element.97), channel_id=1, source_target_pairs={{0,6},{2,4},{4,2},{6,0},{8,14},{10,12},{12,10},{14,8},{16,22},{18,... | collective-permute-start | bytes 393224 | tf_op jit(solution)/shard_map/ppermute | solution.py:21
  45.8 1.6 %collective-permute-start.16 = (bf16[128,1024]{1,0:T(8,128)(2,1)S(1)}, bf16[128,1024]{1,0:T(8,128)(2,1)S(1)}, u32[]{:S(2)}, u32[]{:S(2)}) collective-permute-start(bf16[128,1024]{1,0:T(8,128)(2,1)S(1)} %get-tuple-element.104), channel_id=1, source_target_pairs={{0,1},{1,0},{2,3},{3,2},{4,5},{5,4},{6,7},{7,6},{8,9},{9,8},{10,11... | collective-permute-start | bytes 786440 | tf_op jit(solution)/shard_map/ppermute | solution.py:25

commit v9 on v8

--- a/solution.py
+++ b/solution.py
@@ -9,6 +9,7 @@
 
 HDIM = 128
 ORDER = (0, 1, 2, 3)
+BACK = (0, 2, 1, 3)
 BLOCK = 128
 BF16 = jnp.bfloat16
 F32 = jnp.float32
@@ -62,8 +63,8 @@
     )(*operands)
 
 
-def by_mask(refs):
-    return [refs[ORDER.index(mask)] for mask in range(len(refs))]
+def by_mask(refs, order=ORDER):
+    return [refs[order.index(mask)] for mask in range(len(refs))]
 
 
 def level_pool(rows, level):
@@ -270,7 +271,7 @@
 
 
 def send_kernel(slots, at_ref, w_ref, *refs):
-    in_refs, att_ref, send_refs = by_mask(refs[:slots]), refs[slots], refs[slots + 1 :]
+    in_refs, att_ref, send_refs = by_mask(refs[:slots], BACK), refs[slots], refs[slots + 1 :]
     low, core = at_ref[0], at_ref[1]
     tok, half = att_ref.shape
     width = in_refs[0].shape[1]
@@ -283,7 +284,7 @@
 
 
 def keep_kernel(slots, at_ref, w_ref, att_ref, *refs):
-    home_refs, (keep_ref, dq_ref) = by_mask(refs[:slots]), refs[slots:]
+    home_refs, (keep_ref, dq_ref) = by_mask(refs[:slots], BACK), refs[slots:]
     tok, half = att_ref.shape
     width = home_refs[0].shape[1]
     for mask in range(slots):
@@ -301,7 +302,7 @@
 
 
 def finish_kernel(slots, at_ref, out_ref, dq_ref, *refs):
-    last_refs, refs = by_mask(refs[:slots]), refs[slots:]
+    last_refs, refs = by_mask(refs[:slots], BACK), refs[slots:]
     hbm_refs, (dk_ref, dv_ref, sems) = refs[:4], refs[4:]
     tok, width = BLOCK, last_refs[0].shape[1]
     copies = [
@@ -417,9 +418,9 @@
     def over(rows):
         return [shape((rows, width))] * slots
 
-    def exchange(chunks):
+    def exchange(chunks, order=ORDER):
         moved = [chunks[0]] + [swap_seq(chunks[mask], mask) for mask in range(1, slots)]
-        return [moved[mask] for mask in ORDER]
+        return [moved[mask] for mask in order]
 
     held = call(
         load_kernel,
@@ -494,9 +495,9 @@
         vmem=16,
     )
     made = list(made)
-    late = ORDER[-1]
+    late = BACK[-1]
     made[late], key_sum, *shares = lax.optimization_barrier((made[late], key_sum, *shares))
-    home = exchange(made)
+    home = exchange(made, BACK)
     chunks = call(
         lambda *refs: merge_kernel(slots, share_levels, *refs),
         over(2 * tok),
@@ -505,7 +506,7 @@
     )
     home, _ = lax.optimization_barrier((home, chunks))
     chunks = list(chunks)
-    last = exchange(chunks)
+    last = exchange(chunks, BACK)
     wide = shape((tok, columns))
     attended, *send = call(
         lambda *refs: send_kernel(slots, *refs),

time: 49.6 us -> 49.3 us (level)
  transfers between devices with their start and end apart: 20 -> 20, of which waited for: 9 -> 8; matrix products, arithmetic and copies ran while one was open for 0% -> 0% of each run, Pallas kernels for 17% -> 18%
where the time goes in v9:
time: 49.3 us; the launch traced here: 49.1 us
  starting transfers between devices  25.4 us (52%)
  Pallas kernels  12.5 us (25%)
  waiting for transfers between devices  10.3 us (21%)
  between operations  0.81 us (2%)
    ppermute x18, starting transfers between devices, swap_seq(): lax.ppermute(array, 'seq', [(i, i ^ mask) for i in range(lax.axis_size('s...  24.8 us
    pallas_call x13, Pallas kernels, call(): pl.pallas_call(kernel, out_shape=out_shape, in_specs=specs, out_specs=jax...  12.5 us
    ppermute x18, waiting for transfers between devices, swap_seq(): lax.ppermute(array, 'seq', [(i, i ^ mask) for i in range(lax.axis_size('s...  9.84 us
  transfers between devices with their start and end apart: 20, of which 8 were waited for; matrix products, arithmetic and copies ran while one was open for 0% of the time, Pallas kernels for 18%

profile of v9, /device:TPU:0, one launch (start us, length us, event | category | flops | bytes accessed | tf_op | source)
XLA Modules:
  0.0 49.1 jit_solution(8081619755325617699)
XLA Ops:
  0.6 0.5 %collective-permute-start.3 = (bf16[128,1024]{1,0:T(8,128)(2,1)}, bf16[128,1024]{1,0:T(8,128)(2,1)S(1)}, u32[]{:S(2)}, u32[]{:S(2)}) collective-permute-start(bf16[128,1024]{1,0:T(8,128)(2,1)} %refs_2_.1), channel_id=1, source_target_pairs={{0,1},{1,0},{2,3},{3,2},{4,5},{5,4},{6,7},{7,6},{8,9},{9,8},{10,11... | collective-permute-start | bytes 786440 | tf_op jit(solution)/shard_map/ppermute | solution.py:26
  1.1 0.1 pad_add_fusion.refs_0_
  1.2 1.0 %shard_map.84 = (bf16[128,1024]{1,0:T(8,128)(2,1)S(1)}, bf16[128,1024]{1,0:T(8,128)(2,1)S(1)}) custom-call(bf16[128,1024]{1,0:T(8,128)(2,1)} %refs_0_.1, bf16[128,1024]{1,0:T(8,128)(2,1)} %refs_1_.2), custom_call_target="tpu_custom_call" | custom-call | bytes 524288 | tf_op jit(solution)/shard_map/pallas_call | solution.py:55
  2.3 0.0 copy-start
  2.3 0.0 copy-start.1
  2.3 0.0 copy-start.2
  2.3 0.6 %shard_map.85 = (bf16[256,256]{1,0:T(8,128)(2,1)S(1)}, bf16[256,256]{1,0:T(8,128)(2,1)S(1)}, bf16[256,256]{1,0:T(8,128)(2,1)S(1)}, bf16[256,256]{1,0:T(8,128)(2,1)S(1)}) custom-call(s32[2]{0:T(128)S(1)} %pad_add_fusion.refs_0_, bf16[128,1024]{1,0:T(8,128)(2,1)S(1)} %get-tuple-element.55.refs_1_, bf16[128,1024]{1,0:T(8,128)(2,1)S(1)} %get-tuple-element.56.refs_2_), custom_call_target="tpu_custom_call" | custom-call | flops 6000000000 | bytes 524296 | tf_op jit(solution)/shard_map/pallas_call | solution.py:55
  2.9 2.6 %collective-permute-start = (bf16[256,256]{1,0:T(8,128)(2,1)S(1)}, bf16[256,256]{1,0:T(8,128)(2,1)S(1)}, u32[]{:S(2)}, u32[]{:S(2)}) collective-permute-start(bf16[256,256]{1,0:T(8,128)(2,1)S(1)} %get-tuple-element.58), channel_id=1, source_target_pairs={{0,2},{2,0},{4,6},{6,4},{8,10},{10,8},{12,14},{14,12},{16,18},{18,... | collective-permute-start | bytes 393224 | tf_op jit(solution)/shard_map/ppermute | solution.py:22
  5.5 1.5 %collective-permute-start.1 = (bf16[256,256]{1,0:T(8,128)(2,1)S(1)}, bf16[256,256]{1,0:T(8,128)(2,1)S(1)}, u32[]{:S(2)}, u32[]{:S(2)}) collective-permute-start(bf16[256,256]{1,0:T(8,128)(2,1)S(1)} %get-tuple-element.59), channel_id=1, source_target_pairs={{0,4},{2,6},{4,0},{6,2},{8,12},{10,14},{12,8},{14,10},{16,20},{18,... | collective-permute-start | bytes 393224 | tf_op jit(solution)/shard_map/ppermute | solution.py:22
  7.0 0.0 collective-permute-start.2
  7.1 0.0 collective-permute-done.3.refs_4_
  7.1 0.0 copy-done
  7.1 0.0 copy-done.1
  7.1 0.0 copy-done.2
  7.1 1.3 %shard_map.87 = (bf16[256,256]{1,0:T(8,128)(2,1)S(1)}, bf16[256,256]{1,0:T(8,128)(2,1)S(1)}, bf16[256,256]{1,0:T(8,128)(2,1)S(1)}, bf16[256,256]{1,0:T(8,128)(2,1)S(1)}) custom-call(s32[2]{0:T(128)S(1)} %pad_add_fusion.refs_0_, bf16[128,1024]{1,0:T(8,128)(2,1)S(1)} %copy-done.1, bf16[128,1024]{1,0:T(8,128)(2,1)S(1)} %copy-done.2, ...), custom_call_target="tpu_custom_call" | custom-call | flops 6000000000 | bytes 4980744 | tf_op jit(solution)/shard_map/pallas_call | solution.py:55
  8.4 2.0 %collective-permute-start.4 = (bf16[256,256]{1,0:T(8,128)(2,1)S(1)}, bf16[256,256]{1,0:T(8,128)(2,1)S(1)}, u32[]{:S(2)}, u32[]{:S(2)}) collective-permute-start(bf16[256,256]{1,0:T(8,128)(2,1)S(1)} %get-tuple-element.62), channel_id=1, source_target_pairs={{0,2},{2,0},{4,6},{6,4},{8,10},{10,8},{12,14},{14,12},{16,18},{18,... | collective-permute-start | bytes 393224 | tf_op jit(solution)/shard_map/ppermute | solution.py:22
  10.4 1.2 %shard_map.86.refs_1_ = bf16[1024,2048]{1,0:T(8,128)(2,1)S(1)} custom-call(bf16[2048,1024]{1,0:T(8,128)(2,1)S(1)} %copy-done), custom_call_target="tpu_custom_call" | custom-call | tf_op jit(solution)/shard_map/pallas_call | solution.py:55
  11.6 1.6 %collective-permute-start.5 = (bf16[256,256]{1,0:T(8,128)(2,1)S(1)}, bf16[256,256]{1,0:T(8,128)(2,1)S(1)}, u32[]{:S(2)}, u32[]{:S(2)}) collective-permute-start(bf16[256,256]{1,0:T(8,128)(2,1)S(1)} %get-tuple-element.65), channel_id=1, source_target_pairs={{0,4},{2,6},{4,0},{6,2},{8,12},{10,14},{12,8},{14,10},{16,20},{18,... | collective-permute-start | bytes 393224 | tf_op jit(solution)/shard_map/ppermute | solution.py:22
  13.2 0.0 collective-permute-done.refs_1_
  13.2 0.1 collective-permute-start.6
  13.3 0.1 collective-permute-done.1.refs_2_
  13.4 1.0 %collective-permute-done.2.refs_3_ = bf16[256,256]{1,0:T(8,128)(2,1)S(1)} collective-permute-done((bf16[256,256]{1,0:T(8,128)(2,1)S(1)}, bf16[256,256]{1,0:T(8,128)(2,1)S(1)}, u32[]{:S(2)}, u32[]{:S(2)}) %collective-permute-start.2) | collective-permute-done | bytes 131104 | tf_op jit(solution)/shard_map/ppermute | solution.py:22
  14.4 1.3 %collective-permute-done.4.refs_5_ = bf16[256,256]{1,0:T(8,128)(2,1)S(1)} collective-permute-done((bf16[256,256]{1,0:T(8,128)(2,1)S(1)}, bf16[256,256]{1,0:T(8,128)(2,1)S(1)}, u32[]{:S(2)}, u32[]{:S(2)}) %collective-permute-start.4) | collective-permute-done | bytes 131104 | tf_op jit(solution)/shard_map/ppermute | solution.py:22
  15.7 0.3 shard_map.88
  16.0 2.2 %collective-permute-start.7 = (bf16[256,256]{1,0:T(8,128)(2,1)S(1)}, bf16[256,256]{1,0:T(8,128)(2,1)S(1)}, u32[]{:S(2)}, u32[]{:S(2)}) collective-permute-start(bf16[256,256]{1,0:T(8,128)(2,1)S(1)} %get-tuple-element.71), channel_id=1, source_target_pairs={{0,8},{2,10},{4,12},{6,14},{8,0},{10,2},{12,4},{14,6},{16,24},{18,... | collective-permute-start | bytes 393224 | tf_op jit(solution)/shard_map/ppermute | solution.py:22
  18.2 2.5 %collective-permute-start.9 = (bf16[128,256]{1,0:T(8,128)(2,1)S(1)}, bf16[128,256]{1,0:T(8,128)(2,1)S(1)}, u32[]{:S(2)}, u32[]{:S(2)}) collective-permute-start(bf16[128,256]{1,0:T(8,128)(2,1)S(1)} %get-tuple-element.72), channel_id=1, source_target_pairs={{0,24},{2,26},{4,28},{6,30},{8,16},{10,18},{12,20},{14,22},{16,8},... | collective-permute-start | bytes 196616 | tf_op jit(solution)/shard_map/ppermute | solution.py:22
  20.6 0.1 collective-permute-start.8
  20.8 0.0 collective-permute-done.5.refs_6_
  20.8 0.0 collective-permute-done.6.refs_7_
  20.8 4.3 %collective-permute-done.9.refs_10_ = bf16[128,256]{1,0:T(8,128)(2,1)S(1)} collective-permute-done((bf16[128,256]{1,0:T(8,128)(2,1)S(1)}, bf16[128,256]{1,0:T(8,128)(2,1)S(1)}, u32[]{:S(2)}, u32[]{:S(2)}) %collective-permute-start.9) | collective-permute-done | bytes 65568 | tf_op jit(solution)/shard_map/ppermute | solution.py:22
  25.1 1.4 %collective-permute-done.8.refs_9_ = bf16[128,256]{1,0:T(8,128)(2,1)S(1)} collective-permute-done((bf16[128,256]{1,0:T(8,128)(2,1)S(1)}, bf16[128,256]{1,0:T(8,128)(2,1)S(1)}, u32[]{:S(2)}, u32[]{:S(2)}) %collective-permute-start.8) | collective-permute-done | bytes 65568 | tf_op jit(solution)/shard_map/ppermute | solution.py:22
  26.5 0.0 collective-permute-done.7.refs_8_
  26.5 2.3 %shard_map.89 = (bf16[256,256]{1,0:T(8,128)(2,1)S(1)}, bf16[128,256]{1,0:T(8,128)(2,1)S(1)}, bf16[128,256]{1,0:T(8,128)(2,1)S(1)}, bf16[2,640,256]{2,1,0:T(8,128...) custom-call(bf16[256,256]{1,0:T(8,128)(2,1)S(1)} %get-tuple-element., ...), custom_call_target="tpu_custom_call" | custom-call | flops 503316480 | bytes 1310720 | tf_op jit(solution)/shard_map/pallas_call | solution.py:55
  28.8 0.5 %collective-permute-start.13 = (bf16[128,256]{1,0:T(8,128)(2,1)S(1)}, bf16[128,256]{1,0:T(8,128)(2,1)S(1)}, u32[]{:S(2)}, u32[]{:S(2)}) collective-permute-start(bf16[128,256]{1,0:T(8,128)(2,1)S(1)} %get-tuple-element.86), channel_id=1, source_target_pairs={{0,16},{2,18},{4,20},{6,22},{8,24},{10,26},{12,28},{14,30},{16,0},... | collective-permute-start | bytes 196616 | tf_op jit(solution)/shard_map/ppermute | solution.py:22
  29.3 1.9 %collective-permute-start.14 = (bf16[128,256]{1,0:T(8,128)(2,1)S(1)}, bf16[128,256]{1,0:T(8,128)(2,1)S(1)}, u32[]{:S(2)}, u32[]{:S(2)}) collective-permute-start(bf16[128,256]{1,0:T(8,128)(2,1)S(1)} %get-tuple-element.87), channel_id=1, source_target_pairs={{0,24},{2,26},{4,28},{6,30},{8,16},{10,18},{12,20},{14,22},{16,8},... | collective-permute-start | bytes 196616 | tf_op jit(solution)/shard_map/ppermute | solution.py:22
  31.3 1.1 %collective-permute-start.12 = (bf16[256,256]{1,0:T(8,128)(2,1)S(1)}, bf16[256,256]{1,0:T(8,128)(2,1)S(1)}, u32[]{:S(2)}, u32[]{:S(2)}) collective-permute-start(bf16[256,256]{1,0:T(8,128)(2,1)S(1)} %get-tuple-element.85), channel_id=1, source_target_pairs={{0,8},{2,10},{4,12},{6,14},{8,0},{10,2},{12,4},{14,6},{16,24},{18,... | collective-permute-start | bytes 393224 | tf_op jit(solution)/shard_map/ppermute | solution.py:22
  32.4 0.8 %shard_map.90 = (bf16[256,256]{1,0:T(8,128)(2,1)S(1)}, bf16[256,256]{1,0:T(8,128)(2,1)S(1)}, bf16[256,256]{1,0:T(8,128)(2,1)S(1)}, bf16[256,256]{1,0:T(8,128)(2,1)S(1)}) custom-call(bf16[2,640,256]{2,1,0:T(8,128)(2,1)S(1)} %get-tuple-element.73.refs_0_, bf16[2,640,256]{2,1,0:T(8,128)(2,1)S(1)} %get-tuple-element.74.refs_1_, ...), custom_call_target="tpu_custom_call" | custom-call | flops 6000000000 | bytes 4456448 | tf_op jit(solution)/shard_map/pallas_call | solution.py:55
  33.2 1.6 %collective-permute-start.10 = (bf16[256,256]{1,0:T(8,128)(2,1)S(1)}, bf16[256,256]{1,0:T(8,128)(2,1)S(1)}, u32[]{:S(2)}, u32[]{:S(2)}) collective-permute-start(bf16[256,256]{1,0:T(8,128)(2,1)S(1)} %get-tuple-element.79), channel_id=1, source_target_pairs={{0,4},{2,6},{4,0},{6,2},{8,12},{10,14},{12,8},{14,10},{16,20},{18,... | collective-permute-start | bytes 393224 | tf_op jit(solution)/shard_map/ppermute | solution.py:22
  34.8 1.5 %collective-permute-start.11 = (bf16[256,256]{1,0:T(8,128)(2,1)S(1)}, bf16[256,256]{1,0:T(8,128)(2,1)S(1)}, u32[]{:S(2)}, u32[]{:S(2)}) collective-permute-start(bf16[256,256]{1,0:T(8,128)(2,1)S(1)} %get-tuple-element.80), channel_id=1, source_target_pairs={{0,2},{2,0},{4,6},{6,4},{8,10},{10,8},{12,14},{14,12},{16,18},{18,... | collective-permute-start | bytes 393224 | tf_op jit(solution)/shard_map/ppermute | solution.py:22
  36.3 0.9 %shard_map.91 = (f32[512,256]{1,0:T(8,128)S(1)}, f32[512,256]{1,0:T(8,128)S(1)}) custom-call(bf16[2,256,256]{2,1,0:T(8,128)(2,1)S(1)} %get-tuple-element.82.refs_0_, bf16[2,256,256]{2,1,0:T(8,128)(2,1)S(1)} %get-tuple-element.83.refs_1_, bf16[4,256,640]{2,1,0:T(8,128)(2,1)S(1)} %get-tuple-element.75.refs_2_, bf16[4,256,640]{2,1,0:T(8,128)(2,1)S(1)} %get-tuple-element.76.refs_3_), custom_call_target="tpu_custom_call" | custom-call | flops 335544320 | bytes 3145728 | tf_op jit(solution)/shard_map/pallas_call | solution.py:55
  37.2 0.0 collective-permute-done.13.refs_3_
  37.2 0.0 collective-permute-done.14.refs_4_
  37.2 0.0 collective-permute-done.12.refs_2_
  37.3 2.1 %collective-permute-start.15 = (bf16[256,256]{1,0:T(8,128)(2,1)S(1)}, bf16[256,256]{1,0:T(8,128)(2,1)S(1)}, u32[]{:S(2)}, u32[]{:S(2)}) collective-permute-start(bf16[256,256]{1,0:T(8,128)(2,1)S(1)} %get-tuple-element.88), channel_id=1, source_target_pairs={{0,6},{2,4},{4,2},{6,0},{8,14},{10,12},{12,10},{14,8},{16,22},{18,... | collective-permute-start | bytes 393224 | tf_op jit(solution)/shard_map/ppermute | solution.py:22
  39.3 0.4 shard_map.92
  39.7 0.6 %collective-permute-start.18 = (bf16[256,256]{1,0:T(8,128)(2,1)S(1)}, bf16[256,256]{1,0:T(8,128)(2,1)S(1)}, u32[]{:S(2)}, u32[]{:S(2)}) collective-permute-start(bf16[256,256]{1,0:T(8,128)(2,1)S(1)} %get-tuple-element.95), channel_id=1, source_target_pairs={{0,2},{2,0},{4,6},{6,4},{8,10},{10,8},{12,14},{14,12},{16,18},{18,... | collective-permute-start | bytes 393224 | tf_op jit(solution)/shard_map/ppermute | solution.py:22
  40.3 0.9 %collective-permute-start.17 = (bf16[256,256]{1,0:T(8,128)(2,1)S(1)}, bf16[256,256]{1,0:T(8,128)(2,1)S(1)}, u32[]{:S(2)}, u32[]{:S(2)}) collective-permute-start(bf16[256,256]{1,0:T(8,128)(2,1)S(1)} %get-tuple-element.96), channel_id=1, source_target_pairs={{0,4},{2,6},{4,0},{6,2},{8,12},{10,14},{12,8},{14,10},{16,20},{18,... | collective-permute-start | bytes 393224 | tf_op jit(solution)/shard_map/ppermute | solution.py:22
  41.2 0.0 collective-permute-done.10.refs_3_.refs_4_
  41.2 2.0 %collective-permute-start.19 = (bf16[256,256]{1,0:T(8,128)(2,1)S(1)}, bf16[256,256]{1,0:T(8,128)(2,1)S(1)}, u32[]{:S(2)}, u32[]{:S(2)}) collective-permute-start(bf16[256,256]{1,0:T(8,128)(2,1)S(1)} %get-tuple-element.97), channel_id=1, source_target_pairs={{0,6},{2,4},{4,2},{6,0},{8,14},{10,12},{12,10},{14,8},{16,22},{18,... | collective-permute-start | bytes 393224 | tf_op jit(solution)/shard_map/ppermute | solution.py:22
  43.3 0.0 collective-permute-done.11.refs_4_.refs_5_
  43.3 1.5 %collective-permute-done.15.refs_5_.refs_6_ = bf16[256,256]{1,0:T(8,128)(2,1)S(1)} collective-permute-done((bf16[256,256]{1,0:T(8,128)(2,1)S(1)}, bf16[256,256]{1,0:T(8,128)(2,1)S(1)}, u32[]{:S(2)}, u32[]{:S(2)}) %collective-permute-start.15) | collective-permute-done | bytes 131104 | tf_op jit(solution)/shard_map/ppermute | solution.py:22
  44.7 1.0 %shard_map.93 = (bf16[128,1024]{1,0:T(8,128)(2,1)S(1)}, bf16[128,1024]{1,0:T(8,128)(2,1)S(1)}) custom-call(s32[2]{0:T(128)S(1)} %pad_add_fusion.refs_0_, bf16[1024,2048]{1,0:T(8,128)(2,1)S(1)} %shard_map.86.refs_1_, bf16[256,256]{1,0:T(8,128)(2,1)S(1)} %get-tuple-element.98.refs_2_.refs_3_, bf16[256,256]{1,0:T(8,128)(2,1)S(1)} %collective-permute-done.10.refs_3_.refs_4_, ...), custom_call_target="tpu_custom_call" | custom-call | flops 268435456 | bytes 4718600 | tf_op jit(solution)/shard_map/pallas_call | solution.py:55
  45.8 0.1 collective-permute-start.16
  45.8 1.0 %shard_map.94 = (f32[128,1024]{1,0:T(8,128)S(1)}, bf16[128,1024]{1,0:T(8,128)(2,1)S(1)}) custom-call(s32[2]{0:T(128)S(1)} %pad_add_fusion.refs_0_, bf16[1024,2048]{1,0:T(8,128)(2,1)S(1)} %shard_map.86.refs_1_, bf16[128,1024]{1,0:T(8,128)(2,1)S(1)} %get-tuple-element.102.refs_2_, bf16[256,256]{1,0:T(8,128)(2,1)S(1)} %get-tuple-element.98.refs_2_.refs_3_, ...), custom_call_target="tpu_custom_call" | custom-call | flops 4000000000 | bytes 4980744 | tf_op jit(solution)/shard_map/pallas_call | solution.py:55
  46.9 0.5 %collective-permute-done.16.refs_0_ = bf16[128,1024]{1,0:T(8,128)(2,1)S(1)} collective-permute-done((bf16[128,1024]{1,0:T(8,128)(2,1)S(1)}, bf16[128,1024]{1,0:T(8,128)(2,1)S(1)}, u32[]{:S(2)}, u32[]{:S(2)}) %collective-permute-start.16) | collective-permute-done | bytes 262176 | tf_op jit(solution)/shard_map/ppermute | solution.py:26
  47.4 0.1 shard_map.95.refs_1_
  47.4 0.0 collective-permute-done.18.refs_5_
  47.4 0.0 collective-permute-done.17.refs_4_
  47.4 0.2 collective-permute-done.19.refs_6_
  47.6 1.5 %shard_map.96 = (bf16[128,1024]{1,0:T(8,128)(2,1)}, bf16[128,1024]{1,0:T(8,128)(2,1)}, bf16[128,1024]{1,0:T(8,128)(2,1)}, bf16[128,1024]{1,0:T(8,128)(2,1)}) custom-call(s32[2]{0:T(128)S(1)} %pad_add_fusion.refs_0_, bf16[128,1024]{1,0:T(8,128)(2,1)S(1)} %shard_map.95.refs_1_, bf16[128,1024]{1,0:T(8,128)(2,1)S(1)} %get-tuple-element.105.refs_2_, ...), custom_call_target="tpu_custom_call" | custom-call | bytes 1048584 | tf_op jit(solution)/shard_map/pallas_call | solution.py:55
Async XLA Ops:
  0.6 6.4 %collective-permute-start.3 = (bf16[128,1024]{1,0:T(8,128)(2,1)}, bf16[128,1024]{1,0:T(8,128)(2,1)S(1)}, u32[]{:S(2)}, u32[]{:S(2)}) collective-permute-start(bf16[128,1024]{1,0:T(8,128)(2,1)} %refs_2_.1), channel_id=1, source_target_pairs={{0,1},{1,0},{2,3},{3,2},{4,5},{5,4},{6,7},{7,6},{8,9},{9,8},{10,11... | collective-permute-start | bytes 786440 | tf_op jit(solution)/shard_map/ppermute | solution.py:26
  2.3 4.8 %copy-start = (bf16[2048,1024]{1,0:T(8,128)(2,1)S(1)}, bf16[2048,1024]{1,0:T(8,128)(2,1)}, u32[]{:S(2)}) copy-start(bf16[2048,1024]{1,0:T(8,128)(2,1)} %refs_3_.1) | copy-start | bytes 12582916
  2.3 4.8 %copy-start.1 = (bf16[128,1024]{1,0:T(8,128)(2,1)S(1)}, bf16[128,1024]{1,0:T(8,128)(2,1)}, u32[]{:S(2)}) copy-start(bf16[128,1024]{1,0:T(8,128)(2,1)} %refs_1_.3) | copy-start | bytes 786436
  2.3 4.8 %copy-start.2 = (bf16[128,1024]{1,0:T(8,128)(2,1)S(1)}, bf16[128,1024]{1,0:T(8,128)(2,1)}, u32[]{:S(2)}) copy-start(bf16[128,1024]{1,0:T(8,128)(2,1)} %refs_2_.1) | copy-start | bytes 786436
  2.9 10.3 %collective-permute-start = (bf16[256,256]{1,0:T(8,128)(2,1)S(1)}, bf16[256,256]{1,0:T(8,128)(2,1)S(1)}, u32[]{:S(2)}, u32[]{:S(2)}) collective-permute-start(bf16[256,256]{1,0:T(8,128)(2,1)S(1)} %get-tuple-element.58), channel_id=1, source_target_pairs={{0,2},{2,0},{4,6},{6,4},{8,10},{10,8},{12,14},{14,12},{16,18},{18,... | collective-permute-start | bytes 393224 | tf_op jit(solution)/shard_map/ppermute | solution.py:22
  5.5 7.9 %collective-permute-start.1 = (bf16[256,256]{1,0:T(8,128)(2,1)S(1)}, bf16[256,256]{1,0:T(8,128)(2,1)S(1)}, u32[]{:S(2)}, u32[]{:S(2)}) collective-permute-start(bf16[256,256]{1,0:T(8,128)(2,1)S(1)} %get-tuple-element.59), channel_id=1, source_target_pairs={{0,4},{2,6},{4,0},{6,2},{8,12},{10,14},{12,8},{14,10},{16,20},{18,... | collective-permute-start | bytes 393224 | tf_op jit(solution)/shard_map/ppermute | solution.py:22
  7.0 7.4 %collective-permute-start.2 = (bf16[256,256]{1,0:T(8,128)(2,1)S(1)}, bf16[256,256]{1,0:T(8,128)(2,1)S(1)}, u32[]{:S(2)}, u32[]{:S(2)}) collective-permute-start(bf16[256,256]{1,0:T(8,128)(2,1)S(1)} %get-tuple-element.60), channel_id=1, source_target_pairs={{0,6},{2,4},{4,2},{6,0},{8,14},{10,12},{12,10},{14,8},{16,22},{18,... | collective-permute-start | bytes 393224 | tf_op jit(solution)/shard_map/ppermute | solution.py:22
  8.4 7.3 %collective-permute-start.4 = (bf16[256,256]{1,0:T(8,128)(2,1)S(1)}, bf16[256,256]{1,0:T(8,128)(2,1)S(1)}, u32[]{:S(2)}, u32[]{:S(2)}) collective-permute-start(bf16[256,256]{1,0:T(8,128)(2,1)S(1)} %get-tuple-element.62), channel_id=1, source_target_pairs={{0,2},{2,0},{4,6},{6,4},{8,10},{10,8},{12,14},{14,12},{16,18},{18,... | collective-permute-start | bytes 393224 | tf_op jit(solution)/shard_map/ppermute | solution.py:22
  11.6 9.1 %collective-permute-start.5 = (bf16[256,256]{1,0:T(8,128)(2,1)S(1)}, bf16[256,256]{1,0:T(8,128)(2,1)S(1)}, u32[]{:S(2)}, u32[]{:S(2)}) collective-permute-start(bf16[256,256]{1,0:T(8,128)(2,1)S(1)} %get-tuple-element.65), channel_id=1, source_target_pairs={{0,4},{2,6},{4,0},{6,2},{8,12},{10,14},{12,8},{14,10},{16,20},{18,... | collective-permute-start | bytes 393224 | tf_op jit(solution)/shard_map/ppermute | solution.py:22
  13.2 7.5 %collective-permute-start.6 = (bf16[256,256]{1,0:T(8,128)(2,1)S(1)}, bf16[256,256]{1,0:T(8,128)(2,1)S(1)}, u32[]{:S(2)}, u32[]{:S(2)}) collective-permute-start(bf16[256,256]{1,0:T(8,128)(2,1)S(1)} %get-tuple-element.66), channel_id=1, source_target_pairs={{0,6},{2,4},{4,2},{6,0},{8,14},{10,12},{12,10},{14,8},{16,22},{18,... | collective-permute-start | bytes 393224 | tf_op jit(solution)/shard_map/ppermute | solution.py:22
  16.0 10.5 %collective-permute-start.7 = (bf16[256,256]{1,0:T(8,128)(2,1)S(1)}, bf16[256,256]{1,0:T(8,128)(2,1)S(1)}, u32[]{:S(2)}, u32[]{:S(2)}) collective-permute-start(bf16[256,256]{1,0:T(8,128)(2,1)S(1)} %get-tuple-element.71), channel_id=1, source_target_pairs={{0,8},{2,10},{4,12},{6,14},{8,0},{10,2},{12,4},{14,6},{16,24},{18,... | collective-permute-start | bytes 393224 | tf_op jit(solution)/shard_map/ppermute | solution.py:22
  18.2 6.9 %collective-permute-start.9 = (bf16[128,256]{1,0:T(8,128)(2,1)S(1)}, bf16[128,256]{1,0:T(8,128)(2,1)S(1)}, u32[]{:S(2)}, u32[]{:S(2)}) collective-permute-start(bf16[128,256]{1,0:T(8,128)(2,1)S(1)} %get-tuple-element.72), channel_id=1, source_target_pairs={{0,24},{2,26},{4,28},{6,30},{8,16},{10,18},{12,20},{14,22},{16,8},... | collective-permute-start | bytes 196616 | tf_op jit(solution)/shard_map/ppermute | solution.py:22
  20.6 5.9 %collective-permute-start.8 = (bf16[128,256]{1,0:T(8,128)(2,1)S(1)}, bf16[128,256]{1,0:T(8,128)(2,1)S(1)}, u32[]{:S(2)}, u32[]{:S(2)}) collective-permute-start(bf16[128,256]{1,0:T(8,128)(2,1)S(1)} %get-tuple-element.72), channel_id=1, source_target_pairs={{0,16},{2,18},{4,20},{6,22},{8,24},{10,26},{12,28},{14,30},{16,0},... | collective-permute-start | bytes 196616 | tf_op jit(solution)/shard_map/ppermute | solution.py:22
  28.8 8.4 %collective-permute-start.13 = (bf16[128,256]{1,0:T(8,128)(2,1)S(1)}, bf16[128,256]{1,0:T(8,128)(2,1)S(1)}, u32[]{:S(2)}, u32[]{:S(2)}) collective-permute-start(bf16[128,256]{1,0:T(8,128)(2,1)S(1)} %get-tuple-element.86), channel_id=1, source_target_pairs={{0,16},{2,18},{4,20},{6,22},{8,24},{10,26},{12,28},{14,30},{16,0},... | collective-permute-start | bytes 196616 | tf_op jit(solution)/shard_map/ppermute | solution.py:22
  29.3 7.9 %collective-permute-start.14 = (bf16[128,256]{1,0:T(8,128)(2,1)S(1)}, bf16[128,256]{1,0:T(8,128)(2,1)S(1)}, u32[]{:S(2)}, u32[]{:S(2)}) collective-permute-start(bf16[128,256]{1,0:T(8,128)(2,1)S(1)} %get-tuple-element.87), channel_id=1, source_target_pairs={{0,24},{2,26},{4,28},{6,30},{8,16},{10,18},{12,20},{14,22},{16,8},... | collective-permute-start | bytes 196616 | tf_op jit(solution)/shard_map/ppermute | solution.py:22
  31.3 6.0 %collective-permute-start.12 = (bf16[256,256]{1,0:T(8,128)(2,1)S(1)}, bf16[256,256]{1,0:T(8,128)(2,1)S(1)}, u32[]{:S(2)}, u32[]{:S(2)}) collective-permute-start(bf16[256,256]{1,0:T(8,128)(2,1)S(1)} %get-tuple-element.85), channel_id=1, source_target_pairs={{0,8},{2,10},{4,12},{6,14},{8,0},{10,2},{12,4},{14,6},{16,24},{18,... | collective-permute-start | bytes 393224 | tf_op jit(solution)/shard_map/ppermute | solution.py:22
  33.2 8.0 %collective-permute-start.10 = (bf16[256,256]{1,0:T(8,128)(2,1)S(1)}, bf16[256,256]{1,0:T(8,128)(2,1)S(1)}, u32[]{:S(2)}, u32[]{:S(2)}) collective-permute-start(bf16[256,256]{1,0:T(8,128)(2,1)S(1)} %get-tuple-element.79), channel_id=1, source_target_pairs={{0,4},{2,6},{4,0},{6,2},{8,12},{10,14},{12,8},{14,10},{16,20},{18,... | collective-permute-start | bytes 393224 | tf_op jit(solution)/shard_map/ppermute | solution.py:22
  34.8 8.4 %collective-permute-start.11 = (bf16[256,256]{1,0:T(8,128)(2,1)S(1)}, bf16[256,256]{1,0:T(8,128)(2,1)S(1)}, u32[]{:S(2)}, u32[]{:S(2)}) collective-permute-start(bf16[256,256]{1,0:T(8,128)(2,1)S(1)} %get-tuple-element.80), channel_id=1, source_target_pairs={{0,2},{2,0},{4,6},{6,4},{8,10},{10,8},{12,14},{14,12},{16,18},{18,... | collective-permute-start | bytes 393224 | tf_op jit(solution)/shard_map/ppermute | solution.py:22
  37.3 7.5 %collective-permute-start.15 = (bf16[256,256]{1,0:T(8,128)(2,1)S(1)}, bf16[256,256]{1,0:T(8,128)(2,1)S(1)}, u32[]{:S(2)}, u32[]{:S(2)}) collective-permute-start(bf16[256,256]{1,0:T(8,128)(2,1)S(1)} %get-tuple-element.88), channel_id=1, source_target_pairs={{0,6},{2,4},{4,2},{6,0},{8,14},{10,12},{12,10},{14,8},{16,22},{18,... | collective-permute-start | bytes 393224 | tf_op jit(solution)/shard_map/ppermute | solution.py:22
  39.7 7.7 %collective-permute-start.18 = (bf16[256,256]{1,0:T(8,128)(2,1)S(1)}, bf16[256,256]{1,0:T(8,128)(2,1)S(1)}, u32[]{:S(2)}, u32[]{:S(2)}) collective-permute-start(bf16[256,256]{1,0:T(8,128)(2,1)S(1)} %get-tuple-element.95), channel_id=1, source_target_pairs={{0,2},{2,0},{4,6},{6,4},{8,10},{10,8},{12,14},{14,12},{16,18},{18,... | collective-permute-start | bytes 393224 | tf_op jit(solution)/shard_map/ppermute | solution.py:22
  40.3 7.1 %collective-permute-start.17 = (bf16[256,256]{1,0:T(8,128)(2,1)S(1)}, bf16[256,256]{1,0:T(8,128)(2,1)S(1)}, u32[]{:S(2)}, u32[]{:S(2)}) collective-permute-start(bf16[256,256]{1,0:T(8,128)(2,1)S(1)} %get-tuple-element.96), channel_id=1, source_target_pairs={{0,4},{2,6},{4,0},{6,2},{8,12},{10,14},{12,8},{14,10},{16,20},{18,... | collective-permute-start | bytes 393224 | tf_op jit(solution)/shard_map/ppermute | solution.py:22
  41.2 6.4 %collective-permute-start.19 = (bf16[256,256]{1,0:T(8,128)(2,1)S(1)}, bf16[256,256]{1,0:T(8,128)(2,1)S(1)}, u32[]{:S(2)}, u32[]{:S(2)}) collective-permute-start(bf16[256,256]{1,0:T(8,128)(2,1)S(1)} %get-tuple-element.97), channel_id=1, source_target_pairs={{0,6},{2,4},{4,2},{6,0},{8,14},{10,12},{12,10},{14,8},{16,22},{18,... | collective-permute-start | bytes 393224 | tf_op jit(solution)/shard_map/ppermute | solution.py:22
  45.8 1.6 %collective-permute-start.16 = (bf16[128,1024]{1,0:T(8,128)(2,1)S(1)}, bf16[128,1024]{1,0:T(8,128)(2,1)S(1)}, u32[]{:S(2)}, u32[]{:S(2)}) collective-permute-start(bf16[128,1024]{1,0:T(8,128)(2,1)S(1)} %get-tuple-element.104), channel_id=1, source_target_pairs={{0,1},{1,0},{2,3},{3,2},{4,5},{5,4},{6,7},{7,6},{8,9},{9,8},{10,11... | collective-permute-start | bytes 786440 | tf_op jit(solution)/shard_map/ppermute | solution.py:26

commit v10 on v9

--- a/solution.py
+++ b/solution.py
@@ -9,7 +9,7 @@
 
 HDIM = 128
 ORDER = (0, 1, 2, 3)
-BACK = (0, 2, 1, 3)
+BACK = (0, 3, 1, 2)
 BLOCK = 128
 BF16 = jnp.bfloat16
 F32 = jnp.float32

time: 49.3 us -> 48.8 us (0.990)
  starting transfers between devices: 25.4 us -> 24.8 us
    ppermute x18, starting transfers between devices: 24.8 us -> 24.2 us  [swap_seq(): lax.ppermute(array, 'seq', [(i, i ^ mask) for i in range(lax.axis_size('s...]
  transfers between devices with their start and end apart: 20 -> 20, of which waited for: 8 -> 9; matrix products, arithmetic and copies ran while one was open for 0% -> 0% of each run, Pallas kernels for 18% -> 18%
where the time goes in v10:
time: 48.8 us; the launch traced here: 48.6 us
  starting transfers between devices  24.8 us (51%)
  Pallas kernels  12.5 us (26%)
  waiting for transfers between devices  10.4 us (21%)
  between operations  0.81 us (2%)
    ppermute x18, starting transfers between devices, swap_seq(): lax.ppermute(array, 'seq', [(i, i ^ mask) for i in range(lax.axis_size('s...  24.2 us
    pallas_call x13, Pallas kernels, call(): pl.pallas_call(kernel, out_shape=out_shape, in_specs=specs, out_specs=jax...  12.5 us
    ppermute x18, waiting for transfers between devices, swap_seq(): lax.ppermute(array, 'seq', [(i, i ^ mask) for i in range(lax.axis_size('s...  9.94 us
  transfers between devices with their start and end apart: 20, of which 9 were waited for; matrix products, arithmetic and copies ran while one was open for 0% of the time, Pallas kernels for 18%

profile of v10, /device:TPU:0, one launch (start us, length us, event | category | flops | bytes accessed | tf_op | source)
XLA Modules:
  0.0 48.6 jit_solution(5320194514271461033)
XLA Ops:
  0.6 0.5 %collective-permute-start.3 = (bf16[128,1024]{1,0:T(8,128)(2,1)}, bf16[128,1024]{1,0:T(8,128)(2,1)S(1)}, u32[]{:S(2)}, u32[]{:S(2)}) collective-permute-start(bf16[128,1024]{1,0:T(8,128)(2,1)} %refs_2_.1), channel_id=1, source_target_pairs={{0,1},{1,0},{2,3},{3,2},{4,5},{5,4},{6,7},{7,6},{8,9},{9,8},{10,11... | collective-permute-start | bytes 786440 | tf_op jit(solution)/shard_map/ppermute | solution.py:26
  1.1 0.1 pad_add_fusion.refs_0_
  1.2 1.0 %shard_map.84 = (bf16[128,1024]{1,0:T(8,128)(2,1)S(1)}, bf16[128,1024]{1,0:T(8,128)(2,1)S(1)}) custom-call(bf16[128,1024]{1,0:T(8,128)(2,1)} %refs_0_.1, bf16[128,1024]{1,0:T(8,128)(2,1)} %refs_1_.2), custom_call_target="tpu_custom_call" | custom-call | bytes 524288 | tf_op jit(solution)/shard_map/pallas_call | solution.py:55
  2.3 0.0 copy-start
  2.3 0.0 copy-start.1
  2.3 0.0 copy-start.2
  2.3 0.6 %shard_map.85 = (bf16[256,256]{1,0:T(8,128)(2,1)S(1)}, bf16[256,256]{1,0:T(8,128)(2,1)S(1)}, bf16[256,256]{1,0:T(8,128)(2,1)S(1)}, bf16[256,256]{1,0:T(8,128)(2,1)S(1)}) custom-call(s32[2]{0:T(128)S(1)} %pad_add_fusion.refs_0_, bf16[128,1024]{1,0:T(8,128)(2,1)S(1)} %get-tuple-element.55.refs_1_, bf16[128,1024]{1,0:T(8,128)(2,1)S(1)} %get-tuple-element.56.refs_2_), custom_call_target="tpu_custom_call" | custom-call | flops 6000000000 | bytes 524296 | tf_op jit(solution)/shard_map/pallas_call | solution.py:55
  2.9 2.6 %collective-permute-start = (bf16[256,256]{1,0:T(8,128)(2,1)S(1)}, bf16[256,256]{1,0:T(8,128)(2,1)S(1)}, u32[]{:S(2)}, u32[]{:S(2)}) collective-permute-start(bf16[256,256]{1,0:T(8,128)(2,1)S(1)} %get-tuple-element.58), channel_id=1, source_target_pairs={{0,2},{2,0},{4,6},{6,4},{8,10},{10,8},{12,14},{14,12},{16,18},{18,... | collective-permute-start | bytes 393224 | tf_op jit(solution)/shard_map/ppermute | solution.py:22
  5.5 1.5 %collective-permute-start.1 = (bf16[256,256]{1,0:T(8,128)(2,1)S(1)}, bf16[256,256]{1,0:T(8,128)(2,1)S(1)}, u32[]{:S(2)}, u32[]{:S(2)}) collective-permute-start(bf16[256,256]{1,0:T(8,128)(2,1)S(1)} %get-tuple-element.59), channel_id=1, source_target_pairs={{0,4},{2,6},{4,0},{6,2},{8,12},{10,14},{12,8},{14,10},{16,20},{18,... | collective-permute-start | bytes 393224 | tf_op jit(solution)/shard_map/ppermute | solution.py:22
  7.0 0.0 collective-permute-start.2
  7.1 0.0 collective-permute-done.3.refs_4_
  7.1 0.0 copy-done
  7.1 0.0 copy-done.1
  7.1 0.0 copy-done.2
  7.1 1.3 %shard_map.87 = (bf16[256,256]{1,0:T(8,128)(2,1)S(1)}, bf16[256,256]{1,0:T(8,128)(2,1)S(1)}, bf16[256,256]{1,0:T(8,128)(2,1)S(1)}, bf16[256,256]{1,0:T(8,128)(2,1)S(1)}) custom-call(s32[2]{0:T(128)S(1)} %pad_add_fusion.refs_0_, bf16[128,1024]{1,0:T(8,128)(2,1)S(1)} %copy-done.1, bf16[128,1024]{1,0:T(8,128)(2,1)S(1)} %copy-done.2, ...), custom_call_target="tpu_custom_call" | custom-call | flops 6000000000 | bytes 4980744 | tf_op jit(solution)/shard_map/pallas_call | solution.py:55
  8.4 2.0 %collective-permute-start.4 = (bf16[256,256]{1,0:T(8,128)(2,1)S(1)}, bf16[256,256]{1,0:T(8,128)(2,1)S(1)}, u32[]{:S(2)}, u32[]{:S(2)}) collective-permute-start(bf16[256,256]{1,0:T(8,128)(2,1)S(1)} %get-tuple-element.62), channel_id=1, source_target_pairs={{0,2},{2,0},{4,6},{6,4},{8,10},{10,8},{12,14},{14,12},{16,18},{18,... | collective-permute-start | bytes 393224 | tf_op jit(solution)/shard_map/ppermute | solution.py:22
  10.4 1.2 %shard_map.86.refs_1_ = bf16[1024,2048]{1,0:T(8,128)(2,1)S(1)} custom-call(bf16[2048,1024]{1,0:T(8,128)(2,1)S(1)} %copy-done), custom_call_target="tpu_custom_call" | custom-call | tf_op jit(solution)/shard_map/pallas_call | solution.py:55
  11.6 1.6 %collective-permute-start.5 = (bf16[256,256]{1,0:T(8,128)(2,1)S(1)}, bf16[256,256]{1,0:T(8,128)(2,1)S(1)}, u32[]{:S(2)}, u32[]{:S(2)}) collective-permute-start(bf16[256,256]{1,0:T(8,128)(2,1)S(1)} %get-tuple-element.65), channel_id=1, source_target_pairs={{0,4},{2,6},{4,0},{6,2},{8,12},{10,14},{12,8},{14,10},{16,20},{18,... | collective-permute-start | bytes 393224 | tf_op jit(solution)/shard_map/ppermute | solution.py:22
  13.2 0.0 collective-permute-done.refs_1_
  13.2 0.1 collective-permute-start.6
  13.3 0.1 collective-permute-done.1.refs_2_
  13.4 1.0 %collective-permute-done.2.refs_3_ = bf16[256,256]{1,0:T(8,128)(2,1)S(1)} collective-permute-done((bf16[256,256]{1,0:T(8,128)(2,1)S(1)}, bf16[256,256]{1,0:T(8,128)(2,1)S(1)}, u32[]{:S(2)}, u32[]{:S(2)}) %collective-permute-start.2) | collective-permute-done | bytes 131104 | tf_op jit(solution)/shard_map/ppermute | solution.py:22
  14.4 1.3 %collective-permute-done.4.refs_5_ = bf16[256,256]{1,0:T(8,128)(2,1)S(1)} collective-permute-done((bf16[256,256]{1,0:T(8,128)(2,1)S(1)}, bf16[256,256]{1,0:T(8,128)(2,1)S(1)}, u32[]{:S(2)}, u32[]{:S(2)}) %collective-permute-start.4) | collective-permute-done | bytes 131104 | tf_op jit(solution)/shard_map/ppermute | solution.py:22
  15.7 0.3 shard_map.88
  16.0 2.2 %collective-permute-start.7 = (bf16[256,256]{1,0:T(8,128)(2,1)S(1)}, bf16[256,256]{1,0:T(8,128)(2,1)S(1)}, u32[]{:S(2)}, u32[]{:S(2)}) collective-permute-start(bf16[256,256]{1,0:T(8,128)(2,1)S(1)} %get-tuple-element.71), channel_id=1, source_target_pairs={{0,8},{2,10},{4,12},{6,14},{8,0},{10,2},{12,4},{14,6},{16,24},{18,... | collective-permute-start | bytes 393224 | tf_op jit(solution)/shard_map/ppermute | solution.py:22
  18.2 2.5 %collective-permute-start.9 = (bf16[128,256]{1,0:T(8,128)(2,1)S(1)}, bf16[128,256]{1,0:T(8,128)(2,1)S(1)}, u32[]{:S(2)}, u32[]{:S(2)}) collective-permute-start(bf16[128,256]{1,0:T(8,128)(2,1)S(1)} %get-tuple-element.72), channel_id=1, source_target_pairs={{0,24},{2,26},{4,28},{6,30},{8,16},{10,18},{12,20},{14,22},{16,8},... | collective-permute-start | bytes 196616 | tf_op jit(solution)/shard_map/ppermute | solution.py:22
  20.6 0.1 collective-permute-start.8
  20.8 0.0 collective-permute-done.5.refs_6_
  20.8 0.0 collective-permute-done.6.refs_7_
  20.8 4.3 %collective-permute-done.9.refs_10_ = bf16[128,256]{1,0:T(8,128)(2,1)S(1)} collective-permute-done((bf16[128,256]{1,0:T(8,128)(2,1)S(1)}, bf16[128,256]{1,0:T(8,128)(2,1)S(1)}, u32[]{:S(2)}, u32[]{:S(2)}) %collective-permute-start.9) | collective-permute-done | bytes 65568 | tf_op jit(solution)/shard_map/ppermute | solution.py:22
  25.1 1.4 %collective-permute-done.8.refs_9_ = bf16[128,256]{1,0:T(8,128)(2,1)S(1)} collective-permute-done((bf16[128,256]{1,0:T(8,128)(2,1)S(1)}, bf16[128,256]{1,0:T(8,128)(2,1)S(1)}, u32[]{:S(2)}, u32[]{:S(2)}) %collective-permute-start.8) | collective-permute-done | bytes 65568 | tf_op jit(solution)/shard_map/ppermute | solution.py:22
  26.5 0.0 collective-permute-done.7.refs_8_
  26.5 2.3 %shard_map.89 = (bf16[256,256]{1,0:T(8,128)(2,1)S(1)}, bf16[128,256]{1,0:T(8,128)(2,1)S(1)}, bf16[128,256]{1,0:T(8,128)(2,1)S(1)}, bf16[2,640,256]{2,1,0:T(8,128...) custom-call(bf16[256,256]{1,0:T(8,128)(2,1)S(1)} %get-tuple-element., ...), custom_call_target="tpu_custom_call" | custom-call | flops 503316480 | bytes 1310720 | tf_op jit(solution)/shard_map/pallas_call | solution.py:55
  28.8 0.5 %collective-permute-start.13 = (bf16[128,256]{1,0:T(8,128)(2,1)S(1)}, bf16[128,256]{1,0:T(8,128)(2,1)S(1)}, u32[]{:S(2)}, u32[]{:S(2)}) collective-permute-start(bf16[128,256]{1,0:T(8,128)(2,1)S(1)} %get-tuple-element.86), channel_id=1, source_target_pairs={{0,16},{2,18},{4,20},{6,22},{8,24},{10,26},{12,28},{14,30},{16,0},... | collective-permute-start | bytes 196616 | tf_op jit(solution)/shard_map/ppermute | solution.py:22
  29.3 1.9 %collective-permute-start.14 = (bf16[128,256]{1,0:T(8,128)(2,1)S(1)}, bf16[128,256]{1,0:T(8,128)(2,1)S(1)}, u32[]{:S(2)}, u32[]{:S(2)}) collective-permute-start(bf16[128,256]{1,0:T(8,128)(2,1)S(1)} %get-tuple-element.87), channel_id=1, source_target_pairs={{0,24},{2,26},{4,28},{6,30},{8,16},{10,18},{12,20},{14,22},{16,8},... | collective-permute-start | bytes 196616 | tf_op jit(solution)/shard_map/ppermute | solution.py:22
  31.3 1.1 %collective-permute-start.12 = (bf16[256,256]{1,0:T(8,128)(2,1)S(1)}, bf16[256,256]{1,0:T(8,128)(2,1)S(1)}, u32[]{:S(2)}, u32[]{:S(2)}) collective-permute-start(bf16[256,256]{1,0:T(8,128)(2,1)S(1)} %get-tuple-element.85), channel_id=1, source_target_pairs={{0,8},{2,10},{4,12},{6,14},{8,0},{10,2},{12,4},{14,6},{16,24},{18,... | collective-permute-start | bytes 393224 | tf_op jit(solution)/shard_map/ppermute | solution.py:22
  32.4 0.8 %shard_map.90 = (bf16[256,256]{1,0:T(8,128)(2,1)S(1)}, bf16[256,256]{1,0:T(8,128)(2,1)S(1)}, bf16[256,256]{1,0:T(8,128)(2,1)S(1)}, bf16[256,256]{1,0:T(8,128)(2,1)S(1)}) custom-call(bf16[2,640,256]{2,1,0:T(8,128)(2,1)S(1)} %get-tuple-element.73.refs_0_, bf16[2,640,256]{2,1,0:T(8,128)(2,1)S(1)} %get-tuple-element.74.refs_1_, ...), custom_call_target="tpu_custom_call" | custom-call | flops 6000000000 | bytes 4456448 | tf_op jit(solution)/shard_map/pallas_call | solution.py:55
  33.2 2.5 %collective-permute-start.10 = (bf16[256,256]{1,0:T(8,128)(2,1)S(1)}, bf16[256,256]{1,0:T(8,128)(2,1)S(1)}, u32[]{:S(2)}, u32[]{:S(2)}) collective-permute-start(bf16[256,256]{1,0:T(8,128)(2,1)S(1)} %get-tuple-element.79), channel_id=1, source_target_pairs={{0,6},{2,4},{4,2},{6,0},{8,14},{10,12},{12,10},{14,8},{16,22},{18,... | collective-permute-start | bytes 393224 | tf_op jit(solution)/shard_map/ppermute | solution.py:22
  35.8 0.5 %collective-permute-start.11 = (bf16[256,256]{1,0:T(8,128)(2,1)S(1)}, bf16[256,256]{1,0:T(8,128)(2,1)S(1)}, u32[]{:S(2)}, u32[]{:S(2)}) collective-permute-start(bf16[256,256]{1,0:T(8,128)(2,1)S(1)} %get-tuple-element.80), channel_id=1, source_target_pairs={{0,2},{2,0},{4,6},{6,4},{8,10},{10,8},{12,14},{14,12},{16,18},{18,... | collective-permute-start | bytes 393224 | tf_op jit(solution)/shard_map/ppermute | solution.py:22
  36.3 0.9 %shard_map.91 = (f32[512,256]{1,0:T(8,128)S(1)}, f32[512,256]{1,0:T(8,128)S(1)}) custom-call(bf16[2,256,256]{2,1,0:T(8,128)(2,1)S(1)} %get-tuple-element.82.refs_0_, bf16[2,256,256]{2,1,0:T(8,128)(2,1)S(1)} %get-tuple-element.83.refs_1_, bf16[4,256,640]{2,1,0:T(8,128)(2,1)S(1)} %get-tuple-element.75.refs_2_, bf16[4,256,640]{2,1,0:T(8,128)(2,1)S(1)} %get-tuple-element.76.refs_3_), custom_call_target="tpu_custom_call" | custom-call | flops 335544320 | bytes 3145728 | tf_op jit(solution)/shard_map/pallas_call | solution.py:55
  37.2 0.0 collective-permute-done.13.refs_3_
  37.2 0.0 collective-permute-done.14.refs_4_
  37.2 0.0 collective-permute-done.12.refs_2_
  37.2 1.2 %collective-permute-start.15 = (bf16[256,256]{1,0:T(8,128)(2,1)S(1)}, bf16[256,256]{1,0:T(8,128)(2,1)S(1)}, u32[]{:S(2)}, u32[]{:S(2)}) collective-permute-start(bf16[256,256]{1,0:T(8,128)(2,1)S(1)} %get-tuple-element.88), channel_id=1, source_target_pairs={{0,4},{2,6},{4,0},{6,2},{8,12},{10,14},{12,8},{14,10},{16,20},{18,... | collective-permute-start | bytes 393224 | tf_op jit(solution)/shard_map/ppermute | solution.py:22
  38.4 0.4 shard_map.92
  38.8 1.6 %collective-permute-start.18 = (bf16[256,256]{1,0:T(8,128)(2,1)S(1)}, bf16[256,256]{1,0:T(8,128)(2,1)S(1)}, u32[]{:S(2)}, u32[]{:S(2)}) collective-permute-start(bf16[256,256]{1,0:T(8,128)(2,1)S(1)} %get-tuple-element.95), channel_id=1, source_target_pairs={{0,2},{2,0},{4,6},{6,4},{8,10},{10,8},{12,14},{14,12},{16,18},{18,... | collective-permute-start | bytes 393224 | tf_op jit(solution)/shard_map/ppermute | solution.py:22
  40.3 0.9 %collective-permute-start.19 = (bf16[256,256]{1,0:T(8,128)(2,1)S(1)}, bf16[256,256]{1,0:T(8,128)(2,1)S(1)}, u32[]{:S(2)}, u32[]{:S(2)}) collective-permute-start(bf16[256,256]{1,0:T(8,128)(2,1)S(1)} %get-tuple-element.96), channel_id=1, source_target_pairs={{0,4},{2,6},{4,0},{6,2},{8,12},{10,14},{12,8},{14,10},{16,20},{18,... | collective-permute-start | bytes 393224 | tf_op jit(solution)/shard_map/ppermute | solution.py:22
  41.2 0.0 collective-permute-done.10.refs_3_.refs_4_
  41.2 1.4 %collective-permute-start.17 = (bf16[256,256]{1,0:T(8,128)(2,1)S(1)}, bf16[256,256]{1,0:T(8,128)(2,1)S(1)}, u32[]{:S(2)}, u32[]{:S(2)}) collective-permute-start(bf16[256,256]{1,0:T(8,128)(2,1)S(1)} %get-tuple-element.97), channel_id=1, source_target_pairs={{0,6},{2,4},{4,2},{6,0},{8,14},{10,12},{12,10},{14,8},{16,22},{18,... | collective-permute-start | bytes 393224 | tf_op jit(solution)/shard_map/ppermute | solution.py:22
  42.7 0.1 collective-permute-done.11.refs_4_.refs_5_
  42.8 1.3 %collective-permute-done.15.refs_5_.refs_6_ = bf16[256,256]{1,0:T(8,128)(2,1)S(1)} collective-permute-done((bf16[256,256]{1,0:T(8,128)(2,1)S(1)}, bf16[256,256]{1,0:T(8,128)(2,1)S(1)}, u32[]{:S(2)}, u32[]{:S(2)}) %collective-permute-start.15) | collective-permute-done | bytes 131104 | tf_op jit(solution)/shard_map/ppermute | solution.py:22
  44.1 1.0 %shard_map.93 = (bf16[128,1024]{1,0:T(8,128)(2,1)S(1)}, bf16[128,1024]{1,0:T(8,128)(2,1)S(1)}) custom-call(s32[2]{0:T(128)S(1)} %pad_add_fusion.refs_0_, bf16[1024,2048]{1,0:T(8,128)(2,1)S(1)} %shard_map.86.refs_1_, bf16[256,256]{1,0:T(8,128)(2,1)S(1)} %get-tuple-element.98.refs_2_.refs_3_, bf16[256,256]{1,0:T(8,128)(2,1)S(1)} %collective-permute-done.10.refs_3_.refs_4_, ...), custom_call_target="tpu_custom_call" | custom-call | flops 268435456 | bytes 4718600 | tf_op jit(solution)/shard_map/pallas_call | solution.py:55
  45.1 0.1 collective-permute-start.16
  45.2 1.0 %shard_map.94 = (f32[128,1024]{1,0:T(8,128)S(1)}, bf16[128,1024]{1,0:T(8,128)(2,1)S(1)}) custom-call(s32[2]{0:T(128)S(1)} %pad_add_fusion.refs_0_, bf16[1024,2048]{1,0:T(8,128)(2,1)S(1)} %shard_map.86.refs_1_, bf16[128,1024]{1,0:T(8,128)(2,1)S(1)} %get-tuple-element.102.refs_2_, bf16[256,256]{1,0:T(8,128)(2,1)S(1)} %get-tuple-element.98.refs_2_.refs_3_, ...), custom_call_target="tpu_custom_call" | custom-call | flops 4000000000 | bytes 4980744 | tf_op jit(solution)/shard_map/pallas_call | solution.py:55
  46.2 0.5 %collective-permute-done.16.refs_0_ = bf16[128,1024]{1,0:T(8,128)(2,1)S(1)} collective-permute-done((bf16[128,1024]{1,0:T(8,128)(2,1)S(1)}, bf16[128,1024]{1,0:T(8,128)(2,1)S(1)}, u32[]{:S(2)}, u32[]{:S(2)}) %collective-permute-start.16) | collective-permute-done | bytes 262176 | tf_op jit(solution)/shard_map/ppermute | solution.py:26
  46.7 0.1 shard_map.95.refs_1_
  46.8 0.0 collective-permute-done.18.refs_5_
  46.8 0.0 collective-permute-done.19.refs_6_
  46.8 0.3 collective-permute-done.17.refs_4_
  47.1 1.5 %shard_map.96 = (bf16[128,1024]{1,0:T(8,128)(2,1)}, bf16[128,1024]{1,0:T(8,128)(2,1)}, bf16[128,1024]{1,0:T(8,128)(2,1)}, bf16[128,1024]{1,0:T(8,128)(2,1)}) custom-call(s32[2]{0:T(128)S(1)} %pad_add_fusion.refs_0_, bf16[128,1024]{1,0:T(8,128)(2,1)S(1)} %shard_map.95.refs_1_, bf16[128,1024]{1,0:T(8,128)(2,1)S(1)} %get-tuple-element.105.refs_2_, ...), custom_call_target="tpu_custom_call" | custom-call | bytes 1048584 | tf_op jit(solution)/shard_map/pallas_call | solution.py:55
Async XLA Ops:
  0.6 6.4 %collective-permute-start.3 = (bf16[128,1024]{1,0:T(8,128)(2,1)}, bf16[128,1024]{1,0:T(8,128)(2,1)S(1)}, u32[]{:S(2)}, u32[]{:S(2)}) collective-permute-start(bf16[128,1024]{1,0:T(8,128)(2,1)} %refs_2_.1), channel_id=1, source_target_pairs={{0,1},{1,0},{2,3},{3,2},{4,5},{5,4},{6,7},{7,6},{8,9},{9,8},{10,11... | collective-permute-start | bytes 786440 | tf_op jit(solution)/shard_map/ppermute | solution.py:26
  2.3 4.8 %copy-start = (bf16[2048,1024]{1,0:T(8,128)(2,1)S(1)}, bf16[2048,1024]{1,0:T(8,128)(2,1)}, u32[]{:S(2)}) copy-start(bf16[2048,1024]{1,0:T(8,128)(2,1)} %refs_3_.1) | copy-start | bytes 12582916
  2.3 4.8 %copy-start.1 = (bf16[128,1024]{1,0:T(8,128)(2,1)S(1)}, bf16[128,1024]{1,0:T(8,128)(2,1)}, u32[]{:S(2)}) copy-start(bf16[128,1024]{1,0:T(8,128)(2,1)} %refs_1_.3) | copy-start | bytes 786436
  2.3 4.8 %copy-start.2 = (bf16[128,1024]{1,0:T(8,128)(2,1)S(1)}, bf16[128,1024]{1,0:T(8,128)(2,1)}, u32[]{:S(2)}) copy-start(bf16[128,1024]{1,0:T(8,128)(2,1)} %refs_2_.1) | copy-start | bytes 786436
  2.9 10.3 %collective-permute-start = (bf16[256,256]{1,0:T(8,128)(2,1)S(1)}, bf16[256,256]{1,0:T(8,128)(2,1)S(1)}, u32[]{:S(2)}, u32[]{:S(2)}) collective-permute-start(bf16[256,256]{1,0:T(8,128)(2,1)S(1)} %get-tuple-element.58), channel_id=1, source_target_pairs={{0,2},{2,0},{4,6},{6,4},{8,10},{10,8},{12,14},{14,12},{16,18},{18,... | collective-permute-start | bytes 393224 | tf_op jit(solution)/shard_map/ppermute | solution.py:22
  5.5 7.9 %collective-permute-start.1 = (bf16[256,256]{1,0:T(8,128)(2,1)S(1)}, bf16[256,256]{1,0:T(8,128)(2,1)S(1)}, u32[]{:S(2)}, u32[]{:S(2)}) collective-permute-start(bf16[256,256]{1,0:T(8,128)(2,1)S(1)} %get-tuple-element.59), channel_id=1, source_target_pairs={{0,4},{2,6},{4,0},{6,2},{8,12},{10,14},{12,8},{14,10},{16,20},{18,... | collective-permute-start | bytes 393224 | tf_op jit(solution)/shard_map/ppermute | solution.py:22
  7.0 7.4 %collective-permute-start.2 = (bf16[256,256]{1,0:T(8,128)(2,1)S(1)}, bf16[256,256]{1,0:T(8,128)(2,1)S(1)}, u32[]{:S(2)}, u32[]{:S(2)}) collective-permute-start(bf16[256,256]{1,0:T(8,128)(2,1)S(1)} %get-tuple-element.60), channel_id=1, source_target_pairs={{0,6},{2,4},{4,2},{6,0},{8,14},{10,12},{12,10},{14,8},{16,22},{18,... | collective-permute-start | bytes 393224 | tf_op jit(solution)/shard_map/ppermute | solution.py:22
  8.4 7.3 %collective-permute-start.4 = (bf16[256,256]{1,0:T(8,128)(2,1)S(1)}, bf16[256,256]{1,0:T(8,128)(2,1)S(1)}, u32[]{:S(2)}, u32[]{:S(2)}) collective-permute-start(bf16[256,256]{1,0:T(8,128)(2,1)S(1)} %get-tuple-element.62), channel_id=1, source_target_pairs={{0,2},{2,0},{4,6},{6,4},{8,10},{10,8},{12,14},{14,12},{16,18},{18,... | collective-permute-start | bytes 393224 | tf_op jit(solution)/shard_map/ppermute | solution.py:22
  11.6 9.1 %collective-permute-start.5 = (bf16[256,256]{1,0:T(8,128)(2,1)S(1)}, bf16[256,256]{1,0:T(8,128)(2,1)S(1)}, u32[]{:S(2)}, u32[]{:S(2)}) collective-permute-start(bf16[256,256]{1,0:T(8,128)(2,1)S(1)} %get-tuple-element.65), channel_id=1, source_target_pairs={{0,4},{2,6},{4,0},{6,2},{8,12},{10,14},{12,8},{14,10},{16,20},{18,... | collective-permute-start | bytes 393224 | tf_op jit(solution)/shard_map/ppermute | solution.py:22
  13.2 7.5 %collective-permute-start.6 = (bf16[256,256]{1,0:T(8,128)(2,1)S(1)}, bf16[256,256]{1,0:T(8,128)(2,1)S(1)}, u32[]{:S(2)}, u32[]{:S(2)}) collective-permute-start(bf16[256,256]{1,0:T(8,128)(2,1)S(1)} %get-tuple-element.66), channel_id=1, source_target_pairs={{0,6},{2,4},{4,2},{6,0},{8,14},{10,12},{12,10},{14,8},{16,22},{18,... | collective-permute-start | bytes 393224 | tf_op jit(solution)/shard_map/ppermute | solution.py:22
  16.0 10.5 %collective-permute-start.7 = (bf16[256,256]{1,0:T(8,128)(2,1)S(1)}, bf16[256,256]{1,0:T(8,128)(2,1)S(1)}, u32[]{:S(2)}, u32[]{:S(2)}) collective-permute-start(bf16[256,256]{1,0:T(8,128)(2,1)S(1)} %get-tuple-element.71), channel_id=1, source_target_pairs={{0,8},{2,10},{4,12},{6,14},{8,0},{10,2},{12,4},{14,6},{16,24},{18,... | collective-permute-start | bytes 393224 | tf_op jit(solution)/shard_map/ppermute | solution.py:22
  18.2 6.9 %collective-permute-start.9 = (bf16[128,256]{1,0:T(8,128)(2,1)S(1)}, bf16[128,256]{1,0:T(8,128)(2,1)S(1)}, u32[]{:S(2)}, u32[]{:S(2)}) collective-permute-start(bf16[128,256]{1,0:T(8,128)(2,1)S(1)} %get-tuple-element.72), channel_id=1, source_target_pairs={{0,24},{2,26},{4,28},{6,30},{8,16},{10,18},{12,20},{14,22},{16,8},... | collective-permute-start | bytes 196616 | tf_op jit(solution)/shard_map/ppermute | solution.py:22
  20.6 5.9 %collective-permute-start.8 = (bf16[128,256]{1,0:T(8,128)(2,1)S(1)}, bf16[128,256]{1,0:T(8,128)(2,1)S(1)}, u32[]{:S(2)}, u32[]{:S(2)}) collective-permute-start(bf16[128,256]{1,0:T(8,128)(2,1)S(1)} %get-tuple-element.72), channel_id=1, source_target_pairs={{0,16},{2,18},{4,20},{6,22},{8,24},{10,26},{12,28},{14,30},{16,0},... | collective-permute-start | bytes 196616 | tf_op jit(solution)/shard_map/ppermute | solution.py:22
  28.8 8.3 %collective-permute-start.13 = (bf16[128,256]{1,0:T(8,128)(2,1)S(1)}, bf16[128,256]{1,0:T(8,128)(2,1)S(1)}, u32[]{:S(2)}, u32[]{:S(2)}) collective-permute-start(bf16[128,256]{1,0:T(8,128)(2,1)S(1)} %get-tuple-element.86), channel_id=1, source_target_pairs={{0,16},{2,18},{4,20},{6,22},{8,24},{10,26},{12,28},{14,30},{16,0},... | collective-permute-start | bytes 196616 | tf_op jit(solution)/shard_map/ppermute | solution.py:22
  29.3 7.9 %collective-permute-start.14 = (bf16[128,256]{1,0:T(8,128)(2,1)S(1)}, bf16[128,256]{1,0:T(8,128)(2,1)S(1)}, u32[]{:S(2)}, u32[]{:S(2)}) collective-permute-start(bf16[128,256]{1,0:T(8,128)(2,1)S(1)} %get-tuple-element.87), channel_id=1, source_target_pairs={{0,24},{2,26},{4,28},{6,30},{8,16},{10,18},{12,20},{14,22},{16,8},... | collective-permute-start | bytes 196616 | tf_op jit(solution)/shard_map/ppermute | solution.py:22
  31.3 5.9 %collective-permute-start.12 = (bf16[256,256]{1,0:T(8,128)(2,1)S(1)}, bf16[256,256]{1,0:T(8,128)(2,1)S(1)}, u32[]{:S(2)}, u32[]{:S(2)}) collective-permute-start(bf16[256,256]{1,0:T(8,128)(2,1)S(1)} %get-tuple-element.85), channel_id=1, source_target_pairs={{0,8},{2,10},{4,12},{6,14},{8,0},{10,2},{12,4},{14,6},{16,24},{18,... | collective-permute-start | bytes 393224 | tf_op jit(solution)/shard_map/ppermute | solution.py:22
  33.2 8.0 %collective-permute-start.10 = (bf16[256,256]{1,0:T(8,128)(2,1)S(1)}, bf16[256,256]{1,0:T(8,128)(2,1)S(1)}, u32[]{:S(2)}, u32[]{:S(2)}) collective-permute-start(bf16[256,256]{1,0:T(8,128)(2,1)S(1)} %get-tuple-element.79), channel_id=1, source_target_pairs={{0,6},{2,4},{4,2},{6,0},{8,14},{10,12},{12,10},{14,8},{16,22},{18,... | collective-permute-start | bytes 393224 | tf_op jit(solution)/shard_map/ppermute | solution.py:22
  35.8 7.0 %collective-permute-start.11 = (bf16[256,256]{1,0:T(8,128)(2,1)S(1)}, bf16[256,256]{1,0:T(8,128)(2,1)S(1)}, u32[]{:S(2)}, u32[]{:S(2)}) collective-permute-start(bf16[256,256]{1,0:T(8,128)(2,1)S(1)} %get-tuple-element.80), channel_id=1, source_target_pairs={{0,2},{2,0},{4,6},{6,4},{8,10},{10,8},{12,14},{14,12},{16,18},{18,... | collective-permute-start | bytes 393224 | tf_op jit(solution)/shard_map/ppermute | solution.py:22
  37.2 6.9 %collective-permute-start.15 = (bf16[256,256]{1,0:T(8,128)(2,1)S(1)}, bf16[256,256]{1,0:T(8,128)(2,1)S(1)}, u32[]{:S(2)}, u32[]{:S(2)}) collective-permute-start(bf16[256,256]{1,0:T(8,128)(2,1)S(1)} %get-tuple-element.88), channel_id=1, source_target_pairs={{0,4},{2,6},{4,0},{6,2},{8,12},{10,14},{12,8},{14,10},{16,20},{18,... | collective-permute-start | bytes 393224 | tf_op jit(solution)/shard_map/ppermute | solution.py:22
  38.8 8.0 %collective-permute-start.18 = (bf16[256,256]{1,0:T(8,128)(2,1)S(1)}, bf16[256,256]{1,0:T(8,128)(2,1)S(1)}, u32[]{:S(2)}, u32[]{:S(2)}) collective-permute-start(bf16[256,256]{1,0:T(8,128)(2,1)S(1)} %get-tuple-element.95), channel_id=1, source_target_pairs={{0,2},{2,0},{4,6},{6,4},{8,10},{10,8},{12,14},{14,12},{16,18},{18,... | collective-permute-start | bytes 393224 | tf_op jit(solution)/shard_map/ppermute | solution.py:22
  40.3 6.4 %collective-permute-start.19 = (bf16[256,256]{1,0:T(8,128)(2,1)S(1)}, bf16[256,256]{1,0:T(8,128)(2,1)S(1)}, u32[]{:S(2)}, u32[]{:S(2)}) collective-permute-start(bf16[256,256]{1,0:T(8,128)(2,1)S(1)} %get-tuple-element.96), channel_id=1, source_target_pairs={{0,4},{2,6},{4,0},{6,2},{8,12},{10,14},{12,8},{14,10},{16,20},{18,... | collective-permute-start | bytes 393224 | tf_op jit(solution)/shard_map/ppermute | solution.py:22
  41.2 5.9 %collective-permute-start.17 = (bf16[256,256]{1,0:T(8,128)(2,1)S(1)}, bf16[256,256]{1,0:T(8,128)(2,1)S(1)}, u32[]{:S(2)}, u32[]{:S(2)}) collective-permute-start(bf16[256,256]{1,0:T(8,128)(2,1)S(1)} %get-tuple-element.97), channel_id=1, source_target_pairs={{0,6},{2,4},{4,2},{6,0},{8,14},{10,12},{12,10},{14,8},{16,22},{18,... | collective-permute-start | bytes 393224 | tf_op jit(solution)/shard_map/ppermute | solution.py:22
  45.1 1.6 %collective-permute-start.16 = (bf16[128,1024]{1,0:T(8,128)(2,1)S(1)}, bf16[128,1024]{1,0:T(8,128)(2,1)S(1)}, u32[]{:S(2)}, u32[]{:S(2)}) collective-permute-start(bf16[128,1024]{1,0:T(8,128)(2,1)S(1)} %get-tuple-element.104), channel_id=1, source_target_pairs={{0,1},{1,0},{2,3},{3,2},{4,5},{5,4},{6,7},{7,6},{8,9},{9,8},{10,11... | collective-permute-start | bytes 786440 | tf_op jit(solution)/shard_map/ppermute | solution.py:26

commit v11 on v10

--- a/solution.py
+++ b/solution.py
@@ -496,7 +496,7 @@
     )
     made = list(made)
     late = BACK[-1]
-    made[late], key_sum, *shares = lax.optimization_barrier((made[late], key_sum, *shares))
+    made[late], *shares = lax.optimization_barrier((made[late], *shares))
     home = exchange(made, BACK)
     chunks = call(
         lambda *refs: merge_kernel(slots, share_levels, *refs),

time: 48.8 us -> 49.6 us (1.016)
  waiting for transfers between devices: 10.4 us -> 11.3 us
    ppermute x18, waiting for transfers between devices: 9.94 us -> 10.8 us  [swap_seq(): lax.ppermute(array, 'seq', [(i, i ^ mask) for i in range(lax.axis_size('s...]
  transfers between devices with their start and end apart: 20 -> 20, of which waited for: 9 -> 9; matrix products, arithmetic and copies ran while one was open for 0% -> 0% of each run, Pallas kernels for 18% -> 17%
where the time goes in v11:
time: 49.6 us; the launch traced here: 49.4 us
  starting transfers between devices  24.8 us (50%)
  Pallas kernels  12.5 us (25%)
  waiting for transfers between devices  11.3 us (23%)
  between operations  0.78 us (2%)
    ppermute x18, starting transfers between devices, swap_seq(): lax.ppermute(array, 'seq', [(i, i ^ mask) for i in range(lax.axis_size('s...  24.2 us
    pallas_call x13, Pallas kernels, call(): pl.pallas_call(kernel, out_shape=out_shape, in_specs=specs, out_specs=jax...  12.5 us
    ppermute x18, waiting for transfers between devices, swap_seq(): lax.ppermute(array, 'seq', [(i, i ^ mask) for i in range(lax.axis_size('s...  10.8 us
  transfers between devices with their start and end apart: 20, of which 9 were waited for; matrix products, arithmetic and copies ran while one was open for 0% of the time, Pallas kernels for 17%

profile of v11, /device:TPU:0, one launch (start us, length us, event | category | flops | bytes accessed | tf_op | source)
XLA Modules:
  0.0 49.4 jit_solution(13278074889874030043)
XLA Ops:
  0.6 0.5 %collective-permute-start.3 = (bf16[128,1024]{1,0:T(8,128)(2,1)}, bf16[128,1024]{1,0:T(8,128)(2,1)S(1)}, u32[]{:S(2)}, u32[]{:S(2)}) collective-permute-start(bf16[128,1024]{1,0:T(8,128)(2,1)} %refs_2_.1), channel_id=1, source_target_pairs={{0,1},{1,0},{2,3},{3,2},{4,5},{5,4},{6,7},{7,6},{8,9},{9,8},{10,11... | collective-permute-start | bytes 786440 | tf_op jit(solution)/shard_map/ppermute | solution.py:26
  1.1 0.1 pad_add_fusion.refs_0_
  1.2 1.0 %shard_map.84 = (bf16[128,1024]{1,0:T(8,128)(2,1)S(1)}, bf16[128,1024]{1,0:T(8,128)(2,1)S(1)}) custom-call(bf16[128,1024]{1,0:T(8,128)(2,1)} %refs_0_.1, bf16[128,1024]{1,0:T(8,128)(2,1)} %refs_1_.2), custom_call_target="tpu_custom_call" | custom-call | bytes 524288 | tf_op jit(solution)/shard_map/pallas_call | solution.py:55
  2.3 0.0 copy-start
  2.3 0.0 copy-start.1
  2.3 0.0 copy-start.2
  2.3 0.6 %shard_map.85 = (bf16[256,256]{1,0:T(8,128)(2,1)S(1)}, bf16[256,256]{1,0:T(8,128)(2,1)S(1)}, bf16[256,256]{1,0:T(8,128)(2,1)S(1)}, bf16[256,256]{1,0:T(8,128)(2,1)S(1)}) custom-call(s32[2]{0:T(128)S(1)} %pad_add_fusion.refs_0_, bf16[128,1024]{1,0:T(8,128)(2,1)S(1)} %get-tuple-element.54.refs_1_, bf16[128,1024]{1,0:T(8,128)(2,1)S(1)} %get-tuple-element.55.refs_2_), custom_call_target="tpu_custom_call" | custom-call | flops 6000000000 | bytes 524296 | tf_op jit(solution)/shard_map/pallas_call | solution.py:55
  2.9 2.6 %collective-permute-start = (bf16[256,256]{1,0:T(8,128)(2,1)S(1)}, bf16[256,256]{1,0:T(8,128)(2,1)S(1)}, u32[]{:S(2)}, u32[]{:S(2)}) collective-permute-start(bf16[256,256]{1,0:T(8,128)(2,1)S(1)} %get-tuple-element.57), channel_id=1, source_target_pairs={{0,2},{2,0},{4,6},{6,4},{8,10},{10,8},{12,14},{14,12},{16,18},{18,... | collective-permute-start | bytes 393224 | tf_op jit(solution)/shard_map/ppermute | solution.py:22
  5.5 1.5 %collective-permute-start.1 = (bf16[256,256]{1,0:T(8,128)(2,1)S(1)}, bf16[256,256]{1,0:T(8,128)(2,1)S(1)}, u32[]{:S(2)}, u32[]{:S(2)}) collective-permute-start(bf16[256,256]{1,0:T(8,128)(2,1)S(1)} %get-tuple-element.58), channel_id=1, source_target_pairs={{0,4},{2,6},{4,0},{6,2},{8,12},{10,14},{12,8},{14,10},{16,20},{18,... | collective-permute-start | bytes 393224 | tf_op jit(solution)/shard_map/ppermute | solution.py:22
  7.0 0.0 collective-permute-start.2
  7.1 0.0 collective-permute-done.3.refs_4_
  7.1 0.0 copy-done
  7.1 0.0 copy-done.1
  7.1 0.0 copy-done.2
  7.1 1.3 %shard_map.87 = (bf16[256,256]{1,0:T(8,128)(2,1)S(1)}, bf16[256,256]{1,0:T(8,128)(2,1)S(1)}, bf16[256,256]{1,0:T(8,128)(2,1)S(1)}, bf16[256,256]{1,0:T(8,128)(2,1)S(1)}) custom-call(s32[2]{0:T(128)S(1)} %pad_add_fusion.refs_0_, bf16[128,1024]{1,0:T(8,128)(2,1)S(1)} %copy-done.1, bf16[128,1024]{1,0:T(8,128)(2,1)S(1)} %copy-done.2, ...), custom_call_target="tpu_custom_call" | custom-call | flops 6000000000 | bytes 4980744 | tf_op jit(solution)/shard_map/pallas_call | solution.py:55
  8.4 2.0 %collective-permute-start.4 = (bf16[256,256]{1,0:T(8,128)(2,1)S(1)}, bf16[256,256]{1,0:T(8,128)(2,1)S(1)}, u32[]{:S(2)}, u32[]{:S(2)}) collective-permute-start(bf16[256,256]{1,0:T(8,128)(2,1)S(1)} %get-tuple-element.61), channel_id=1, source_target_pairs={{0,2},{2,0},{4,6},{6,4},{8,10},{10,8},{12,14},{14,12},{16,18},{18,... | collective-permute-start | bytes 393224 | tf_op jit(solution)/shard_map/ppermute | solution.py:22
  10.4 1.2 %shard_map.86.refs_1_ = bf16[1024,2048]{1,0:T(8,128)(2,1)S(1)} custom-call(bf16[2048,1024]{1,0:T(8,128)(2,1)S(1)} %copy-done), custom_call_target="tpu_custom_call" | custom-call | tf_op jit(solution)/shard_map/pallas_call | solution.py:55
  11.6 1.6 %collective-permute-start.5 = (bf16[256,256]{1,0:T(8,128)(2,1)S(1)}, bf16[256,256]{1,0:T(8,128)(2,1)S(1)}, u32[]{:S(2)}, u32[]{:S(2)}) collective-permute-start(bf16[256,256]{1,0:T(8,128)(2,1)S(1)} %get-tuple-element.64), channel_id=1, source_target_pairs={{0,4},{2,6},{4,0},{6,2},{8,12},{10,14},{12,8},{14,10},{16,20},{18,... | collective-permute-start | bytes 393224 | tf_op jit(solution)/shard_map/ppermute | solution.py:22
  13.2 0.0 collective-permute-done.refs_1_
  13.2 0.1 collective-permute-start.6
  13.3 0.1 collective-permute-done.1.refs_2_
  13.4 1.0 %collective-permute-done.2.refs_3_ = bf16[256,256]{1,0:T(8,128)(2,1)S(1)} collective-permute-done((bf16[256,256]{1,0:T(8,128)(2,1)S(1)}, bf16[256,256]{1,0:T(8,128)(2,1)S(1)}, u32[]{:S(2)}, u32[]{:S(2)}) %collective-permute-start.2) | collective-permute-done | bytes 131104 | tf_op jit(solution)/shard_map/ppermute | solution.py:22
  14.4 1.3 %collective-permute-done.4.refs_5_ = bf16[256,256]{1,0:T(8,128)(2,1)S(1)} collective-permute-done((bf16[256,256]{1,0:T(8,128)(2,1)S(1)}, bf16[256,256]{1,0:T(8,128)(2,1)S(1)}, u32[]{:S(2)}, u32[]{:S(2)}) %collective-permute-start.4) | collective-permute-done | bytes 131104 | tf_op jit(solution)/shard_map/ppermute | solution.py:22
  15.7 0.3 shard_map.88
  16.0 2.2 %collective-permute-start.7 = (bf16[256,256]{1,0:T(8,128)(2,1)S(1)}, bf16[256,256]{1,0:T(8,128)(2,1)S(1)}, u32[]{:S(2)}, u32[]{:S(2)}) collective-permute-start(bf16[256,256]{1,0:T(8,128)(2,1)S(1)} %get-tuple-element.70), channel_id=1, source_target_pairs={{0,8},{2,10},{4,12},{6,14},{8,0},{10,2},{12,4},{14,6},{16,24},{18,... | collective-permute-start | bytes 393224 | tf_op jit(solution)/shard_map/ppermute | solution.py:22
  18.2 2.5 %collective-permute-start.9 = (bf16[128,256]{1,0:T(8,128)(2,1)S(1)}, bf16[128,256]{1,0:T(8,128)(2,1)S(1)}, u32[]{:S(2)}, u32[]{:S(2)}) collective-permute-start(bf16[128,256]{1,0:T(8,128)(2,1)S(1)} %get-tuple-element.71), channel_id=1, source_target_pairs={{0,24},{2,26},{4,28},{6,30},{8,16},{10,18},{12,20},{14,22},{16,8},... | collective-permute-start | bytes 196616 | tf_op jit(solution)/shard_map/ppermute | solution.py:22
  20.6 0.1 collective-permute-start.8
  20.8 0.0 collective-permute-done.5.refs_6_
  20.8 0.0 collective-permute-done.6.refs_7_
  20.8 4.3 %collective-permute-done.9.refs_10_ = bf16[128,256]{1,0:T(8,128)(2,1)S(1)} collective-permute-done((bf16[128,256]{1,0:T(8,128)(2,1)S(1)}, bf16[128,256]{1,0:T(8,128)(2,1)S(1)}, u32[]{:S(2)}, u32[]{:S(2)}) %collective-permute-start.9) | collective-permute-done | bytes 65568 | tf_op jit(solution)/shard_map/ppermute | solution.py:22
  25.1 1.4 %collective-permute-done.8.refs_9_ = bf16[128,256]{1,0:T(8,128)(2,1)S(1)} collective-permute-done((bf16[128,256]{1,0:T(8,128)(2,1)S(1)}, bf16[128,256]{1,0:T(8,128)(2,1)S(1)}, u32[]{:S(2)}, u32[]{:S(2)}) %collective-permute-start.8) | collective-permute-done | bytes 65568 | tf_op jit(solution)/shard_map/ppermute | solution.py:22
  26.5 0.0 collective-permute-done.7.refs_8_
  26.5 2.3 %shard_map.89 = (bf16[256,256]{1,0:T(8,128)(2,1)S(1)}, bf16[128,256]{1,0:T(8,128)(2,1)S(1)}, bf16[128,256]{1,0:T(8,128)(2,1)S(1)}, bf16[2,640,256]{2,1,0:T(8,128...) custom-call(bf16[256,256]{1,0:T(8,128)(2,1)S(1)} %get-tuple-element., ...), custom_call_target="tpu_custom_call" | custom-call | flops 503316480 | bytes 1310720 | tf_op jit(solution)/shard_map/pallas_call | solution.py:55
  28.8 0.5 collective-permute-start.13
  29.3 1.9 %collective-permute-start.14 = (bf16[128,256]{1,0:T(8,128)(2,1)S(1)}, bf16[128,256]{1,0:T(8,128)(2,1)S(1)}, u32[]{:S(2)}, u32[]{:S(2)}) collective-permute-start(bf16[128,256]{1,0:T(8,128)(2,1)S(1)} %get-tuple-element.83), channel_id=1, source_target_pairs={{0,24},{2,26},{4,28},{6,30},{8,16},{10,18},{12,20},{14,22},{16,8},... | collective-permute-start | bytes 196616 | tf_op jit(solution)/shard_map/ppermute | solution.py:22
  31.3 1.1 %collective-permute-start.12 = (bf16[256,256]{1,0:T(8,128)(2,1)S(1)}, bf16[256,256]{1,0:T(8,128)(2,1)S(1)}, u32[]{:S(2)}, u32[]{:S(2)}) collective-permute-start(bf16[256,256]{1,0:T(8,128)(2,1)S(1)} %get-tuple-element.81), channel_id=1, source_target_pairs={{0,8},{2,10},{4,12},{6,14},{8,0},{10,2},{12,4},{14,6},{16,24},{18,... | collective-permute-start | bytes 393224 | tf_op jit(solution)/shard_map/ppermute | solution.py:22
  32.4 0.8 %shard_map.90 = (bf16[256,256]{1,0:T(8,128)(2,1)S(1)}, bf16[256,256]{1,0:T(8,128)(2,1)S(1)}, bf16[256,256]{1,0:T(8,128)(2,1)S(1)}, bf16[256,256]{1,0:T(8,128)(2,1)S(1)}) custom-call(bf16[2,640,256]{2,1,0:T(8,128)(2,1)S(1)} %get-tuple-element.72.refs_0_, bf16[2,640,256]{2,1,0:T(8,128)(2,1)S(1)} %get-tuple-element.73.refs_1_, ...), custom_call_target="tpu_custom_call" | custom-call | flops 6000000000 | bytes 4456448 | tf_op jit(solution)/shard_map/pallas_call | solution.py:55
  33.2 2.5 %collective-permute-start.10 = (bf16[256,256]{1,0:T(8,128)(2,1)S(1)}, bf16[256,256]{1,0:T(8,128)(2,1)S(1)}, u32[]{:S(2)}, u32[]{:S(2)}) collective-permute-start(bf16[256,256]{1,0:T(8,128)(2,1)S(1)} %get-tuple-element.78), channel_id=1, source_target_pairs={{0,6},{2,4},{4,2},{6,0},{8,14},{10,12},{12,10},{14,8},{16,22},{18,... | collective-permute-start | bytes 393224 | tf_op jit(solution)/shard_map/ppermute | solution.py:22
  35.8 0.5 %collective-permute-start.11 = (bf16[256,256]{1,0:T(8,128)(2,1)S(1)}, bf16[256,256]{1,0:T(8,128)(2,1)S(1)}, u32[]{:S(2)}, u32[]{:S(2)}) collective-permute-start(bf16[256,256]{1,0:T(8,128)(2,1)S(1)} %get-tuple-element.79), channel_id=1, source_target_pairs={{0,2},{2,0},{4,6},{6,4},{8,10},{10,8},{12,14},{14,12},{16,18},{18,... | collective-permute-start | bytes 393224 | tf_op jit(solution)/shard_map/ppermute | solution.py:22
  36.3 0.0 collective-permute-done.13.refs_3_
  36.3 0.0 collective-permute-done.14.refs_4_
  36.3 0.6 %collective-permute-done.12.refs_2_ = bf16[256,256]{1,0:T(8,128)(2,1)S(1)} collective-permute-done((bf16[256,256]{1,0:T(8,128)(2,1)S(1)}, bf16[256,256]{1,0:T(8,128)(2,1)S(1)}, u32[]{:S(2)}, u32[]{:S(2)}) %collective-permute-start.12) | collective-permute-done | bytes 131104 | tf_op jit(solution)/shard_map/ppermute | solution.py:22
  36.9 1.5 %collective-permute-start.15 = (bf16[256,256]{1,0:T(8,128)(2,1)S(1)}, bf16[256,256]{1,0:T(8,128)(2,1)S(1)}, u32[]{:S(2)}, u32[]{:S(2)}) collective-permute-start(bf16[256,256]{1,0:T(8,128)(2,1)S(1)} %get-tuple-element.84), channel_id=1, source_target_pairs={{0,4},{2,6},{4,0},{6,2},{8,12},{10,14},{12,8},{14,10},{16,20},{18,... | collective-permute-start | bytes 393224 | tf_op jit(solution)/shard_map/ppermute | solution.py:22
  38.4 0.9 %shard_map.91 = (f32[512,256]{1,0:T(8,128)S(1)}, f32[512,256]{1,0:T(8,128)S(1)}) custom-call(bf16[2,256,256]{2,1,0:T(8,128)(2,1)S(1)} %get-tuple-element.85.refs_0_, bf16[2,256,256]{2,1,0:T(8,128)(2,1)S(1)} %get-tuple-element.86.refs_1_, bf16[4,256,640]{2,1,0:T(8,128)(2,1)S(1)} %get-tuple-element.74.refs_2_, bf16[4,256,640]{2,1,0:T(8,128)(2,1)S(1)} %get-tuple-element.75.refs_3_), custom_call_target="tpu_custom_call" | custom-call | flops 335544320 | bytes 3145728 | tf_op jit(solution)/shard_map/pallas_call | solution.py:55
  39.3 0.4 shard_map.92
  39.7 1.6 %collective-permute-start.18 = (bf16[256,256]{1,0:T(8,128)(2,1)S(1)}, bf16[256,256]{1,0:T(8,128)(2,1)S(1)}, u32[]{:S(2)}, u32[]{:S(2)}) collective-permute-start(bf16[256,256]{1,0:T(8,128)(2,1)S(1)} %get-tuple-element.93), channel_id=1, source_target_pairs={{0,2},{2,0},{4,6},{6,4},{8,10},{10,8},{12,14},{14,12},{16,18},{18,... | collective-permute-start | bytes 393224 | tf_op jit(solution)/shard_map/ppermute | solution.py:22
  41.2 0.8 %collective-permute-start.19 = (bf16[256,256]{1,0:T(8,128)(2,1)S(1)}, bf16[256,256]{1,0:T(8,128)(2,1)S(1)}, u32[]{:S(2)}, u32[]{:S(2)}) collective-permute-start(bf16[256,256]{1,0:T(8,128)(2,1)S(1)} %get-tuple-element.94), channel_id=1, source_target_pairs={{0,4},{2,6},{4,0},{6,2},{8,12},{10,14},{12,8},{14,10},{16,20},{18,... | collective-permute-start | bytes 393224 | tf_op jit(solution)/shard_map/ppermute | solution.py:22
  42.0 0.0 collective-permute-done.10.refs_3_.refs_4_
  42.0 1.2 %collective-permute-start.17 = (bf16[256,256]{1,0:T(8,128)(2,1)S(1)}, bf16[256,256]{1,0:T(8,128)(2,1)S(1)}, u32[]{:S(2)}, u32[]{:S(2)}) collective-permute-start(bf16[256,256]{1,0:T(8,128)(2,1)S(1)} %get-tuple-element.95), channel_id=1, source_target_pairs={{0,6},{2,4},{4,2},{6,0},{8,14},{10,12},{12,10},{14,8},{16,22},{18,... | collective-permute-start | bytes 393224 | tf_op jit(solution)/shard_map/ppermute | solution.py:22
  43.2 0.0 collective-permute-done.11.refs_4_.refs_5_
  43.2 0.9 %collective-permute-done.15.refs_5_.refs_6_ = bf16[256,256]{1,0:T(8,128)(2,1)S(1)} collective-permute-done((bf16[256,256]{1,0:T(8,128)(2,1)S(1)}, bf16[256,256]{1,0:T(8,128)(2,1)S(1)}, u32[]{:S(2)}, u32[]{:S(2)}) %collective-permute-start.15) | collective-permute-done | bytes 131104 | tf_op jit(solution)/shard_map/ppermute | solution.py:22
  44.1 1.0 %shard_map.93 = (bf16[128,1024]{1,0:T(8,128)(2,1)S(1)}, bf16[128,1024]{1,0:T(8,128)(2,1)S(1)}) custom-call(s32[2]{0:T(128)S(1)} %pad_add_fusion.refs_0_, bf16[1024,2048]{1,0:T(8,128)(2,1)S(1)} %shard_map.86.refs_1_, bf16[256,256]{1,0:T(8,128)(2,1)S(1)} %get-tuple-element.96.refs_2_.refs_3_, bf16[256,256]{1,0:T(8,128)(2,1)S(1)} %collective-permute-done.10.refs_3_.refs_4_, ...), custom_call_target="tpu_custom_call" | custom-call | flops 268435456 | bytes 4718600 | tf_op jit(solution)/shard_map/pallas_call | solution.py:55
  45.1 0.1 collective-permute-start.16
  45.2 1.0 %shard_map.94 = (f32[128,1024]{1,0:T(8,128)S(1)}, bf16[128,1024]{1,0:T(8,128)(2,1)S(1)}) custom-call(s32[2]{0:T(128)S(1)} %pad_add_fusion.refs_0_, bf16[1024,2048]{1,0:T(8,128)(2,1)S(1)} %shard_map.86.refs_1_, bf16[128,1024]{1,0:T(8,128)(2,1)S(1)} %get-tuple-element.100.refs_2_, bf16[256,256]{1,0:T(8,128)(2,1)S(1)} %get-tuple-element.96.refs_2_.refs_3_, ...), custom_call_target="tpu_custom_call" | custom-call | flops 4000000000 | bytes 4980744 | tf_op jit(solution)/shard_map/pallas_call | solution.py:55
  46.2 0.5 %collective-permute-done.16.refs_0_ = bf16[128,1024]{1,0:T(8,128)(2,1)S(1)} collective-permute-done((bf16[128,1024]{1,0:T(8,128)(2,1)S(1)}, bf16[128,1024]{1,0:T(8,128)(2,1)S(1)}, u32[]{:S(2)}, u32[]{:S(2)}) %collective-permute-start.16) | collective-permute-done | bytes 262176 | tf_op jit(solution)/shard_map/ppermute | solution.py:26
  46.7 0.1 shard_map.95.refs_1_
  46.8 0.0 collective-permute-done.18.refs_5_
  46.8 0.0 collective-permute-done.19.refs_6_
  46.8 1.1 %collective-permute-done.17.refs_4_ = bf16[256,256]{1,0:T(8,128)(2,1)S(1)} collective-permute-done((bf16[256,256]{1,0:T(8,128)(2,1)S(1)}, bf16[256,256]{1,0:T(8,128)(2,1)S(1)}, u32[]{:S(2)}, u32[]{:S(2)}) %collective-permute-start.17) | collective-permute-done | bytes 131104 | tf_op jit(solution)/shard_map/ppermute | solution.py:22
  47.9 1.5 %shard_map.96 = (bf16[128,1024]{1,0:T(8,128)(2,1)}, bf16[128,1024]{1,0:T(8,128)(2,1)}, bf16[128,1024]{1,0:T(8,128)(2,1)}, bf16[128,1024]{1,0:T(8,128)(2,1)}) custom-call(s32[2]{0:T(128)S(1)} %pad_add_fusion.refs_0_, bf16[128,1024]{1,0:T(8,128)(2,1)S(1)} %shard_map.95.refs_1_, bf16[128,1024]{1,0:T(8,128)(2,1)S(1)} %get-tuple-element.103.refs_2_, ...), custom_call_target="tpu_custom_call" | custom-call | bytes 1048584 | tf_op jit(solution)/shard_map/pallas_call | solution.py:55
Async XLA Ops:
  0.6 6.4 %collective-permute-start.3 = (bf16[128,1024]{1,0:T(8,128)(2,1)}, bf16[128,1024]{1,0:T(8,128)(2,1)S(1)}, u32[]{:S(2)}, u32[]{:S(2)}) collective-permute-start(bf16[128,1024]{1,0:T(8,128)(2,1)} %refs_2_.1), channel_id=1, source_target_pairs={{0,1},{1,0},{2,3},{3,2},{4,5},{5,4},{6,7},{7,6},{8,9},{9,8},{10,11... | collective-permute-start | bytes 786440 | tf_op jit(solution)/shard_map/ppermute | solution.py:26
  2.3 4.8 %copy-start = (bf16[2048,1024]{1,0:T(8,128)(2,1)S(1)}, bf16[2048,1024]{1,0:T(8,128)(2,1)}, u32[]{:S(2)}) copy-start(bf16[2048,1024]{1,0:T(8,128)(2,1)} %refs_3_.1) | copy-start | bytes 12582916
  2.3 4.8 %copy-start.1 = (bf16[128,1024]{1,0:T(8,128)(2,1)S(1)}, bf16[128,1024]{1,0:T(8,128)(2,1)}, u32[]{:S(2)}) copy-start(bf16[128,1024]{1,0:T(8,128)(2,1)} %refs_1_.3) | copy-start | bytes 786436
  2.3 4.8 %copy-start.2 = (bf16[128,1024]{1,0:T(8,128)(2,1)S(1)}, bf16[128,1024]{1,0:T(8,128)(2,1)}, u32[]{:S(2)}) copy-start(bf16[128,1024]{1,0:T(8,128)(2,1)} %refs_2_.1) | copy-start | bytes 786436
  2.9 10.3 %collective-permute-start = (bf16[256,256]{1,0:T(8,128)(2,1)S(1)}, bf16[256,256]{1,0:T(8,128)(2,1)S(1)}, u32[]{:S(2)}, u32[]{:S(2)}) collective-permute-start(bf16[256,256]{1,0:T(8,128)(2,1)S(1)} %get-tuple-element.57), channel_id=1, source_target_pairs={{0,2},{2,0},{4,6},{6,4},{8,10},{10,8},{12,14},{14,12},{16,18},{18,... | collective-permute-start | bytes 393224 | tf_op jit(solution)/shard_map/ppermute | solution.py:22
  5.5 7.9 %collective-permute-start.1 = (bf16[256,256]{1,0:T(8,128)(2,1)S(1)}, bf16[256,256]{1,0:T(8,128)(2,1)S(1)}, u32[]{:S(2)}, u32[]{:S(2)}) collective-permute-start(bf16[256,256]{1,0:T(8,128)(2,1)S(1)} %get-tuple-element.58), channel_id=1, source_target_pairs={{0,4},{2,6},{4,0},{6,2},{8,12},{10,14},{12,8},{14,10},{16,20},{18,... | collective-permute-start | bytes 393224 | tf_op jit(solution)/shard_map/ppermute | solution.py:22
  7.0 7.4 %collective-permute-start.2 = (bf16[256,256]{1,0:T(8,128)(2,1)S(1)}, bf16[256,256]{1,0:T(8,128)(2,1)S(1)}, u32[]{:S(2)}, u32[]{:S(2)}) collective-permute-start(bf16[256,256]{1,0:T(8,128)(2,1)S(1)} %get-tuple-element.59), channel_id=1, source_target_pairs={{0,6},{2,4},{4,2},{6,0},{8,14},{10,12},{12,10},{14,8},{16,22},{18,... | collective-permute-start | bytes 393224 | tf_op jit(solution)/shard_map/ppermute | solution.py:22
  8.4 7.3 %collective-permute-start.4 = (bf16[256,256]{1,0:T(8,128)(2,1)S(1)}, bf16[256,256]{1,0:T(8,128)(2,1)S(1)}, u32[]{:S(2)}, u32[]{:S(2)}) collective-permute-start(bf16[256,256]{1,0:T(8,128)(2,1)S(1)} %get-tuple-element.61), channel_id=1, source_target_pairs={{0,2},{2,0},{4,6},{6,4},{8,10},{10,8},{12,14},{14,12},{16,18},{18,... | collective-permute-start | bytes 393224 | tf_op jit(solution)/shard_map/ppermute | solution.py:22
  11.6 9.1 %collective-permute-start.5 = (bf16[256,256]{1,0:T(8,128)(2,1)S(1)}, bf16[256,256]{1,0:T(8,128)(2,1)S(1)}, u32[]{:S(2)}, u32[]{:S(2)}) collective-permute-start(bf16[256,256]{1,0:T(8,128)(2,1)S(1)} %get-tuple-element.64), channel_id=1, source_target_pairs={{0,4},{2,6},{4,0},{6,2},{8,12},{10,14},{12,8},{14,10},{16,20},{18,... | collective-permute-start | bytes 393224 | tf_op jit(solution)/shard_map/ppermute | solution.py:22
  13.2 7.5 %collective-permute-start.6 = (bf16[256,256]{1,0:T(8,128)(2,1)S(1)}, bf16[256,256]{1,0:T(8,128)(2,1)S(1)}, u32[]{:S(2)}, u32[]{:S(2)}) collective-permute-start(bf16[256,256]{1,0:T(8,128)(2,1)S(1)} %get-tuple-element.65), channel_id=1, source_target_pairs={{0,6},{2,4},{4,2},{6,0},{8,14},{10,12},{12,10},{14,8},{16,22},{18,... | collective-permute-start | bytes 393224 | tf_op jit(solution)/shard_map/ppermute | solution.py:22
  16.0 10.5 %collective-permute-start.7 = (bf16[256,256]{1,0:T(8,128)(2,1)S(1)}, bf16[256,256]{1,0:T(8,128)(2,1)S(1)}, u32[]{:S(2)}, u32[]{:S(2)}) collective-permute-start(bf16[256,256]{1,0:T(8,128)(2,1)S(1)} %get-tuple-element.70), channel_id=1, source_target_pairs={{0,8},{2,10},{4,12},{6,14},{8,0},{10,2},{12,4},{14,6},{16,24},{18,... | collective-permute-start | bytes 393224 | tf_op jit(solution)/shard_map/ppermute | solution.py:22
  18.2 6.9 %collective-permute-start.9 = (bf16[128,256]{1,0:T(8,128)(2,1)S(1)}, bf16[128,256]{1,0:T(8,128)(2,1)S(1)}, u32[]{:S(2)}, u32[]{:S(2)}) collective-permute-start(bf16[128,256]{1,0:T(8,128)(2,1)S(1)} %get-tuple-element.71), channel_id=1, source_target_pairs={{0,24},{2,26},{4,28},{6,30},{8,16},{10,18},{12,20},{14,22},{16,8},... | collective-permute-start | bytes 196616 | tf_op jit(solution)/shard_map/ppermute | solution.py:22
  20.6 5.9 %collective-permute-start.8 = (bf16[128,256]{1,0:T(8,128)(2,1)S(1)}, bf16[128,256]{1,0:T(8,128)(2,1)S(1)}, u32[]{:S(2)}, u32[]{:S(2)}) collective-permute-start(bf16[128,256]{1,0:T(8,128)(2,1)S(1)} %get-tuple-element.71), channel_id=1, source_target_pairs={{0,16},{2,18},{4,20},{6,22},{8,24},{10,26},{12,28},{14,30},{16,0},... | collective-permute-start | bytes 196616 | tf_op jit(solution)/shard_map/ppermute | solution.py:22
  28.8 7.4 %collective-permute-start.13 = (bf16[128,256]{1,0:T(8,128)(2,1)S(1)}, bf16[128,256]{1,0:T(8,128)(2,1)S(1)}, u32[]{:S(2)}, u32[]{:S(2)}) collective-permute-start(bf16[128,256]{1,0:T(8,128)(2,1)S(1)} %get-tuple-element.82), channel_id=1, source_target_pairs={{0,16},{2,18},{4,20},{6,22},{8,24},{10,26},{12,28},{14,30},{16,0},... | collective-permute-start | bytes 196616 | tf_op jit(solution)/shard_map/ppermute | solution.py:22
  29.3 7.0 %collective-permute-start.14 = (bf16[128,256]{1,0:T(8,128)(2,1)S(1)}, bf16[128,256]{1,0:T(8,128)(2,1)S(1)}, u32[]{:S(2)}, u32[]{:S(2)}) collective-permute-start(bf16[128,256]{1,0:T(8,128)(2,1)S(1)} %get-tuple-element.83), channel_id=1, source_target_pairs={{0,24},{2,26},{4,28},{6,30},{8,16},{10,18},{12,20},{14,22},{16,8},... | collective-permute-start | bytes 196616 | tf_op jit(solution)/shard_map/ppermute | solution.py:22
  31.3 5.6 %collective-permute-start.12 = (bf16[256,256]{1,0:T(8,128)(2,1)S(1)}, bf16[256,256]{1,0:T(8,128)(2,1)S(1)}, u32[]{:S(2)}, u32[]{:S(2)}) collective-permute-start(bf16[256,256]{1,0:T(8,128)(2,1)S(1)} %get-tuple-element.81), channel_id=1, source_target_pairs={{0,8},{2,10},{4,12},{6,14},{8,0},{10,2},{12,4},{14,6},{16,24},{18,... | collective-permute-start | bytes 393224 | tf_op jit(solution)/shard_map/ppermute | solution.py:22
  33.2 8.8 %collective-permute-start.10 = (bf16[256,256]{1,0:T(8,128)(2,1)S(1)}, bf16[256,256]{1,0:T(8,128)(2,1)S(1)}, u32[]{:S(2)}, u32[]{:S(2)}) collective-permute-start(bf16[256,256]{1,0:T(8,128)(2,1)S(1)} %get-tuple-element.78), channel_id=1, source_target_pairs={{0,6},{2,4},{4,2},{6,0},{8,14},{10,12},{12,10},{14,8},{16,22},{18,... | collective-permute-start | bytes 393224 | tf_op jit(solution)/shard_map/ppermute | solution.py:22
  35.8 7.5 %collective-permute-start.11 = (bf16[256,256]{1,0:T(8,128)(2,1)S(1)}, bf16[256,256]{1,0:T(8,128)(2,1)S(1)}, u32[]{:S(2)}, u32[]{:S(2)}) collective-permute-start(bf16[256,256]{1,0:T(8,128)(2,1)S(1)} %get-tuple-element.79), channel_id=1, source_target_pairs={{0,2},{2,0},{4,6},{6,4},{8,10},{10,8},{12,14},{14,12},{16,18},{18,... | collective-permute-start | bytes 393224 | tf_op jit(solution)/shard_map/ppermute | solution.py:22
  36.9 7.2 %collective-permute-start.15 = (bf16[256,256]{1,0:T(8,128)(2,1)S(1)}, bf16[256,256]{1,0:T(8,128)(2,1)S(1)}, u32[]{:S(2)}, u32[]{:S(2)}) collective-permute-start(bf16[256,256]{1,0:T(8,128)(2,1)S(1)} %get-tuple-element.84), channel_id=1, source_target_pairs={{0,4},{2,6},{4,0},{6,2},{8,12},{10,14},{12,8},{14,10},{16,20},{18,... | collective-permute-start | bytes 393224 | tf_op jit(solution)/shard_map/ppermute | solution.py:22
  39.7 7.1 %collective-permute-start.18 = (bf16[256,256]{1,0:T(8,128)(2,1)S(1)}, bf16[256,256]{1,0:T(8,128)(2,1)S(1)}, u32[]{:S(2)}, u32[]{:S(2)}) collective-permute-start(bf16[256,256]{1,0:T(8,128)(2,1)S(1)} %get-tuple-element.93), channel_id=1, source_target_pairs={{0,2},{2,0},{4,6},{6,4},{8,10},{10,8},{12,14},{14,12},{16,18},{18,... | collective-permute-start | bytes 393224 | tf_op jit(solution)/shard_map/ppermute | solution.py:22
  41.2 5.6 %collective-permute-start.19 = (bf16[256,256]{1,0:T(8,128)(2,1)S(1)}, bf16[256,256]{1,0:T(8,128)(2,1)S(1)}, u32[]{:S(2)}, u32[]{:S(2)}) collective-permute-start(bf16[256,256]{1,0:T(8,128)(2,1)S(1)} %get-tuple-element.94), channel_id=1, source_target_pairs={{0,4},{2,6},{4,0},{6,2},{8,12},{10,14},{12,8},{14,10},{16,20},{18,... | collective-permute-start | bytes 393224 | tf_op jit(solution)/shard_map/ppermute | solution.py:22
  42.0 5.9 %collective-permute-start.17 = (bf16[256,256]{1,0:T(8,128)(2,1)S(1)}, bf16[256,256]{1,0:T(8,128)(2,1)S(1)}, u32[]{:S(2)}, u32[]{:S(2)}) collective-permute-start(bf16[256,256]{1,0:T(8,128)(2,1)S(1)} %get-tuple-element.95), channel_id=1, source_target_pairs={{0,6},{2,4},{4,2},{6,0},{8,14},{10,12},{12,10},{14,8},{16,22},{18,... | collective-permute-start | bytes 393224 | tf_op jit(solution)/shard_map/ppermute | solution.py:22
  45.1 1.6 %collective-permute-start.16 = (bf16[128,1024]{1,0:T(8,128)(2,1)S(1)}, bf16[128,1024]{1,0:T(8,128)(2,1)S(1)}, u32[]{:S(2)}, u32[]{:S(2)}) collective-permute-start(bf16[128,1024]{1,0:T(8,128)(2,1)S(1)} %get-tuple-element.102), channel_id=1, source_target_pairs={{0,1},{1,0},{2,3},{3,2},{4,5},{5,4},{6,7},{7,6},{8,9},{9,8},{10,11... | collective-permute-start | bytes 786440 | tf_op jit(solution)/shard_map/ppermute | solution.py:26

commit v12 on v10

--- a/solution.py
+++ b/solution.py
@@ -120,7 +120,7 @@
 
 
 def coarse_kernel(slots, levels, *refs):
-    in_refs, piece_refs = by_mask(refs[:slots]), refs[slots:]
+    in_refs, piece_refs = by_mask(refs[:slots], BACK), refs[slots:]
     tok = BLOCK
     for level, piece in zip(levels, piece_refs):
         rows = piece_rows(level)
@@ -134,7 +134,8 @@
 
 
 def attend_kernel(slots, far_levels, entries, *refs):
-    key_refs, query_refs = by_mask(refs[:slots]), by_mask(refs[slots : 2 * slots])
+    key_refs = by_mask(refs[:slots], BACK)
+    query_refs = by_mask(refs[slots : 2 * slots])
     refs = refs[2 * slots :]
     count = len(entries)
     got_refs, far_refs, refs = refs[:count], refs[count : 2 * count], refs[2 * count :]
@@ -438,7 +439,7 @@
         specs=[SMEM] + [VMEM] * 2,
         vmem=8,
     )
-    keys = exchange(chunks)
+    keys = exchange(chunks, BACK)
     later, *_ = lax.optimization_barrier((place, *chunks))
     other_grad = swap_head(output_grad)
     chunks = call(

time: 48.8 us -> 49.8 us (1.020)
  waiting for transfers between devices: 10.4 us -> 13.6 us
  starting transfers between devices: 24.8 us -> 22.7 us
    ppermute x18, waiting for transfers between devices: 9.94 us -> 13.1 us  [swap_seq(): lax.ppermute(array, 'seq', [(i, i ^ mask) for i in range(lax.axis_size('s...]
    ppermute x18, starting transfers between devices: 24.2 us -> 22.2 us  [swap_seq(): lax.ppermute(array, 'seq', [(i, i ^ mask) for i in range(lax.axis_size('s...]
  transfers between devices with their start and end apart: 20 -> 20, of which waited for: 9 -> 8; matrix products, arithmetic and copies ran while one was open for 0% -> 0% of each run, Pallas kernels for 18% -> 17%
where the time goes in v12:
time: 49.8 us; the launch traced here: 49.7 us
  starting transfers between devices  22.7 us (46%)
  waiting for transfers between devices  13.6 us (27%)
  Pallas kernels  12.5 us (25%)
  between operations  0.78 us (2%)
    ppermute x18, starting transfers between devices, swap_seq(): lax.ppermute(array, 'seq', [(i, i ^ mask) for i in range(lax.axis_size('s...  22.2 us
    ppermute x18, waiting for transfers between devices, swap_seq(): lax.ppermute(array, 'seq', [(i, i ^ mask) for i in range(lax.axis_size('s...  13.1 us
    pallas_call x13, Pallas kernels, call(): pl.pallas_call(kernel, out_shape=out_shape, in_specs=specs, out_specs=jax...  12.5 us
  transfers between devices with their start and end apart: 20, of which 8 were waited for; matrix products, arithmetic and copies ran while one was open for 0% of the time, Pallas kernels for 17%

profile of v12, /device:TPU:0, one launch (start us, length us, event | category | flops | bytes accessed | tf_op | source)
XLA Modules:
  0.0 49.7 jit_solution(8991151047955177112)
XLA Ops:
  0.6 0.5 %collective-permute-start.3 = (bf16[128,1024]{1,0:T(8,128)(2,1)}, bf16[128,1024]{1,0:T(8,128)(2,1)S(1)}, u32[]{:S(2)}, u32[]{:S(2)}) collective-permute-start(bf16[128,1024]{1,0:T(8,128)(2,1)} %refs_2_.1), channel_id=1, source_target_pairs={{0,1},{1,0},{2,3},{3,2},{4,5},{5,4},{6,7},{7,6},{8,9},{9,8},{10,11... | collective-permute-start | bytes 786440 | tf_op jit(solution)/shard_map/ppermute | solution.py:26
  1.1 0.1 pad_add_fusion.refs_0_
  1.2 1.0 %shard_map.84 = (bf16[128,1024]{1,0:T(8,128)(2,1)S(1)}, bf16[128,1024]{1,0:T(8,128)(2,1)S(1)}) custom-call(bf16[128,1024]{1,0:T(8,128)(2,1)} %refs_0_.1, bf16[128,1024]{1,0:T(8,128)(2,1)} %refs_1_.2), custom_call_target="tpu_custom_call" | custom-call | bytes 524288 | tf_op jit(solution)/shard_map/pallas_call | solution.py:55
  2.3 0.0 copy-start
  2.3 0.0 copy-start.1
  2.3 0.0 copy-start.2
  2.3 0.6 %shard_map.85 = (bf16[256,256]{1,0:T(8,128)(2,1)S(1)}, bf16[256,256]{1,0:T(8,128)(2,1)S(1)}, bf16[256,256]{1,0:T(8,128)(2,1)S(1)}, bf16[256,256]{1,0:T(8,128)(2,1)S(1)}) custom-call(s32[2]{0:T(128)S(1)} %pad_add_fusion.refs_0_, bf16[128,1024]{1,0:T(8,128)(2,1)S(1)} %get-tuple-element.55.refs_1_, bf16[128,1024]{1,0:T(8,128)(2,1)S(1)} %get-tuple-element.56.refs_2_), custom_call_target="tpu_custom_call" | custom-call | flops 6000000000 | bytes 524296 | tf_op jit(solution)/shard_map/pallas_call | solution.py:55
  2.9 3.5 %collective-permute-start = (bf16[256,256]{1,0:T(8,128)(2,1)S(1)}, bf16[256,256]{1,0:T(8,128)(2,1)S(1)}, u32[]{:S(2)}, u32[]{:S(2)}) collective-permute-start(bf16[256,256]{1,0:T(8,128)(2,1)S(1)} %get-tuple-element.58), channel_id=1, source_target_pairs={{0,6},{2,4},{4,2},{6,0},{8,14},{10,12},{12,10},{14,8},{16,22},{18,... | collective-permute-start | bytes 393224 | tf_op jit(solution)/shard_map/ppermute | solution.py:22
  6.5 0.5 %collective-permute-start.1 = (bf16[256,256]{1,0:T(8,128)(2,1)S(1)}, bf16[256,256]{1,0:T(8,128)(2,1)S(1)}, u32[]{:S(2)}, u32[]{:S(2)}) collective-permute-start(bf16[256,256]{1,0:T(8,128)(2,1)S(1)} %get-tuple-element.59), channel_id=1, source_target_pairs={{0,2},{2,0},{4,6},{6,4},{8,10},{10,8},{12,14},{14,12},{16,18},{18,... | collective-permute-start | bytes 393224 | tf_op jit(solution)/shard_map/ppermute | solution.py:22
  7.0 0.1 collective-permute-start.2
  7.1 0.0 collective-permute-done.3.refs_4_
  7.1 0.0 copy-done
  7.1 0.0 copy-done.1
  7.1 0.0 copy-done.2
  7.1 1.3 %shard_map.87 = (bf16[256,256]{1,0:T(8,128)(2,1)S(1)}, bf16[256,256]{1,0:T(8,128)(2,1)S(1)}, bf16[256,256]{1,0:T(8,128)(2,1)S(1)}, bf16[256,256]{1,0:T(8,128)(2,1)S(1)}) custom-call(s32[2]{0:T(128)S(1)} %pad_add_fusion.refs_0_, bf16[128,1024]{1,0:T(8,128)(2,1)S(1)} %copy-done.1, bf16[128,1024]{1,0:T(8,128)(2,1)S(1)} %copy-done.2, ...), custom_call_target="tpu_custom_call" | custom-call | flops 6000000000 | bytes 4980744 | tf_op jit(solution)/shard_map/pallas_call | solution.py:55
  8.4 2.0 %collective-permute-start.4 = (bf16[256,256]{1,0:T(8,128)(2,1)S(1)}, bf16[256,256]{1,0:T(8,128)(2,1)S(1)}, u32[]{:S(2)}, u32[]{:S(2)}) collective-permute-start(bf16[256,256]{1,0:T(8,128)(2,1)S(1)} %get-tuple-element.62), channel_id=1, source_target_pairs={{0,2},{2,0},{4,6},{6,4},{8,10},{10,8},{12,14},{14,12},{16,18},{18,... | collective-permute-start | bytes 393224 | tf_op jit(solution)/shard_map/ppermute | solution.py:22
  10.4 1.2 %shard_map.86.refs_1_ = bf16[1024,2048]{1,0:T(8,128)(2,1)S(1)} custom-call(bf16[2048,1024]{1,0:T(8,128)(2,1)S(1)} %copy-done), custom_call_target="tpu_custom_call" | custom-call | tf_op jit(solution)/shard_map/pallas_call | solution.py:55
  11.6 1.6 %collective-permute-start.5 = (bf16[256,256]{1,0:T(8,128)(2,1)S(1)}, bf16[256,256]{1,0:T(8,128)(2,1)S(1)}, u32[]{:S(2)}, u32[]{:S(2)}) collective-permute-start(bf16[256,256]{1,0:T(8,128)(2,1)S(1)} %get-tuple-element.65), channel_id=1, source_target_pairs={{0,4},{2,6},{4,0},{6,2},{8,12},{10,14},{12,8},{14,10},{16,20},{18,... | collective-permute-start | bytes 393224 | tf_op jit(solution)/shard_map/ppermute | solution.py:22
  13.2 0.0 collective-permute-done.refs_1_
  13.2 0.5 collective-permute-start.6
  13.7 0.4 collective-permute-done.1.refs_2_
  14.1 0.0 collective-permute-done.2.refs_3_
  14.1 2.8 %collective-permute-done.4.refs_5_ = bf16[256,256]{1,0:T(8,128)(2,1)S(1)} collective-permute-done((bf16[256,256]{1,0:T(8,128)(2,1)S(1)}, bf16[256,256]{1,0:T(8,128)(2,1)S(1)}, u32[]{:S(2)}, u32[]{:S(2)}) %collective-permute-start.4) | collective-permute-done | bytes 131104 | tf_op jit(solution)/shard_map/ppermute | solution.py:22
  16.9 0.3 shard_map.88
  17.2 1.6 %collective-permute-start.7 = (bf16[256,256]{1,0:T(8,128)(2,1)S(1)}, bf16[256,256]{1,0:T(8,128)(2,1)S(1)}, u32[]{:S(2)}, u32[]{:S(2)}) collective-permute-start(bf16[256,256]{1,0:T(8,128)(2,1)S(1)} %get-tuple-element.71), channel_id=1, source_target_pairs={{0,8},{2,10},{4,12},{6,14},{8,0},{10,2},{12,4},{14,6},{16,24},{18,... | collective-permute-start | bytes 393224 | tf_op jit(solution)/shard_map/ppermute | solution.py:22
  18.8 2.5 %collective-permute-start.9 = (bf16[128,256]{1,0:T(8,128)(2,1)S(1)}, bf16[128,256]{1,0:T(8,128)(2,1)S(1)}, u32[]{:S(2)}, u32[]{:S(2)}) collective-permute-start(bf16[128,256]{1,0:T(8,128)(2,1)S(1)} %get-tuple-element.72), channel_id=1, source_target_pairs={{0,24},{2,26},{4,28},{6,30},{8,16},{10,18},{12,20},{14,22},{16,8},... | collective-permute-start | bytes 196616 | tf_op jit(solution)/shard_map/ppermute | solution.py:22
  21.3 0.1 collective-permute-start.8
  21.4 0.0 collective-permute-done.5.refs_6_
  21.4 0.0 collective-permute-done.6.refs_7_
  21.4 4.7 %collective-permute-done.9.refs_10_ = bf16[128,256]{1,0:T(8,128)(2,1)S(1)} collective-permute-done((bf16[128,256]{1,0:T(8,128)(2,1)S(1)}, bf16[128,256]{1,0:T(8,128)(2,1)S(1)}, u32[]{:S(2)}, u32[]{:S(2)}) %collective-permute-start.9) | collective-permute-done | bytes 65568 | tf_op jit(solution)/shard_map/ppermute | solution.py:22
  26.1 1.4 %collective-permute-done.8.refs_9_ = bf16[128,256]{1,0:T(8,128)(2,1)S(1)} collective-permute-done((bf16[128,256]{1,0:T(8,128)(2,1)S(1)}, bf16[128,256]{1,0:T(8,128)(2,1)S(1)}, u32[]{:S(2)}, u32[]{:S(2)}) %collective-permute-start.8) | collective-permute-done | bytes 65568 | tf_op jit(solution)/shard_map/ppermute | solution.py:22
  27.5 0.0 collective-permute-done.7.refs_8_
  27.5 2.3 %shard_map.89 = (bf16[256,256]{1,0:T(8,128)(2,1)S(1)}, bf16[128,256]{1,0:T(8,128)(2,1)S(1)}, bf16[128,256]{1,0:T(8,128)(2,1)S(1)}, bf16[2,640,256]{2,1,0:T(8,128...) custom-call(bf16[256,256]{1,0:T(8,128)(2,1)S(1)} %get-tuple-element., ...), custom_call_target="tpu_custom_call" | custom-call | flops 503316480 | bytes 1310720 | tf_op jit(solution)/shard_map/pallas_call | solution.py:55
  29.8 0.7 %collective-permute-start.13 = (bf16[128,256]{1,0:T(8,128)(2,1)S(1)}, bf16[128,256]{1,0:T(8,128)(2,1)S(1)}, u32[]{:S(2)}, u32[]{:S(2)}) collective-permute-start(bf16[128,256]{1,0:T(8,128)(2,1)S(1)} %get-tuple-element.86), channel_id=1, source_target_pairs={{0,16},{2,18},{4,20},{6,22},{8,24},{10,26},{12,28},{14,30},{16,0},... | collective-permute-start | bytes 196616 | tf_op jit(solution)/shard_map/ppermute | solution.py:22
  30.5 1.7 %collective-permute-start.14 = (bf16[128,256]{1,0:T(8,128)(2,1)S(1)}, bf16[128,256]{1,0:T(8,128)(2,1)S(1)}, u32[]{:S(2)}, u32[]{:S(2)}) collective-permute-start(bf16[128,256]{1,0:T(8,128)(2,1)S(1)} %get-tuple-element.87), channel_id=1, source_target_pairs={{0,24},{2,26},{4,28},{6,30},{8,16},{10,18},{12,20},{14,22},{16,8},... | collective-permute-start | bytes 196616 | tf_op jit(solution)/shard_map/ppermute | solution.py:22
  32.2 1.2 %collective-permute-start.12 = (bf16[256,256]{1,0:T(8,128)(2,1)S(1)}, bf16[256,256]{1,0:T(8,128)(2,1)S(1)}, u32[]{:S(2)}, u32[]{:S(2)}) collective-permute-start(bf16[256,256]{1,0:T(8,128)(2,1)S(1)} %get-tuple-element.85), channel_id=1, source_target_pairs={{0,8},{2,10},{4,12},{6,14},{8,0},{10,2},{12,4},{14,6},{16,24},{18,... | collective-permute-start | bytes 393224 | tf_op jit(solution)/shard_map/ppermute | solution.py:22
  33.4 0.8 %shard_map.90 = (bf16[256,256]{1,0:T(8,128)(2,1)S(1)}, bf16[256,256]{1,0:T(8,128)(2,1)S(1)}, bf16[256,256]{1,0:T(8,128)(2,1)S(1)}, bf16[256,256]{1,0:T(8,128)(2,1)S(1)}) custom-call(bf16[2,640,256]{2,1,0:T(8,128)(2,1)S(1)} %get-tuple-element.73.refs_0_, bf16[2,640,256]{2,1,0:T(8,128)(2,1)S(1)} %get-tuple-element.74.refs_1_, ...), custom_call_target="tpu_custom_call" | custom-call | flops 6000000000 | bytes 4456448 | tf_op jit(solution)/shard_map/pallas_call | solution.py:55
  34.2 1.5 %collective-permute-start.10 = (bf16[256,256]{1,0:T(8,128)(2,1)S(1)}, bf16[256,256]{1,0:T(8,128)(2,1)S(1)}, u32[]{:S(2)}, u32[]{:S(2)}) collective-permute-start(bf16[256,256]{1,0:T(8,128)(2,1)S(1)} %get-tuple-element.79), channel_id=1, source_target_pairs={{0,6},{2,4},{4,2},{6,0},{8,14},{10,12},{12,10},{14,8},{16,22},{18,... | collective-permute-start | bytes 393224 | tf_op jit(solution)/shard_map/ppermute | solution.py:22
  35.7 0.5 %collective-permute-start.11 = (bf16[256,256]{1,0:T(8,128)(2,1)S(1)}, bf16[256,256]{1,0:T(8,128)(2,1)S(1)}, u32[]{:S(2)}, u32[]{:S(2)}) collective-permute-start(bf16[256,256]{1,0:T(8,128)(2,1)S(1)} %get-tuple-element.80), channel_id=1, source_target_pairs={{0,2},{2,0},{4,6},{6,4},{8,10},{10,8},{12,14},{14,12},{16,18},{18,... | collective-permute-start | bytes 393224 | tf_op jit(solution)/shard_map/ppermute | solution.py:22
  36.2 0.9 %shard_map.91 = (f32[512,256]{1,0:T(8,128)S(1)}, f32[512,256]{1,0:T(8,128)S(1)}) custom-call(bf16[2,256,256]{2,1,0:T(8,128)(2,1)S(1)} %get-tuple-element.82.refs_0_, bf16[2,256,256]{2,1,0:T(8,128)(2,1)S(1)} %get-tuple-element.83.refs_1_, bf16[4,256,640]{2,1,0:T(8,128)(2,1)S(1)} %get-tuple-element.75.refs_2_, bf16[4,256,640]{2,1,0:T(8,128)(2,1)S(1)} %get-tuple-element.76.refs_3_), custom_call_target="tpu_custom_call" | custom-call | flops 335544320 | bytes 3145728 | tf_op jit(solution)/shard_map/pallas_call | solution.py:55
  37.1 0.0 collective-permute-done.13.refs_3_
  37.1 0.0 collective-permute-done.14.refs_4_
  37.2 1.0 %collective-permute-done.12.refs_2_ = bf16[256,256]{1,0:T(8,128)(2,1)S(1)} collective-permute-done((bf16[256,256]{1,0:T(8,128)(2,1)S(1)}, bf16[256,256]{1,0:T(8,128)(2,1)S(1)}, u32[]{:S(2)}, u32[]{:S(2)}) %collective-permute-start.12) | collective-permute-done | bytes 131104 | tf_op jit(solution)/shard_map/ppermute | solution.py:22
  38.1 0.6 %collective-permute-start.15 = (bf16[256,256]{1,0:T(8,128)(2,1)S(1)}, bf16[256,256]{1,0:T(8,128)(2,1)S(1)}, u32[]{:S(2)}, u32[]{:S(2)}) collective-permute-start(bf16[256,256]{1,0:T(8,128)(2,1)S(1)} %get-tuple-element.88), channel_id=1, source_target_pairs={{0,4},{2,6},{4,0},{6,2},{8,12},{10,14},{12,8},{14,10},{16,20},{18,... | collective-permute-start | bytes 393224 | tf_op jit(solution)/shard_map/ppermute | solution.py:22
  38.8 0.4 shard_map.92
  39.1 1.6 %collective-permute-start.18 = (bf16[256,256]{1,0:T(8,128)(2,1)S(1)}, bf16[256,256]{1,0:T(8,128)(2,1)S(1)}, u32[]{:S(2)}, u32[]{:S(2)}) collective-permute-start(bf16[256,256]{1,0:T(8,128)(2,1)S(1)} %get-tuple-element.95), channel_id=1, source_target_pairs={{0,2},{2,0},{4,6},{6,4},{8,10},{10,8},{12,14},{14,12},{16,18},{18,... | collective-permute-start | bytes 393224 | tf_op jit(solution)/shard_map/ppermute | solution.py:22
  40.7 1.4 %collective-permute-start.19 = (bf16[256,256]{1,0:T(8,128)(2,1)S(1)}, bf16[256,256]{1,0:T(8,128)(2,1)S(1)}, u32[]{:S(2)}, u32[]{:S(2)}) collective-permute-start(bf16[256,256]{1,0:T(8,128)(2,1)S(1)} %get-tuple-element.96), channel_id=1, source_target_pairs={{0,4},{2,6},{4,0},{6,2},{8,12},{10,14},{12,8},{14,10},{16,20},{18,... | collective-permute-start | bytes 393224 | tf_op jit(solution)/shard_map/ppermute | solution.py:22
  42.1 0.0 collective-permute-done.10.refs_3_.refs_4_
  42.1 0.6 %collective-permute-start.17 = (bf16[256,256]{1,0:T(8,128)(2,1)S(1)}, bf16[256,256]{1,0:T(8,128)(2,1)S(1)}, u32[]{:S(2)}, u32[]{:S(2)}) collective-permute-start(bf16[256,256]{1,0:T(8,128)(2,1)S(1)} %get-tuple-element.97), channel_id=1, source_target_pairs={{0,6},{2,4},{4,2},{6,0},{8,14},{10,12},{12,10},{14,8},{16,22},{18,... | collective-permute-start | bytes 393224 | tf_op jit(solution)/shard_map/ppermute | solution.py:22
  42.7 0.0 collective-permute-done.11.refs_4_.refs_5_
  42.7 2.5 %collective-permute-done.15.refs_5_.refs_6_ = bf16[256,256]{1,0:T(8,128)(2,1)S(1)} collective-permute-done((bf16[256,256]{1,0:T(8,128)(2,1)S(1)}, bf16[256,256]{1,0:T(8,128)(2,1)S(1)}, u32[]{:S(2)}, u32[]{:S(2)}) %collective-permute-start.15) | collective-permute-done | bytes 131104 | tf_op jit(solution)/shard_map/ppermute | solution.py:22
  45.2 1.0 %shard_map.93 = (bf16[128,1024]{1,0:T(8,128)(2,1)S(1)}, bf16[128,1024]{1,0:T(8,128)(2,1)S(1)}) custom-call(s32[2]{0:T(128)S(1)} %pad_add_fusion.refs_0_, bf16[1024,2048]{1,0:T(8,128)(2,1)S(1)} %shard_map.86.refs_1_, bf16[256,256]{1,0:T(8,128)(2,1)S(1)} %get-tuple-element.98.refs_2_.refs_3_, bf16[256,256]{1,0:T(8,128)(2,1)S(1)} %collective-permute-done.10.refs_3_.refs_4_, ...), custom_call_target="tpu_custom_call" | custom-call | flops 268435456 | bytes 4718600 | tf_op jit(solution)/shard_map/pallas_call | solution.py:55
  46.2 0.1 collective-permute-start.16
  46.3 1.0 %shard_map.94 = (f32[128,1024]{1,0:T(8,128)S(1)}, bf16[128,1024]{1,0:T(8,128)(2,1)S(1)}) custom-call(s32[2]{0:T(128)S(1)} %pad_add_fusion.refs_0_, bf16[1024,2048]{1,0:T(8,128)(2,1)S(1)} %shard_map.86.refs_1_, bf16[128,1024]{1,0:T(8,128)(2,1)S(1)} %get-tuple-element.102.refs_2_, bf16[256,256]{1,0:T(8,128)(2,1)S(1)} %get-tuple-element.98.refs_2_.refs_3_, ...), custom_call_target="tpu_custom_call" | custom-call | flops 4000000000 | bytes 4980744 | tf_op jit(solution)/shard_map/pallas_call | solution.py:55
  47.3 0.5 %collective-permute-done.16.refs_0_ = bf16[128,1024]{1,0:T(8,128)(2,1)S(1)} collective-permute-done((bf16[128,1024]{1,0:T(8,128)(2,1)S(1)}, bf16[128,1024]{1,0:T(8,128)(2,1)S(1)}, u32[]{:S(2)}, u32[]{:S(2)}) %collective-permute-start.16) | collective-permute-done | bytes 262176 | tf_op jit(solution)/shard_map/ppermute | solution.py:26
  47.8 0.1 shard_map.95.refs_1_
  47.9 0.0 collective-permute-done.18.refs_5_
  47.9 0.2 collective-permute-done.19.refs_6_
  48.1 0.0 collective-permute-done.17.refs_4_
  48.1 1.5 %shard_map.96 = (bf16[128,1024]{1,0:T(8,128)(2,1)}, bf16[128,1024]{1,0:T(8,128)(2,1)}, bf16[128,1024]{1,0:T(8,128)(2,1)}, bf16[128,1024]{1,0:T(8,128)(2,1)}) custom-call(s32[2]{0:T(128)S(1)} %pad_add_fusion.refs_0_, bf16[128,1024]{1,0:T(8,128)(2,1)S(1)} %shard_map.95.refs_1_, bf16[128,1024]{1,0:T(8,128)(2,1)S(1)} %get-tuple-element.105.refs_2_, ...), custom_call_target="tpu_custom_call" | custom-call | bytes 1048584 | tf_op jit(solution)/shard_map/pallas_call | solution.py:55
Async XLA Ops:
  0.6 6.5 %collective-permute-start.3 = (bf16[128,1024]{1,0:T(8,128)(2,1)}, bf16[128,1024]{1,0:T(8,128)(2,1)S(1)}, u32[]{:S(2)}, u32[]{:S(2)}) collective-permute-start(bf16[128,1024]{1,0:T(8,128)(2,1)} %refs_2_.1), channel_id=1, source_target_pairs={{0,1},{1,0},{2,3},{3,2},{4,5},{5,4},{6,7},{7,6},{8,9},{9,8},{10,11... | collective-permute-start | bytes 786440 | tf_op jit(solution)/shard_map/ppermute | solution.py:26
  2.3 4.8 %copy-start = (bf16[2048,1024]{1,0:T(8,128)(2,1)S(1)}, bf16[2048,1024]{1,0:T(8,128)(2,1)}, u32[]{:S(2)}) copy-start(bf16[2048,1024]{1,0:T(8,128)(2,1)} %refs_3_.1) | copy-start | bytes 12582916
  2.3 4.8 %copy-start.1 = (bf16[128,1024]{1,0:T(8,128)(2,1)S(1)}, bf16[128,1024]{1,0:T(8,128)(2,1)}, u32[]{:S(2)}) copy-start(bf16[128,1024]{1,0:T(8,128)(2,1)} %refs_1_.3) | copy-start | bytes 786436
  2.3 4.8 %copy-start.2 = (bf16[128,1024]{1,0:T(8,128)(2,1)S(1)}, bf16[128,1024]{1,0:T(8,128)(2,1)}, u32[]{:S(2)}) copy-start(bf16[128,1024]{1,0:T(8,128)(2,1)} %refs_2_.1) | copy-start | bytes 786436
  2.9 10.3 %collective-permute-start = (bf16[256,256]{1,0:T(8,128)(2,1)S(1)}, bf16[256,256]{1,0:T(8,128)(2,1)S(1)}, u32[]{:S(2)}, u32[]{:S(2)}) collective-permute-start(bf16[256,256]{1,0:T(8,128)(2,1)S(1)} %get-tuple-element.58), channel_id=1, source_target_pairs={{0,6},{2,4},{4,2},{6,0},{8,14},{10,12},{12,10},{14,8},{16,22},{18,... | collective-permute-start | bytes 393224 | tf_op jit(solution)/shard_map/ppermute | solution.py:22
  6.5 7.7 %collective-permute-start.1 = (bf16[256,256]{1,0:T(8,128)(2,1)S(1)}, bf16[256,256]{1,0:T(8,128)(2,1)S(1)}, u32[]{:S(2)}, u32[]{:S(2)}) collective-permute-start(bf16[256,256]{1,0:T(8,128)(2,1)S(1)} %get-tuple-element.59), channel_id=1, source_target_pairs={{0,2},{2,0},{4,6},{6,4},{8,10},{10,8},{12,14},{14,12},{16,18},{18,... | collective-permute-start | bytes 393224 | tf_op jit(solution)/shard_map/ppermute | solution.py:22
  7.0 7.1 %collective-permute-start.2 = (bf16[256,256]{1,0:T(8,128)(2,1)S(1)}, bf16[256,256]{1,0:T(8,128)(2,1)S(1)}, u32[]{:S(2)}, u32[]{:S(2)}) collective-permute-start(bf16[256,256]{1,0:T(8,128)(2,1)S(1)} %get-tuple-element.60), channel_id=1, source_target_pairs={{0,4},{2,6},{4,0},{6,2},{8,12},{10,14},{12,8},{14,10},{16,20},{18,... | collective-permute-start | bytes 393224 | tf_op jit(solution)/shard_map/ppermute | solution.py:22
  8.4 8.5 %collective-permute-start.4 = (bf16[256,256]{1,0:T(8,128)(2,1)S(1)}, bf16[256,256]{1,0:T(8,128)(2,1)S(1)}, u32[]{:S(2)}, u32[]{:S(2)}) collective-permute-start(bf16[256,256]{1,0:T(8,128)(2,1)S(1)} %get-tuple-element.62), channel_id=1, source_target_pairs={{0,2},{2,0},{4,6},{6,4},{8,10},{10,8},{12,14},{14,12},{16,18},{18,... | collective-permute-start | bytes 393224 | tf_op jit(solution)/shard_map/ppermute | solution.py:22
  11.6 9.8 %collective-permute-start.5 = (bf16[256,256]{1,0:T(8,128)(2,1)S(1)}, bf16[256,256]{1,0:T(8,128)(2,1)S(1)}, u32[]{:S(2)}, u32[]{:S(2)}) collective-permute-start(bf16[256,256]{1,0:T(8,128)(2,1)S(1)} %get-tuple-element.65), channel_id=1, source_target_pairs={{0,4},{2,6},{4,0},{6,2},{8,12},{10,14},{12,8},{14,10},{16,20},{18,... | collective-permute-start | bytes 393224 | tf_op jit(solution)/shard_map/ppermute | solution.py:22
  13.2 8.2 %collective-permute-start.6 = (bf16[256,256]{1,0:T(8,128)(2,1)S(1)}, bf16[256,256]{1,0:T(8,128)(2,1)S(1)}, u32[]{:S(2)}, u32[]{:S(2)}) collective-permute-start(bf16[256,256]{1,0:T(8,128)(2,1)S(1)} %get-tuple-element.66), channel_id=1, source_target_pairs={{0,6},{2,4},{4,2},{6,0},{8,14},{10,12},{12,10},{14,8},{16,22},{18,... | collective-permute-start | bytes 393224 | tf_op jit(solution)/shard_map/ppermute | solution.py:22
  17.2 10.3 %collective-permute-start.7 = (bf16[256,256]{1,0:T(8,128)(2,1)S(1)}, bf16[256,256]{1,0:T(8,128)(2,1)S(1)}, u32[]{:S(2)}, u32[]{:S(2)}) collective-permute-start(bf16[256,256]{1,0:T(8,128)(2,1)S(1)} %get-tuple-element.71), channel_id=1, source_target_pairs={{0,8},{2,10},{4,12},{6,14},{8,0},{10,2},{12,4},{14,6},{16,24},{18,... | collective-permute-start | bytes 393224 | tf_op jit(solution)/shard_map/ppermute | solution.py:22
  18.8 7.3 %collective-permute-start.9 = (bf16[128,256]{1,0:T(8,128)(2,1)S(1)}, bf16[128,256]{1,0:T(8,128)(2,1)S(1)}, u32[]{:S(2)}, u32[]{:S(2)}) collective-permute-start(bf16[128,256]{1,0:T(8,128)(2,1)S(1)} %get-tuple-element.72), channel_id=1, source_target_pairs={{0,24},{2,26},{4,28},{6,30},{8,16},{10,18},{12,20},{14,22},{16,8},... | collective-permute-start | bytes 196616 | tf_op jit(solution)/shard_map/ppermute | solution.py:22
  21.3 6.2 %collective-permute-start.8 = (bf16[128,256]{1,0:T(8,128)(2,1)S(1)}, bf16[128,256]{1,0:T(8,128)(2,1)S(1)}, u32[]{:S(2)}, u32[]{:S(2)}) collective-permute-start(bf16[128,256]{1,0:T(8,128)(2,1)S(1)} %get-tuple-element.72), channel_id=1, source_target_pairs={{0,16},{2,18},{4,20},{6,22},{8,24},{10,26},{12,28},{14,30},{16,0},... | collective-permute-start | bytes 196616 | tf_op jit(solution)/shard_map/ppermute | solution.py:22
  29.8 7.3 %collective-permute-start.13 = (bf16[128,256]{1,0:T(8,128)(2,1)S(1)}, bf16[128,256]{1,0:T(8,128)(2,1)S(1)}, u32[]{:S(2)}, u32[]{:S(2)}) collective-permute-start(bf16[128,256]{1,0:T(8,128)(2,1)S(1)} %get-tuple-element.86), channel_id=1, source_target_pairs={{0,16},{2,18},{4,20},{6,22},{8,24},{10,26},{12,28},{14,30},{16,0},... | collective-permute-start | bytes 196616 | tf_op jit(solution)/shard_map/ppermute | solution.py:22
  30.5 6.7 %collective-permute-start.14 = (bf16[128,256]{1,0:T(8,128)(2,1)S(1)}, bf16[128,256]{1,0:T(8,128)(2,1)S(1)}, u32[]{:S(2)}, u32[]{:S(2)}) collective-permute-start(bf16[128,256]{1,0:T(8,128)(2,1)S(1)} %get-tuple-element.87), channel_id=1, source_target_pairs={{0,24},{2,26},{4,28},{6,30},{8,16},{10,18},{12,20},{14,22},{16,8},... | collective-permute-start | bytes 196616 | tf_op jit(solution)/shard_map/ppermute | solution.py:22
  32.2 6.0 %collective-permute-start.12 = (bf16[256,256]{1,0:T(8,128)(2,1)S(1)}, bf16[256,256]{1,0:T(8,128)(2,1)S(1)}, u32[]{:S(2)}, u32[]{:S(2)}) collective-permute-start(bf16[256,256]{1,0:T(8,128)(2,1)S(1)} %get-tuple-element.85), channel_id=1, source_target_pairs={{0,8},{2,10},{4,12},{6,14},{8,0},{10,2},{12,4},{14,6},{16,24},{18,... | collective-permute-start | bytes 393224 | tf_op jit(solution)/shard_map/ppermute | solution.py:22
  34.2 7.8 %collective-permute-start.10 = (bf16[256,256]{1,0:T(8,128)(2,1)S(1)}, bf16[256,256]{1,0:T(8,128)(2,1)S(1)}, u32[]{:S(2)}, u32[]{:S(2)}) collective-permute-start(bf16[256,256]{1,0:T(8,128)(2,1)S(1)} %get-tuple-element.79), channel_id=1, source_target_pairs={{0,6},{2,4},{4,2},{6,0},{8,14},{10,12},{12,10},{14,8},{16,22},{18,... | collective-permute-start | bytes 393224 | tf_op jit(solution)/shard_map/ppermute | solution.py:22
  35.7 7.0 %collective-permute-start.11 = (bf16[256,256]{1,0:T(8,128)(2,1)S(1)}, bf16[256,256]{1,0:T(8,128)(2,1)S(1)}, u32[]{:S(2)}, u32[]{:S(2)}) collective-permute-start(bf16[256,256]{1,0:T(8,128)(2,1)S(1)} %get-tuple-element.80), channel_id=1, source_target_pairs={{0,2},{2,0},{4,6},{6,4},{8,10},{10,8},{12,14},{14,12},{16,18},{18,... | collective-permute-start | bytes 393224 | tf_op jit(solution)/shard_map/ppermute | solution.py:22
  38.1 7.1 %collective-permute-start.15 = (bf16[256,256]{1,0:T(8,128)(2,1)S(1)}, bf16[256,256]{1,0:T(8,128)(2,1)S(1)}, u32[]{:S(2)}, u32[]{:S(2)}) collective-permute-start(bf16[256,256]{1,0:T(8,128)(2,1)S(1)} %get-tuple-element.88), channel_id=1, source_target_pairs={{0,4},{2,6},{4,0},{6,2},{8,12},{10,14},{12,8},{14,10},{16,20},{18,... | collective-permute-start | bytes 393224 | tf_op jit(solution)/shard_map/ppermute | solution.py:22
  39.1 8.7 %collective-permute-start.18 = (bf16[256,256]{1,0:T(8,128)(2,1)S(1)}, bf16[256,256]{1,0:T(8,128)(2,1)S(1)}, u32[]{:S(2)}, u32[]{:S(2)}) collective-permute-start(bf16[256,256]{1,0:T(8,128)(2,1)S(1)} %get-tuple-element.95), channel_id=1, source_target_pairs={{0,2},{2,0},{4,6},{6,4},{8,10},{10,8},{12,14},{14,12},{16,18},{18,... | collective-permute-start | bytes 393224 | tf_op jit(solution)/shard_map/ppermute | solution.py:22
  40.7 7.4 %collective-permute-start.19 = (bf16[256,256]{1,0:T(8,128)(2,1)S(1)}, bf16[256,256]{1,0:T(8,128)(2,1)S(1)}, u32[]{:S(2)}, u32[]{:S(2)}) collective-permute-start(bf16[256,256]{1,0:T(8,128)(2,1)S(1)} %get-tuple-element.96), channel_id=1, source_target_pairs={{0,4},{2,6},{4,0},{6,2},{8,12},{10,14},{12,8},{14,10},{16,20},{18,... | collective-permute-start | bytes 393224 | tf_op jit(solution)/shard_map/ppermute | solution.py:22
  42.1 6.0 %collective-permute-start.17 = (bf16[256,256]{1,0:T(8,128)(2,1)S(1)}, bf16[256,256]{1,0:T(8,128)(2,1)S(1)}, u32[]{:S(2)}, u32[]{:S(2)}) collective-permute-start(bf16[256,256]{1,0:T(8,128)(2,1)S(1)} %get-tuple-element.97), channel_id=1, source_target_pairs={{0,6},{2,4},{4,2},{6,0},{8,14},{10,12},{12,10},{14,8},{16,22},{18,... | collective-permute-start | bytes 393224 | tf_op jit(solution)/shard_map/ppermute | solution.py:22
  46.2 1.6 %collective-permute-start.16 = (bf16[128,1024]{1,0:T(8,128)(2,1)S(1)}, bf16[128,1024]{1,0:T(8,128)(2,1)S(1)}, u32[]{:S(2)}, u32[]{:S(2)}) collective-permute-start(bf16[128,1024]{1,0:T(8,128)(2,1)S(1)} %get-tuple-element.104), channel_id=1, source_target_pairs={{0,1},{1,0},{2,3},{3,2},{4,5},{5,4},{6,7},{7,6},{8,9},{9,8},{10,11... | collective-permute-start | bytes 786440 | tf_op jit(solution)/shard_map/ppermute | solution.py:26
